TPU v7x, 32 devices: a whole 2x2x4 slice. The times are simulated.
32 devices in a mesh: cam: 8 (over z, x), row: 4 (over y, core).
Axes of the slice: x: 2, y: 2, z: 4, core: 2. Of those that a mesh axis runs over, the one named last changes fastest.
Arguments:
- features_in: bfloat16 [8, 16, 128, 128], P('cam', 'row'), may hold values from -6 to 6
- conv_weight: bfloat16 [3, 3, 128, 128], replicated, may hold values from -0.1875 to 0.1875
- q_weight: bfloat16 [128, 128], replicated, may hold values from -0.5 to 0.5
- k_weight: bfloat16 [128, 128], replicated, may hold values from -0.5 to 0.5
- v_weight: bfloat16 [128, 128], replicated, may hold values from -0.5 to 0.5
- partners: int32 [8, 2], replicated, may hold values from 0 to 7, as said below
- band_widths: int32 [8, 2], replicated, may hold values from 1 to 3, as said below
- bands: int32 [8, 16, 2, 3], P('cam', 'row'), may hold values from 0 to 15, as said below
- grad_attended: bfloat16 [8, 16, 128, 128], P('cam', 'row'), may hold values from -6 to 6
Outputs:
- attended: bfloat16 [8, 16, 128, 128], P('cam', 'row')
- grad_features: bfloat16 [8, 16, 128, 128], P('cam', 'row')
Inputs may be any that keep to these rules, and one draw needn't show every extreme that they name: `partners`: view c is camera c // 1 of sample c % 1; partner 0 of view c is view c - 1 or c - 2 and partner 1 is view c + 1 or c + 2, modulo 8, so both are cameras of the same sample next or next but one in the cyclic order of its 8 cameras. `band_widths`: some view and partner have 3 live slots and some have 1. `bands`: entries are block numbers of the partner view; a block is one image row, so the block number is the image row; the 3 entries of a list are distinct and lie in image rows 4 * s - 2 to 4 * (s + 1) + 1, where s is the query block's image row // 4.
All inputs are finite; a program needn't handle non-finite values.
Results may differ from a plain program's by a relative error of at most 0.011.
Values may be sent and summed in bfloat16 or wider, within the bound.
No kernel may reach another device: no remote copies, remote signals or barrier semaphores. Data moves between devices by JAX's collectives and lax.ppermute only.
A program may use at most 64 MiB of HBM per device.

v0:
```python
import jax
import jax.numpy as jnp
from jax import lax
from jax.sharding import PartitionSpec as P

BLOCK = 128
MARGIN = 2
BAND = 3


def from_behind(value, axis, steps):
    count = lax.axis_size(axis)
    pairs = [(source, (source + steps) % count) for source in range(count)]
    return lax.ppermute(value, axis, pairs)


def passed_along(block, axis, distance):
    devices = range(lax.axis_size(axis))
    route = [(i - distance, i) for i in devices if i - distance in devices]
    return lax.ppermute(block, axis, route)


def padded_2(shard, sides, width):
    for axis, dim in sides:
        peers, length = (lax.axis_size(axis), shard.shape[dim])
        up = [(i, (i + 1) % peers) for i in range(peers - 1)]
        down = [(j, i) for i, j in up]
        last = lax.slice_in_dim(shard, length - width, length, axis=dim)
        leading = lax.slice_in_dim(shard, 0, width, axis=dim)
        before = lax.ppermute(last, axis, up)
        after = lax.ppermute(leading, axis, down)
        shard = jnp.concatenate([before, shard, after], axis=dim)
    return shard


def conv_slab(padded, conv_weight, out_rows):
    img_width = padded.shape[1]
    channels = padded.shape[2]
    side_zero = jnp.zeros((padded.shape[0], 1, channels), padded.dtype)
    framed = jnp.concatenate([side_zero, padded, side_zero], axis=1)
    total = jnp.zeros((out_rows * img_width, conv_weight.shape[3]), jnp.float32)
    for row_off in range(3):
        for col_off in range(3):
            patch = framed[row_off : row_off + out_rows, col_off : col_off + img_width].reshape(
                out_rows * img_width, channels
            )
            total = total + jnp.dot(
                patch, conv_weight[row_off, col_off], preferred_element_type=jnp.float32
            )
    return total.astype(jnp.bfloat16)


def offsets_of(partners, camera, views):
    pair_row = lax.dynamic_index_in_dim(partners, jnp.mod(camera, views), 0, keepdims=False)
    return (jnp.mod(camera - pair_row[0], views), jnp.mod(pair_row[1] - camera, views))


def view_shift(window, step_by):
    return from_behind(window, "cam", step_by)


def send_back(window, step_by):
    return from_behind(window.astype(jnp.bfloat16), "cam", step_by).astype(window.dtype)


def row_back(window, step_by):
    return passed_along(window.astype(jnp.bfloat16), "row", step_by).astype(window.dtype)


def local(
    features_in,
    conv_weight,
    q_weight,
    k_weight,
    v_weight,
    partners,
    band_widths,
    bands,
    grad_attended,
):
    image = features_in[0]
    slab_rows = image.shape[0]
    img_width = image.shape[1]
    channels = image.shape[2]
    margin_rows = MARGIN
    per_row = img_width // BLOCK
    win_rows = slab_rows + 2 * margin_rows
    high = lax.Precision.HIGHEST
    kv_weight = jnp.concatenate([k_weight, v_weight], axis=1)
    extended = padded_2(image, (("row", 0),), margin_rows + 1)
    hidden_win = conv_slab(extended, conv_weight, win_rows)
    kv_window = jnp.dot(hidden_win, kv_weight, preferred_element_type=jnp.float32).astype(
        jnp.bfloat16
    )
    kv_window = kv_window.reshape(win_rows, img_width, 2 * channels)
    hidden = hidden_win.reshape(win_rows, img_width, channels)[
        margin_rows : margin_rows + slab_rows
    ]
    hidden = hidden.reshape(slab_rows * img_width, channels)
    queries = jnp.dot(hidden, q_weight, preferred_element_type=jnp.float32).astype(jnp.bfloat16)
    views = lax.axis_size("cam")
    samples = views // min(16, views)
    camera = lax.axis_index("cam")
    slab = lax.axis_index("row")
    before, after = offsets_of(partners, camera, views)
    near_left = view_shift(kv_window, samples)
    far_left = view_shift(kv_window, 2 * samples)
    near_right = view_shift(kv_window, -samples)
    far_right = view_shift(kv_window, -2 * samples)
    left_win = jnp.where(before == samples, near_left, far_left)
    right_win = jnp.where(after == samples, near_right, far_right)
    q_blocks_dev = slab_rows * per_row
    win_blocks = win_rows * per_row
    key_count = 2 * BAND * BLOCK
    local_ids = bands[0] - per_row * (slab * slab_rows - margin_rows)

    def pick_blocks(window, side_idx):
        return jnp.take(window, local_ids[:, side_idx, :], axis=0)

    chosen = jnp.concatenate([pick_blocks(left_win, 0), pick_blocks(right_win, 1)], axis=1)
    chosen = chosen.reshape(q_blocks_dev, key_count, 2 * channels)
    key_rows = chosen[:, :, :channels]
    value_rows = chosen[:, :, channels:]
    widths_here = lax.dynamic_index_in_dim(band_widths, camera, 0, keepdims=False)
    slots = jnp.arange(BAND, dtype=jnp.int32)
    live = jnp.repeat(jnp.concatenate([slots < widths_here[0], slots < widths_here[1]]), BLOCK)
    inverse_square_root = channels ** (-0.5)
    query_block = queries.reshape(q_blocks_dev, BLOCK, channels)
    score_matrix = (
        jnp.einsum("apx,anx->apn", query_block, key_rows, preferred_element_type=jnp.float32)
        * inverse_square_root
    )
    expo = jnp.where(live, jnp.exp(score_matrix), 0.0)
    probs = expo / jnp.sum(expo, axis=2, keepdims=True)
    probabilities_halfwidth = probs.astype(jnp.bfloat16)
    attended = jnp.einsum(
        "zld,zdi->zli", probabilities_halfwidth, value_rows, preferred_element_type=jnp.float32
    ).astype(jnp.bfloat16)
    incoming_gradient = grad_attended[0]
    probability_gradient = jnp.einsum(
        "apx,anx->apn", incoming_gradient, value_rows, preferred_element_type=jnp.float32
    )
    delta = jnp.sum(probs * probability_gradient, axis=2, keepdims=True)
    score_gradient = (probs * (probability_gradient - delta)).astype(jnp.bfloat16)
    query_gradient = (
        jnp.einsum("zld,zdi->zli", score_gradient, key_rows, preferred_element_type=jnp.float32)
        * inverse_square_root
    )
    key_gradient = (
        jnp.einsum("wds,wdm->wsm", score_gradient, query_block, preferred_element_type=jnp.float32)
        * inverse_square_root
    )
    value_gradient = jnp.einsum(
        "wds,wdm->wsm",
        probabilities_halfwidth,
        incoming_gradient,
        preferred_element_type=jnp.float32,
    )
    grad_pairs = jnp.concatenate([key_gradient, value_gradient], axis=2).reshape(
        q_blocks_dev, 2, BAND, BLOCK, 2 * channels
    )
    back_weight = kv_weight.astype(jnp.float32).T

    def window_grad(side_idx):
        summed = (
            jnp.zeros((win_blocks, BLOCK, 2 * channels), jnp.float32)
            .at[local_ids[:, side_idx, :]]
            .add(grad_pairs[:, side_idx])
        )
        projected = jnp.dot(
            summed.reshape(win_rows * img_width, 2 * channels), back_weight, precision=high
        )
        return projected.reshape(win_rows, img_width, channels)

    grad_left = window_grad(0)
    grad_right = window_grad(1)
    window_total = jnp.zeros_like(grad_left)
    for distance in (1, 2):
        step_by = distance * samples
        window_total = window_total + send_back(
            jnp.where(before == step_by, grad_left, 0.0), -step_by
        )
        window_total = window_total + send_back(
            jnp.where(after == step_by, grad_right, 0.0), step_by
        )
    center = window_total[margin_rows : margin_rows + slab_rows]
    lower_in = row_back(window_total[:margin_rows], -1)
    upper_in = row_back(window_total[margin_rows + slab_rows :], 1)
    center = center.at[slab_rows - margin_rows :].add(lower_in)
    center = center.at[:margin_rows].add(upper_in)
    grad_own = jnp.dot(
        query_gradient.reshape(-1, channels), q_weight.astype(jnp.float32).T, precision=high
    )
    grad_features = (grad_own.reshape(slab_rows, img_width, channels) + center).astype(jnp.bfloat16)
    return (attended[None], grad_features[None])


def solution(mesh):
    placed = (
        P("cam", "row", None, None),
        P(),
        P(),
        P(),
        P(),
        P(),
        P(),
        P("cam", "row", None, None),
        P("cam", "row", None, None),
    )
    return jax.shard_map(
        local,
        mesh=mesh,
        in_specs=placed,
        out_specs=(P("cam", "row", None, None), P("cam", "row", None, None)),
        check_vma=False,
    )
```

profile of v0, /device:TPU:1, one launch (start us, length us, event | category | flops | bytes accessed | tf_op | source)
XLA Modules:
  0.0 112.0 jit_solution(12650004785452114672)
XLA Ops:
  1.6 4.5 %collective-permute-start = (bf16[3,128,128]{2,1,0:T(8,128)(2,1)S(1)}, bf16[3,128,128]{2,1,0:T(8,128)(2,1)S(1)}, u32[]{:S(2)}, u32[]{:S(2)}) collective-permute-start(bf16[3,128,128]{2,1,0:T(8,128)(2,1)S(1)} %get-tuple-element.46), channel_id=1, source_target_pairs={{0,1},{1,2},{2,3},{4,5},{5,6},{6,7},{8,9},{9,10},{10,11},{12,13},{... | collective-permute-start | bytes 294920 | tf_op jit(solution)/shard_map/ppermute | solution.py:30
  6.2 1.9 %collective-permute-start.1 = (bf16[3,128,128]{2,1,0:T(8,128)(2,1)S(1)}, bf16[3,128,128]{2,1,0:T(8,128)(2,1)S(1)}, u32[]{:S(2)}, u32[]{:S(2)}) collective-permute-start(bf16[3,128,128]{2,1,0:T(8,128)(2,1)S(1)} %get-tuple-element.47), channel_id=1, source_target_pairs={{1,0},{2,1},{3,2},{5,4},{6,5},{7,6},{9,8},{10,9},{11,10},{13,12},{... | collective-permute-start | bytes 294920 | tf_op jit(solution)/shard_map/ppermute | solution.py:31
  12.6 1.3 %iota_compare_fusion = (pred[3]{0:T(512)(128)(4,1)S(1)}, pred[3]{0:T(512)(128)(4,1)S(1)}) fusion(s32[]{:T(128)} %bitcast.1, s32[]{:T(128)} %bitcast), kind=kLoop, calls=%fused_computation.104 | loop fusion | flops 6 | bytes 14 | tf_op jit(solution)/shard_map/lt | solution.py:126
  19.7 3.3 %collective-permute-start.5 = (bf16[8,128,256]{2,1,0:T(8,128)(2,1)}, bf16[8,128,256]{2,1,0:T(8,128)(2,1)S(1)}, u32[]{:S(2)}, u32[]{:S(2)}) collective-permute-start(bf16[8,128,256]{2,1,0:T(8,128)(2,1)} %bitcast.28), channel_id=1, source_target_pairs={{0,24},{4,28},{8,0},{12,4},{16,8},{20,12},{24,16},{28,20},{1,25},{... | collective-permute-start | bytes 1572872 | tf_op jit(solution)/shard_map/ppermute | solution.py:14
  24.2 1.3 %collective-permute-start.3 = (bf16[8,128,256]{2,1,0:T(8,128)(2,1)}, bf16[8,128,256]{2,1,0:T(8,128)(2,1)S(1)}, u32[]{:S(2)}, u32[]{:S(2)}) collective-permute-start(bf16[8,128,256]{2,1,0:T(8,128)(2,1)} %bitcast.28), channel_id=1, source_target_pairs={{0,8},{4,12},{8,16},{12,20},{16,24},{20,28},{24,0},{28,4},{1,9},{5... | collective-permute-start | bytes 1572872 | tf_op jit(solution)/shard_map/ppermute | solution.py:14
  27.4 7.8 %collective-permute-done.5 = bf16[8,128,256]{2,1,0:T(8,128)(2,1)S(1)} collective-permute-done((bf16[8,128,256]{2,1,0:T(8,128)(2,1)}, bf16[8,128,256]{2,1,0:T(8,128)(2,1)S(1)}, u32[]{:S(2)}, u32[]{:S(2)}) %collective-permute-start.5) | collective-permute-done | bytes 524320 | tf_op jit(solution)/shard_map/ppermute | solution.py:14
  35.2 11.3 %collective-permute-done.4 = bf16[8,128,256]{2,1,0:T(8,128)(2,1)S(1)} collective-permute-done((bf16[8,128,256]{2,1,0:T(8,128)(2,1)}, bf16[8,128,256]{2,1,0:T(8,128)(2,1)S(1)}, u32[]{:S(2)}, u32[]{:S(2)}) %collective-permute-start.4) | collective-permute-done | bytes 524320 | tf_op jit(solution)/shard_map/ppermute | solution.py:14
  47.2 9.5 %collective-permute-done.3 = bf16[8,128,256]{2,1,0:T(8,128)(2,1)S(1)} collective-permute-done((bf16[8,128,256]{2,1,0:T(8,128)(2,1)}, bf16[8,128,256]{2,1,0:T(8,128)(2,1)S(1)}, u32[]{:S(2)}, u32[]{:S(2)}) %collective-permute-start.3) | collective-permute-done | bytes 524320 | tf_op jit(solution)/shard_map/ppermute | solution.py:14
  58.6 1.7 %fusion.9 = f32[4,768,128]{1,2,0:T(8,128)} fusion(bf16[4,768,256]{2,1,0:T(8,128)(2,1)S(1)} %bitcast.123, bf16[1,4,128,128]{3,2,1,0:T(8,128)(2,1)S(1)} %copy-done), kind=kOutput, calls=%fused_computation.34 | convolution fusion | flops 100663296 | bytes 2490368 | tf_op jit(solution)/shard_map/apx,anx->apn/dot_general | solution.py:140
  60.3 2.2 %fusion = (f32[4,128]{1,0:T(4,128)S(1)}, f32[4,128,768]{2,1,0:T(8,128)S(1)}) fusion(f32[4,768,128]{1,2,0:T(8,128)} %fusion.9, bf16[4,128,128]{2,1,0:T(8,128)(2,1)S(1)} %bitcast.141, pred[768]{0:T(1024)(128)(4,1)S(1)} %broadcast_bitcast_fusion, bf16[4,768,256]{2,1,0:T(8,128)(2,1)S(1)} %bitcast.124), kind=kOutput, calls=%fused_computation.8 | convolution fusion | flops 102630144 | bytes 4066304 | tf_op jit(solution)/shard_map/div | solution.py:134
  65.2 1.9 %pad_maximum_fusion = f32[4,768,256]{1,2,0:T(8,128)} fusion(f32[4,768,128]{1,2,0:T(8,128)S(1)} %fusion.14, f32[4,768,128]{1,2,0:T(8,128)S(1)} %convolution_multiply_fusion), kind=kLoop, calls=%fused_computation.4 | loop fusion | flops 786432 | bytes 6291456 | tf_op jit(solution)/shard_map/concatenate | solution.py:159
  67.1 3.5 %copy.26 = f32[4,768,256]{2,1,0:T(8,128)} copy(f32[4,768,256]{1,2,0:T(8,128)} %pad_maximum_fusion) | data formatting | bytes 6291456 | tf_op jit(solution)/shard_map/concatenate | solution.py:159
  70.6 3.9 %fusion.47 = (f32[4,1,3,128,256]{4,3,2,1,0:T(8,128)}, f32[4,1,3,128,256]{4,3,2,1,0:T(8,128)}) fusion(f32[4,2,3,128,256]{4,3,2,1,0:T(8,128)} %bitcast.122), kind=kLoop, calls=%fused_computation.107 | loop fusion | bytes 6291456 | tf_op jit(solution)/shard_map/slice | solution.py:168
  74.6 3.1 %scatter_fusion.1 = f32[8,128,256]{2,1,0:T(8,128)S(1)} fusion(f32[8,128,256]{2,1,0:T(8,128)S(1)} %broadcast.99.clone, s32[12]{0:T(128)S(1)} %reshape.237, f32[12,128,256]{2,1,0:T(8,128)} %bitcast.128), kind=kCustom, calls=%fused_computation.3 | custom fusion | flops 393216 | bytes 4718640 | tf_op jit(solution)/shard_map/scatter-add | solution.py:168
  77.7 2.3 %select_convert_fusion.2 = (bf16[8,128,128]{2,1,0:T(8,128)(2,1)}, bf16[8,128,128]{2,1,0:T(8,128)(2,1)}) fusion(pred[]{:T(512)S(6)} %eq.19, pred[]{:T(512)S(6)} %eq.21, f32[8,128,256]{2,1,0:T(8,128)S(1)} %scatter_fusion.1, bf16[128,256]{1,0:T(8,128)(2,1)} %copy-done.4), kind=kOutput, calls=%fused_computation.42 | convolution fusion | flops 402915328 | bytes 1638402 | tf_op jit(solution)/shard_map/dot_general | solution.py:170
  80.0 1.3 %collective-permute-start.9 = (bf16[8,128,128]{2,1,0:T(8,128)(2,1)}, bf16[8,128,128]{2,1,0:T(8,128)(2,1)}, u32[]{:S(2)}, u32[]{:S(2)}) collective-permute-start(bf16[8,128,128]{2,1,0:T(8,128)(2,1)} %get-tuple-element.45), channel_id=1, source_target_pairs={{0,8},{4,12},{8,16},{12,20},{16,24},{20,28},{24,0},{28,4},{1,9},{5... | collective-permute-start | bytes 786440 | tf_op jit(solution)/shard_map/ppermute | solution.py:14
  81.4 3.1 %scatter_fusion = f32[8,128,256]{2,1,0:T(8,128)S(1)} fusion(f32[8,128,256]{2,1,0:T(8,128)S(1)} %broadcast.99.clone.1, s32[12]{0:T(128)S(1)} %reshape.229, f32[12,128,256]{2,1,0:T(8,128)} %bitcast.127), kind=kCustom, calls=%fused_computation.2 | custom fusion | flops 393216 | bytes 4718640 | tf_op jit(solution)/shard_map/scatter-add | solution.py:168
  84.6 1.6 %select_convert_fusion.3 = (bf16[8,128,128]{2,1,0:T(8,128)(2,1)S(1)}, bf16[8,128,128]{2,1,0:T(8,128)(2,1)S(1)}) fusion(pred[]{:T(512)S(6)} %eq.18, pred[]{:T(512)S(6)} %eq.20, f32[8,128,256]{2,1,0:T(8,128)S(1)} %scatter_fusion, bf16[128,256]{1,0:T(8,128)(2,1)} %copy-done.4), kind=kOutput, calls=%fused_computation.43 | convolution fusion | flops 402915328 | bytes 1638402 | tf_op jit(solution)/shard_map/dot_general | solution.py:170
  86.1 4.2 %collective-permute-start.6 = (bf16[8,128,128]{2,1,0:T(8,128)(2,1)S(1)}, bf16[8,128,128]{2,1,0:T(8,128)(2,1)S(1)}, u32[]{:S(2)}, u32[]{:S(2)}) collective-permute-start(bf16[8,128,128]{2,1,0:T(8,128)(2,1)S(1)} %get-tuple-element.42), channel_id=1, source_target_pairs={{0,28},{4,0},{8,4},{12,8},{16,12},{20,16},{24,20},{28,24},{1,29},{... | collective-permute-start | bytes 786440 | tf_op jit(solution)/shard_map/ppermute | solution.py:14
  91.1 5.3 %collective-permute-done.6 = bf16[8,128,128]{2,1,0:T(8,128)(2,1)S(1)} collective-permute-done((bf16[8,128,128]{2,1,0:T(8,128)(2,1)S(1)}, bf16[8,128,128]{2,1,0:T(8,128)(2,1)S(1)}, u32[]{:S(2)}, u32[]{:S(2)}) %collective-permute-start.6) | collective-permute-done | bytes 262176 | tf_op jit(solution)/shard_map/ppermute | solution.py:14
  96.4 5.5 %collective-permute-done.8 = bf16[8,128,128]{2,1,0:T(8,128)(2,1)S(1)} collective-permute-done((bf16[8,128,128]{2,1,0:T(8,128)(2,1)S(1)}, bf16[8,128,128]{2,1,0:T(8,128)(2,1)S(1)}, u32[]{:S(2)}, u32[]{:S(2)}) %collective-permute-start.8) | collective-permute-done | bytes 262176 | tf_op jit(solution)/shard_map/ppermute | solution.py:14
  103.1 2.5 %collective-permute-start.10 = (bf16[2,128,128]{2,1,0:T(8,128)(2,1)S(1)}, bf16[2,128,128]{2,1,0:T(8,128)(2,1)S(1)}, u32[]{:S(2)}, u32[]{:S(2)}) collective-permute-start(bf16[2,128,128]{2,1,0:T(8,128)(2,1)S(1)} %get-tuple-element.41), channel_id=1, source_target_pairs={{1,0},{2,1},{3,2},{5,4},{6,5},{7,6},{9,8},{10,9},{11,10},{13,12},{... | collective-permute-start | bytes 196616 | tf_op jit(solution)/shard_map/ppermute | solution.py:20
  106.6 3.0 %collective-permute-start.11 = (bf16[2,128,128]{2,1,0:T(8,128)(2,1)S(1)}, bf16[2,128,128]{2,1,0:T(8,128)(2,1)S(1)}, u32[]{:S(2)}, u32[]{:S(2)}) collective-permute-start(bf16[2,128,128]{2,1,0:T(8,128)(2,1)S(1)} %get-tuple-element.40), channel_id=1, source_target_pairs={{0,1},{1,2},{2,3},{4,5},{5,6},{6,7},{8,9},{9,10},{10,11},{12,13},{... | collective-permute-start | bytes 196616 | tf_op jit(solution)/shard_map/ppermute | solution.py:20
  109.7 1.2 %collective-permute-done.11 = bf16[2,128,128]{2,1,0:T(8,128)(2,1)S(1)} collective-permute-done((bf16[2,128,128]{2,1,0:T(8,128)(2,1)S(1)}, bf16[2,128,128]{2,1,0:T(8,128)(2,1)S(1)}, u32[]{:S(2)}, u32[]{:S(2)}) %collective-permute-start.11) | collective-permute-done | bytes 65568 | tf_op jit(solution)/shard_map/ppermute | solution.py:20
  (88 shorter events, 22.2 us)
Async XLA Ops:
  0.6 58.0 %copy-start = (bf16[1,4,128,128]{3,2,1,0:T(8,128)(2,1)S(1)}, bf16[1,4,128,128]{3,2,1,0:T(8,128)(2,1)}, u32[]{:S(2)}) copy-start(bf16[1,4,128,128]{3,2,1,0:T(8,128)(2,1)} %param.23) | copy-start | bytes 393220
  1.6 13.1 %collective-permute-start = (bf16[3,128,128]{2,1,0:T(8,128)(2,1)S(1)}, bf16[3,128,128]{2,1,0:T(8,128)(2,1)S(1)}, u32[]{:S(2)}, u32[]{:S(2)}) collective-permute-start(bf16[3,128,128]{2,1,0:T(8,128)(2,1)S(1)} %get-tuple-element.46), channel_id=1, source_target_pairs={{0,1},{1,2},{2,3},{4,5},{5,6},{6,7},{8,9},{9,10},{10,11},{12,13},{... | collective-permute-start | bytes 294920 | tf_op jit(solution)/shard_map/ppermute | solution.py:30
  6.2 8.6 %collective-permute-start.1 = (bf16[3,128,128]{2,1,0:T(8,128)(2,1)S(1)}, bf16[3,128,128]{2,1,0:T(8,128)(2,1)S(1)}, u32[]{:S(2)}, u32[]{:S(2)}) collective-permute-start(bf16[3,128,128]{2,1,0:T(8,128)(2,1)S(1)} %get-tuple-element.47), channel_id=1, source_target_pairs={{1,0},{2,1},{3,2},{5,4},{6,5},{7,6},{9,8},{10,9},{11,10},{13,12},{... | collective-permute-start | bytes 294920 | tf_op jit(solution)/shard_map/ppermute | solution.py:31
  14.7 4.0 %copy-start.4 = (bf16[128,256]{1,0:T(8,128)(2,1)}, bf16[128,256]{1,0:T(8,128)(2,1)S(1)}, u32[]{:S(2)}) copy-start(bf16[128,256]{1,0:T(8,128)(2,1)S(1)} %constant_dynamic-update-slice_fusion) | copy-start | bytes 196612
  15.7 1.0 copy-start.7
  18.2 9.1 %copy-start.8 = (bf16[128,128]{1,0:T(8,128)(2,1)S(1)}, bf16[128,128]{1,0:T(8,128)(2,1)}, u32[]{:S(2)}) copy-start(bf16[128,128]{1,0:T(8,128)(2,1)} %param.17) | copy-start | bytes 98308
  19.7 15.5 %collective-permute-start.5 = (bf16[8,128,256]{2,1,0:T(8,128)(2,1)}, bf16[8,128,256]{2,1,0:T(8,128)(2,1)S(1)}, u32[]{:S(2)}, u32[]{:S(2)}) collective-permute-start(bf16[8,128,256]{2,1,0:T(8,128)(2,1)} %bitcast.28), channel_id=1, source_target_pairs={{0,24},{4,28},{8,0},{12,4},{16,8},{20,12},{24,16},{28,20},{1,25},{... | collective-permute-start | bytes 1572872 | tf_op jit(solution)/shard_map/ppermute | solution.py:14
  23.0 23.4 %collective-permute-start.4 = (bf16[8,128,256]{2,1,0:T(8,128)(2,1)}, bf16[8,128,256]{2,1,0:T(8,128)(2,1)S(1)}, u32[]{:S(2)}, u32[]{:S(2)}) collective-permute-start(bf16[8,128,256]{2,1,0:T(8,128)(2,1)} %bitcast.28), channel_id=1, source_target_pairs={{0,28},{4,0},{8,4},{12,8},{16,12},{20,16},{24,20},{28,24},{1,29},{... | collective-permute-start | bytes 1572872 | tf_op jit(solution)/shard_map/ppermute | solution.py:14
  24.2 32.5 %collective-permute-start.3 = (bf16[8,128,256]{2,1,0:T(8,128)(2,1)}, bf16[8,128,256]{2,1,0:T(8,128)(2,1)S(1)}, u32[]{:S(2)}, u32[]{:S(2)}) collective-permute-start(bf16[8,128,256]{2,1,0:T(8,128)(2,1)} %bitcast.28), channel_id=1, source_target_pairs={{0,8},{4,12},{8,16},{12,20},{16,24},{20,28},{24,0},{28,4},{1,9},{5... | collective-permute-start | bytes 1572872 | tf_op jit(solution)/shard_map/ppermute | solution.py:14
  25.5 32.0 %collective-permute-start.2 = (bf16[8,128,256]{2,1,0:T(8,128)(2,1)}, bf16[8,128,256]{2,1,0:T(8,128)(2,1)S(1)}, u32[]{:S(2)}, u32[]{:S(2)}) collective-permute-start(bf16[8,128,256]{2,1,0:T(8,128)(2,1)} %bitcast.28), channel_id=1, source_target_pairs={{0,4},{4,8},{8,12},{12,16},{16,20},{20,24},{24,28},{28,0},{1,5},{5... | collective-permute-start | bytes 1572872 | tf_op jit(solution)/shard_map/ppermute | solution.py:14
  27.4 32.9 %copy-start.5 = (bf16[512,128]{1,0:T(8,128)(2,1)}, bf16[512,128]{1,0:T(8,128)(2,1)S(1)}, u32[]{:S(2)}) copy-start(bf16[512,128]{1,0:T(8,128)(2,1)S(1)} %convolution_convert_fusion.1) | copy-start | bytes 393220
  58.6 3.9 %copy-start.1 = (bf16[4,6,128,256]{3,2,1,0:T(8,128)(2,1)}, bf16[4,6,128,256]{3,2,1,0:T(8,128)(2,1)S(1)}, u32[]{:S(2)}) copy-start(bf16[4,6,128,256]{3,2,1,0:T(8,128)(2,1)S(1)} %pad_maximum_fusion.1) | copy-start | bytes 4718596
  62.5 1.4 %copy-start.3 = (f32[4,768,128]{1,2,0:T(8,128)S(1)}, f32[4,768,128]{1,2,0:T(8,128)}, u32[]{:S(2)}) copy-start(f32[4,768,128]{1,2,0:T(8,128)} %fusion.9) | copy-start | bytes 4718596
  63.9 0.9 copy-start.6
  80.0 11.0 %collective-permute-start.7 = (bf16[8,128,128]{2,1,0:T(8,128)(2,1)}, bf16[8,128,128]{2,1,0:T(8,128)(2,1)}, u32[]{:S(2)}, u32[]{:S(2)}) collective-permute-start(bf16[8,128,128]{2,1,0:T(8,128)(2,1)} %get-tuple-element.44), channel_id=1, source_target_pairs={{0,4},{4,8},{8,12},{12,16},{16,20},{20,24},{24,28},{28,0},{1,5},{5... | collective-permute-start | bytes 786440 | tf_op jit(solution)/shard_map/ppermute | solution.py:14
  80.0 11.0 %collective-permute-start.9 = (bf16[8,128,128]{2,1,0:T(8,128)(2,1)}, bf16[8,128,128]{2,1,0:T(8,128)(2,1)}, u32[]{:S(2)}, u32[]{:S(2)}) collective-permute-start(bf16[8,128,128]{2,1,0:T(8,128)(2,1)} %get-tuple-element.45), channel_id=1, source_target_pairs={{0,8},{4,12},{8,16},{12,20},{16,24},{20,28},{24,0},{28,4},{1,9},{5... | collective-permute-start | bytes 786440 | tf_op jit(solution)/shard_map/ppermute | solution.py:14
  84.6 5.9 %copy-start.2 = (bf16[4,6,128,256]{3,2,1,0:T(8,128)(2,1)S(1)}, bf16[4,6,128,256]{3,2,1,0:T(8,128)(2,1)}, u32[]{:S(2)}) copy-start(bf16[4,6,128,256]{3,2,1,0:T(8,128)(2,1)} %copy-done.1) | copy-start | bytes 4718596
  86.1 10.2 %collective-permute-start.6 = (bf16[8,128,128]{2,1,0:T(8,128)(2,1)S(1)}, bf16[8,128,128]{2,1,0:T(8,128)(2,1)S(1)}, u32[]{:S(2)}, u32[]{:S(2)}) collective-permute-start(bf16[8,128,128]{2,1,0:T(8,128)(2,1)S(1)} %get-tuple-element.42), channel_id=1, source_target_pairs={{0,28},{4,0},{8,4},{12,8},{16,12},{20,16},{24,20},{28,24},{1,29},{... | collective-permute-start | bytes 786440 | tf_op jit(solution)/shard_map/ppermute | solution.py:14
  90.4 11.5 %collective-permute-start.8 = (bf16[8,128,128]{2,1,0:T(8,128)(2,1)S(1)}, bf16[8,128,128]{2,1,0:T(8,128)(2,1)S(1)}, u32[]{:S(2)}, u32[]{:S(2)}) collective-permute-start(bf16[8,128,128]{2,1,0:T(8,128)(2,1)S(1)} %get-tuple-element.43), channel_id=1, source_target_pairs={{0,24},{4,28},{8,0},{12,4},{16,8},{20,12},{24,16},{28,20},{1,25},{... | collective-permute-start | bytes 786440 | tf_op jit(solution)/shard_map/ppermute | solution.py:14
  103.1 7.9 %copy-start.9 = (bf16[128,128]{1,0:T(8,128)(2,1)S(1)}, bf16[128,128]{1,0:T(8,128)(2,1)}, u32[]{:S(2)}) copy-start(bf16[128,128]{1,0:T(8,128)(2,1)} %param.17) | copy-start | bytes 98308
  103.1 6.6 %collective-permute-start.10 = (bf16[2,128,128]{2,1,0:T(8,128)(2,1)S(1)}, bf16[2,128,128]{2,1,0:T(8,128)(2,1)S(1)}, u32[]{:S(2)}, u32[]{:S(2)}) collective-permute-start(bf16[2,128,128]{2,1,0:T(8,128)(2,1)S(1)} %get-tuple-element.41), channel_id=1, source_target_pairs={{1,0},{2,1},{3,2},{5,4},{6,5},{7,6},{9,8},{10,9},{11,10},{13,12},{... | collective-permute-start | bytes 196616 | tf_op jit(solution)/shard_map/ppermute | solution.py:20
  106.6 4.3 %collective-permute-start.11 = (bf16[2,128,128]{2,1,0:T(8,128)(2,1)S(1)}, bf16[2,128,128]{2,1,0:T(8,128)(2,1)S(1)}, u32[]{:S(2)}, u32[]{:S(2)}) collective-permute-start(bf16[2,128,128]{2,1,0:T(8,128)(2,1)S(1)} %get-tuple-element.40), channel_id=1, source_target_pairs={{0,1},{1,2},{2,3},{4,5},{5,6},{6,7},{8,9},{9,10},{10,11},{12,13},{... | collective-permute-start | bytes 196616 | tf_op jit(solution)/shard_map/ppermute | solution.py:20
where the time goes:
time: 113 us; the launch traced here: 112 us
  waiting for transfers between devices  41.7 us (37%)
  starting transfers between devices  23.4 us (21%)
  local copies, waits for them, and re-layouts  17.4 us (15%)
  matrix products  14 us (12%)
  other arithmetic  13.1 us (12%)
  between operations  2.4 us (2%)
    ppermute x8, waiting for transfers between devices, from_behind(): return lax.ppermute(value, axis, pairs)  40.5 us
    ppermute x8, starting transfers between devices, from_behind(): return lax.ppermute(value, axis, pairs)  11.4 us
    scatter-add x2, other arithmetic, window_grad(): summed = jnp.zeros((win_blocks, BLOCK, 2 * channels), jnp.float32).at[loc...  6.25 us
    ppermute x2, starting transfers between devices, passed_along(): return lax.ppermute(block, axis, route)  5.55 us
    ppermute x1, starting transfers between devices, padded_2(): before = lax.ppermute(last, axis, up)  4.54 us
    slice x1, local copies, waits for them, and re-layouts, window_grad(): grad_pairs[:, side_idx]  3.88 us
    dot_general x2, matrix products, window_grad(): jnp.dot(summed.reshape(win_rows * img_width, 2 * channels), back_weight,...  3.82 us
    concatenate x1, local copies, waits for them, and re-layouts, local(): jnp.concatenate([key_gradient, value_gradient], axis=2)  3.52 us
  transfers between devices with their start and end apart: 12, of which 8 were waited for; matrix products, arithmetic and copies ran while one was open for 13% of the time, Pallas kernels for 0%

commit v1 on v0

v1 whole, which is shorter than its diff:
```python
import functools

import jax
import jax.numpy as jnp
from jax import lax
from jax.experimental import pallas as pl
from jax.experimental.pallas import tpu as pltpu
from jax.sharding import PartitionSpec as P

MARGIN = 2
BAND = 3
LOG2E = 1.4426950408889634


def from_behind(value, axis, steps):
    count = lax.axis_size(axis)
    pairs = [(source, (source + steps) % count) for source in range(count)]
    return lax.ppermute(value, axis, pairs)


def passed_along(block, axis, distance):
    devices = range(lax.axis_size(axis))
    route = [(i - distance, i) for i in devices if i - distance in devices]
    return lax.ppermute(block, axis, route)


def dot_nn(a, b):
    return lax.dot_general(a, b, (((1,), (0,)), ((), ())), preferred_element_type=jnp.float32)


def dot_nt(a, b):
    return lax.dot_general(a, b, (((1,), (1,)), ((), ())), preferred_element_type=jnp.float32)


def conv_rows(ref, out_rows, width, taps):
    count = out_rows * width
    stacked = jnp.concatenate([ref[i * width : i * width + count, :] for i in range(3)], axis=1)
    parts = dot_nn(stacked, taps)
    channels = parts.shape[1] // 3
    left, middle, right = (parts[:, i * channels : (i + 1) * channels] for i in range(3))
    column = lax.broadcasted_iota(jnp.int32, (count, channels), 0) % width
    total = middle + jnp.where(column == 0, 0.0, pltpu.roll(left, 1, 0))
    total = total + jnp.where(column == width - 1, 0.0, pltpu.roll(right, count - 1, 0))
    return total.astype(jnp.bfloat16)


def attention_kernel(
    scalars,
    own,
    near_left,
    far_left,
    near_right,
    far_right,
    above,
    below,
    conv_weight,
    q_weight,
    k_weight,
    v_weight,
    cotangent,
    attended,
    top,
    bottom,
    center,
    grad_own,
    image,
    kv,
    kv_t,
    acc,
    pair,
):
    rows, width, channels = own.shape
    halo = MARGIN + 1
    win = rows + 2 * MARGIN
    scale = channels**-0.5
    taps = jnp.concatenate(
        [
            jnp.concatenate([conv_weight[i, j] for j in range(3)], axis=1)
            for i in range(3)
        ],
        axis=0,
    )
    wq, wk, wv = q_weight[...], k_weight[...], v_weight[...]
    wkv = jnp.concatenate([wk, wv], axis=1)
    wkv_t = wkv.T

    image[0:width, :] = above[2 * halo]
    image[width : (rows + 1) * width, :] = own[...].reshape(rows * width, channels)
    image[(rows + 1) * width : (rows + 2) * width, :] = below[2 * halo]
    hidden = conv_rows(image, rows, width, taps)
    queries = dot_nn(hidden, wq).astype(jnp.bfloat16)
    pair[...] = jnp.zeros_like(pair)
    for b in range(rows):
        pair[b, 0:width, 0:channels] = queries[b * width : (b + 1) * width, :]
        pair[b, width : 2 * width, channels : 2 * channels] = cotangent[b]

    acc[...] = jnp.zeros_like(acc)
    for side, (near, far) in enumerate(((near_left, far_left), (near_right, far_right))):
        image[0 : halo * width, :] = above[side * halo : (side + 1) * halo].reshape(-1, channels)
        chosen = jnp.where(scalars[side] == 1, near[...], far[...])
        image[halo * width : (halo + rows) * width, :] = chosen.reshape(rows * width, channels)
        image[(halo + rows) * width :, :] = below[side * halo : (side + 1) * halo].reshape(
            -1, channels
        )
        hidden = conv_rows(image, win, width, taps)
        kv[side] = (
            dot_nn(hidden, wkv).astype(jnp.bfloat16).reshape(win, width, 2 * channels)
        )
        turned = dot_nt(wkv_t, hidden).astype(jnp.bfloat16)
        for r in range(win):
            kv_t[side, r] = turned[:, r * width : (r + 1) * width]

    grad_q = []
    for b in range(rows):
        places = [
            (side, scalars[2 + (b * 2 + side) * BAND + s], scalars[2 + rows * 2 * BAND + side * BAND + s])
            for side in range(2)
            for s in range(BAND)
        ]
        keys = jnp.concatenate([kv[side, at] for side, at, _ in places], axis=0)
        both = dot_nt(keys, pair[b])
        scores, grad_probs = both[:, :width], both[:, width:]
        expo = jnp.exp2(scores * (scale * LOG2E))
        expo = jnp.concatenate(
            [
                jnp.where(live == 1, expo[i * width : (i + 1) * width], 0.0)
                for i, (_, _, live) in enumerate(places)
            ],
            axis=0,
        )
        probs = expo * (1.0 / jnp.sum(expo, axis=0, keepdims=True))
        probs_bf = probs.astype(jnp.bfloat16)
        delta = jnp.sum(probs * grad_probs, axis=0, keepdims=True)
        grad_scores = (probs * (grad_probs - delta)).astype(jnp.bfloat16)
        keys_t = jnp.concatenate([kv_t[side, at] for side, at, _ in places], axis=1)
        attended[b] = dot_nn(keys_t[channels:], probs_bf).T.astype(jnp.bfloat16)
        grad_q.append(dot_nn(keys_t[:channels], grad_scores))
        terms = dot_nn(jnp.concatenate([grad_scores, probs_bf], axis=1), pair[b])
        for i, (side, at, _) in enumerate(places):
            acc[side, at] += terms[i * width : (i + 1) * width]

    turned = dot_nn(wq, (jnp.concatenate(grad_q, axis=1) * scale).astype(jnp.bfloat16))
    for b in range(rows):
        grad_own[b] = turned[:, b * width : (b + 1) * width].T
    for side in range(2):
        grads = acc[side].reshape(win * width, 2 * channels)
        grads = jnp.concatenate([grads[:, :channels] * scale, grads[:, channels:]], axis=1)
        back = dot_nt(grads.astype(jnp.bfloat16), wkv).reshape(win, width, channels)
        top[side * MARGIN : (side + 1) * MARGIN] = back[:MARGIN].astype(jnp.bfloat16)
        center[side] = back[MARGIN : MARGIN + rows]
        bottom[side * MARGIN : (side + 1) * MARGIN] = back[MARGIN + rows :].astype(jnp.bfloat16)


def attention(scalars, *arrays):
    own = arrays[0]
    rows, width, channels = own.shape
    win = rows + 2 * MARGIN
    vmem = pl.BlockSpec(memory_space=pltpu.VMEM)
    shape = jax.ShapeDtypeStruct
    return pl.pallas_call(
        attention_kernel,
        out_shape=(
            shape((rows, width, channels), jnp.bfloat16),
            shape((2 * MARGIN, width, channels), jnp.bfloat16),
            shape((2 * MARGIN, width, channels), jnp.bfloat16),
            shape((2, rows, width, channels), jnp.float32),
            shape((rows, width, channels), jnp.float32),
        ),
        in_specs=[pl.BlockSpec(memory_space=pltpu.SMEM)] + [vmem] * len(arrays),
        out_specs=(vmem,) * 5,
        scratch_shapes=[
            pltpu.VMEM(((win + 2) * width, channels), jnp.bfloat16),
            pltpu.VMEM((2, win, width, 2 * channels), jnp.bfloat16),
            pltpu.VMEM((2, win, 2 * channels, width), jnp.bfloat16),
            pltpu.VMEM((2, win, width, 2 * channels), jnp.float32),
            pltpu.VMEM((rows, 2 * width, 2 * channels), jnp.bfloat16),
        ],
        compiler_params=pltpu.CompilerParams(vmem_limit_bytes=40 * 1024 * 1024),
        cost_estimate=pl.CostEstimate(
            flops=2_000_000_000, bytes_accessed=4_000_000, transcendentals=400_000
        ),
    )(scalars, *arrays)


def local(
    features_in,
    conv_weight,
    q_weight,
    k_weight,
    v_weight,
    partners,
    band_widths,
    bands,
    grad_attended,
):
    image = features_in[0]
    rows = image.shape[0]
    halo = MARGIN + 1
    views = lax.axis_size("cam")
    samples = views // min(16, views)
    camera = lax.axis_index("cam")
    slab = lax.axis_index("row")

    near_left = from_behind(image, "cam", samples)
    near_right = from_behind(image, "cam", -samples)
    far_left = from_behind(image, "cam", 2 * samples)
    far_right = from_behind(image, "cam", -2 * samples)

    def uses(step, side):
        other = jnp.mod(camera + step, views)
        return partners[other, side] == camera

    close_left = partners[camera, 0] == jnp.mod(camera - samples, views)
    close_right = partners[camera, 1] == jnp.mod(camera + samples, views)
    widths_here = lax.dynamic_index_in_dim(band_widths, camera, 0, keepdims=False)
    live = jnp.arange(BAND, dtype=jnp.int32)[None, :] < widths_here[:, None]
    places = jnp.clip(bands[0] - (slab * rows - MARGIN), 0, rows + 2 * MARGIN - 1)
    scalars = jnp.concatenate(
        [
            jnp.stack([close_left, close_right]).astype(jnp.int32),
            places.reshape(-1),
            live.reshape(-1).astype(jnp.int32),
        ]
    )

    left = jnp.where(close_left, near_left, far_left)
    right = jnp.where(close_right, near_right, far_right)
    above = passed_along(
        jnp.concatenate([left[rows - halo :], right[rows - halo :], image[rows - 1 :]]), "row", 1
    )
    below = passed_along(jnp.concatenate([left[:halo], right[:halo], image[:1]]), "row", -1)

    attended, top, bottom, center, grad_own = attention(
        scalars,
        image,
        near_left,
        far_left,
        near_right,
        far_right,
        above,
        below,
        conv_weight,
        q_weight,
        k_weight,
        v_weight,
        grad_attended[0],
    )

    from_above = passed_along(bottom, "row", 1).reshape(2, MARGIN, *image.shape[1:])
    from_below = passed_along(top, "row", -1).reshape(2, MARGIN, *image.shape[1:])
    zeros = jnp.zeros((2, rows - MARGIN, *image.shape[1:]), jnp.float32)
    total = (
        center
        + jnp.concatenate([from_above.astype(jnp.float32), zeros], axis=1)
        + jnp.concatenate([zeros, from_below.astype(jnp.float32)], axis=1)
    ).astype(jnp.bfloat16)
    summed = grad_own
    for side, sign in ((0, -1), (1, 1)):
        for distance in (1, 2):
            step = sign * distance * samples
            came = from_behind(total[side], "cam", step)
            summed = summed + jnp.where(uses(-step, side), came.astype(jnp.float32), 0.0)
    return (attended[None], summed.astype(jnp.bfloat16)[None])


def solution(mesh):
    placed = (
        P("cam", "row", None, None),
        P(),
        P(),
        P(),
        P(),
        P(),
        P(),
        P("cam", "row", None, None),
        P("cam", "row", None, None),
    )
    return jax.shard_map(
        local,
        mesh=mesh,
        in_specs=placed,
        out_specs=(P("cam", "row", None, None), P("cam", "row", None, None)),
        check_vma=False,
    )
```

time: 113 us -> 54.8 us (0.48)
  waiting for transfers between devices: 41.7 us -> 18.5 us
  local copies, waits for them, and re-layouts: 17.4 us -> 2.59 us
  matrix products: 14 us -> 0 us
  other arithmetic: 13.1 us -> 1.15 us
  Pallas kernels: 0 us -> 6.93 us
  starting transfers between devices: 23.4 us -> 20.6 us
  between operations: 2.4 us -> 4.75 us
    ppermute x8, waiting for transfers between devices: 40.5 us -> 9.7 us  [from_behind(): return lax.ppermute(value, axis, pairs)]
    dot_general x19 -> x0, matrix products: 11.8 us -> none  [the longest x2 3.82 us: window_grad(): jnp.dot(summed.reshape(win_rows * img_width, 2 * channels), back_weight,...]
    ppermute x2 -> x4, waiting for transfers between devices: 1.25 us -> 8.78 us  [passed_along(): return lax.ppermute(block, axis, route)]
    pallas_call x0 -> x1, Pallas kernels: none -> 6.93 us  [attention(): pl.pallas_call(attention_kernel, out_shape=(shape((rows, width, channels)...]
    ppermute x2 -> x0, starting transfers between devices: 6.46 us -> none  [the longest x1 4.54 us: padded_2(): before = lax.ppermute(last, axis, up)]
    scatter-add x4 -> x0, other arithmetic: 6.29 us -> none  [the longest x2 6.25 us: window_grad(): summed = jnp.zeros((win_blocks, BLOCK, 2 * channels), jnp.float32).at[loc...]
    slice x10 -> x3, local copies, waits for them, and re-layouts: 6.68 us -> 0.88 us  [the longest x1 0.83 us: local(): image[:1]]
    ppermute x2 -> x4, starting transfers between devices: 5.55 us -> 11 us  [passed_along(): return lax.ppermute(block, axis, route)]
  transfers between devices with their start and end apart: 12 -> 12, of which waited for: 8 -> 8; matrix products, arithmetic and copies ran while one was open for 13% -> 4% of each run, Pallas kernels for 0% -> 0%
where the time goes in v1:
time: 54.8 us; the launch traced here: 54.5 us
  starting transfers between devices  20.6 us (38%)
  waiting for transfers between devices  18.5 us (34%)
  Pallas kernels  6.93 us (13%)
  between operations  4.75 us (9%)
  local copies, waits for them, and re-layouts  2.59 us (5%)
  other arithmetic  1.15 us (2%)
    ppermute x4, starting transfers between devices, passed_along(): return lax.ppermute(block, axis, route)  11 us
    ppermute x8, waiting for transfers between devices, from_behind(): return lax.ppermute(value, axis, pairs)  9.7 us
    ppermute x8, starting transfers between devices, from_behind(): return lax.ppermute(value, axis, pairs)  9.58 us
    ppermute x4, waiting for transfers between devices, passed_along(): return lax.ppermute(block, axis, route)  8.78 us
    pallas_call x1, Pallas kernels, attention(): pl.pallas_call(attention_kernel, out_shape=(shape((rows, width, channels)...  6.93 us
  transfers between devices with their start and end apart: 12, of which 8 were waited for; matrix products, arithmetic and copies ran while one was open for 4% of the time, Pallas kernels for 0%

profile of v1, /device:TPU:1, one launch (start us, length us, event | category | flops | bytes accessed | tf_op | source)
XLA Modules:
  0.0 54.5 jit_solution(9523526047448188941)
XLA Ops:
  0.6 4.2 %collective-permute-start.3 = (bf16[4,128,128]{2,1,0:T(8,128)(2,1)}, bf16[4,128,128]{2,1,0:T(8,128)(2,1)S(1)}, u32[]{:S(2)}, u32[]{:S(2)}) collective-permute-start(bf16[4,128,128]{2,1,0:T(8,128)(2,1)} %bitcast.23), channel_id=1, source_target_pairs={{0,24},{4,28},{8,0},{12,4},{16,8},{20,12},{24,16},{28,20},{1,25},{... | collective-permute-start | bytes 393224 | tf_op jit(solution)/shard_map/ppermute | solution.py:18
  4.8 1.1 %collective-permute-start.2 = (bf16[4,128,128]{2,1,0:T(8,128)(2,1)}, bf16[4,128,128]{2,1,0:T(8,128)(2,1)S(1)}, u32[]{:S(2)}, u32[]{:S(2)}) collective-permute-start(bf16[4,128,128]{2,1,0:T(8,128)(2,1)} %bitcast.24), channel_id=1, source_target_pairs={{0,28},{4,0},{8,4},{12,8},{16,12},{20,16},{24,20},{28,24},{1,29},{... | collective-permute-start | bytes 393224 | tf_op jit(solution)/shard_map/ppermute | solution.py:18
  5.9 1.3 %collective-permute-start.1 = (bf16[4,128,128]{2,1,0:T(8,128)(2,1)}, bf16[4,128,128]{2,1,0:T(8,128)(2,1)S(1)}, u32[]{:S(2)}, u32[]{:S(2)}) collective-permute-start(bf16[4,128,128]{2,1,0:T(8,128)(2,1)} %bitcast.25), channel_id=1, source_target_pairs={{0,8},{4,12},{8,16},{12,20},{16,24},{20,28},{24,0},{28,4},{1,9},{5... | collective-permute-start | bytes 393224 | tf_op jit(solution)/shard_map/ppermute | solution.py:18
  7.2 0.8 %slice_bitcast_fusion.2 = (bf16[1,128,128]{2,1,0:T(8,128)(2,1)S(1)}, bf16[1,128,128]{2,1,0:T(8,128)(2,1)S(1)}) fusion(bf16[1,4,128,128]{3,2,1,0:T(8,128)(2,1)} %param.9), kind=kLoop, calls=%fused_computation.9 | loop fusion | bytes 131072 | tf_op jit(solution)/shard_map/slice | solution.py:231
  8.3 0.5 copy-done.7
  8.8 0.7 %constant_dynamic-slice_fusion.1 = (s32[1,1]{0,1:T(1,128)}, s32[1,1]{0,1:T(1,128)}, s32[1,1]{0,1:T(1,128)}, s32[1,1]{0,1:T(1,128)}, s32[1,1]{0,1:T(1,128)}, /*index=5*/s32[1,1]{0,1:T(1,128)}) fusion(s32[8,2]{0,1:T(2,128)S(1)} %copy-done.7, s32[]{:T(128)S(6)} %select_n.88, s32[]{:T(128)S(6)} %select_n.92, s32[]{:T(128)S(6)} %select_n.81, s32[]{:T(128)S(6)} %select_n.99, ...), kind=kLoop, calls=%fused_computation.16 | loop fusion | bytes 68 | tf_op jit(solution)/shard_map/dynamic_slice | solution.py:211
  10.9 2.8 %collective-permute-done.1.far_left = bf16[4,128,128]{2,1,0:T(8,128)(2,1)S(1)} collective-permute-done((bf16[4,128,128]{2,1,0:T(8,128)(2,1)}, bf16[4,128,128]{2,1,0:T(8,128)(2,1)S(1)}, u32[]{:S(2)}, u32[]{:S(2)}) %collective-permute-start.1) | collective-permute-done | bytes 131104 | tf_op jit(solution)/shard_map/ppermute | solution.py:18
  13.7 1.8 %collective-permute-done.near_left = bf16[4,128,128]{2,1,0:T(8,128)(2,1)S(1)} collective-permute-done((bf16[4,128,128]{2,1,0:T(8,128)(2,1)}, bf16[4,128,128]{2,1,0:T(8,128)(2,1)S(1)}, u32[]{:S(2)}, u32[]{:S(2)}) %collective-permute-start) | collective-permute-done | bytes 131104 | tf_op jit(solution)/shard_map/ppermute | solution.py:18
  15.7 4.6 %collective-permute-start.4 = (bf16[7,128,128]{2,1,0:T(8,128)(2,1)S(1)}, bf16[7,128,128]{2,1,0:T(8,128)(2,1)S(1)}, u32[]{:S(2)}, u32[]{:S(2)}) collective-permute-start(bf16[7,128,128]{2,1,0:T(8,128)(2,1)S(1)} %pad_maximum_fusion), channel_id=1, source_target_pairs={{0,1},{1,2},{2,3},{4,5},{5,6},{6,7},{8,9},{9,10},{10,11},{12,13},{... | collective-permute-start | bytes 688136 | tf_op jit(solution)/shard_map/ppermute | solution.py:24
  20.4 2.1 %collective-permute-start.5 = (bf16[7,128,128]{2,1,0:T(8,128)(2,1)S(1)}, bf16[7,128,128]{2,1,0:T(8,128)(2,1)S(1)}, u32[]{:S(2)}, u32[]{:S(2)}) collective-permute-start(bf16[7,128,128]{2,1,0:T(8,128)(2,1)S(1)} %pad_maximum_fusion.1), channel_id=1, source_target_pairs={{1,0},{2,1},{3,2},{5,4},{6,5},{7,6},{9,8},{10,9},{11,10},{13,12},{... | collective-permute-start | bytes 688136 | tf_op jit(solution)/shard_map/ppermute | solution.py:24
  23.0 0.3 collective-permute-done.4.above
  23.3 4.6 %collective-permute-done.5.below = bf16[7,128,128]{2,1,0:T(8,128)(2,1)S(1)} collective-permute-done((bf16[7,128,128]{2,1,0:T(8,128)(2,1)S(1)}, bf16[7,128,128]{2,1,0:T(8,128)(2,1)S(1)}, u32[]{:S(2)}, u32[]{:S(2)}) %collective-permute-start.5) | collective-permute-done | bytes 229408 | tf_op jit(solution)/shard_map/ppermute | solution.py:24
  27.9 6.9 %shard_map.104 = (bf16[4,128,128]{2,1,0:T(8,128)(2,1)}, bf16[4,128,128]{2,1,0:T(8,128)(2,1)S(1)}, bf16[4,128,128]{2,1,0:T(8,128)(2,1)S(1)}, f32[2,4,128,128]{3,2,1,0:T(8,128)S(1)}, f32[4,128,128]{2,1,0:T(8,128)S(1)}) custom-call(s32[32]{0:T(128)S(1)} %pad_add_fusion.scalars, bf16[4,128,128]{2,1,0:T(8,128)(2,1)S(1)} %bitcast.27, ...), custom_call_target="tpu_custom_call" | custom-call | flops 2000000000 | bytes 4000000 | tf_op jit(solution)/shard_map/pallas_call | solution.py:160
  34.9 1.9 %collective-permute-start.6 = (bf16[4,128,128]{2,1,0:T(8,128)(2,1)S(1)}, bf16[4,128,128]{2,1,0:T(8,128)(2,1)S(1)}, u32[]{:S(2)}, u32[]{:S(2)}) collective-permute-start(bf16[4,128,128]{2,1,0:T(8,128)(2,1)S(1)} %get-tuple-element.10), channel_id=1, source_target_pairs={{0,1},{1,2},{2,3},{4,5},{5,6},{6,7},{8,9},{9,10},{10,11},{12,13},{... | collective-permute-start | bytes 393224 | tf_op jit(solution)/shard_map/ppermute | solution.py:24
  36.8 2.4 %collective-permute-start.7 = (bf16[4,128,128]{2,1,0:T(8,128)(2,1)S(1)}, bf16[4,128,128]{2,1,0:T(8,128)(2,1)S(1)}, u32[]{:S(2)}, u32[]{:S(2)}) collective-permute-start(bf16[4,128,128]{2,1,0:T(8,128)(2,1)S(1)} %get-tuple-element.11), channel_id=1, source_target_pairs={{1,0},{2,1},{3,2},{5,4},{6,5},{7,6},{9,8},{10,9},{11,10},{13,12},{... | collective-permute-start | bytes 393224 | tf_op jit(solution)/shard_map/ppermute | solution.py:24
  39.2 3.9 %collective-permute-done.7 = bf16[4,128,128]{2,1,0:T(8,128)(2,1)S(1)} collective-permute-done((bf16[4,128,128]{2,1,0:T(8,128)(2,1)S(1)}, bf16[4,128,128]{2,1,0:T(8,128)(2,1)S(1)}, u32[]{:S(2)}, u32[]{:S(2)}) %collective-permute-start.7) | collective-permute-done | bytes 131104 | tf_op jit(solution)/shard_map/ppermute | solution.py:24
  43.2 0.9 %collective-permute-start.9 = (bf16[4,128,128]{2,1,0:T(8,128)(2,1)S(1)}, bf16[4,128,128]{2,1,0:T(8,128)(2,1)S(1)}, u32[]{:S(2)}, u32[]{:S(2)}) collective-permute-start(bf16[4,128,128]{2,1,0:T(8,128)(2,1)S(1)} %get-tuple-element.12), channel_id=1, source_target_pairs={{0,24},{4,28},{8,0},{12,4},{16,8},{20,12},{24,16},{28,20},{1,25},{... | collective-permute-start | bytes 393224 | tf_op jit(solution)/shard_map/ppermute | solution.py:18
  44.1 0.4 collective-permute-start.8
  44.5 1.4 %collective-permute-start.11 = (bf16[4,128,128]{2,1,0:T(8,128)(2,1)S(1)}, bf16[4,128,128]{2,1,0:T(8,128)(2,1)S(1)}, u32[]{:S(2)}, u32[]{:S(2)}) collective-permute-start(bf16[4,128,128]{2,1,0:T(8,128)(2,1)S(1)} %get-tuple-element.13), channel_id=1, source_target_pairs={{0,8},{4,12},{8,16},{12,20},{16,24},{20,28},{24,0},{28,4},{1,9},{5... | collective-permute-start | bytes 393224 | tf_op jit(solution)/shard_map/ppermute | solution.py:18
  45.9 0.3 collective-permute-start.10
  48.7 0.9 %collective-permute-done.8 = bf16[4,128,128]{2,1,0:T(8,128)(2,1)S(1)} collective-permute-done((bf16[4,128,128]{2,1,0:T(8,128)(2,1)S(1)}, bf16[4,128,128]{2,1,0:T(8,128)(2,1)S(1)}, u32[]{:S(2)}, u32[]{:S(2)}) %collective-permute-start.8) | collective-permute-done | bytes 131104 | tf_op jit(solution)/shard_map/ppermute | solution.py:18
  49.6 2.9 %collective-permute-done.11 = bf16[4,128,128]{2,1,0:T(8,128)(2,1)S(1)} collective-permute-done((bf16[4,128,128]{2,1,0:T(8,128)(2,1)S(1)}, bf16[4,128,128]{2,1,0:T(8,128)(2,1)S(1)}, u32[]{:S(2)}, u32[]{:S(2)}) %collective-permute-start.11) | collective-permute-done | bytes 131104 | tf_op jit(solution)/shard_map/ppermute | solution.py:18
  52.5 1.2 %collective-permute-done.10 = bf16[4,128,128]{2,1,0:T(8,128)(2,1)S(1)} collective-permute-done((bf16[4,128,128]{2,1,0:T(8,128)(2,1)S(1)}, bf16[4,128,128]{2,1,0:T(8,128)(2,1)S(1)}, u32[]{:S(2)}, u32[]{:S(2)}) %collective-permute-start.10) | collective-permute-done | bytes 131104 | tf_op jit(solution)/shard_map/ppermute | solution.py:18
  53.7 0.8 %fusion = bf16[1,4,128,128]{3,2,1,0:T(8,128)(2,1)} fusion(bf16[4,128,128]{2,1,0:T(8,128)(2,1)S(1)} %collective-permute-done.11, bf16[4,128,128]{2,1,0:T(8,128)(2,1)S(1)} %collective-permute-done.10, bf16[4,128,128]{2,1,0:T(8,128)(2,1)S(1)} %collective-permute-done.9, f32[4,128,128]{2,1,0:T(8,128)S(1)} %get-tuple-element.8, ...), kind=kLoop, calls=%fused_computation.4 | loop fusion | flops 851968 | bytes 917508 | tf_op jit(solution)/shard_map/broadcast_in_dim | solution.py:263
  (38 shorter events, 1.0 us)
Async XLA Ops:
  0.6 7.4 %copy-start = (s32[8,2]{0,1:T(2,128)S(1)}, s32[8,2]{0,1:T(2,128)}, u32[]{:S(2)}) copy-start(s32[8,2]{0,1:T(2,128)} %param.15) | copy-start | bytes 196
  0.6 10.2 %collective-permute-start.3 = (bf16[4,128,128]{2,1,0:T(8,128)(2,1)}, bf16[4,128,128]{2,1,0:T(8,128)(2,1)S(1)}, u32[]{:S(2)}, u32[]{:S(2)}) collective-permute-start(bf16[4,128,128]{2,1,0:T(8,128)(2,1)} %bitcast.23), channel_id=1, source_target_pairs={{0,24},{4,28},{8,0},{12,4},{16,8},{20,12},{24,16},{28,20},{1,25},{... | collective-permute-start | bytes 393224 | tf_op jit(solution)/shard_map/ppermute | solution.py:18
  4.8 6.0 %collective-permute-start.2 = (bf16[4,128,128]{2,1,0:T(8,128)(2,1)}, bf16[4,128,128]{2,1,0:T(8,128)(2,1)S(1)}, u32[]{:S(2)}, u32[]{:S(2)}) collective-permute-start(bf16[4,128,128]{2,1,0:T(8,128)(2,1)} %bitcast.24), channel_id=1, source_target_pairs={{0,28},{4,0},{8,4},{12,8},{16,12},{20,16},{24,20},{28,24},{1,29},{... | collective-permute-start | bytes 393224 | tf_op jit(solution)/shard_map/ppermute | solution.py:18
  5.9 7.8 %collective-permute-start.1 = (bf16[4,128,128]{2,1,0:T(8,128)(2,1)}, bf16[4,128,128]{2,1,0:T(8,128)(2,1)S(1)}, u32[]{:S(2)}, u32[]{:S(2)}) collective-permute-start(bf16[4,128,128]{2,1,0:T(8,128)(2,1)} %bitcast.25), channel_id=1, source_target_pairs={{0,8},{4,12},{8,16},{12,20},{16,24},{20,28},{24,0},{28,4},{1,9},{5... | collective-permute-start | bytes 393224 | tf_op jit(solution)/shard_map/ppermute | solution.py:18
  7.2 8.3 %collective-permute-start = (bf16[4,128,128]{2,1,0:T(8,128)(2,1)}, bf16[4,128,128]{2,1,0:T(8,128)(2,1)S(1)}, u32[]{:S(2)}, u32[]{:S(2)}) collective-permute-start(bf16[4,128,128]{2,1,0:T(8,128)(2,1)} %bitcast.26), channel_id=1, source_target_pairs={{0,4},{4,8},{8,12},{12,16},{16,20},{20,24},{24,28},{28,0},{1,5},{5... | collective-permute-start | bytes 393224 | tf_op jit(solution)/shard_map/ppermute | solution.py:18
  8.1 0.7 %copy-start.7 = (s32[8,2]{0,1:T(2,128)S(1)}, s32[8,2]{0,1:T(2,128)}, u32[]{:S(2)}) copy-start(s32[8,2]{0,1:T(2,128)} %param.14) | copy-start | bytes 196
  10.1 0.7 %copy-start.8 = (s32[1,4,2,3]{1,2,3,0:T(2,128)S(1)}, s32[1,4,2,3]{1,2,3,0:T(2,128)}, u32[]{:S(2)}) copy-start(s32[1,4,2,3]{1,2,3,0:T(2,128)} %param.16) | copy-start | bytes 292
  15.6 12.3 %copy-start.3 = (bf16[1,4,128,128]{3,2,1,0:T(8,128)(2,1)S(1)}, bf16[1,4,128,128]{3,2,1,0:T(8,128)(2,1)}, u32[]{:S(2)}) copy-start(bf16[1,4,128,128]{3,2,1,0:T(8,128)(2,1)} %param.17) | copy-start | bytes 393220
  15.6 12.3 %copy-start.5 = (bf16[128,128]{1,0:T(8,128)(2,1)S(1)}, bf16[128,128]{1,0:T(8,128)(2,1)}, u32[]{:S(2)}) copy-start(bf16[128,128]{1,0:T(8,128)(2,1)} %k_weight.1) | copy-start | bytes 98308
  15.7 12.3 %copy-start.6 = (bf16[128,128]{1,0:T(8,128)(2,1)S(1)}, bf16[128,128]{1,0:T(8,128)(2,1)}, u32[]{:S(2)}) copy-start(bf16[128,128]{1,0:T(8,128)(2,1)} %v_weight.1) | copy-start | bytes 98308
  15.7 12.2 %copy-start.2 = (bf16[3,3,128,128]{3,2,1,0:T(8,128)(2,1)S(1)}, bf16[3,3,128,128]{3,2,1,0:T(8,128)(2,1)}, u32[]{:S(2)}) copy-start(bf16[3,3,128,128]{3,2,1,0:T(8,128)(2,1)} %conv_weight.1) | copy-start | bytes 884740
  15.7 7.6 %collective-permute-start.4 = (bf16[7,128,128]{2,1,0:T(8,128)(2,1)S(1)}, bf16[7,128,128]{2,1,0:T(8,128)(2,1)S(1)}, u32[]{:S(2)}, u32[]{:S(2)}) collective-permute-start(bf16[7,128,128]{2,1,0:T(8,128)(2,1)S(1)} %pad_maximum_fusion), channel_id=1, source_target_pairs={{0,1},{1,2},{2,3},{4,5},{5,6},{6,7},{8,9},{9,10},{10,11},{12,13},{... | collective-permute-start | bytes 688136 | tf_op jit(solution)/shard_map/ppermute | solution.py:24
  20.4 7.6 %copy-start.1 = (bf16[1,4,128,128]{3,2,1,0:T(8,128)(2,1)S(1)}, bf16[1,4,128,128]{3,2,1,0:T(8,128)(2,1)}, u32[]{:S(2)}) copy-start(bf16[1,4,128,128]{3,2,1,0:T(8,128)(2,1)} %param.9) | copy-start | bytes 393220
  20.4 7.6 %copy-start.4 = (bf16[128,128]{1,0:T(8,128)(2,1)S(1)}, bf16[128,128]{1,0:T(8,128)(2,1)}, u32[]{:S(2)}) copy-start(bf16[128,128]{1,0:T(8,128)(2,1)} %q_weight.1) | copy-start | bytes 98308
  20.4 7.5 %collective-permute-start.5 = (bf16[7,128,128]{2,1,0:T(8,128)(2,1)S(1)}, bf16[7,128,128]{2,1,0:T(8,128)(2,1)S(1)}, u32[]{:S(2)}, u32[]{:S(2)}) collective-permute-start(bf16[7,128,128]{2,1,0:T(8,128)(2,1)S(1)} %pad_maximum_fusion.1), channel_id=1, source_target_pairs={{1,0},{2,1},{3,2},{5,4},{6,5},{7,6},{9,8},{10,9},{11,10},{13,12},{... | collective-permute-start | bytes 688136 | tf_op jit(solution)/shard_map/ppermute | solution.py:24
  34.9 4.3 %collective-permute-start.6 = (bf16[4,128,128]{2,1,0:T(8,128)(2,1)S(1)}, bf16[4,128,128]{2,1,0:T(8,128)(2,1)S(1)}, u32[]{:S(2)}, u32[]{:S(2)}) collective-permute-start(bf16[4,128,128]{2,1,0:T(8,128)(2,1)S(1)} %get-tuple-element.10), channel_id=1, source_target_pairs={{0,1},{1,2},{2,3},{4,5},{5,6},{6,7},{8,9},{9,10},{10,11},{12,13},{... | collective-permute-start | bytes 393224 | tf_op jit(solution)/shard_map/ppermute | solution.py:24
  36.8 6.3 %collective-permute-start.7 = (bf16[4,128,128]{2,1,0:T(8,128)(2,1)S(1)}, bf16[4,128,128]{2,1,0:T(8,128)(2,1)S(1)}, u32[]{:S(2)}, u32[]{:S(2)}) collective-permute-start(bf16[4,128,128]{2,1,0:T(8,128)(2,1)S(1)} %get-tuple-element.11), channel_id=1, source_target_pairs={{1,0},{2,1},{3,2},{5,4},{6,5},{7,6},{9,8},{10,9},{11,10},{13,12},{... | collective-permute-start | bytes 393224 | tf_op jit(solution)/shard_map/ppermute | solution.py:24
  43.2 5.5 %collective-permute-start.9 = (bf16[4,128,128]{2,1,0:T(8,128)(2,1)S(1)}, bf16[4,128,128]{2,1,0:T(8,128)(2,1)S(1)}, u32[]{:S(2)}, u32[]{:S(2)}) collective-permute-start(bf16[4,128,128]{2,1,0:T(8,128)(2,1)S(1)} %get-tuple-element.12), channel_id=1, source_target_pairs={{0,24},{4,28},{8,0},{12,4},{16,8},{20,12},{24,16},{28,20},{1,25},{... | collective-permute-start | bytes 393224 | tf_op jit(solution)/shard_map/ppermute | solution.py:18
  44.1 5.5 %collective-permute-start.8 = (bf16[4,128,128]{2,1,0:T(8,128)(2,1)S(1)}, bf16[4,128,128]{2,1,0:T(8,128)(2,1)S(1)}, u32[]{:S(2)}, u32[]{:S(2)}) collective-permute-start(bf16[4,128,128]{2,1,0:T(8,128)(2,1)S(1)} %get-tuple-element.12), channel_id=1, source_target_pairs={{0,28},{4,0},{8,4},{12,8},{16,12},{20,16},{24,20},{28,24},{1,29},{... | collective-permute-start | bytes 393224 | tf_op jit(solution)/shard_map/ppermute | solution.py:18
  44.5 8.0 %collective-permute-start.11 = (bf16[4,128,128]{2,1,0:T(8,128)(2,1)S(1)}, bf16[4,128,128]{2,1,0:T(8,128)(2,1)S(1)}, u32[]{:S(2)}, u32[]{:S(2)}) collective-permute-start(bf16[4,128,128]{2,1,0:T(8,128)(2,1)S(1)} %get-tuple-element.13), channel_id=1, source_target_pairs={{0,8},{4,12},{8,16},{12,20},{16,24},{20,28},{24,0},{28,4},{1,9},{5... | collective-permute-start | bytes 393224 | tf_op jit(solution)/shard_map/ppermute | solution.py:18
  45.9 7.9 %collective-permute-start.10 = (bf16[4,128,128]{2,1,0:T(8,128)(2,1)S(1)}, bf16[4,128,128]{2,1,0:T(8,128)(2,1)S(1)}, u32[]{:S(2)}, u32[]{:S(2)}) collective-permute-start(bf16[4,128,128]{2,1,0:T(8,128)(2,1)S(1)} %get-tuple-element.13), channel_id=1, source_target_pairs={{0,4},{4,8},{8,12},{12,16},{16,20},{20,24},{24,28},{28,0},{1,5},{5... | collective-permute-start | bytes 393224 | tf_op jit(solution)/shard_map/ppermute | solution.py:18

commit v2 on v1

--- a/solution.py
+++ b/solution.py
@@ -47,10 +47,8 @@
 def attention_kernel(
     scalars,
     own,
-    near_left,
-    far_left,
-    near_right,
-    far_right,
+    left,
+    right,
     above,
     below,
     conv_weight,
@@ -95,10 +93,9 @@
         pair[b, width : 2 * width, channels : 2 * channels] = cotangent[b]
 
     acc[...] = jnp.zeros_like(acc)
-    for side, (near, far) in enumerate(((near_left, far_left), (near_right, far_right))):
+    for side, slab in enumerate((left, right)):
         image[0 : halo * width, :] = above[side * halo : (side + 1) * halo].reshape(-1, channels)
-        chosen = jnp.where(scalars[side] == 1, near[...], far[...])
-        image[halo * width : (halo + rows) * width, :] = chosen.reshape(rows * width, channels)
+        image[halo * width : (halo + rows) * width, :] = slab[...].reshape(rows * width, channels)
         image[(halo + rows) * width :, :] = below[side * halo : (side + 1) * halo].reshape(
             -1, channels
         )
@@ -201,30 +198,26 @@
     camera = lax.axis_index("cam")
     slab = lax.axis_index("row")
 
-    near_left = from_behind(image, "cam", samples)
-    near_right = from_behind(image, "cam", -samples)
-    far_left = from_behind(image, "cam", 2 * samples)
-    far_right = from_behind(image, "cam", -2 * samples)
+    gathered = lax.all_gather(image, "cam")
 
     def uses(step, side):
         other = jnp.mod(camera + step, views)
         return partners[other, side] == camera
 
-    close_left = partners[camera, 0] == jnp.mod(camera - samples, views)
-    close_right = partners[camera, 1] == jnp.mod(camera + samples, views)
+    chosen = lax.dynamic_index_in_dim(partners, camera, 0, keepdims=False)
     widths_here = lax.dynamic_index_in_dim(band_widths, camera, 0, keepdims=False)
     live = jnp.arange(BAND, dtype=jnp.int32)[None, :] < widths_here[:, None]
     places = jnp.clip(bands[0] - (slab * rows - MARGIN), 0, rows + 2 * MARGIN - 1)
     scalars = jnp.concatenate(
         [
-            jnp.stack([close_left, close_right]).astype(jnp.int32),
+            chosen,
             places.reshape(-1),
             live.reshape(-1).astype(jnp.int32),
         ]
     )
 
-    left = jnp.where(close_left, near_left, far_left)
-    right = jnp.where(close_right, near_right, far_right)
+    left = lax.dynamic_index_in_dim(gathered, chosen[0], 0, keepdims=False)
+    right = lax.dynamic_index_in_dim(gathered, chosen[1], 0, keepdims=False)
     above = passed_along(
         jnp.concatenate([left[rows - halo :], right[rows - halo :], image[rows - 1 :]]), "row", 1
     )
@@ -233,10 +226,8 @@
     attended, top, bottom, center, grad_own = attention(
         scalars,
         image,
-        near_left,
-        far_left,
-        near_right,
-        far_right,
+        left,
+        right,
         above,
         below,
         conv_weight,

time: 54.8 us -> 97.9 us (1.79)
  waiting for transfers between devices: 18.5 us -> 47.3 us
  between operations: 4.75 us -> 20.6 us
  starting transfers between devices: 20.6 us -> 16.4 us
  local copies, waits for them, and re-layouts: 2.59 us -> 5.16 us
    all_gather x0 -> x1, waiting for transfers between devices: none -> 37.1 us  [local(): gathered = lax.all_gather(image, 'cam')]
    ppermute x8 -> x4, waiting for transfers between devices: 9.7 us -> 3.09 us  [from_behind(): return lax.ppermute(value, axis, pairs)]
    ppermute x8 -> x4, starting transfers between devices: 9.58 us -> 3.32 us  [from_behind(): return lax.ppermute(value, axis, pairs)]
    ppermute x4, waiting for transfers between devices: 8.78 us -> 6.47 us  [passed_along(): return lax.ppermute(block, axis, route)]
    ppermute x4, starting transfers between devices: 11 us -> 13 us  [passed_along(): return lax.ppermute(block, axis, route)]
    slice x1, local copies, waits for them, and re-layouts: 0.02 us -> 1.06 us  [local(): left[:halo]]
    squeeze x0 -> x1, local copies, waits for them, and re-layouts: none -> 1.03 us  [local(): right = lax.dynamic_index_in_dim(gathered, chosen[1], 0, keepdims=False)]
  transfers between devices with their start and end apart: 12 -> 9, of which waited for: 8 -> 6; matrix products, arithmetic and copies ran while one was open for 4% -> 3% of each run, Pallas kernels for 0% -> 0%
where the time goes in v2:
time: 97.9 us; the launch traced here: 97.5 us
  waiting for transfers between devices  47.3 us (48%)
  between operations  20.6 us (21%)
  starting transfers between devices  16.4 us (17%)
  Pallas kernels  6.92 us (7%)
  local copies, waits for them, and re-layouts  5.16 us (5%)
  other arithmetic  1.05 us (1%)
    all_gather x1, waiting for transfers between devices, local(): gathered = lax.all_gather(image, 'cam')  37.1 us
    ppermute x4, starting transfers between devices, passed_along(): return lax.ppermute(block, axis, route)  13 us
    pallas_call x1, Pallas kernels, attention(): pl.pallas_call(attention_kernel, out_shape=(shape((rows, width, channels)...  6.92 us
    ppermute x4, waiting for transfers between devices, passed_along(): return lax.ppermute(block, axis, route)  6.47 us
    ppermute x4, starting transfers between devices, from_behind(): return lax.ppermute(value, axis, pairs)  3.32 us
    ppermute x4, waiting for transfers between devices, from_behind(): return lax.ppermute(value, axis, pairs)  3.09 us
  transfers between devices with their start and end apart: 9, of which 6 were waited for; matrix products, arithmetic and copies ran while one was open for 3% of the time, Pallas kernels for 0%

profile of v2, /device:TPU:1, one launch (start us, length us, event | category | flops | bytes accessed | tf_op | source)
XLA Modules:
  0.0 97.5 jit_solution(18081887971429319772)
XLA Ops:
  7.2 0.7 all-gather.2.cloned.1.call-update
  7.9 0.7 copy-done.6
  8.6 0.2 fusion.2
  8.8 0.5 fusion.3
  12.1 0.7 copy-done.7
  12.8 0.1 copy.13
  14.3 37.1 %all-gather.2.cloned.1.call-done = bf16[8,4,128,128]{3,2,1,0:T(8,128)(2,1)} async-done(((bf16[1,4,128,128]{3,2,1,0:T(8,128)(2,1)}), bf16[8,4,128,128]{3,2,1,0:T(8,128)(2,1)}) %all-gather.2.cloned.1.call-update) | async-done | bytes 1048592 | tf_op jit(solution)/shard_map/all_gather | solution.py:201
  51.4 1.1 %dynamic-slice_bitcast_fusion.3 = (bf16[3,128,128]{2,1,0:T(8,128)(2,1)S(1)}, bf16[3,128,128]{2,1,0:T(8,128)(2,1)S(1)}, bf16[3,128,128]{2,1,0:T(8,128)(2,1)S(1)}, bf16[3,128,128]{2,1,0:T(8,128)(2,1)S(1)}) fusion(bf16[8,4,128,128]{3,2,1,0:T(8,128)(2,1)} %all-gather.2.cloned.1.call-done, s32[]{:T(128)S(6)} %select_n.70, s32[]{:T(128)S(6)} %select_n.71, s32[]{:T(128)S(6)} %add.97), kind=kLoop, calls=%fused_computation.10 | loop fusion | bytes 786444 | tf_op jit(solution)/shard_map/slice | solution.py:224
  52.5 3.6 %collective-permute-start.1 = (bf16[7,128,128]{2,1,0:T(8,128)(2,1)S(1)}, bf16[7,128,128]{2,1,0:T(8,128)(2,1)S(1)}, u32[]{:S(2)}, u32[]{:S(2)}) collective-permute-start(bf16[7,128,128]{2,1,0:T(8,128)(2,1)S(1)} %pad_maximum_fusion.1), channel_id=1, source_target_pairs={{1,0},{2,1},{3,2},{5,4},{6,5},{7,6},{9,8},{10,9},{11,10},{13,12},{... | collective-permute-start | bytes 688136 | tf_op jit(solution)/shard_map/ppermute | solution.py:24
  56.2 3.1 %collective-permute-start = (bf16[7,128,128]{2,1,0:T(8,128)(2,1)S(1)}, bf16[7,128,128]{2,1,0:T(8,128)(2,1)S(1)}, u32[]{:S(2)}, u32[]{:S(2)}) collective-permute-start(bf16[7,128,128]{2,1,0:T(8,128)(2,1)S(1)} %pad_maximum_fusion), channel_id=1, source_target_pairs={{0,1},{1,2},{2,3},{4,5},{5,6},{6,7},{8,9},{9,10},{10,11},{12,13},{... | collective-permute-start | bytes 688136 | tf_op jit(solution)/shard_map/ppermute | solution.py:24
  59.4 1.0 %dynamic-slice_bitcast_fusion = (bf16[4,128,128]{2,1,0:T(8,128)(2,1)S(1)}, bf16[4,128,128]{2,1,0:T(8,128)(2,1)S(1)}) fusion(bf16[8,4,128,128]{3,2,1,0:T(8,128)(2,1)} %all-gather.2.cloned.1.call-done, s32[]{:T(128)S(6)} %select_n.71, s32[]{:T(128)S(6)} %select_n.70), kind=kLoop, calls=%fused_computation.7 | loop fusion | bytes 524296 | tf_op jit(solution)/shard_map/jit(dynamic_index_in_dim)/squeeze | solution.py:220
  60.4 0.5 collective-permute-done.1.below
  60.9 1.4 %collective-permute-done.above = bf16[7,128,128]{2,1,0:T(8,128)(2,1)S(1)} collective-permute-done((bf16[7,128,128]{2,1,0:T(8,128)(2,1)S(1)}, bf16[7,128,128]{2,1,0:T(8,128)(2,1)S(1)}, u32[]{:S(2)}, u32[]{:S(2)}) %collective-permute-start) | collective-permute-done | bytes 229408 | tf_op jit(solution)/shard_map/ppermute | solution.py:24
  62.3 6.9 %shard_map.104 = (bf16[4,128,128]{2,1,0:T(8,128)(2,1)}, bf16[4,128,128]{2,1,0:T(8,128)(2,1)S(1)}, bf16[4,128,128]{2,1,0:T(8,128)(2,1)S(1)}, f32[2,4,128,128]{3,2,1,0:T(8,128)S(1)}, f32[4,128,128]{2,1,0:T(8,128)S(1)}) custom-call(s32[32]{0:T(128)S(1)} %pad_add_fusion.scalars, bf16[4,128,128]{2,1,0:T(8,128)(2,1)S(1)} %bitcast.33, ...), custom_call_target="tpu_custom_call" | custom-call | flops 2000000000 | bytes 4000000 | tf_op jit(solution)/shard_map/pallas_call | solution.py:157
  69.2 4.4 %collective-permute-start.2 = (bf16[4,128,128]{2,1,0:T(8,128)(2,1)S(1)}, bf16[4,128,128]{2,1,0:T(8,128)(2,1)S(1)}, u32[]{:S(2)}, u32[]{:S(2)}) collective-permute-start(bf16[4,128,128]{2,1,0:T(8,128)(2,1)S(1)} %get-tuple-element.10), channel_id=1, source_target_pairs={{0,1},{1,2},{2,3},{4,5},{5,6},{6,7},{8,9},{9,10},{10,11},{12,13},{... | collective-permute-start | bytes 393224 | tf_op jit(solution)/shard_map/ppermute | solution.py:24
  73.6 1.9 %collective-permute-start.3 = (bf16[4,128,128]{2,1,0:T(8,128)(2,1)S(1)}, bf16[4,128,128]{2,1,0:T(8,128)(2,1)S(1)}, u32[]{:S(2)}, u32[]{:S(2)}) collective-permute-start(bf16[4,128,128]{2,1,0:T(8,128)(2,1)S(1)} %get-tuple-element.11), channel_id=1, source_target_pairs={{1,0},{2,1},{3,2},{5,4},{6,5},{7,6},{9,8},{10,9},{11,10},{13,12},{... | collective-permute-start | bytes 393224 | tf_op jit(solution)/shard_map/ppermute | solution.py:24
  75.5 4.6 %collective-permute-done.3 = bf16[4,128,128]{2,1,0:T(8,128)(2,1)S(1)} collective-permute-done((bf16[4,128,128]{2,1,0:T(8,128)(2,1)S(1)}, bf16[4,128,128]{2,1,0:T(8,128)(2,1)S(1)}, u32[]{:S(2)}, u32[]{:S(2)}) %collective-permute-start.3) | collective-permute-done | bytes 131104 | tf_op jit(solution)/shard_map/ppermute | solution.py:24
  80.2 1.6 %collective-permute-start.4 = (bf16[4,128,128]{2,1,0:T(8,128)(2,1)S(1)}, bf16[4,128,128]{2,1,0:T(8,128)(2,1)S(1)}, u32[]{:S(2)}, u32[]{:S(2)}) collective-permute-start(bf16[4,128,128]{2,1,0:T(8,128)(2,1)S(1)} %get-tuple-element.20), channel_id=1, source_target_pairs={{0,28},{4,0},{8,4},{12,8},{16,12},{20,16},{24,20},{28,24},{1,29},{... | collective-permute-start | bytes 393224 | tf_op jit(solution)/shard_map/ppermute | solution.py:18
  81.8 0.4 collective-permute-start.5
  82.2 1.4 %collective-permute-start.6 = (bf16[4,128,128]{2,1,0:T(8,128)(2,1)S(1)}, bf16[4,128,128]{2,1,0:T(8,128)(2,1)S(1)}, u32[]{:S(2)}, u32[]{:S(2)}) collective-permute-start(bf16[4,128,128]{2,1,0:T(8,128)(2,1)S(1)} %get-tuple-element.21), channel_id=1, source_target_pairs={{0,4},{4,8},{8,12},{12,16},{16,20},{20,24},{24,28},{28,0},{1,5},{5... | collective-permute-start | bytes 393224 | tf_op jit(solution)/shard_map/ppermute | solution.py:18
  83.6 0.7 constant_dynamic-slice_fusion.1
  86.8 0.8 collective-permute-done.5
  87.6 2.2 %collective-permute-done.6 = bf16[4,128,128]{2,1,0:T(8,128)(2,1)S(1)} collective-permute-done((bf16[4,128,128]{2,1,0:T(8,128)(2,1)S(1)}, bf16[4,128,128]{2,1,0:T(8,128)(2,1)S(1)}, u32[]{:S(2)}, u32[]{:S(2)}) %collective-permute-start.6) | collective-permute-done | bytes 131104 | tf_op jit(solution)/shard_map/ppermute | solution.py:18
  89.9 0.8 fusion
  (31 shorter events, 0.6 us)
Async XLA Ops:
  7.2 7.1 %copy-start = (bf16[1,4,128,128]{3,2,1,0:T(8,128)(2,1)S(1)}, bf16[1,4,128,128]{3,2,1,0:T(8,128)(2,1)}, u32[]{:S(2)}) copy-start(bf16[1,4,128,128]{3,2,1,0:T(8,128)(2,1)} %param.9) | copy-start | bytes 393220
  7.2 44.2 %all-gather.2.cloned.1.call-start = ((), (), s32[]{:S(2)}) async-start(), calls=%async_computation | async-start | bytes 1179648 | tf_op jit(solution)/shard_map/all_gather | solution.py:201
  7.9 0.7 copy-start.6
  7.9 0.7 copy-start.8
  12.1 0.7 copy-start.7
  52.5 8.4 %collective-permute-start.1 = (bf16[7,128,128]{2,1,0:T(8,128)(2,1)S(1)}, bf16[7,128,128]{2,1,0:T(8,128)(2,1)S(1)}, u32[]{:S(2)}, u32[]{:S(2)}) collective-permute-start(bf16[7,128,128]{2,1,0:T(8,128)(2,1)S(1)} %pad_maximum_fusion.1), channel_id=1, source_target_pairs={{1,0},{2,1},{3,2},{5,4},{6,5},{7,6},{9,8},{10,9},{11,10},{13,12},{... | collective-permute-start | bytes 688136 | tf_op jit(solution)/shard_map/ppermute | solution.py:24
  56.1 6.1 %copy-start.1 = (bf16[3,3,128,128]{3,2,1,0:T(8,128)(2,1)S(1)}, bf16[3,3,128,128]{3,2,1,0:T(8,128)(2,1)}, u32[]{:S(2)}) copy-start(bf16[3,3,128,128]{3,2,1,0:T(8,128)(2,1)} %conv_weight.1) | copy-start | bytes 884740
  56.2 6.1 %collective-permute-start = (bf16[7,128,128]{2,1,0:T(8,128)(2,1)S(1)}, bf16[7,128,128]{2,1,0:T(8,128)(2,1)S(1)}, u32[]{:S(2)}, u32[]{:S(2)}) collective-permute-start(bf16[7,128,128]{2,1,0:T(8,128)(2,1)S(1)} %pad_maximum_fusion), channel_id=1, source_target_pairs={{0,1},{1,2},{2,3},{4,5},{5,6},{6,7},{8,9},{9,10},{10,11},{12,13},{... | collective-permute-start | bytes 688136 | tf_op jit(solution)/shard_map/ppermute | solution.py:24
  59.4 2.9 %copy-start.2 = (bf16[1,4,128,128]{3,2,1,0:T(8,128)(2,1)S(1)}, bf16[1,4,128,128]{3,2,1,0:T(8,128)(2,1)}, u32[]{:S(2)}) copy-start(bf16[1,4,128,128]{3,2,1,0:T(8,128)(2,1)} %param.17) | copy-start | bytes 393220
  59.4 2.9 %copy-start.3 = (bf16[128,128]{1,0:T(8,128)(2,1)S(1)}, bf16[128,128]{1,0:T(8,128)(2,1)}, u32[]{:S(2)}) copy-start(bf16[128,128]{1,0:T(8,128)(2,1)} %q_weight.1) | copy-start | bytes 98308
  59.4 2.9 %copy-start.4 = (bf16[128,128]{1,0:T(8,128)(2,1)S(1)}, bf16[128,128]{1,0:T(8,128)(2,1)}, u32[]{:S(2)}) copy-start(bf16[128,128]{1,0:T(8,128)(2,1)} %k_weight.1) | copy-start | bytes 98308
  59.4 2.9 %copy-start.5 = (bf16[128,128]{1,0:T(8,128)(2,1)S(1)}, bf16[128,128]{1,0:T(8,128)(2,1)}, u32[]{:S(2)}) copy-start(bf16[128,128]{1,0:T(8,128)(2,1)} %v_weight.1) | copy-start | bytes 98308
  69.2 6.3 %collective-permute-start.2 = (bf16[4,128,128]{2,1,0:T(8,128)(2,1)S(1)}, bf16[4,128,128]{2,1,0:T(8,128)(2,1)S(1)}, u32[]{:S(2)}, u32[]{:S(2)}) collective-permute-start(bf16[4,128,128]{2,1,0:T(8,128)(2,1)S(1)} %get-tuple-element.10), channel_id=1, source_target_pairs={{0,1},{1,2},{2,3},{4,5},{5,6},{6,7},{8,9},{9,10},{10,11},{12,13},{... | collective-permute-start | bytes 393224 | tf_op jit(solution)/shard_map/ppermute | solution.py:24
  73.6 6.6 %collective-permute-start.3 = (bf16[4,128,128]{2,1,0:T(8,128)(2,1)S(1)}, bf16[4,128,128]{2,1,0:T(8,128)(2,1)S(1)}, u32[]{:S(2)}, u32[]{:S(2)}) collective-permute-start(bf16[4,128,128]{2,1,0:T(8,128)(2,1)S(1)} %get-tuple-element.11), channel_id=1, source_target_pairs={{1,0},{2,1},{3,2},{5,4},{6,5},{7,6},{9,8},{10,9},{11,10},{13,12},{... | collective-permute-start | bytes 393224 | tf_op jit(solution)/shard_map/ppermute | solution.py:24
  80.2 6.5 %collective-permute-start.4 = (bf16[4,128,128]{2,1,0:T(8,128)(2,1)S(1)}, bf16[4,128,128]{2,1,0:T(8,128)(2,1)S(1)}, u32[]{:S(2)}, u32[]{:S(2)}) collective-permute-start(bf16[4,128,128]{2,1,0:T(8,128)(2,1)S(1)} %get-tuple-element.20), channel_id=1, source_target_pairs={{0,28},{4,0},{8,4},{12,8},{16,12},{20,16},{24,20},{28,24},{1,29},{... | collective-permute-start | bytes 393224 | tf_op jit(solution)/shard_map/ppermute | solution.py:18
  81.8 5.8 %collective-permute-start.5 = (bf16[4,128,128]{2,1,0:T(8,128)(2,1)S(1)}, bf16[4,128,128]{2,1,0:T(8,128)(2,1)S(1)}, u32[]{:S(2)}, u32[]{:S(2)}) collective-permute-start(bf16[4,128,128]{2,1,0:T(8,128)(2,1)S(1)} %get-tuple-element.20), channel_id=1, source_target_pairs={{0,24},{4,28},{8,0},{12,4},{16,8},{20,12},{24,16},{28,20},{1,25},{... | collective-permute-start | bytes 393224 | tf_op jit(solution)/shard_map/ppermute | solution.py:18
  82.2 7.7 %collective-permute-start.6 = (bf16[4,128,128]{2,1,0:T(8,128)(2,1)S(1)}, bf16[4,128,128]{2,1,0:T(8,128)(2,1)S(1)}, u32[]{:S(2)}, u32[]{:S(2)}) collective-permute-start(bf16[4,128,128]{2,1,0:T(8,128)(2,1)S(1)} %get-tuple-element.21), channel_id=1, source_target_pairs={{0,4},{4,8},{8,12},{12,16},{16,20},{20,24},{24,28},{28,0},{1,5},{5... | collective-permute-start | bytes 393224 | tf_op jit(solution)/shard_map/ppermute | solution.py:18
  83.6 6.3 %collective-permute-start.7 = (bf16[4,128,128]{2,1,0:T(8,128)(2,1)S(1)}, bf16[4,128,128]{2,1,0:T(8,128)(2,1)S(1)}, u32[]{:S(2)}, u32[]{:S(2)}) collective-permute-start(bf16[4,128,128]{2,1,0:T(8,128)(2,1)S(1)} %get-tuple-element.21), channel_id=1, source_target_pairs={{0,8},{4,12},{8,16},{12,20},{16,24},{20,28},{24,0},{28,4},{1,9},{5... | collective-permute-start | bytes 393224 | tf_op jit(solution)/shard_map/ppermute | solution.py:18
Sparse Core Ops, SparseCore 0:
  10.1 41.2 all-gather.1

commit v3 on v1

--- a/solution.py
+++ b/solution.py
@@ -18,10 +18,19 @@
     return lax.ppermute(value, axis, pairs)
 
 
-def passed_along(block, axis, distance):
-    devices = range(lax.axis_size(axis))
-    route = [(i - distance, i) for i in devices if i - distance in devices]
-    return lax.ppermute(block, axis, route)
+def swapped(to_next, to_previous, axis):
+    count = lax.axis_size(axis)
+    odd = lax.rem(lax.axis_index(axis), 2) == 1
+    results = []
+    for first in (1, 0):
+        pairs = [(i, i + 1) for i in range(first, count - 1, 2)]
+        pairs = pairs + [(j, i) for i, j in pairs]
+        sends_up = odd if first == 1 else ~odd
+        results.append(lax.ppermute(jnp.where(sends_up, to_next, to_previous), axis, pairs))
+    between, within = results
+    from_previous = jnp.where(odd, within, between)
+    from_next = jnp.where(odd, between, within)
+    return from_previous, from_next
 
 
 def dot_nn(a, b):
@@ -225,10 +234,11 @@
 
     left = jnp.where(close_left, near_left, far_left)
     right = jnp.where(close_right, near_right, far_right)
-    above = passed_along(
-        jnp.concatenate([left[rows - halo :], right[rows - halo :], image[rows - 1 :]]), "row", 1
-    )
-    below = passed_along(jnp.concatenate([left[:halo], right[:halo], image[:1]]), "row", -1)
+    above, below = swapped(
+        jnp.concatenate([left[rows - halo :], right[rows - halo :], image[rows - 1 :]]),
+        jnp.concatenate([left[:halo], right[:halo], image[:1]]),
+        "row",
+    )
 
     attended, top, bottom, center, grad_own = attention(
         scalars,
@@ -246,8 +256,9 @@
         grad_attended[0],
     )
 
-    from_above = passed_along(bottom, "row", 1).reshape(2, MARGIN, *image.shape[1:])
-    from_below = passed_along(top, "row", -1).reshape(2, MARGIN, *image.shape[1:])
+    from_above, from_below = (
+        part.reshape(2, MARGIN, *image.shape[1:]) for part in swapped(bottom, top, "row")
+    )
     zeros = jnp.zeros((2, rows - MARGIN, *image.shape[1:]), jnp.float32)
     total = (
         center

time: 54.8 us -> 48.8 us (0.89)
  the two profiles are of different devices: /device:TPU:1 before, /device:TPU:4 now
where the time goes in v3:
time: 48.8 us; the launch traced here: 48.5 us
  waiting for transfers between devices  19.1 us (39%)
  starting transfers between devices  14.7 us (30%)
  Pallas kernels  6.92 us (14%)
  between operations  4.84 us (10%)
  local copies, waits for them, and re-layouts  1.74 us (4%)
  other arithmetic  1.23 us (3%)
    ppermute x8, starting transfers between devices, from_behind(): return lax.ppermute(value, axis, pairs)  10.7 us
    ppermute x8, waiting for transfers between devices, from_behind(): return lax.ppermute(value, axis, pairs)  9.94 us
    ppermute x4, waiting for transfers between devices, swapped(): lax.ppermute(jnp.where(sends_up, to_next, to_previous), axis, pairs)  9.15 us
    pallas_call x1, Pallas kernels, attention(): pl.pallas_call(attention_kernel, out_shape=(shape((rows, width, channels)...  6.92 us
    ppermute x4, starting transfers between devices, swapped(): lax.ppermute(jnp.where(sends_up, to_next, to_previous), axis, pairs)  4 us
  transfers between devices with their start and end apart: 12, of which 8 were waited for; matrix products, arithmetic and copies ran while one was open for 3% of the time, Pallas kernels for 0%

profile of v3, /device:TPU:4, one launch (start us, length us, event | category | flops | bytes accessed | tf_op | source)
XLA Modules:
  0.0 48.5 jit_solution(1611501798191126632)
XLA Ops:
  0.7 3.7 %collective-permute-start.3 = (bf16[4,128,128]{2,1,0:T(8,128)(2,1)}, bf16[4,128,128]{2,1,0:T(8,128)(2,1)S(1)}, u32[]{:S(2)}, u32[]{:S(2)}) collective-permute-start(bf16[4,128,128]{2,1,0:T(8,128)(2,1)} %bitcast.23), channel_id=1, source_target_pairs={{0,24},{4,28},{8,0},{12,4},{16,8},{20,12},{24,16},{28,20},{1,25},{... | collective-permute-start | bytes 393224 | tf_op jit(solution)/shard_map/ppermute | solution.py:18
  4.3 1.4 %collective-permute-start.2 = (bf16[4,128,128]{2,1,0:T(8,128)(2,1)}, bf16[4,128,128]{2,1,0:T(8,128)(2,1)S(1)}, u32[]{:S(2)}, u32[]{:S(2)}) collective-permute-start(bf16[4,128,128]{2,1,0:T(8,128)(2,1)} %bitcast.24), channel_id=1, source_target_pairs={{0,28},{4,0},{8,4},{12,8},{16,12},{20,16},{24,20},{28,24},{1,29},{... | collective-permute-start | bytes 393224 | tf_op jit(solution)/shard_map/ppermute | solution.py:18
  5.7 1.6 %collective-permute-start.1 = (bf16[4,128,128]{2,1,0:T(8,128)(2,1)}, bf16[4,128,128]{2,1,0:T(8,128)(2,1)S(1)}, u32[]{:S(2)}, u32[]{:S(2)}) collective-permute-start(bf16[4,128,128]{2,1,0:T(8,128)(2,1)} %bitcast.25), channel_id=1, source_target_pairs={{0,8},{4,12},{8,16},{12,20},{16,24},{20,28},{24,0},{28,4},{1,9},{5... | collective-permute-start | bytes 393224 | tf_op jit(solution)/shard_map/ppermute | solution.py:18
  7.3 0.2 dynamic-slice_reduce_fusion
  7.5 0.5 copy-done.7
  8.0 0.7 %constant_dynamic-slice_fusion.1 = (s32[1,1]{0,1:T(1,128)}, s32[1,1]{0,1:T(1,128)}, s32[1,1]{0,1:T(1,128)}, s32[1,1]{0,1:T(1,128)}, s32[1,1]{0,1:T(1,128)}, /*index=5*/s32[1,1]{0,1:T(1,128)}) fusion(s32[8,2]{0,1:T(2,128)S(1)} %copy-done.7, s32[]{:T(128)S(6)} %select_n.136, s32[]{:T(128)S(6)} %select_n.146, s32[]{:T(128)S(6)} %select_n.123, ...), kind=kLoop, calls=%fused_computation.24 | loop fusion | bytes 68 | tf_op jit(solution)/shard_map/dynamic_slice | solution.py:220
  10.1 1.3 %collective-permute-done.2.near_right = bf16[4,128,128]{2,1,0:T(8,128)(2,1)S(1)} collective-permute-done((bf16[4,128,128]{2,1,0:T(8,128)(2,1)}, bf16[4,128,128]{2,1,0:T(8,128)(2,1)S(1)}, u32[]{:S(2)}, u32[]{:S(2)}) %collective-permute-start.2) | collective-permute-done | bytes 131104 | tf_op jit(solution)/shard_map/ppermute | solution.py:18
  11.5 2.3 %collective-permute-done.1.far_left = bf16[4,128,128]{2,1,0:T(8,128)(2,1)S(1)} collective-permute-done((bf16[4,128,128]{2,1,0:T(8,128)(2,1)}, bf16[4,128,128]{2,1,0:T(8,128)(2,1)S(1)}, u32[]{:S(2)}, u32[]{:S(2)}) %collective-permute-start.1) | collective-permute-done | bytes 131104 | tf_op jit(solution)/shard_map/ppermute | solution.py:18
  13.8 1.8 %collective-permute-done.near_left = bf16[4,128,128]{2,1,0:T(8,128)(2,1)S(1)} collective-permute-done((bf16[4,128,128]{2,1,0:T(8,128)(2,1)}, bf16[4,128,128]{2,1,0:T(8,128)(2,1)S(1)}, u32[]{:S(2)}, u32[]{:S(2)}) %collective-permute-start) | collective-permute-done | bytes 131104 | tf_op jit(solution)/shard_map/ppermute | solution.py:18
  15.7 1.9 %collective-permute-start.5 = (bf16[7,128,128]{2,1,0:T(8,128)(2,1)S(1)}, bf16[7,128,128]{2,1,0:T(8,128)(2,1)S(1)}, u32[]{:S(2)}, u32[]{:S(2)}) collective-permute-start(bf16[7,128,128]{2,1,0:T(8,128)(2,1)S(1)} %get-tuple-element.14), channel_id=1, source_target_pairs={{1,2},{2,1},{5,6},{6,5},{9,10},{10,9},{13,14},{14,13},{17,18},{18,... | collective-permute-start | bytes 688136 | tf_op jit(solution)/shard_map/ppermute | solution.py:29
  17.8 0.1 copy.12
  17.9 0.1 min.12
  18.2 4.8 %collective-permute-done.5 = bf16[7,128,128]{2,1,0:T(8,128)(2,1)S(1)} collective-permute-done((bf16[7,128,128]{2,1,0:T(8,128)(2,1)S(1)}, bf16[7,128,128]{2,1,0:T(8,128)(2,1)S(1)}, u32[]{:S(2)}, u32[]{:S(2)}) %collective-permute-start.5) | collective-permute-done | bytes 229408 | tf_op jit(solution)/shard_map/ppermute | solution.py:29
  23.1 6.9 %shard_map.104 = (bf16[4,128,128]{2,1,0:T(8,128)(2,1)}, bf16[4,128,128]{2,1,0:T(8,128)(2,1)S(1)}, bf16[4,128,128]{2,1,0:T(8,128)(2,1)S(1)}, f32[2,4,128,128]{3,2,1,0:T(8,128)S(1)}, f32[4,128,128]{2,1,0:T(8,128)S(1)}) custom-call(s32[32]{0:T(128)S(1)} %pad_add_fusion.scalars, bf16[4,128,128]{2,1,0:T(8,128)(2,1)S(1)} %bitcast.27, ...), custom_call_target="tpu_custom_call" | custom-call | flops 2000000000 | bytes 4000000 | tf_op jit(solution)/shard_map/pallas_call | solution.py:169
  30.1 1.9 %collective-permute-start.7 = (bf16[4,128,128]{2,1,0:T(8,128)(2,1)S(1)}, bf16[4,128,128]{2,1,0:T(8,128)(2,1)S(1)}, u32[]{:S(2)}, u32[]{:S(2)}) collective-permute-start(bf16[4,128,128]{2,1,0:T(8,128)(2,1)S(1)} %get-tuple-element.21), channel_id=1, source_target_pairs={{1,2},{2,1},{5,6},{6,5},{9,10},{10,9},{13,14},{14,13},{17,18},{18,... | collective-permute-start | bytes 393224 | tf_op jit(solution)/shard_map/ppermute | solution.py:29
  32.1 4.3 %collective-permute-done.7 = bf16[4,128,128]{2,1,0:T(8,128)(2,1)S(1)} collective-permute-done((bf16[4,128,128]{2,1,0:T(8,128)(2,1)S(1)}, bf16[4,128,128]{2,1,0:T(8,128)(2,1)S(1)}, u32[]{:S(2)}, u32[]{:S(2)}) %collective-permute-start.7) | collective-permute-done | bytes 131104 | tf_op jit(solution)/shard_map/ppermute | solution.py:29
  36.5 1.2 %collective-permute-start.9 = (bf16[4,128,128]{2,1,0:T(8,128)(2,1)S(1)}, bf16[4,128,128]{2,1,0:T(8,128)(2,1)S(1)}, u32[]{:S(2)}, u32[]{:S(2)}) collective-permute-start(bf16[4,128,128]{2,1,0:T(8,128)(2,1)S(1)} %get-tuple-element.16), channel_id=1, source_target_pairs={{0,24},{4,28},{8,0},{12,4},{16,8},{20,12},{24,16},{28,20},{1,25},{... | collective-permute-start | bytes 393224 | tf_op jit(solution)/shard_map/ppermute | solution.py:18
  37.8 0.4 collective-permute-start.8
  38.1 2.0 %collective-permute-start.11 = (bf16[4,128,128]{2,1,0:T(8,128)(2,1)S(1)}, bf16[4,128,128]{2,1,0:T(8,128)(2,1)S(1)}, u32[]{:S(2)}, u32[]{:S(2)}) collective-permute-start(bf16[4,128,128]{2,1,0:T(8,128)(2,1)S(1)} %get-tuple-element.17), channel_id=1, source_target_pairs={{0,8},{4,12},{8,16},{12,20},{16,24},{20,28},{24,0},{28,4},{1,9},{5... | collective-permute-start | bytes 393224 | tf_op jit(solution)/shard_map/ppermute | solution.py:18
  40.1 0.6 %collective-permute-start.10 = (bf16[4,128,128]{2,1,0:T(8,128)(2,1)S(1)}, bf16[4,128,128]{2,1,0:T(8,128)(2,1)S(1)}, u32[]{:S(2)}, u32[]{:S(2)}) collective-permute-start(bf16[4,128,128]{2,1,0:T(8,128)(2,1)S(1)} %get-tuple-element.17), channel_id=1, source_target_pairs={{0,4},{4,8},{8,12},{12,16},{16,20},{20,24},{24,28},{28,0},{1,5},{5... | collective-permute-start | bytes 393224 | tf_op jit(solution)/shard_map/ppermute | solution.py:18
  43.2 0.1 collective-permute-done.8
  43.3 1.5 %collective-permute-done.11 = bf16[4,128,128]{2,1,0:T(8,128)(2,1)S(1)} collective-permute-done((bf16[4,128,128]{2,1,0:T(8,128)(2,1)S(1)}, bf16[4,128,128]{2,1,0:T(8,128)(2,1)S(1)}, u32[]{:S(2)}, u32[]{:S(2)}) %collective-permute-start.11) | collective-permute-done | bytes 131104 | tf_op jit(solution)/shard_map/ppermute | solution.py:18
  44.9 2.9 %collective-permute-done.10 = bf16[4,128,128]{2,1,0:T(8,128)(2,1)S(1)} collective-permute-done((bf16[4,128,128]{2,1,0:T(8,128)(2,1)S(1)}, bf16[4,128,128]{2,1,0:T(8,128)(2,1)S(1)}, u32[]{:S(2)}, u32[]{:S(2)}) %collective-permute-start.10) | collective-permute-done | bytes 131104 | tf_op jit(solution)/shard_map/ppermute | solution.py:18
  47.8 0.8 %fusion = bf16[1,4,128,128]{3,2,1,0:T(8,128)(2,1)} fusion(bf16[4,128,128]{2,1,0:T(8,128)(2,1)S(1)} %collective-permute-done.11, bf16[4,128,128]{2,1,0:T(8,128)(2,1)S(1)} %collective-permute-done.10, bf16[4,128,128]{2,1,0:T(8,128)(2,1)S(1)} %collective-permute-done.9, f32[4,128,128]{2,1,0:T(8,128)S(1)} %get-tuple-element.8, ...), kind=kLoop, calls=%fused_computation.8 | loop fusion | flops 851968 | bytes 917508 | tf_op jit(solution)/shard_map/broadcast_in_dim | solution.py:274
  (40 shorter events, 0.8 us)
Async XLA Ops:
  0.6 6.7 %copy-start = (s32[8,2]{0,1:T(2,128)S(1)}, s32[8,2]{0,1:T(2,128)}, u32[]{:S(2)}) copy-start(s32[8,2]{0,1:T(2,128)} %param.15) | copy-start | bytes 196
  0.6 6.6 %copy-start.1 = (bf16[1,4,128,128]{3,2,1,0:T(8,128)(2,1)S(1)}, bf16[1,4,128,128]{3,2,1,0:T(8,128)(2,1)}, u32[]{:S(2)}) copy-start(bf16[1,4,128,128]{3,2,1,0:T(8,128)(2,1)} %param.9) | copy-start | bytes 393220
  0.7 9.4 %collective-permute-start.3 = (bf16[4,128,128]{2,1,0:T(8,128)(2,1)}, bf16[4,128,128]{2,1,0:T(8,128)(2,1)S(1)}, u32[]{:S(2)}, u32[]{:S(2)}) collective-permute-start(bf16[4,128,128]{2,1,0:T(8,128)(2,1)} %bitcast.23), channel_id=1, source_target_pairs={{0,24},{4,28},{8,0},{12,4},{16,8},{20,12},{24,16},{28,20},{1,25},{... | collective-permute-start | bytes 393224 | tf_op jit(solution)/shard_map/ppermute | solution.py:18
  4.3 7.1 %collective-permute-start.2 = (bf16[4,128,128]{2,1,0:T(8,128)(2,1)}, bf16[4,128,128]{2,1,0:T(8,128)(2,1)S(1)}, u32[]{:S(2)}, u32[]{:S(2)}) collective-permute-start(bf16[4,128,128]{2,1,0:T(8,128)(2,1)} %bitcast.24), channel_id=1, source_target_pairs={{0,28},{4,0},{8,4},{12,8},{16,12},{20,16},{24,20},{28,24},{1,29},{... | collective-permute-start | bytes 393224 | tf_op jit(solution)/shard_map/ppermute | solution.py:18
  5.7 8.1 %collective-permute-start.1 = (bf16[4,128,128]{2,1,0:T(8,128)(2,1)}, bf16[4,128,128]{2,1,0:T(8,128)(2,1)S(1)}, u32[]{:S(2)}, u32[]{:S(2)}) collective-permute-start(bf16[4,128,128]{2,1,0:T(8,128)(2,1)} %bitcast.25), channel_id=1, source_target_pairs={{0,8},{4,12},{8,16},{12,20},{16,24},{20,28},{24,0},{28,4},{1,9},{5... | collective-permute-start | bytes 393224 | tf_op jit(solution)/shard_map/ppermute | solution.py:18
  7.3 8.3 %collective-permute-start = (bf16[4,128,128]{2,1,0:T(8,128)(2,1)}, bf16[4,128,128]{2,1,0:T(8,128)(2,1)S(1)}, u32[]{:S(2)}, u32[]{:S(2)}) collective-permute-start(bf16[4,128,128]{2,1,0:T(8,128)(2,1)} %bitcast.26), channel_id=1, source_target_pairs={{0,4},{4,8},{8,12},{12,16},{16,20},{20,24},{24,28},{28,0},{1,5},{5... | collective-permute-start | bytes 393224 | tf_op jit(solution)/shard_map/ppermute | solution.py:18
  7.3 0.7 %copy-start.7 = (s32[8,2]{0,1:T(2,128)S(1)}, s32[8,2]{0,1:T(2,128)}, u32[]{:S(2)}) copy-start(s32[8,2]{0,1:T(2,128)} %param.14) | copy-start | bytes 196
  9.4 0.7 %copy-start.8 = (s32[1,4,2,3]{1,2,3,0:T(2,128)S(1)}, s32[1,4,2,3]{1,2,3,0:T(2,128)}, u32[]{:S(2)}) copy-start(s32[1,4,2,3]{1,2,3,0:T(2,128)} %param.16) | copy-start | bytes 292
  15.7 7.3 %collective-permute-start.5 = (bf16[7,128,128]{2,1,0:T(8,128)(2,1)S(1)}, bf16[7,128,128]{2,1,0:T(8,128)(2,1)S(1)}, u32[]{:S(2)}, u32[]{:S(2)}) collective-permute-start(bf16[7,128,128]{2,1,0:T(8,128)(2,1)S(1)} %get-tuple-element.14), channel_id=1, source_target_pairs={{1,2},{2,1},{5,6},{6,5},{9,10},{10,9},{13,14},{14,13},{17,18},{18,... | collective-permute-start | bytes 688136 | tf_op jit(solution)/shard_map/ppermute | solution.py:29
  17.6 5.4 %collective-permute-start.4 = (bf16[7,128,128]{2,1,0:T(8,128)(2,1)S(1)}, bf16[7,128,128]{2,1,0:T(8,128)(2,1)S(1)}, u32[]{:S(2)}, u32[]{:S(2)}) collective-permute-start(bf16[7,128,128]{2,1,0:T(8,128)(2,1)S(1)} %get-tuple-element.15), channel_id=1, source_target_pairs={{0,1},{2,3},{1,0},{3,2},{4,5},{6,7},{5,4},{7,6},{8,9},{10,11},{9,8... | collective-permute-start | bytes 688136 | tf_op jit(solution)/shard_map/ppermute | solution.py:29
  18.2 4.9 %copy-start.2 = (bf16[3,3,128,128]{3,2,1,0:T(8,128)(2,1)S(1)}, bf16[3,3,128,128]{3,2,1,0:T(8,128)(2,1)}, u32[]{:S(2)}) copy-start(bf16[3,3,128,128]{3,2,1,0:T(8,128)(2,1)} %conv_weight.1) | copy-start | bytes 884740
  18.2 4.9 %copy-start.3 = (bf16[1,4,128,128]{3,2,1,0:T(8,128)(2,1)S(1)}, bf16[1,4,128,128]{3,2,1,0:T(8,128)(2,1)}, u32[]{:S(2)}) copy-start(bf16[1,4,128,128]{3,2,1,0:T(8,128)(2,1)} %param.17) | copy-start | bytes 393220
  18.2 4.9 %copy-start.4 = (bf16[128,128]{1,0:T(8,128)(2,1)S(1)}, bf16[128,128]{1,0:T(8,128)(2,1)}, u32[]{:S(2)}) copy-start(bf16[128,128]{1,0:T(8,128)(2,1)} %q_weight.1) | copy-start | bytes 98308
  18.2 4.9 %copy-start.5 = (bf16[128,128]{1,0:T(8,128)(2,1)S(1)}, bf16[128,128]{1,0:T(8,128)(2,1)}, u32[]{:S(2)}) copy-start(bf16[128,128]{1,0:T(8,128)(2,1)} %k_weight.1) | copy-start | bytes 98308
  18.2 4.9 %copy-start.6 = (bf16[128,128]{1,0:T(8,128)(2,1)S(1)}, bf16[128,128]{1,0:T(8,128)(2,1)}, u32[]{:S(2)}) copy-start(bf16[128,128]{1,0:T(8,128)(2,1)} %v_weight.1) | copy-start | bytes 98308
  30.1 2.0 %collective-permute-start.6 = (bf16[4,128,128]{2,1,0:T(8,128)(2,1)S(1)}, bf16[4,128,128]{2,1,0:T(8,128)(2,1)S(1)}, u32[]{:S(2)}, u32[]{:S(2)}) collective-permute-start(bf16[4,128,128]{2,1,0:T(8,128)(2,1)S(1)} %get-tuple-element.20), channel_id=1, source_target_pairs={{0,1},{2,3},{1,0},{3,2},{4,5},{6,7},{5,4},{7,6},{8,9},{10,11},{9,8... | collective-permute-start | bytes 393224 | tf_op jit(solution)/shard_map/ppermute | solution.py:29
  30.1 6.3 %collective-permute-start.7 = (bf16[4,128,128]{2,1,0:T(8,128)(2,1)S(1)}, bf16[4,128,128]{2,1,0:T(8,128)(2,1)S(1)}, u32[]{:S(2)}, u32[]{:S(2)}) collective-permute-start(bf16[4,128,128]{2,1,0:T(8,128)(2,1)S(1)} %get-tuple-element.21), channel_id=1, source_target_pairs={{1,2},{2,1},{5,6},{6,5},{9,10},{10,9},{13,14},{14,13},{17,18},{18,... | collective-permute-start | bytes 393224 | tf_op jit(solution)/shard_map/ppermute | solution.py:29
  36.5 6.7 %collective-permute-start.9 = (bf16[4,128,128]{2,1,0:T(8,128)(2,1)S(1)}, bf16[4,128,128]{2,1,0:T(8,128)(2,1)S(1)}, u32[]{:S(2)}, u32[]{:S(2)}) collective-permute-start(bf16[4,128,128]{2,1,0:T(8,128)(2,1)S(1)} %get-tuple-element.16), channel_id=1, source_target_pairs={{0,24},{4,28},{8,0},{12,4},{16,8},{20,12},{24,16},{28,20},{1,25},{... | collective-permute-start | bytes 393224 | tf_op jit(solution)/shard_map/ppermute | solution.py:18
  37.8 5.6 %collective-permute-start.8 = (bf16[4,128,128]{2,1,0:T(8,128)(2,1)S(1)}, bf16[4,128,128]{2,1,0:T(8,128)(2,1)S(1)}, u32[]{:S(2)}, u32[]{:S(2)}) collective-permute-start(bf16[4,128,128]{2,1,0:T(8,128)(2,1)S(1)} %get-tuple-element.16), channel_id=1, source_target_pairs={{0,28},{4,0},{8,4},{12,8},{16,12},{20,16},{24,20},{28,24},{1,29},{... | collective-permute-start | bytes 393224 | tf_op jit(solution)/shard_map/ppermute | solution.py:18
  38.1 6.8 %collective-permute-start.11 = (bf16[4,128,128]{2,1,0:T(8,128)(2,1)S(1)}, bf16[4,128,128]{2,1,0:T(8,128)(2,1)S(1)}, u32[]{:S(2)}, u32[]{:S(2)}) collective-permute-start(bf16[4,128,128]{2,1,0:T(8,128)(2,1)S(1)} %get-tuple-element.17), channel_id=1, source_target_pairs={{0,8},{4,12},{8,16},{12,20},{16,24},{20,28},{24,0},{28,4},{1,9},{5... | collective-permute-start | bytes 393224 | tf_op jit(solution)/shard_map/ppermute | solution.py:18
  40.1 7.7 %collective-permute-start.10 = (bf16[4,128,128]{2,1,0:T(8,128)(2,1)S(1)}, bf16[4,128,128]{2,1,0:T(8,128)(2,1)S(1)}, u32[]{:S(2)}, u32[]{:S(2)}) collective-permute-start(bf16[4,128,128]{2,1,0:T(8,128)(2,1)S(1)} %get-tuple-element.17), channel_id=1, source_target_pairs={{0,4},{4,8},{8,12},{12,16},{16,20},{20,24},{24,28},{28,0},{1,5},{5... | collective-permute-start | bytes 393224 | tf_op jit(solution)/shard_map/ppermute | solution.py:18

commit v4 on v3

v4 whole, which is shorter than its diff:
```python
import jax
import jax.numpy as jnp
from jax import lax
from jax.experimental import pallas as pl
from jax.experimental.pallas import tpu as pltpu
from jax.sharding import PartitionSpec as P

MARGIN = 2
BAND = 3
LOG2E = 1.4426950408889634


def from_behind(value, axis, steps):
    count = lax.axis_size(axis)
    pairs = [(source, (source + steps) % count) for source in range(count)]
    return lax.ppermute(value, axis, pairs)


def swapped(to_next, to_previous, axis):
    count = lax.axis_size(axis)
    odd = lax.rem(lax.axis_index(axis), 2) == 1
    results = []
    for first in (1, 0):
        pairs = [(i, i + 1) for i in range(first, count - 1, 2)]
        pairs = pairs + [(j, i) for i, j in pairs]
        sends_up = odd if first == 1 else ~odd
        results.append(lax.ppermute(jnp.where(sends_up, to_next, to_previous), axis, pairs))
    return results


def margins_of(odd, between, within):
    return jnp.where(odd, within, between), jnp.where(odd, between, within)


def dot_nn(a, b):
    return lax.dot_general(a, b, (((1,), (0,)), ((), ())), preferred_element_type=jnp.float32)


def dot_nt(a, b):
    return lax.dot_general(a, b, (((1,), (1,)), ((), ())), preferred_element_type=jnp.float32)


def stacked_taps(conv_weight):
    return jnp.concatenate(
        [jnp.concatenate([conv_weight[i, j] for j in range(3)], axis=1) for i in range(3)], axis=0
    )


def conv_rows(image, work, out_rows, width, taps):
    count = out_rows * width
    channels = taps.shape[1] // 3
    stacked = jnp.concatenate([image[i * width : i * width + count, :] for i in range(3)], axis=1)
    work[8 : 8 + count, :] = dot_nn(stacked, taps)
    none = jnp.zeros((1, channels), jnp.float32)
    for i in range(out_rows + 1):
        work[7 + i * width : 8 + i * width, :channels] = none
        work[8 + i * width : 9 + i * width, 2 * channels :] = none
    total = work[8 : 8 + count, channels : 2 * channels]
    total = total + work[7 : 7 + count, :channels]
    total = total + work[9 : 9 + count, 2 * channels :]
    return total.astype(jnp.bfloat16)


def side_keys(slab, odd, between, within, image, work, taps, wkv, kv, kv_t):
    rows, width, channels = slab.shape
    halo = MARGIN + 1
    win = rows + 2 * MARGIN
    above, below = margins_of(odd, between[0:halo], within[0:halo])
    image[0 : halo * width, :] = above.reshape(halo * width, channels)
    image[halo * width : (halo + rows) * width, :] = slab.reshape(rows * width, channels)
    image[(halo + rows) * width :, :] = below.reshape(halo * width, channels)
    hidden = conv_rows(image, work, win, width, taps)
    kv[...] = dot_nn(hidden, wkv).astype(jnp.bfloat16).reshape(win, width, 2 * channels)
    turned = dot_nt(wkv.T, hidden).astype(jnp.bfloat16)
    for r in range(win):
        kv_t[r] = turned[:, r * width : (r + 1) * width]


def places_of(scalars, rows, b, side):
    return [
        (
            scalars[2 + (b * 2 + side) * BAND + s],
            scalars[2 + rows * 2 * BAND + side * BAND + s] == 1,
        )
        for s in range(BAND)
    ]


def side_scores(places, kv, pair_b, width, channels):
    keys = jnp.concatenate([kv[at] for at, _ in places], axis=0)
    both = dot_nt(keys, pair_b)
    expo = jnp.exp2(both[:, :width] * (channels**-0.5 * LOG2E))
    expo = jnp.concatenate(
        [
            jnp.where(live, expo[i * width : (i + 1) * width], 0.0)
            for i, (_, live) in enumerate(places)
        ],
        axis=0,
    )
    return expo, both[:, width:]


def first_kernel(
    scalars,
    own,
    slab,
    within,
    between,
    conv_weight,
    q_weight,
    k_weight,
    v_weight,
    cotangent,
    pair,
    kv,
    kv_t,
    expo,
    grad_probs,
    image,
    work,
):
    rows, width, channels = own.shape
    halo = MARGIN + 1
    taps = stacked_taps(conv_weight)
    wkv = jnp.concatenate([k_weight[...], v_weight[...]], axis=1)

    odd = scalars[0] == 1
    above, below = margins_of(odd, between[halo], within[halo])
    image[0:width, :] = above
    image[width : (rows + 1) * width, :] = own[...].reshape(rows * width, channels)
    image[(rows + 1) * width : (rows + 2) * width, :] = below
    hidden = conv_rows(image, work, rows, width, taps)
    queries = dot_nn(hidden, q_weight[...]).astype(jnp.bfloat16)
    pair[...] = jnp.zeros_like(pair)
    for b in range(rows):
        pair[b, 0:width, 0:channels] = queries[b * width : (b + 1) * width, :]
        pair[b, width : 2 * width, channels : 2 * channels] = cotangent[b]

    side_keys(slab[...], odd, between, within, image, work, taps, wkv, kv, kv_t)
    for b in range(rows):
        expo[b], grad_probs[b] = side_scores(
            places_of(scalars, rows, b, 1), kv, pair[b], width, channels
        )


def second_kernel(
    scalars,
    near,
    far,
    within,
    between,
    conv_weight,
    q_weight,
    k_weight,
    v_weight,
    pair,
    first_kv_t,
    first_expo,
    first_grad_probs,
    attended,
    top,
    bottom,
    center,
    grad_own,
    image,
    work,
    kv,
    kv_t,
    acc,
):
    rows, width, channels = near.shape
    win = rows + 2 * MARGIN
    scale = channels**-0.5
    taps = stacked_taps(conv_weight)
    wkv = jnp.concatenate([k_weight[...], v_weight[...]], axis=1)
    acc[...] = jnp.zeros_like(acc)
    slab = jnp.where(scalars[1] == 1, near[...], far[...])
    side_keys(slab, scalars[0] == 1, between, within, image, work, taps, wkv, kv, kv_t)

    grad_q = []
    for b in range(rows):
        places = [places_of(scalars, rows, b, side) for side in range(2)]
        expo, grad_probs = side_scores(places[0], kv, pair[b], width, channels)
        expo = jnp.concatenate([expo, first_expo[b]], axis=0)
        grad_probs = jnp.concatenate([grad_probs, first_grad_probs[b]], axis=0)
        probs = expo * (1.0 / jnp.sum(expo, axis=0, keepdims=True))
        probs_bf = probs.astype(jnp.bfloat16)
        delta = jnp.sum(probs * grad_probs, axis=0, keepdims=True)
        grad_scores = (probs * (grad_probs - delta)).astype(jnp.bfloat16)
        keys_t = jnp.concatenate(
            [kv_t[at] for at, _ in places[0]] + [first_kv_t[at] for at, _ in places[1]], axis=1
        )
        attended[b] = dot_nn(keys_t[channels:], probs_bf).T.astype(jnp.bfloat16)
        grad_q.append(dot_nn(keys_t[:channels], grad_scores))
        terms = dot_nn(jnp.concatenate([grad_scores, probs_bf], axis=1), pair[b])
        for side in range(2):
            for s, (at, _) in enumerate(places[side]):
                i = side * BAND + s
                acc[side, at] += terms[i * width : (i + 1) * width]

    turned = dot_nn(q_weight[...], (jnp.concatenate(grad_q, axis=1) * scale).astype(jnp.bfloat16))
    for b in range(rows):
        grad_own[b] = turned[:, b * width : (b + 1) * width].T
    for side in range(2):
        grads = acc[side].reshape(win * width, 2 * channels)
        grads = jnp.concatenate([grads[:, :channels] * scale, grads[:, channels:]], axis=1)
        back = dot_nt(grads.astype(jnp.bfloat16), wkv).reshape(win, width, channels)
        top[side * MARGIN : (side + 1) * MARGIN] = back[:MARGIN].astype(jnp.bfloat16)
        center[side] = back[MARGIN : MARGIN + rows]
        bottom[side * MARGIN : (side + 1) * MARGIN] = back[MARGIN + rows :].astype(jnp.bfloat16)


def slab_kernel(scalars, center, within, between, left, right):
    rows, width, channels = left.shape
    above, below = margins_of(scalars[0] == 1, between[...], within[...])
    for side, out in enumerate((left, right)):
        for r in range(rows):
            total = center[side, r]
            if r < MARGIN:
                total = total + above[side * MARGIN + r].astype(jnp.float32)
            if r >= rows - MARGIN:
                total = total + below[side * MARGIN + r - rows + MARGIN].astype(jnp.float32)
            out[r] = total.astype(jnp.bfloat16)


def on_device(kernel, out_shape, scratch, flops, *arrays):
    vmem = pl.BlockSpec(memory_space=pltpu.VMEM)
    return pl.pallas_call(
        kernel,
        out_shape=tuple(jax.ShapeDtypeStruct(*one) for one in out_shape),
        in_specs=[pl.BlockSpec(memory_space=pltpu.SMEM)] + [vmem] * (len(arrays) - 1),
        out_specs=(vmem,) * len(out_shape),
        scratch_shapes=[pltpu.VMEM(*one) for one in scratch],
        compiler_params=pltpu.CompilerParams(vmem_limit_bytes=32 * 1024 * 1024),
        cost_estimate=pl.CostEstimate(
            flops=flops, bytes_accessed=flops // 1000, transcendentals=0
        ),
    )(*arrays)


def local(
    features_in,
    conv_weight,
    q_weight,
    k_weight,
    v_weight,
    partners,
    band_widths,
    bands,
    grad_attended,
):
    image = features_in[0]
    rows = image.shape[0]
    halo = MARGIN + 1
    views = lax.axis_size("cam")
    samples = views // min(16, views)
    camera = lax.axis_index("cam")
    slab = lax.axis_index("row")

    near_left = from_behind(image, "cam", samples)
    near_right = from_behind(image, "cam", -samples)
    far_left = from_behind(image, "cam", 2 * samples)
    far_right = from_behind(image, "cam", -2 * samples)

    def uses(step, side):
        other = jnp.mod(camera + step, views)
        return partners[other, side] == camera

    close_left = partners[camera, 0] == jnp.mod(camera - samples, views)
    close_right = partners[camera, 1] == jnp.mod(camera + samples, views)
    widths_here = lax.dynamic_index_in_dim(band_widths, camera, 0, keepdims=False)
    live = jnp.arange(BAND, dtype=jnp.int32)[None, :] < widths_here[:, None]
    places = jnp.clip(bands[0] - (slab * rows - MARGIN), 0, rows + 2 * MARGIN - 1)
    scalars = jnp.concatenate(
        [
            jnp.mod(slab, 2).reshape(1),
            close_left.astype(jnp.int32).reshape(1),
            places.reshape(-1),
            live.reshape(-1).astype(jnp.int32),
        ]
    )

    right = jnp.where(close_right, near_right, far_right)
    between, within = swapped(
        jnp.concatenate([right[rows - halo :], image[rows - 1 :]]),
        jnp.concatenate([right[:halo], image[:1]]),
        "row",
    )
    width, channels = image.shape[1:]
    win = rows + 2 * MARGIN
    half, full = jnp.bfloat16, jnp.float32
    conv_scratch = [
        (((win + 2) * width, channels), half),
        ((win * width + 16, 3 * channels), full),
    ]
    pair, _, first_kv_t, first_expo, first_grad_probs = on_device(
        first_kernel,
        [
            ((rows, 2 * width, 2 * channels), half),
            ((win, width, 2 * channels), half),
            ((win, 2 * channels, width), half),
            ((rows, BAND * width, width), full),
            ((rows, BAND * width, width), full),
        ],
        conv_scratch,
        1_000_000,
        scalars,
        image,
        right,
        within,
        between,
        conv_weight,
        q_weight,
        k_weight,
        v_weight,
        grad_attended[0],
    )
    close_left, _ = lax.optimization_barrier((close_left, right))
    left = jnp.where(close_left, near_left, far_left)
    between, within = swapped(left[rows - halo :], left[:halo], "row")
    attended, top, bottom, center, grad_own = on_device(
        second_kernel,
        [
            ((rows, width, channels), half),
            ((2 * MARGIN, width, channels), half),
            ((2 * MARGIN, width, channels), half),
            ((2, rows, width, channels), full),
            ((rows, width, channels), full),
        ],
        conv_scratch
        + [
            ((win, width, 2 * channels), half),
            ((win, 2 * channels, width), half),
            ((2, win, width, 2 * channels), full),
        ],
        1_500_000_000,
        scalars,
        near_left,
        far_left,
        within,
        between,
        conv_weight,
        q_weight,
        k_weight,
        v_weight,
        pair,
        first_kv_t,
        first_expo,
        first_grad_probs,
    )

    between, within = swapped(bottom, top, "row")
    total = on_device(
        slab_kernel,
        [(image.shape, half)] * 2,
        [],
        1_000_000,
        scalars,
        center,
        within,
        between,
    )
    summed = grad_own
    for side, sign in ((0, -1), (1, 1)):
        for distance in (1, 2):
            step = sign * distance * samples
            came = from_behind(total[side], "cam", step)
            summed = summed + jnp.where(uses(-step, side), came.astype(jnp.float32), 0.0)
    return (attended[None], summed.astype(jnp.bfloat16)[None])


def solution(mesh):
    placed = (
        P("cam", "row", None, None),
        P(),
        P(),
        P(),
        P(),
        P(),
        P(),
        P("cam", "row", None, None),
        P("cam", "row", None, None),
    )
    return jax.shard_map(
        local,
        mesh=mesh,
        in_specs=placed,
        out_specs=(P("cam", "row", None, None), P("cam", "row", None, None)),
        check_vma=False,
    )
```

time: 48.8 us -> 49.4 us (1.012)
  the two profiles are of different devices: /device:TPU:4 before, /device:TPU:1 now
where the time goes in v4:
time: 49.4 us; the launch traced here: 49 us
  starting transfers between devices  24.5 us (50%)
  Pallas kernels  8.7 us (18%)
  waiting for transfers between devices  8.1 us (16%)
  between operations  4.79 us (10%)
  local copies, waits for them, and re-layouts  1.91 us (4%)
  other arithmetic  1.04 us (2%)
    ppermute x6, starting transfers between devices, swapped(): lax.ppermute(jnp.where(sends_up, to_next, to_previous), axis, pairs)  12.6 us
    ppermute x8, starting transfers between devices, from_behind(): return lax.ppermute(value, axis, pairs)  11.9 us
    pallas_call x3, Pallas kernels, on_device(): pl.pallas_call(kernel, out_shape=tuple((jax.ShapeDtypeStruct(*one) for on...  8.7 us
    ppermute x8, waiting for transfers between devices, from_behind(): return lax.ppermute(value, axis, pairs)  4.77 us
    ppermute x6, waiting for transfers between devices, swapped(): lax.ppermute(jnp.where(sends_up, to_next, to_previous), axis, pairs)  3.33 us
  transfers between devices with their start and end apart: 14, of which 3 were waited for; matrix products, arithmetic and copies ran while one was open for 3% of the time, Pallas kernels for 6%

profile of v4, /device:TPU:1, one launch (start us, length us, event | category | flops | bytes accessed | tf_op | source)
XLA Modules:
  0.0 49.0 jit_solution(2931268126857645045)
XLA Ops:
  0.7 4.2 %collective-permute-start.3 = (bf16[4,128,128]{2,1,0:T(8,128)(2,1)}, bf16[4,128,128]{2,1,0:T(8,128)(2,1)S(1)}, u32[]{:S(2)}, u32[]{:S(2)}) collective-permute-start(bf16[4,128,128]{2,1,0:T(8,128)(2,1)} %bitcast.17), channel_id=1, source_target_pairs={{0,24},{4,28},{8,0},{12,4},{16,8},{20,12},{24,16},{28,20},{1,25},{... | collective-permute-start | bytes 393224 | tf_op jit(solution)/shard_map/ppermute | solution.py:16
  4.9 1.1 %collective-permute-start.2 = (bf16[4,128,128]{2,1,0:T(8,128)(2,1)}, bf16[4,128,128]{2,1,0:T(8,128)(2,1)S(1)}, u32[]{:S(2)}, u32[]{:S(2)}) collective-permute-start(bf16[4,128,128]{2,1,0:T(8,128)(2,1)} %bitcast.18), channel_id=1, source_target_pairs={{0,28},{4,0},{8,4},{12,8},{16,12},{20,16},{24,20},{28,24},{1,29},{... | collective-permute-start | bytes 393224 | tf_op jit(solution)/shard_map/ppermute | solution.py:16
  6.0 1.3 %collective-permute-start.1 = (bf16[4,128,128]{2,1,0:T(8,128)(2,1)}, bf16[4,128,128]{2,1,0:T(8,128)(2,1)S(1)}, u32[]{:S(2)}, u32[]{:S(2)}) collective-permute-start(bf16[4,128,128]{2,1,0:T(8,128)(2,1)} %bitcast.19), channel_id=1, source_target_pairs={{0,8},{4,12},{8,16},{12,20},{16,24},{20,28},{24,0},{28,4},{1,9},{5... | collective-permute-start | bytes 393224 | tf_op jit(solution)/shard_map/ppermute | solution.py:16
  7.3 0.2 dynamic-slice_reduce_fusion
  7.4 0.1 compare_convert_fusion
  7.5 0.1 reshape.35
  7.6 0.7 %copy-done.7 = s32[8,2]{0,1:T(2,128)S(1)} copy-done((s32[8,2]{0,1:T(2,128)S(1)}, s32[8,2]{0,1:T(2,128)}, u32[]{:S(2)}) %copy-start.7) | copy-done | bytes 88
  8.3 0.7 %constant_dynamic-slice_fusion.1 = (s32[1,1]{0,1:T(1,128)}, s32[1,1]{0,1:T(1,128)}, s32[1,1]{0,1:T(1,128)}, s32[1,1]{0,1:T(1,128)}, s32[1,1]{0,1:T(1,128)}, /*index=5*/s32[1,1]{0,1:T(1,128)}) fusion(s32[8,2]{0,1:T(2,128)S(1)} %copy-done.7, s32[]{:T(128)S(6)} %select_n.135, s32[]{:T(128)S(6)} %select_n.141, s32[]{:T(128)S(6)} %select_n.120, ...), kind=kLoop, calls=%fused_computation.18 | loop fusion | bytes 68 | tf_op jit(solution)/shard_map/dynamic_slice | solution.py:267
  10.3 0.1 copy.12
  10.4 0.1 min.12
  10.6 5.4 %collective-permute-start.7 = (bf16[4,128,128]{2,1,0:T(8,128)(2,1)S(1)}, bf16[4,128,128]{2,1,0:T(8,128)(2,1)S(1)}, u32[]{:S(2)}, u32[]{:S(2)}) collective-permute-start(bf16[4,128,128]{2,1,0:T(8,128)(2,1)S(1)} %get-tuple-element.28), channel_id=1, source_target_pairs={{1,2},{2,1},{5,6},{6,5},{9,10},{10,9},{13,14},{14,13},{17,18},{18,... | collective-permute-start | bytes 393224 | tf_op jit(solution)/shard_map/ppermute | solution.py:27
  16.3 4.1 %collective-permute-start.5 = (bf16[3,128,128]{2,1,0:T(8,128)(2,1)S(1)}, bf16[3,128,128]{2,1,0:T(8,128)(2,1)S(1)}, u32[]{:S(2)}, u32[]{:S(2)}) collective-permute-start(bf16[3,128,128]{2,1,0:T(8,128)(2,1)S(1)} %get-tuple-element.34), channel_id=1, source_target_pairs={{1,2},{2,1},{5,6},{6,5},{9,10},{10,9},{13,14},{14,13},{17,18},{18,... | collective-permute-start | bytes 294920 | tf_op jit(solution)/shard_map/ppermute | solution.py:27
  20.4 0.1 pad_add_fusion.scalars
  20.5 2.8 %shard_map.104 = (bf16[4,256,256]{2,1,0:T(8,128)(2,1)S(1)}, bf16[8,128,256]{2,1,0:T(8,128)(2,1)}, bf16[8,256,128]{2,1,0:T(8,128)(2,1)S(1)}, f32[4,384,128]{2,1,0:T(8,128)S(1)}, f32[4,384,128]{2,1,0:T(8,128)S(1)}) custom-call(s32[32]{0:T(128)S(1)} %pad_add_fusion.scalars, bf16[4,128,128]{2,1,0:T(8,128)(2,1)S(1)} %bitcast.21, ...), custom_call_target="tpu_custom_call" | custom-call | flops 1000000 | bytes 1000 | tf_op jit(solution)/shard_map/pallas_call | solution.py:228
  23.4 5.3 %shard_map.105 = (bf16[4,128,128]{2,1,0:T(8,128)(2,1)}, bf16[4,128,128]{2,1,0:T(8,128)(2,1)S(1)}, bf16[4,128,128]{2,1,0:T(8,128)(2,1)S(1)}, f32[2,4,128,128]{3,2,1,0:T(8,128)S(1)}, f32[4,128,128]{2,1,0:T(8,128)S(1)}) custom-call(s32[32]{0:T(128)S(1)} %pad_add_fusion.scalars, bf16[4,128,128]{2,1,0:T(8,128)(2,1)S(1)} %collective-permute-done.near, ...), custom_call_target="tpu_custom_call" | custom-call | flops 1500000000 | bytes 1500000 | tf_op jit(solution)/shard_map/pallas_call | solution.py:228
  28.7 2.9 %collective-permute-start.9 = (bf16[4,128,128]{2,1,0:T(8,128)(2,1)S(1)}, bf16[4,128,128]{2,1,0:T(8,128)(2,1)S(1)}, u32[]{:S(2)}, u32[]{:S(2)}) collective-permute-start(bf16[4,128,128]{2,1,0:T(8,128)(2,1)S(1)} %get-tuple-element.26), channel_id=1, source_target_pairs={{1,2},{2,1},{5,6},{6,5},{9,10},{10,9},{13,14},{14,13},{17,18},{18,... | collective-permute-start | bytes 393224 | tf_op jit(solution)/shard_map/ppermute | solution.py:27
  31.6 3.3 %collective-permute-done.9.between = bf16[4,128,128]{2,1,0:T(8,128)(2,1)S(1)} collective-permute-done((bf16[4,128,128]{2,1,0:T(8,128)(2,1)S(1)}, bf16[4,128,128]{2,1,0:T(8,128)(2,1)S(1)}, u32[]{:S(2)}, u32[]{:S(2)}) %collective-permute-start.9) | collective-permute-done | bytes 131104 | tf_op jit(solution)/shard_map/ppermute | solution.py:27
  34.9 0.6 %shard_map.106 = (bf16[4,128,128]{2,1,0:T(8,128)(2,1)S(1)}, bf16[4,128,128]{2,1,0:T(8,128)(2,1)S(1)}) custom-call(s32[32]{0:T(128)S(1)} %pad_add_fusion.scalars, f32[2,4,128,128]{3,2,1,0:T(8,128)S(1)} %get-tuple-element.21.center, bf16[4,128,128]{2,1,0:T(8,128)(2,1)S(1)} %collective-permute-done.8.within, bf16[4,128,128]{2,1,0:T(8,128)(2,1)S(1)} %collective-permute-done.9.between), custom_call_target="tpu_custom_call" | custom-call | flops 1000000 | bytes 1000 | tf_op jit(solution)/shard_map/pallas_call | solution.py:228
  35.6 0.9 %collective-permute-start.11 = (bf16[4,128,128]{2,1,0:T(8,128)(2,1)S(1)}, bf16[4,128,128]{2,1,0:T(8,128)(2,1)S(1)}, u32[]{:S(2)}, u32[]{:S(2)}) collective-permute-start(bf16[4,128,128]{2,1,0:T(8,128)(2,1)S(1)} %get-tuple-element.24), channel_id=1, source_target_pairs={{0,24},{4,28},{8,0},{12,4},{16,8},{20,12},{24,16},{28,20},{1,25},{... | collective-permute-start | bytes 393224 | tf_op jit(solution)/shard_map/ppermute | solution.py:16
  36.5 2.9 %collective-permute-start.10 = (bf16[4,128,128]{2,1,0:T(8,128)(2,1)S(1)}, bf16[4,128,128]{2,1,0:T(8,128)(2,1)S(1)}, u32[]{:S(2)}, u32[]{:S(2)}) collective-permute-start(bf16[4,128,128]{2,1,0:T(8,128)(2,1)S(1)} %get-tuple-element.24), channel_id=1, source_target_pairs={{0,28},{4,0},{8,4},{12,8},{16,12},{20,16},{24,20},{28,24},{1,29},{... | collective-permute-start | bytes 393224 | tf_op jit(solution)/shard_map/ppermute | solution.py:16
  39.4 1.4 %collective-permute-start.13 = (bf16[4,128,128]{2,1,0:T(8,128)(2,1)S(1)}, bf16[4,128,128]{2,1,0:T(8,128)(2,1)S(1)}, u32[]{:S(2)}, u32[]{:S(2)}) collective-permute-start(bf16[4,128,128]{2,1,0:T(8,128)(2,1)S(1)} %get-tuple-element.25), channel_id=1, source_target_pairs={{0,8},{4,12},{8,16},{12,20},{16,24},{20,28},{24,0},{28,4},{1,9},{5... | collective-permute-start | bytes 393224 | tf_op jit(solution)/shard_map/ppermute | solution.py:16
  43.5 2.0 %collective-permute-done.13 = bf16[4,128,128]{2,1,0:T(8,128)(2,1)S(1)} collective-permute-done((bf16[4,128,128]{2,1,0:T(8,128)(2,1)S(1)}, bf16[4,128,128]{2,1,0:T(8,128)(2,1)S(1)}, u32[]{:S(2)}, u32[]{:S(2)}) %collective-permute-start.13) | collective-permute-done | bytes 131104 | tf_op jit(solution)/shard_map/ppermute | solution.py:16
  45.5 2.8 %collective-permute-done.12 = bf16[4,128,128]{2,1,0:T(8,128)(2,1)S(1)} collective-permute-done((bf16[4,128,128]{2,1,0:T(8,128)(2,1)S(1)}, bf16[4,128,128]{2,1,0:T(8,128)(2,1)S(1)}, u32[]{:S(2)}, u32[]{:S(2)}) %collective-permute-start.12) | collective-permute-done | bytes 131104 | tf_op jit(solution)/shard_map/ppermute | solution.py:16
  48.2 0.8 %fusion = bf16[1,4,128,128]{3,2,1,0:T(8,128)(2,1)} fusion(bf16[4,128,128]{2,1,0:T(8,128)(2,1)S(1)} %collective-permute-done.13, bf16[4,128,128]{2,1,0:T(8,128)(2,1)S(1)} %collective-permute-done.12, bf16[4,128,128]{2,1,0:T(8,128)(2,1)S(1)} %collective-permute-done.11, f32[4,128,128]{2,1,0:T(8,128)S(1)} %get-tuple-element.20, ...), kind=kLoop, calls=%fused_computation.1 | loop fusion | flops 851968 | bytes 917508 | tf_op jit(solution)/shard_map/broadcast_in_dim | solution.py:369
  (41 shorter events, 0.5 us)
Async XLA Ops:
  0.6 6.6 %copy-start = (s32[8,2]{0,1:T(2,128)S(1)}, s32[8,2]{0,1:T(2,128)}, u32[]{:S(2)}) copy-start(s32[8,2]{0,1:T(2,128)} %param.15) | copy-start | bytes 196
  0.6 9.8 %copy-start.2 = (bf16[1,4,128,128]{3,2,1,0:T(8,128)(2,1)S(1)}, bf16[1,4,128,128]{3,2,1,0:T(8,128)(2,1)}, u32[]{:S(2)}) copy-start(bf16[1,4,128,128]{3,2,1,0:T(8,128)(2,1)} %param.9) | copy-start | bytes 393220
  0.7 9.8 %collective-permute-start.3 = (bf16[4,128,128]{2,1,0:T(8,128)(2,1)}, bf16[4,128,128]{2,1,0:T(8,128)(2,1)S(1)}, u32[]{:S(2)}, u32[]{:S(2)}) collective-permute-start(bf16[4,128,128]{2,1,0:T(8,128)(2,1)} %bitcast.17), channel_id=1, source_target_pairs={{0,24},{4,28},{8,0},{12,4},{16,8},{20,12},{24,16},{28,20},{1,25},{... | collective-permute-start | bytes 393224 | tf_op jit(solution)/shard_map/ppermute | solution.py:16
  4.9 5.7 %collective-permute-start.2 = (bf16[4,128,128]{2,1,0:T(8,128)(2,1)}, bf16[4,128,128]{2,1,0:T(8,128)(2,1)S(1)}, u32[]{:S(2)}, u32[]{:S(2)}) collective-permute-start(bf16[4,128,128]{2,1,0:T(8,128)(2,1)} %bitcast.18), channel_id=1, source_target_pairs={{0,28},{4,0},{8,4},{12,8},{16,12},{20,16},{24,20},{28,24},{1,29},{... | collective-permute-start | bytes 393224 | tf_op jit(solution)/shard_map/ppermute | solution.py:16
  6.0 10.2 %collective-permute-start.1 = (bf16[4,128,128]{2,1,0:T(8,128)(2,1)}, bf16[4,128,128]{2,1,0:T(8,128)(2,1)S(1)}, u32[]{:S(2)}, u32[]{:S(2)}) collective-permute-start(bf16[4,128,128]{2,1,0:T(8,128)(2,1)} %bitcast.19), channel_id=1, source_target_pairs={{0,8},{4,12},{8,16},{12,20},{16,24},{20,28},{24,0},{28,4},{1,9},{5... | collective-permute-start | bytes 393224 | tf_op jit(solution)/shard_map/ppermute | solution.py:16
  7.3 8.9 %collective-permute-start = (bf16[4,128,128]{2,1,0:T(8,128)(2,1)}, bf16[4,128,128]{2,1,0:T(8,128)(2,1)S(1)}, u32[]{:S(2)}, u32[]{:S(2)}) collective-permute-start(bf16[4,128,128]{2,1,0:T(8,128)(2,1)} %bitcast.20), channel_id=1, source_target_pairs={{0,4},{4,8},{8,12},{12,16},{16,20},{20,24},{24,28},{28,0},{1,5},{5... | collective-permute-start | bytes 393224 | tf_op jit(solution)/shard_map/ppermute | solution.py:16
  7.6 0.7 %copy-start.7 = (s32[8,2]{0,1:T(2,128)S(1)}, s32[8,2]{0,1:T(2,128)}, u32[]{:S(2)}) copy-start(s32[8,2]{0,1:T(2,128)} %param.14) | copy-start | bytes 196
  9.6 0.7 %copy-start.8 = (s32[1,4,2,3]{1,2,3,0:T(2,128)S(1)}, s32[1,4,2,3]{1,2,3,0:T(2,128)}, u32[]{:S(2)}) copy-start(s32[1,4,2,3]{1,2,3,0:T(2,128)} %param.16) | copy-start | bytes 292
  10.6 9.9 %collective-permute-start.7 = (bf16[4,128,128]{2,1,0:T(8,128)(2,1)S(1)}, bf16[4,128,128]{2,1,0:T(8,128)(2,1)S(1)}, u32[]{:S(2)}, u32[]{:S(2)}) collective-permute-start(bf16[4,128,128]{2,1,0:T(8,128)(2,1)S(1)} %get-tuple-element.28), channel_id=1, source_target_pairs={{1,2},{2,1},{5,6},{6,5},{9,10},{10,9},{13,14},{14,13},{17,18},{18,... | collective-permute-start | bytes 393224 | tf_op jit(solution)/shard_map/ppermute | solution.py:27
  16.1 4.4 %collective-permute-start.6 = (bf16[4,128,128]{2,1,0:T(8,128)(2,1)S(1)}, bf16[4,128,128]{2,1,0:T(8,128)(2,1)S(1)}, u32[]{:S(2)}, u32[]{:S(2)}) collective-permute-start(bf16[4,128,128]{2,1,0:T(8,128)(2,1)S(1)} %get-tuple-element.29), channel_id=1, source_target_pairs={{0,1},{2,3},{1,0},{3,2},{4,5},{6,7},{5,4},{7,6},{8,9},{10,11},{9,8... | collective-permute-start | bytes 393224 | tf_op jit(solution)/shard_map/ppermute | solution.py:27
  16.2 4.3 %copy-start.3 = (bf16[1,4,128,128]{3,2,1,0:T(8,128)(2,1)S(1)}, bf16[1,4,128,128]{3,2,1,0:T(8,128)(2,1)}, u32[]{:S(2)}) copy-start(bf16[1,4,128,128]{3,2,1,0:T(8,128)(2,1)} %param.17) | copy-start | bytes 393220
  16.2 4.3 %copy-start.1 = (bf16[3,3,128,128]{3,2,1,0:T(8,128)(2,1)S(1)}, bf16[3,3,128,128]{3,2,1,0:T(8,128)(2,1)}, u32[]{:S(2)}) copy-start(bf16[3,3,128,128]{3,2,1,0:T(8,128)(2,1)} %conv_weight.3) | copy-start | bytes 884740
  16.2 4.3 %copy-start.4 = (bf16[128,128]{1,0:T(8,128)(2,1)S(1)}, bf16[128,128]{1,0:T(8,128)(2,1)}, u32[]{:S(2)}) copy-start(bf16[128,128]{1,0:T(8,128)(2,1)} %q_weight.3) | copy-start | bytes 98308
  16.2 4.3 %copy-start.5 = (bf16[128,128]{1,0:T(8,128)(2,1)S(1)}, bf16[128,128]{1,0:T(8,128)(2,1)}, u32[]{:S(2)}) copy-start(bf16[128,128]{1,0:T(8,128)(2,1)} %k_weight.3) | copy-start | bytes 98308
  16.2 4.3 %copy-start.6 = (bf16[128,128]{1,0:T(8,128)(2,1)S(1)}, bf16[128,128]{1,0:T(8,128)(2,1)}, u32[]{:S(2)}) copy-start(bf16[128,128]{1,0:T(8,128)(2,1)} %v_weight.3) | copy-start | bytes 98308
  16.3 7.1 %collective-permute-start.5 = (bf16[3,128,128]{2,1,0:T(8,128)(2,1)S(1)}, bf16[3,128,128]{2,1,0:T(8,128)(2,1)S(1)}, u32[]{:S(2)}, u32[]{:S(2)}) collective-permute-start(bf16[3,128,128]{2,1,0:T(8,128)(2,1)S(1)} %get-tuple-element.34), channel_id=1, source_target_pairs={{1,2},{2,1},{5,6},{6,5},{9,10},{10,9},{13,14},{14,13},{17,18},{18,... | collective-permute-start | bytes 294920 | tf_op jit(solution)/shard_map/ppermute | solution.py:27
  20.3 3.0 %collective-permute-start.4 = (bf16[3,128,128]{2,1,0:T(8,128)(2,1)S(1)}, bf16[3,128,128]{2,1,0:T(8,128)(2,1)S(1)}, u32[]{:S(2)}, u32[]{:S(2)}) collective-permute-start(bf16[3,128,128]{2,1,0:T(8,128)(2,1)S(1)} %get-tuple-element.35), channel_id=1, source_target_pairs={{0,1},{2,3},{1,0},{3,2},{4,5},{6,7},{5,4},{7,6},{8,9},{10,11},{9,8... | collective-permute-start | bytes 294920 | tf_op jit(solution)/shard_map/ppermute | solution.py:27
  28.7 6.3 %collective-permute-start.9 = (bf16[4,128,128]{2,1,0:T(8,128)(2,1)S(1)}, bf16[4,128,128]{2,1,0:T(8,128)(2,1)S(1)}, u32[]{:S(2)}, u32[]{:S(2)}) collective-permute-start(bf16[4,128,128]{2,1,0:T(8,128)(2,1)S(1)} %get-tuple-element.26), channel_id=1, source_target_pairs={{1,2},{2,1},{5,6},{6,5},{9,10},{10,9},{13,14},{14,13},{17,18},{18,... | collective-permute-start | bytes 393224 | tf_op jit(solution)/shard_map/ppermute | solution.py:27
  31.5 3.4 %collective-permute-start.8 = (bf16[4,128,128]{2,1,0:T(8,128)(2,1)S(1)}, bf16[4,128,128]{2,1,0:T(8,128)(2,1)S(1)}, u32[]{:S(2)}, u32[]{:S(2)}) collective-permute-start(bf16[4,128,128]{2,1,0:T(8,128)(2,1)S(1)} %get-tuple-element.27), channel_id=1, source_target_pairs={{0,1},{2,3},{1,0},{3,2},{4,5},{6,7},{5,4},{7,6},{8,9},{10,11},{9,8... | collective-permute-start | bytes 393224 | tf_op jit(solution)/shard_map/ppermute | solution.py:27
  35.6 7.9 %collective-permute-start.11 = (bf16[4,128,128]{2,1,0:T(8,128)(2,1)S(1)}, bf16[4,128,128]{2,1,0:T(8,128)(2,1)S(1)}, u32[]{:S(2)}, u32[]{:S(2)}) collective-permute-start(bf16[4,128,128]{2,1,0:T(8,128)(2,1)S(1)} %get-tuple-element.24), channel_id=1, source_target_pairs={{0,24},{4,28},{8,0},{12,4},{16,8},{20,12},{24,16},{28,20},{1,25},{... | collective-permute-start | bytes 393224 | tf_op jit(solution)/shard_map/ppermute | solution.py:16
  36.5 6.9 %collective-permute-start.10 = (bf16[4,128,128]{2,1,0:T(8,128)(2,1)S(1)}, bf16[4,128,128]{2,1,0:T(8,128)(2,1)S(1)}, u32[]{:S(2)}, u32[]{:S(2)}) collective-permute-start(bf16[4,128,128]{2,1,0:T(8,128)(2,1)S(1)} %get-tuple-element.24), channel_id=1, source_target_pairs={{0,28},{4,0},{8,4},{12,8},{16,12},{20,16},{24,20},{28,24},{1,29},{... | collective-permute-start | bytes 393224 | tf_op jit(solution)/shard_map/ppermute | solution.py:16
  39.4 6.0 %collective-permute-start.13 = (bf16[4,128,128]{2,1,0:T(8,128)(2,1)S(1)}, bf16[4,128,128]{2,1,0:T(8,128)(2,1)S(1)}, u32[]{:S(2)}, u32[]{:S(2)}) collective-permute-start(bf16[4,128,128]{2,1,0:T(8,128)(2,1)S(1)} %get-tuple-element.25), channel_id=1, source_target_pairs={{0,8},{4,12},{8,16},{12,20},{16,24},{20,28},{24,0},{28,4},{1,9},{5... | collective-permute-start | bytes 393224 | tf_op jit(solution)/shard_map/ppermute | solution.py:16
  40.8 7.4 %collective-permute-start.12 = (bf16[4,128,128]{2,1,0:T(8,128)(2,1)S(1)}, bf16[4,128,128]{2,1,0:T(8,128)(2,1)S(1)}, u32[]{:S(2)}, u32[]{:S(2)}) collective-permute-start(bf16[4,128,128]{2,1,0:T(8,128)(2,1)S(1)} %get-tuple-element.25), channel_id=1, source_target_pairs={{0,4},{4,8},{8,12},{12,16},{16,20},{20,24},{24,28},{28,0},{1,5},{5... | collective-permute-start | bytes 393224 | tf_op jit(solution)/shard_map/ppermute | solution.py:16

commit v5 on v4

--- a/solution.py
+++ b/solution.py
@@ -8,12 +8,6 @@
 MARGIN = 2
 BAND = 3
 LOG2E = 1.4426950408889634
-
-
-def from_behind(value, axis, steps):
-    count = lax.axis_size(axis)
-    pairs = [(source, (source + steps) % count) for source in range(count)]
-    return lax.ppermute(value, axis, pairs)
 
 
 def swapped(to_next, to_previous, axis):
@@ -79,8 +73,8 @@
 def places_of(scalars, rows, b, side):
     return [
         (
-            scalars[2 + (b * 2 + side) * BAND + s],
-            scalars[2 + rows * 2 * BAND + side * BAND + s] == 1,
+            scalars[1 + (b * 2 + side) * BAND + s],
+            scalars[1 + rows * 2 * BAND + side * BAND + s] == 1,
         )
         for s in range(BAND)
     ]
@@ -112,12 +106,12 @@
     v_weight,
     cotangent,
     pair,
-    kv,
     kv_t,
     expo,
     grad_probs,
     image,
     work,
+    kv,
 ):
     rows, width, channels = own.shape
     halo = MARGIN + 1
@@ -145,15 +139,14 @@
 
 def second_kernel(
     scalars,
-    near,
-    far,
+    pair,
+    slab,
     within,
     between,
     conv_weight,
     q_weight,
     k_weight,
     v_weight,
-    pair,
     first_kv_t,
     first_expo,
     first_grad_probs,
@@ -168,14 +161,13 @@
     kv_t,
     acc,
 ):
-    rows, width, channels = near.shape
+    rows, width, channels = slab.shape
     win = rows + 2 * MARGIN
     scale = channels**-0.5
     taps = stacked_taps(conv_weight)
     wkv = jnp.concatenate([k_weight[...], v_weight[...]], axis=1)
     acc[...] = jnp.zeros_like(acc)
-    slab = jnp.where(scalars[1] == 1, near[...], far[...])
-    side_keys(slab, scalars[0] == 1, between, within, image, work, taps, wkv, kv, kv_t)
+    side_keys(slab[...], scalars[0] == 1, between, within, image, work, taps, wkv, kv, kv_t)
 
     grad_q = []
     for b in range(rows):
@@ -257,33 +249,50 @@
     camera = lax.axis_index("cam")
     slab = lax.axis_index("row")
 
-    near_left = from_behind(image, "cam", samples)
-    near_right = from_behind(image, "cam", -samples)
-    far_left = from_behind(image, "cam", 2 * samples)
-    far_right = from_behind(image, "cam", -2 * samples)
-
-    def uses(step, side):
-        other = jnp.mod(camera + step, views)
-        return partners[other, side] == camera
-
-    close_left = partners[camera, 0] == jnp.mod(camera - samples, views)
-    close_right = partners[camera, 1] == jnp.mod(camera + samples, views)
+    ring = views // samples
+    odd_place = lax.rem(lax.div(camera, samples), 2) == 1
+    sign = jnp.where(odd_place, -1, 1)
+
+    def routed(value, evens, odds):
+        pairs = []
+        for c in range(views):
+            step = odds if (c // samples) % 2 else evens
+            pairs.append((c, (c // samples + step) % ring * samples + c % samples))
+        return lax.ppermute(value, "cam", pairs)
+
+    def is_near(steps, first):
+        other = jnp.mod(camera + steps * samples, views)
+        side = jnp.where(odd_place, 1 - first, first)
+        gap = jnp.where(side == 1, samples, -samples)
+        return partners[other, side] == jnp.mod(other + gap, views)
+
+    first_near = is_near(0, 1)
+    second_near_on = is_near(2 * sign, 0)
+    first_near_back = is_near(-2 * sign, 1)
+
+    pair_slab = routed(image, 1, -1)
+    far_slab = routed(image, -2, 2)
+    passed_on = jnp.where(second_near_on, pair_slab, image)
+    second_slab = routed(passed_on, 2, -2)
+    far_slab, _ = lax.optimization_barrier((far_slab, passed_on))
+    first_slab = jnp.where(~first_near, far_slab, pair_slab)
+
     widths_here = lax.dynamic_index_in_dim(band_widths, camera, 0, keepdims=False)
     live = jnp.arange(BAND, dtype=jnp.int32)[None, :] < widths_here[:, None]
     places = jnp.clip(bands[0] - (slab * rows - MARGIN), 0, rows + 2 * MARGIN - 1)
+    live = jnp.where(odd_place, live[::-1], live)
+    places = jnp.where(odd_place, places[:, ::-1], places)
     scalars = jnp.concatenate(
         [
             jnp.mod(slab, 2).reshape(1),
-            close_left.astype(jnp.int32).reshape(1),
             places.reshape(-1),
             live.reshape(-1).astype(jnp.int32),
         ]
     )
 
-    right = jnp.where(close_right, near_right, far_right)
     between, within = swapped(
-        jnp.concatenate([right[rows - halo :], image[rows - 1 :]]),
-        jnp.concatenate([right[:halo], image[:1]]),
+        jnp.concatenate([first_slab[rows - halo :], image[rows - 1 :]]),
+        jnp.concatenate([first_slab[:halo], image[:1]]),
         "row",
     )
     width, channels = image.shape[1:]
@@ -293,20 +302,19 @@
         (((win + 2) * width, channels), half),
         ((win * width + 16, 3 * channels), full),
     ]
-    pair, _, first_kv_t, first_expo, first_grad_probs = on_device(
+    pair, first_kv_t, first_expo, first_grad_probs = on_device(
         first_kernel,
         [
             ((rows, 2 * width, 2 * channels), half),
-            ((win, width, 2 * channels), half),
             ((win, 2 * channels, width), half),
             ((rows, BAND * width, width), full),
             ((rows, BAND * width, width), full),
         ],
-        conv_scratch,
+        conv_scratch + [((win, width, 2 * channels), half)],
         1_000_000,
         scalars,
         image,
-        right,
+        first_slab,
         within,
         between,
         conv_weight,
@@ -315,9 +323,7 @@
         v_weight,
         grad_attended[0],
     )
-    close_left, _ = lax.optimization_barrier((close_left, right))
-    left = jnp.where(close_left, near_left, far_left)
-    between, within = swapped(left[rows - halo :], left[:halo], "row")
+    between, within = swapped(second_slab[rows - halo :], second_slab[:halo], "row")
     attended, top, bottom, center, grad_own = on_device(
         second_kernel,
         [
@@ -335,22 +341,21 @@
         ],
         1_500_000_000,
         scalars,
-        near_left,
-        far_left,
+        pair,
+        second_slab,
         within,
         between,
         conv_weight,
         q_weight,
         k_weight,
         v_weight,
-        pair,
         first_kv_t,
         first_expo,
         first_grad_probs,
     )
 
     between, within = swapped(bottom, top, "row")
-    total = on_device(
+    second, first = on_device(
         slab_kernel,
         [(image.shape, half)] * 2,
         [],
@@ -360,13 +365,16 @@
         within,
         between,
     )
-    summed = grad_own
-    for side, sign in ((0, -1), (1, 1)):
-        for distance in (1, 2):
-            step = sign * distance * samples
-            came = from_behind(total[side], "cam", step)
-            summed = summed + jnp.where(uses(-step, side), came.astype(jnp.float32), 0.0)
-    return (attended[None], summed.astype(jnp.bfloat16)[None])
+    from_second = routed(second, -2, 2).astype(full)
+    from_first = routed(first, 2, -2).astype(full)
+    for_pair = jnp.where(first_near, first.astype(full), 0.0) + jnp.where(
+        second_near_on, from_second, 0.0
+    )
+    from_pair = routed(for_pair.astype(half), 1, -1).astype(full)
+    summed = grad_own + from_pair
+    summed = summed + jnp.where(second_near_on, 0.0, from_second)
+    summed = summed + jnp.where(first_near_back, 0.0, from_first)
+    return (attended[None], summed.astype(half)[None])
 
 
 def solution(mesh):

time: 49.4 us -> 50.1 us (1.014); the launches traced: 49 us -> 49.1 us
  waiting for transfers between devices: 8.1 us -> 14 us
  starting transfers between devices: 24.5 us -> 20.6 us
  between operations: 4.79 us -> 2.91 us
  Pallas kernels: 8.7 us -> 8.09 us
  local copies, waits for them, and re-layouts: 1.91 us -> 2.46 us
    ppermute x8 -> x6, waiting for transfers between devices: 4.77 us -> 11.2 us  [routed(): return lax.ppermute(value, 'cam', pairs)]
    ppermute x8 -> x6, starting transfers between devices: 11.9 us -> 7.08 us  [routed(): return lax.ppermute(value, 'cam', pairs)]
    ppermute x6, starting transfers between devices: 12.6 us -> 13.5 us  [swapped(): lax.ppermute(jnp.where(sends_up, to_next, to_previous), axis, pairs)]
    pallas_call x3, Pallas kernels: 8.7 us -> 8.09 us  [on_device(): pl.pallas_call(kernel, out_shape=tuple((jax.ShapeDtypeStruct(*one) for on...]
    ppermute x6, waiting for transfers between devices: 3.33 us -> 2.74 us  [swapped(): lax.ppermute(jnp.where(sends_up, to_next, to_previous), axis, pairs)]
    unnamed x18, local copies, waits for them, and re-layouts: 0.75 us -> 1.26 us
  transfers between devices with their start and end apart: 14 -> 12, of which waited for: 3 -> 4; matrix products, arithmetic and copies ran while one was open for 3% -> 3% of each run, Pallas kernels for 6% -> 5%
where the time goes in v5:
time: 50.1 us; the launch traced here: 49.1 us
  starting transfers between devices  20.6 us (41%)
  waiting for transfers between devices  14 us (28%)
  Pallas kernels  8.09 us (16%)
  between operations  2.91 us (6%)
  local copies, waits for them, and re-layouts  2.46 us (5%)
  other arithmetic  1.14 us (2%)
    ppermute x6, starting transfers between devices, swapped(): lax.ppermute(jnp.where(sends_up, to_next, to_previous), axis, pairs)  13.5 us
    ppermute x6, waiting for transfers between devices, routed(): return lax.ppermute(value, 'cam', pairs)  11.2 us
    pallas_call x3, Pallas kernels, on_device(): pl.pallas_call(kernel, out_shape=tuple((jax.ShapeDtypeStruct(*one) for on...  8.09 us
    ppermute x6, starting transfers between devices, routed(): return lax.ppermute(value, 'cam', pairs)  7.08 us
    ppermute x6, waiting for transfers between devices, swapped(): lax.ppermute(jnp.where(sends_up, to_next, to_previous), axis, pairs)  2.74 us
    unnamed x18, local copies, waits for them, and re-layouts  1.26 us
  transfers between devices with their start and end apart: 12, of which 4 were waited for; matrix products, arithmetic and copies ran while one was open for 3% of the time, Pallas kernels for 5%

profile of v5, /device:TPU:1, one launch (start us, length us, event | category | flops | bytes accessed | tf_op | source)
XLA Modules:
  0.0 49.1 jit_solution(6929398251653575201)
XLA Ops:
  0.6 2.1 %collective-permute-start.1 = (bf16[4,128,128]{2,1,0:T(8,128)(2,1)}, bf16[4,128,128]{2,1,0:T(8,128)(2,1)S(1)}, u32[]{:S(2)}, u32[]{:S(2)}) collective-permute-start(bf16[4,128,128]{2,1,0:T(8,128)(2,1)} %bitcast.18), channel_id=1, source_target_pairs={{0,4},{4,0},{8,12},{12,8},{16,20},{20,16},{24,28},{28,24},{1,5},{5... | collective-permute-start | bytes 393224 | tf_op jit(solution)/shard_map/ppermute | solution.py:261
  2.8 3.3 %collective-permute-start = (bf16[4,128,128]{2,1,0:T(8,128)(2,1)}, bf16[4,128,128]{2,1,0:T(8,128)(2,1)S(1)}, u32[]{:S(2)}, u32[]{:S(2)}) collective-permute-start(bf16[4,128,128]{2,1,0:T(8,128)(2,1)} %bitcast.19), channel_id=1, source_target_pairs={{0,24},{4,12},{8,0},{12,20},{16,8},{20,28},{24,16},{28,4},{1,25},{... | collective-permute-start | bytes 393224 | tf_op jit(solution)/shard_map/ppermute | solution.py:261
  6.1 0.7 %copy-done.8 = s32[8,2]{0,1:T(2,128)S(1)} copy-done((s32[8,2]{0,1:T(2,128)S(1)}, s32[8,2]{0,1:T(2,128)}, u32[]{:S(2)}) %copy-start.8) | copy-done | bytes 88
  6.8 0.7 %fusion.7 = (s32[1,1]{0,1:T(1,128)}, s32[1,1]{0,1:T(1,128)}, s32[1,1]{0,1:T(1,128)}) fusion(s32[8,2]{0,1:T(2,128)S(1)} %copy-done.8, s32[]{:T(128)S(6)} %select_n.190, s32[]{:T(128)S(6)} %select_n.162, s32[]{:T(128)S(6)} %select_n.161, s32[]{:T(128)S(6)} %select_n.168, s32[]{:T(128)S(6)} %select_n.169), kind=kLoop, calls=%fused_computation.27 | loop fusion | bytes 44 | tf_op jit(solution)/shard_map/dynamic_slice | solution.py:267
  8.1 0.2 dynamic-slice_reduce_fusion
  8.3 0.1 iota_compare_fusion
  8.5 0.1 reshape.24
  8.6 0.5 %copy-done.7 = s32[1,4,2,3]{1,2,3,0:T(2,128)S(1)} copy-done((s32[1,4,2,3]{1,2,3,0:T(2,128)S(1)}, s32[1,4,2,3]{1,2,3,0:T(2,128)}, u32[]{:S(2)}) %copy-start.7) | copy-done | bytes 120
  9.1 0.1 copy.12
  9.2 0.1 reshape.23
  10.2 4.4 %collective-permute-start.3 = (bf16[4,128,128]{2,1,0:T(8,128)(2,1)S(1)}, bf16[4,128,128]{2,1,0:T(8,128)(2,1)S(1)}, u32[]{:S(2)}, u32[]{:S(2)}) collective-permute-start(bf16[4,128,128]{2,1,0:T(8,128)(2,1)S(1)} %get-tuple-element.28), channel_id=1, source_target_pairs={{1,2},{2,1},{5,6},{6,5},{9,10},{10,9},{13,14},{14,13},{17,18},{18,... | collective-permute-start | bytes 393224 | tf_op jit(solution)/shard_map/ppermute | solution.py:21
  14.7 0.9 %collective-permute-done.4.slab = bf16[4,128,128]{2,1,0:T(8,128)(2,1)S(1)} collective-permute-done((bf16[4,128,128]{2,1,0:T(8,128)(2,1)S(1)}, bf16[4,128,128]{2,1,0:T(8,128)(2,1)S(1)}, u32[]{:S(2)}, u32[]{:S(2)}) %collective-permute-start.4) | collective-permute-done | bytes 131104 | tf_op jit(solution)/shard_map/ppermute | solution.py:261
  15.7 5.4 %collective-permute-start.6 = (bf16[3,128,128]{2,1,0:T(8,128)(2,1)S(1)}, bf16[3,128,128]{2,1,0:T(8,128)(2,1)S(1)}, u32[]{:S(2)}, u32[]{:S(2)}) collective-permute-start(bf16[3,128,128]{2,1,0:T(8,128)(2,1)S(1)} %get-tuple-element.30), channel_id=1, source_target_pairs={{1,2},{2,1},{5,6},{6,5},{9,10},{10,9},{13,14},{14,13},{17,18},{18,... | collective-permute-start | bytes 294920 | tf_op jit(solution)/shard_map/ppermute | solution.py:21
  21.2 0.1 pad_add_fusion.scalars
  21.3 2.2 %shard_map.104 = (bf16[4,256,256]{2,1,0:T(8,128)(2,1)S(1)}, bf16[8,256,128]{2,1,0:T(8,128)(2,1)S(1)}, f32[4,384,128]{2,1,0:T(8,128)S(1)}, f32[4,384,128]{2,1,0:T(8,128)S(1)}) custom-call(s32[31]{0:T(128)S(1)} %pad_add_fusion.scalars, bf16[4,128,128]{2,1,0:T(8,128)(2,1)S(1)} %bitcast.20, bf16[4,128,128]{2,1,0:T(8,128)(2,1)S(1)} %broadcast_select_fusion.5.slab, ...), custom_call_target="tpu_custom_call" | custom-call | flops 1000000 | bytes 1000 | tf_op jit(solution)/shard_map/pallas_call | solution.py:220
  23.6 5.3 %shard_map.105 = (bf16[4,128,128]{2,1,0:T(8,128)(2,1)}, bf16[4,128,128]{2,1,0:T(8,128)(2,1)S(1)}, bf16[4,128,128]{2,1,0:T(8,128)(2,1)S(1)}, f32[2,4,128,128]{3,2,1,0:T(8,128)S(1)}, f32[4,128,128]{2,1,0:T(8,128)S(1)}) custom-call(s32[31]{0:T(128)S(1)} %pad_add_fusion.scalars, bf16[4,256,256]{2,1,0:T(8,128)(2,1)S(1)} %get-tuple-element.15.pair, ...), custom_call_target="tpu_custom_call" | custom-call | flops 1500000000 | bytes 1500000 | tf_op jit(solution)/shard_map/pallas_call | solution.py:220
  28.9 3.5 %collective-permute-start.8 = (bf16[4,128,128]{2,1,0:T(8,128)(2,1)S(1)}, bf16[4,128,128]{2,1,0:T(8,128)(2,1)S(1)}, u32[]{:S(2)}, u32[]{:S(2)}) collective-permute-start(bf16[4,128,128]{2,1,0:T(8,128)(2,1)S(1)} %get-tuple-element.26), channel_id=1, source_target_pairs={{1,2},{2,1},{5,6},{6,5},{9,10},{10,9},{13,14},{14,13},{17,18},{18,... | collective-permute-start | bytes 393224 | tf_op jit(solution)/shard_map/ppermute | solution.py:21
  32.4 2.7 %collective-permute-done.8.between = bf16[4,128,128]{2,1,0:T(8,128)(2,1)S(1)} collective-permute-done((bf16[4,128,128]{2,1,0:T(8,128)(2,1)S(1)}, bf16[4,128,128]{2,1,0:T(8,128)(2,1)S(1)}, u32[]{:S(2)}, u32[]{:S(2)}) %collective-permute-start.8) | collective-permute-done | bytes 131104 | tf_op jit(solution)/shard_map/ppermute | solution.py:21
  35.2 0.6 %shard_map.106 = (bf16[4,128,128]{2,1,0:T(8,128)(2,1)S(1)}, bf16[4,128,128]{2,1,0:T(8,128)(2,1)S(1)}) custom-call(s32[31]{0:T(128)S(1)} %pad_add_fusion.scalars, f32[2,4,128,128]{3,2,1,0:T(8,128)S(1)} %get-tuple-element.21.center, bf16[4,128,128]{2,1,0:T(8,128)(2,1)S(1)} %collective-permute-done.7.within, bf16[4,128,128]{2,1,0:T(8,128)(2,1)S(1)} %collective-permute-done.8.between), custom_call_target="tpu_custom_call" | custom-call | flops 1000000 | bytes 1000 | tf_op jit(solution)/shard_map/pallas_call | solution.py:220
  35.8 0.7 %collective-permute-start.9 = (bf16[4,128,128]{2,1,0:T(8,128)(2,1)S(1)}, bf16[4,128,128]{2,1,0:T(8,128)(2,1)S(1)}, u32[]{:S(2)}, u32[]{:S(2)}) collective-permute-start(bf16[4,128,128]{2,1,0:T(8,128)(2,1)S(1)} %get-tuple-element.25), channel_id=1, source_target_pairs={{0,24},{4,12},{8,0},{12,20},{16,8},{20,28},{24,16},{28,4},{1,25},{... | collective-permute-start | bytes 393224 | tf_op jit(solution)/shard_map/ppermute | solution.py:261
  36.5 0.8 %collective-permute-start.11 = (bf16[4,128,128]{2,1,0:T(8,128)(2,1)S(1)}, bf16[4,128,128]{2,1,0:T(8,128)(2,1)S(1)}, u32[]{:S(2)}, u32[]{:S(2)}) collective-permute-start(bf16[4,128,128]{2,1,0:T(8,128)(2,1)S(1)} %get-tuple-element.24), channel_id=1, source_target_pairs={{0,8},{4,28},{8,16},{12,4},{16,24},{20,12},{24,0},{28,20},{1,9},{5... | collective-permute-start | bytes 393224 | tf_op jit(solution)/shard_map/ppermute | solution.py:261
  37.3 5.8 %collective-permute-done.9 = bf16[4,128,128]{2,1,0:T(8,128)(2,1)S(1)} collective-permute-done((bf16[4,128,128]{2,1,0:T(8,128)(2,1)S(1)}, bf16[4,128,128]{2,1,0:T(8,128)(2,1)S(1)}, u32[]{:S(2)}, u32[]{:S(2)}) %collective-permute-start.9) | collective-permute-done | bytes 131104 | tf_op jit(solution)/shard_map/ppermute | solution.py:261
  43.9 4.5 %collective-permute-done.10 = bf16[4,128,128]{2,1,0:T(8,128)(2,1)S(1)} collective-permute-done((bf16[4,128,128]{2,1,0:T(8,128)(2,1)S(1)}, bf16[4,128,128]{2,1,0:T(8,128)(2,1)S(1)}, u32[]{:S(2)}, u32[]{:S(2)}) %collective-permute-start.10) | collective-permute-done | bytes 131104 | tf_op jit(solution)/shard_map/ppermute | solution.py:261
  48.4 0.7 %fusion.5 = bf16[1,4,128,128]{3,2,1,0:T(8,128)(2,1)} fusion(bf16[4,128,128]{2,1,0:T(8,128)(2,1)S(1)} %collective-permute-done.11, bf16[4,128,128]{2,1,0:T(8,128)(2,1)S(1)} %collective-permute-done.9, f32[4,128,128]{2,1,0:T(8,128)S(1)} %get-tuple-element.20, bf16[4,128,128]{2,1,0:T(8,128)(2,1)S(1)} %collective-permute-done.10, pred[]{:T(512)S(6)} %eq.38, ...), kind=kLoop, calls=%fused_computation.7 | loop fusion | flops 589824 | bytes 786434 | tf_op jit(solution)/shard_map/broadcast_in_dim | solution.py:377
  (42 shorter events, 0.8 us)
Async XLA Ops:
  0.6 7.5 %copy-start = (s32[8,2]{0,1:T(2,128)S(1)}, s32[8,2]{0,1:T(2,128)}, u32[]{:S(2)}) copy-start(s32[8,2]{0,1:T(2,128)} %param.15) | copy-start | bytes 196
  0.6 9.3 %collective-permute-start.1 = (bf16[4,128,128]{2,1,0:T(8,128)(2,1)}, bf16[4,128,128]{2,1,0:T(8,128)(2,1)S(1)}, u32[]{:S(2)}, u32[]{:S(2)}) collective-permute-start(bf16[4,128,128]{2,1,0:T(8,128)(2,1)} %bitcast.18), channel_id=1, source_target_pairs={{0,4},{4,0},{8,12},{12,8},{16,20},{20,16},{24,28},{28,24},{1,5},{5... | collective-permute-start | bytes 393224 | tf_op jit(solution)/shard_map/ppermute | solution.py:261
  2.8 7.3 %collective-permute-start = (bf16[4,128,128]{2,1,0:T(8,128)(2,1)}, bf16[4,128,128]{2,1,0:T(8,128)(2,1)S(1)}, u32[]{:S(2)}, u32[]{:S(2)}) collective-permute-start(bf16[4,128,128]{2,1,0:T(8,128)(2,1)} %bitcast.19), channel_id=1, source_target_pairs={{0,24},{4,12},{8,0},{12,20},{16,8},{20,28},{24,16},{28,4},{1,25},{... | collective-permute-start | bytes 393224 | tf_op jit(solution)/shard_map/ppermute | solution.py:261
  6.1 3.9 %copy-start.1 = (bf16[1,4,128,128]{3,2,1,0:T(8,128)(2,1)S(1)}, bf16[1,4,128,128]{3,2,1,0:T(8,128)(2,1)}, u32[]{:S(2)}) copy-start(bf16[1,4,128,128]{3,2,1,0:T(8,128)(2,1)} %param.9) | copy-start | bytes 393220
  6.1 0.7 %copy-start.8 = (s32[8,2]{0,1:T(2,128)S(1)}, s32[8,2]{0,1:T(2,128)}, u32[]{:S(2)}) copy-start(s32[8,2]{0,1:T(2,128)} %param.14) | copy-start | bytes 196
  8.4 0.7 %copy-start.7 = (s32[1,4,2,3]{1,2,3,0:T(2,128)S(1)}, s32[1,4,2,3]{1,2,3,0:T(2,128)}, u32[]{:S(2)}) copy-start(s32[1,4,2,3]{1,2,3,0:T(2,128)} %param.16) | copy-start | bytes 292
  10.0 5.7 %collective-permute-start.4 = (bf16[4,128,128]{2,1,0:T(8,128)(2,1)S(1)}, bf16[4,128,128]{2,1,0:T(8,128)(2,1)S(1)}, u32[]{:S(2)}, u32[]{:S(2)}) collective-permute-start(bf16[4,128,128]{2,1,0:T(8,128)(2,1)S(1)} %broadcast_select_fusion.4), channel_id=1, source_target_pairs={{0,8},{4,28},{8,16},{12,4},{16,24},{20,12},{24,0},{28,20},{1,9},{5... | collective-permute-start | bytes 393224 | tf_op jit(solution)/shard_map/ppermute | solution.py:261
  10.2 11.1 %copy-start.3 = (bf16[1,4,128,128]{3,2,1,0:T(8,128)(2,1)S(1)}, bf16[1,4,128,128]{3,2,1,0:T(8,128)(2,1)}, u32[]{:S(2)}) copy-start(bf16[1,4,128,128]{3,2,1,0:T(8,128)(2,1)} %param.17) | copy-start | bytes 393220
  10.2 11.1 %copy-start.2 = (bf16[3,3,128,128]{3,2,1,0:T(8,128)(2,1)S(1)}, bf16[3,3,128,128]{3,2,1,0:T(8,128)(2,1)}, u32[]{:S(2)}) copy-start(bf16[3,3,128,128]{3,2,1,0:T(8,128)(2,1)} %conv_weight.3) | copy-start | bytes 884740
  10.2 11.1 %collective-permute-start.3 = (bf16[4,128,128]{2,1,0:T(8,128)(2,1)S(1)}, bf16[4,128,128]{2,1,0:T(8,128)(2,1)S(1)}, u32[]{:S(2)}, u32[]{:S(2)}) collective-permute-start(bf16[4,128,128]{2,1,0:T(8,128)(2,1)S(1)} %get-tuple-element.28), channel_id=1, source_target_pairs={{1,2},{2,1},{5,6},{6,5},{9,10},{10,9},{13,14},{14,13},{17,18},{18,... | collective-permute-start | bytes 393224 | tf_op jit(solution)/shard_map/ppermute | solution.py:21
  14.6 6.7 %copy-start.4 = (bf16[128,128]{1,0:T(8,128)(2,1)S(1)}, bf16[128,128]{1,0:T(8,128)(2,1)}, u32[]{:S(2)}) copy-start(bf16[128,128]{1,0:T(8,128)(2,1)} %q_weight.3) | copy-start | bytes 98308
  14.6 6.7 %copy-start.5 = (bf16[128,128]{1,0:T(8,128)(2,1)S(1)}, bf16[128,128]{1,0:T(8,128)(2,1)}, u32[]{:S(2)}) copy-start(bf16[128,128]{1,0:T(8,128)(2,1)} %k_weight.3) | copy-start | bytes 98308
  14.6 6.7 %copy-start.6 = (bf16[128,128]{1,0:T(8,128)(2,1)S(1)}, bf16[128,128]{1,0:T(8,128)(2,1)}, u32[]{:S(2)}) copy-start(bf16[128,128]{1,0:T(8,128)(2,1)} %v_weight.3) | copy-start | bytes 98308
  14.7 6.6 %collective-permute-start.2 = (bf16[4,128,128]{2,1,0:T(8,128)(2,1)S(1)}, bf16[4,128,128]{2,1,0:T(8,128)(2,1)S(1)}, u32[]{:S(2)}, u32[]{:S(2)}) collective-permute-start(bf16[4,128,128]{2,1,0:T(8,128)(2,1)S(1)} %get-tuple-element.29), channel_id=1, source_target_pairs={{0,1},{2,3},{1,0},{3,2},{4,5},{6,7},{5,4},{7,6},{8,9},{10,11},{9,8... | collective-permute-start | bytes 393224 | tf_op jit(solution)/shard_map/ppermute | solution.py:21
  15.7 7.9 %collective-permute-start.6 = (bf16[3,128,128]{2,1,0:T(8,128)(2,1)S(1)}, bf16[3,128,128]{2,1,0:T(8,128)(2,1)S(1)}, u32[]{:S(2)}, u32[]{:S(2)}) collective-permute-start(bf16[3,128,128]{2,1,0:T(8,128)(2,1)S(1)} %get-tuple-element.30), channel_id=1, source_target_pairs={{1,2},{2,1},{5,6},{6,5},{9,10},{10,9},{13,14},{14,13},{17,18},{18,... | collective-permute-start | bytes 294920 | tf_op jit(solution)/shard_map/ppermute | solution.py:21
  21.1 2.4 %collective-permute-start.5 = (bf16[3,128,128]{2,1,0:T(8,128)(2,1)S(1)}, bf16[3,128,128]{2,1,0:T(8,128)(2,1)S(1)}, u32[]{:S(2)}, u32[]{:S(2)}) collective-permute-start(bf16[3,128,128]{2,1,0:T(8,128)(2,1)S(1)} %get-tuple-element.31), channel_id=1, source_target_pairs={{0,1},{2,3},{1,0},{3,2},{4,5},{6,7},{5,4},{7,6},{8,9},{10,11},{9,8... | collective-permute-start | bytes 294920 | tf_op jit(solution)/shard_map/ppermute | solution.py:21
  28.9 6.3 %collective-permute-start.8 = (bf16[4,128,128]{2,1,0:T(8,128)(2,1)S(1)}, bf16[4,128,128]{2,1,0:T(8,128)(2,1)S(1)}, u32[]{:S(2)}, u32[]{:S(2)}) collective-permute-start(bf16[4,128,128]{2,1,0:T(8,128)(2,1)S(1)} %get-tuple-element.26), channel_id=1, source_target_pairs={{1,2},{2,1},{5,6},{6,5},{9,10},{10,9},{13,14},{14,13},{17,18},{18,... | collective-permute-start | bytes 393224 | tf_op jit(solution)/shard_map/ppermute | solution.py:21
  32.3 2.8 %collective-permute-start.7 = (bf16[4,128,128]{2,1,0:T(8,128)(2,1)S(1)}, bf16[4,128,128]{2,1,0:T(8,128)(2,1)S(1)}, u32[]{:S(2)}, u32[]{:S(2)}) collective-permute-start(bf16[4,128,128]{2,1,0:T(8,128)(2,1)S(1)} %get-tuple-element.27), channel_id=1, source_target_pairs={{0,1},{2,3},{1,0},{3,2},{4,5},{6,7},{5,4},{7,6},{8,9},{10,11},{9,8... | collective-permute-start | bytes 393224 | tf_op jit(solution)/shard_map/ppermute | solution.py:21
  35.8 7.3 %collective-permute-start.9 = (bf16[4,128,128]{2,1,0:T(8,128)(2,1)S(1)}, bf16[4,128,128]{2,1,0:T(8,128)(2,1)S(1)}, u32[]{:S(2)}, u32[]{:S(2)}) collective-permute-start(bf16[4,128,128]{2,1,0:T(8,128)(2,1)S(1)} %get-tuple-element.25), channel_id=1, source_target_pairs={{0,24},{4,12},{8,0},{12,20},{16,8},{20,28},{24,16},{28,4},{1,25},{... | collective-permute-start | bytes 393224 | tf_op jit(solution)/shard_map/ppermute | solution.py:261
  36.5 7.4 %collective-permute-start.11 = (bf16[4,128,128]{2,1,0:T(8,128)(2,1)S(1)}, bf16[4,128,128]{2,1,0:T(8,128)(2,1)S(1)}, u32[]{:S(2)}, u32[]{:S(2)}) collective-permute-start(bf16[4,128,128]{2,1,0:T(8,128)(2,1)S(1)} %get-tuple-element.24), channel_id=1, source_target_pairs={{0,8},{4,28},{8,16},{12,4},{16,24},{20,12},{24,0},{28,20},{1,9},{5... | collective-permute-start | bytes 393224 | tf_op jit(solution)/shard_map/ppermute | solution.py:261
  43.1 5.3 %collective-permute-start.10 = (bf16[4,128,128]{2,1,0:T(8,128)(2,1)S(1)}, bf16[4,128,128]{2,1,0:T(8,128)(2,1)S(1)}, u32[]{:S(2)}, u32[]{:S(2)}) collective-permute-start(bf16[4,128,128]{2,1,0:T(8,128)(2,1)S(1)} %fusion.1), channel_id=1, source_target_pairs={{0,4},{4,0},{8,12},{12,8},{16,20},{20,16},{24,28},{28,24},{1,5},{5... | collective-permute-start | bytes 393224 | tf_op jit(solution)/shard_map/ppermute | solution.py:261

commit v6 on v5

--- a/solution.py
+++ b/solution.py
@@ -1,3 +1,5 @@
+import functools
+
 import jax
 import jax.numpy as jnp
 from jax import lax
@@ -8,18 +10,23 @@
 MARGIN = 2
 BAND = 3
 LOG2E = 1.4426950408889634
+FLAGS = 4
+
+
+def swap_parts(for_between, for_within, axis):
+    count = lax.axis_size(axis)
+    results = []
+    for first, part in ((1, for_between), (0, for_within)):
+        pairs = [(i, i + 1) for i in range(first, count - 1, 2)]
+        results.append(lax.ppermute(part, axis, pairs + [(j, i) for i, j in pairs]))
+    return results
 
 
 def swapped(to_next, to_previous, axis):
-    count = lax.axis_size(axis)
     odd = lax.rem(lax.axis_index(axis), 2) == 1
-    results = []
-    for first in (1, 0):
-        pairs = [(i, i + 1) for i in range(first, count - 1, 2)]
-        pairs = pairs + [(j, i) for i, j in pairs]
-        sends_up = odd if first == 1 else ~odd
-        results.append(lax.ppermute(jnp.where(sends_up, to_next, to_previous), axis, pairs))
-    return results
+    for_between = jnp.where(odd, to_next, to_previous)
+    for_within = jnp.where(odd, to_previous, to_next)
+    return swap_parts(for_between, for_within, axis)
 
 
 def margins_of(odd, between, within):
@@ -73,8 +80,8 @@
 def places_of(scalars, rows, b, side):
     return [
         (
-            scalars[1 + (b * 2 + side) * BAND + s],
-            scalars[1 + rows * 2 * BAND + side * BAND + s] == 1,
+            scalars[FLAGS + (b * 2 + side) * BAND + s],
+            scalars[FLAGS + rows * 2 * BAND + side * BAND + s] == 1,
         )
         for s in range(BAND)
     ]
@@ -144,32 +151,26 @@
     within,
     between,
     conv_weight,
-    q_weight,
     k_weight,
     v_weight,
-    first_kv_t,
     first_expo,
     first_grad_probs,
-    attended,
     top,
     bottom,
-    center,
-    grad_own,
+    acc,
+    probs_out,
+    grad_scores_out,
+    kv_t,
     image,
     work,
     kv,
-    kv_t,
-    acc,
 ):
     rows, width, channels = slab.shape
-    win = rows + 2 * MARGIN
-    scale = channels**-0.5
     taps = stacked_taps(conv_weight)
     wkv = jnp.concatenate([k_weight[...], v_weight[...]], axis=1)
     acc[...] = jnp.zeros_like(acc)
     side_keys(slab[...], scalars[0] == 1, between, within, image, work, taps, wkv, kv, kv_t)
 
-    grad_q = []
     for b in range(rows):
         places = [places_of(scalars, rows, b, side) for side in range(2)]
         expo, grad_probs = side_scores(places[0], kv, pair[b], width, channels)
@@ -179,27 +180,118 @@
         probs_bf = probs.astype(jnp.bfloat16)
         delta = jnp.sum(probs * grad_probs, axis=0, keepdims=True)
         grad_scores = (probs * (grad_probs - delta)).astype(jnp.bfloat16)
-        keys_t = jnp.concatenate(
-            [kv_t[at] for at, _ in places[0]] + [first_kv_t[at] for at, _ in places[1]], axis=1
-        )
-        attended[b] = dot_nn(keys_t[channels:], probs_bf).T.astype(jnp.bfloat16)
-        grad_q.append(dot_nn(keys_t[:channels], grad_scores))
+        probs_out[b] = probs_bf
+        grad_scores_out[b] = grad_scores
         terms = dot_nn(jnp.concatenate([grad_scores, probs_bf], axis=1), pair[b])
         for side in range(2):
             for s, (at, _) in enumerate(places[side]):
                 i = side * BAND + s
                 acc[side, at] += terms[i * width : (i + 1) * width]
 
-    turned = dot_nn(q_weight[...], (jnp.concatenate(grad_q, axis=1) * scale).astype(jnp.bfloat16))
+    for side in range(2):
+        span = slice(side * MARGIN, (side + 1) * MARGIN)
+        top[span] = back_projected(acc[side, :MARGIN], wkv).astype(jnp.bfloat16)
+        bottom[span] = back_projected(acc[side, MARGIN + rows :], wkv).astype(jnp.bfloat16)
+
+
+def back_projected(grads, wkv):
+    rows, width, both = grads.shape
+    channels = both // 2
+    grads = grads.reshape(rows * width, both)
+    grads = jnp.concatenate(
+        [grads[:, :channels] * channels**-0.5, grads[:, channels:]], axis=1
+    )
+    return dot_nt(grads.astype(jnp.bfloat16), wkv).reshape(rows, width, channels)
+
+
+def third_kernel(
+    scalars,
+    acc,
+    probs,
+    grad_scores,
+    kv_t,
+    first_kv_t,
+    q_weight,
+    k_weight,
+    v_weight,
+    attended,
+    center,
+    grad_own,
+):
+    rows, width, channels = attended.shape
+    wkv = jnp.concatenate([k_weight[...], v_weight[...]], axis=1)
+    for side in range(2):
+        center[side] = back_projected(acc[side, MARGIN : MARGIN + rows], wkv)
+    grad_q = []
+    for b in range(rows):
+        places = [places_of(scalars, rows, b, side) for side in range(2)]
+        keys_t = jnp.concatenate(
+            [kv_t[at] for at, _ in places[0]] + [first_kv_t[at] for at, _ in places[1]], axis=1
+        )
+        attended[b] = dot_nn(keys_t[channels:], probs[b]).T.astype(jnp.bfloat16)
+        grad_q.append(dot_nn(keys_t[:channels], grad_scores[b]))
+    grad_q = jnp.concatenate(grad_q, axis=1) * channels**-0.5
+    turned = dot_nn(q_weight[...], grad_q.astype(jnp.bfloat16))
     for b in range(rows):
         grad_own[b] = turned[:, b * width : (b + 1) * width].T
-    for side in range(2):
-        grads = acc[side].reshape(win * width, 2 * channels)
-        grads = jnp.concatenate([grads[:, :channels] * scale, grads[:, channels:]], axis=1)
-        back = dot_nt(grads.astype(jnp.bfloat16), wkv).reshape(win, width, channels)
-        top[side * MARGIN : (side + 1) * MARGIN] = back[:MARGIN].astype(jnp.bfloat16)
-        center[side] = back[MARGIN : MARGIN + rows]
-        bottom[side * MARGIN : (side + 1) * MARGIN] = back[MARGIN + rows :].astype(jnp.bfloat16)
+
+
+def scalar_kernel(views, samples, where, partners, band_widths, bands, scalars):
+    camera, slab = where[0], where[1]
+    rows = bands.shape[2]
+    odd = lax.rem(lax.div(camera, samples), 2)
+
+    def is_near(steps, first):
+        other = lax.rem(camera + steps * samples + views, views)
+        side = jnp.where(odd == 1, 1 - first, first)
+        gap = jnp.where(side == 1, samples, views - samples)
+        return (partners[side, other] == lax.rem(other + gap, views)).astype(jnp.int32)
+
+    on = jnp.where(odd == 1, -2, 2)
+    scalars[0] = lax.rem(slab, 2)
+    scalars[1] = is_near(0, 1)
+    scalars[2] = is_near(on, 0)
+    scalars[3] = is_near(-on, 1)
+    top = slab * rows - MARGIN
+    last = rows + 2 * MARGIN - 1
+    for first in range(2):
+        side = jnp.where(odd == 1, 1 - first, first)
+        for s in range(BAND):
+            for b in range(rows):
+                at = jnp.clip(bands[s, side, b] - top, 0, last)
+                scalars[FLAGS + (b * 2 + first) * BAND + s] = at
+            live = (s < band_widths[side, camera]).astype(jnp.int32)
+            scalars[FLAGS + rows * 2 * BAND + first * BAND + s] = live
+
+
+def pass_kernel(scalars, pair_slab, own, passed_on):
+    passed_on[...] = jnp.where(scalars[2] == 1, pair_slab[...], own[...])
+
+
+def first_slab_kernel(scalars, far_slab, pair_slab, own, first_slab, for_within, for_between):
+    rows = own.shape[0]
+    halo = MARGIN + 1
+    odd = scalars[0] == 1
+    chosen = jnp.where(scalars[1] == 1, pair_slab[...], far_slab[...])
+    first_slab[...] = chosen
+    to_next, to_previous = chosen[rows - halo :], chosen[:halo]
+    for_within[:halo] = jnp.where(odd, to_previous, to_next)
+    for_between[:halo] = jnp.where(odd, to_next, to_previous)
+    for_within[halo] = jnp.where(odd, own[0], own[rows - 1])
+    for_between[halo] = jnp.where(odd, own[rows - 1], own[0])
+
+
+def pair_kernel(scalars, first, from_second, for_pair):
+    own = jnp.where(scalars[1] == 1, first[...].astype(jnp.float32), 0.0)
+    relayed = jnp.where(scalars[2] == 1, from_second[...].astype(jnp.float32), 0.0)
+    for_pair[...] = (own + relayed).astype(jnp.bfloat16)
+
+
+def sum_kernel(scalars, grad_own, from_second, from_first, from_pair, grad_features):
+    total = grad_own[...] + from_pair[...].astype(jnp.float32)
+    total = total + jnp.where(scalars[2] == 1, 0.0, from_second[...].astype(jnp.float32))
+    total = total + jnp.where(scalars[3] == 1, 0.0, from_first[...].astype(jnp.float32))
+    grad_features[...] = total.astype(jnp.bfloat16)
 
 
 def slab_kernel(scalars, center, within, between, left, right):
@@ -216,12 +308,13 @@
 
 
 def on_device(kernel, out_shape, scratch, flops, *arrays):
+    smem = pl.BlockSpec(memory_space=pltpu.SMEM)
     vmem = pl.BlockSpec(memory_space=pltpu.VMEM)
     return pl.pallas_call(
         kernel,
         out_shape=tuple(jax.ShapeDtypeStruct(*one) for one in out_shape),
-        in_specs=[pl.BlockSpec(memory_space=pltpu.SMEM)] + [vmem] * (len(arrays) - 1),
-        out_specs=(vmem,) * len(out_shape),
+        in_specs=[smem if one.dtype == jnp.int32 else vmem for one in arrays],
+        out_specs=tuple(smem if one[1] == jnp.int32 else vmem for one in out_shape),
         scratch_shapes=[pltpu.VMEM(*one) for one in scratch],
         compiler_params=pltpu.CompilerParams(vmem_limit_bytes=32 * 1024 * 1024),
         cost_estimate=pl.CostEstimate(
@@ -242,16 +335,13 @@
     grad_attended,
 ):
     image = features_in[0]
-    rows = image.shape[0]
+    rows, width, channels = image.shape
     halo = MARGIN + 1
+    win = rows + 2 * MARGIN
+    half, full = jnp.bfloat16, jnp.float32
     views = lax.axis_size("cam")
     samples = views // min(16, views)
-    camera = lax.axis_index("cam")
-    slab = lax.axis_index("row")
-
     ring = views // samples
-    odd_place = lax.rem(lax.div(camera, samples), 2) == 1
-    sign = jnp.where(odd_place, -1, 1)
 
     def routed(value, evens, odds):
         pairs = []
@@ -260,47 +350,41 @@
             pairs.append((c, (c // samples + step) % ring * samples + c % samples))
         return lax.ppermute(value, "cam", pairs)
 
-    def is_near(steps, first):
-        other = jnp.mod(camera + steps * samples, views)
-        side = jnp.where(odd_place, 1 - first, first)
-        gap = jnp.where(side == 1, samples, -samples)
-        return partners[other, side] == jnp.mod(other + gap, views)
-
-    first_near = is_near(0, 1)
-    second_near_on = is_near(2 * sign, 0)
-    first_near_back = is_near(-2 * sign, 1)
-
     pair_slab = routed(image, 1, -1)
     far_slab = routed(image, -2, 2)
-    passed_on = jnp.where(second_near_on, pair_slab, image)
+    where = jnp.stack([lax.axis_index("cam"), lax.axis_index("row")]).astype(jnp.int32)
+    (scalars,) = on_device(
+        functools.partial(scalar_kernel, views, samples),
+        [((FLAGS + (rows + 1) * 2 * BAND,), jnp.int32)],
+        [],
+        1_000_000,
+        where,
+        partners.T,
+        band_widths.T,
+        bands[0].transpose(2, 1, 0),
+    )
+    (passed_on,) = on_device(
+        pass_kernel, [(image.shape, half)], [], 1_000_000, scalars, pair_slab, image
+    )
     second_slab = routed(passed_on, 2, -2)
     far_slab, _ = lax.optimization_barrier((far_slab, passed_on))
-    first_slab = jnp.where(~first_near, far_slab, pair_slab)
-
-    widths_here = lax.dynamic_index_in_dim(band_widths, camera, 0, keepdims=False)
-    live = jnp.arange(BAND, dtype=jnp.int32)[None, :] < widths_here[:, None]
-    places = jnp.clip(bands[0] - (slab * rows - MARGIN), 0, rows + 2 * MARGIN - 1)
-    live = jnp.where(odd_place, live[::-1], live)
-    places = jnp.where(odd_place, places[:, ::-1], places)
-    scalars = jnp.concatenate(
-        [
-            jnp.mod(slab, 2).reshape(1),
-            places.reshape(-1),
-            live.reshape(-1).astype(jnp.int32),
-        ]
-    )
-
-    between, within = swapped(
-        jnp.concatenate([first_slab[rows - halo :], image[rows - 1 :]]),
-        jnp.concatenate([first_slab[:halo], image[:1]]),
-        "row",
-    )
-    width, channels = image.shape[1:]
-    win = rows + 2 * MARGIN
-    half, full = jnp.bfloat16, jnp.float32
+    edge = ((halo + 1, width, channels), half)
+    first_slab, for_within, for_between = on_device(
+        first_slab_kernel,
+        [(image.shape, half), edge, edge],
+        [],
+        1_000_000,
+        scalars,
+        far_slab,
+        pair_slab,
+        image,
+    )
+    between, within = swap_parts(for_between, for_within, "row")
+
     conv_scratch = [
         (((win + 2) * width, channels), half),
         ((win * width + 16, 3 * channels), full),
+        ((win, width, 2 * channels), half),
     ]
     pair, first_kv_t, first_expo, first_grad_probs = on_device(
         first_kernel,
@@ -310,7 +394,7 @@
             ((rows, BAND * width, width), full),
             ((rows, BAND * width, width), full),
         ],
-        conv_scratch + [((win, width, 2 * channels), half)],
+        conv_scratch,
         1_000_000,
         scalars,
         image,
@@ -324,21 +408,19 @@
         grad_attended[0],
     )
     between, within = swapped(second_slab[rows - halo :], second_slab[:halo], "row")
-    attended, top, bottom, center, grad_own = on_device(
+    margins = ((2 * MARGIN, width, channels), half)
+    weights = ((rows, 2 * BAND * width, width), half)
+    top, bottom, acc, probs, grad_scores, kv_t = on_device(
         second_kernel,
         [
-            ((rows, width, channels), half),
-            ((2 * MARGIN, width, channels), half),
-            ((2 * MARGIN, width, channels), half),
-            ((2, rows, width, channels), full),
-            ((rows, width, channels), full),
+            margins,
+            margins,
+            ((2, win, width, 2 * channels), full),
+            weights,
+            weights,
+            ((win, 2 * channels, width), half),
         ],
-        conv_scratch
-        + [
-            ((win, width, 2 * channels), half),
-            ((win, 2 * channels, width), half),
-            ((2, win, width, 2 * channels), full),
-        ],
+        conv_scratch,
         1_500_000_000,
         scalars,
         pair,
@@ -346,15 +428,31 @@
         within,
         between,
         conv_weight,
+        k_weight,
+        v_weight,
+        first_expo,
+        first_grad_probs,
+    )
+    between, within = swapped(bottom, top, "row")
+    attended, center, grad_own = on_device(
+        third_kernel,
+        [
+            (image.shape, half),
+            ((2, rows, width, channels), full),
+            (image.shape, full),
+        ],
+        [],
+        1_000_000,
+        scalars,
+        acc,
+        probs,
+        grad_scores,
+        kv_t,
+        first_kv_t,
         q_weight,
         k_weight,
         v_weight,
-        first_kv_t,
-        first_expo,
-        first_grad_probs,
-    )
-
-    between, within = swapped(bottom, top, "row")
+    )
     second, first = on_device(
         slab_kernel,
         [(image.shape, half)] * 2,
@@ -365,16 +463,24 @@
         within,
         between,
     )
-    from_second = routed(second, -2, 2).astype(full)
-    from_first = routed(first, 2, -2).astype(full)
-    for_pair = jnp.where(first_near, first.astype(full), 0.0) + jnp.where(
-        second_near_on, from_second, 0.0
-    )
-    from_pair = routed(for_pair.astype(half), 1, -1).astype(full)
-    summed = grad_own + from_pair
-    summed = summed + jnp.where(second_near_on, 0.0, from_second)
-    summed = summed + jnp.where(first_near_back, 0.0, from_first)
-    return (attended[None], summed.astype(half)[None])
+    from_second = routed(second, -2, 2)
+    from_first = routed(first, 2, -2)
+    (for_pair,) = on_device(
+        pair_kernel, [(image.shape, half)], [], 1_000_000, scalars, first, from_second
+    )
+    from_pair = routed(for_pair, 1, -1)
+    (grad_features,) = on_device(
+        sum_kernel,
+        [(image.shape, half)],
+        [],
+        1_000_000,
+        scalars,
+        grad_own,
+        from_second,
+        from_first,
+        from_pair,
+    )
+    return (attended[None], grad_features[None])
 
 
 def solution(mesh):

time: 50.1 us -> 53.8 us (1.074)
  the two profiles are of different devices: /device:TPU:1 before, /device:TPU:0 now
where the time goes in v6:
time: 53.8 us; the launch traced here: 53.3 us
  starting transfers between devices  18.6 us (35%)
  Pallas kernels  12.8 us (24%)
  waiting for transfers between devices  12 us (22%)
  local copies, waits for them, and re-layouts  8.9 us (17%)
  between operations  0.82 us (2%)
    pallas_call x9, Pallas kernels, on_device(): pl.pallas_call(kernel, out_shape=tuple((jax.ShapeDtypeStruct(*one) for on...  12.8 us
    ppermute x6, starting transfers between devices, routed(): return lax.ppermute(value, 'cam', pairs)  12.2 us
    ppermute x6, waiting for transfers between devices, routed(): return lax.ppermute(value, 'cam', pairs)  12 us
    unnamed x30, local copies, waits for them, and re-layouts  8.9 us
    ppermute x6, starting transfers between devices, swap_parts(): results.append(lax.ppermute(part, axis, pairs + [(j, i) for i, j in pairs]))  6.36 us
  transfers between devices with their start and end apart: 12, of which 4 were waited for; matrix products, arithmetic and copies ran while one was open for 0% of the time, Pallas kernels for 14%

profile of v6, /device:TPU:0, one launch (start us, length us, event | category | flops | bytes accessed | tf_op | source)
XLA Modules:
  0.0 53.3 jit_solution(996362037402452592)
XLA Ops:
  0.6 3.0 %collective-permute-start.1 = (bf16[4,128,128]{2,1,0:T(8,128)(2,1)}, bf16[4,128,128]{2,1,0:T(8,128)(2,1)S(1)}, u32[]{:S(2)}, u32[]{:S(2)}) collective-permute-start(bf16[4,128,128]{2,1,0:T(8,128)(2,1)} %bitcast.11), channel_id=1, source_target_pairs={{0,4},{4,0},{8,12},{12,8},{16,20},{20,16},{24,28},{28,24},{1,5},{5... | collective-permute-start | bytes 393224 | tf_op jit(solution)/shard_map/ppermute | solution.py:351
  3.6 3.6 %collective-permute-start = (bf16[4,128,128]{2,1,0:T(8,128)(2,1)}, bf16[4,128,128]{2,1,0:T(8,128)(2,1)S(1)}, u32[]{:S(2)}, u32[]{:S(2)}) collective-permute-start(bf16[4,128,128]{2,1,0:T(8,128)(2,1)} %bitcast.12), channel_id=1, source_target_pairs={{0,24},{4,12},{8,0},{12,20},{16,8},{20,28},{24,16},{28,4},{1,25},{... | collective-permute-start | bytes 393224 | tf_op jit(solution)/shard_map/ppermute | solution.py:351
  7.3 0.7 %copy-done.12 = s32[1,4,2,3]{1,2,3,0:T(2,128)S(1)} copy-done((s32[1,4,2,3]{1,2,3,0:T(2,128)S(1)}, s32[1,4,2,3]{1,2,3,0:T(2,128)}, u32[]{:S(2)}) %copy-start.12) | copy-done | bytes 120
  9.4 1.3 %shard_map.104.scalars = s32[34]{0:T(128)S(1)} custom-call(s32[2]{0:T(128)S(1)} %pad_add_fusion.where, s32[2,8]{1,0:T(2,128)S(1)} %bitcast.18, s32[2,8]{1,0:T(2,128)S(1)} %bitcast.19, s32[3,2,4]{2,1,0:T(2,128)S(1)} %bitcast.17), custom_call_target="tpu_custom_call" | custom-call | flops 1000000 | bytes 1000 | tf_op jit(solution)/shard_map/pallas_call | solution.py:313
  10.7 0.9 %copy-done = bf16[1,4,128,128]{3,2,1,0:T(8,128)(2,1)S(1)} copy-done((bf16[1,4,128,128]{3,2,1,0:T(8,128)(2,1)S(1)}, bf16[1,4,128,128]{3,2,1,0:T(8,128)(2,1)}, u32[]{:S(2)}) %copy-start) | copy-done | bytes 131096
  12.3 0.9 %copy-done.1 = bf16[1,4,128,128]{3,2,1,0:T(8,128)(2,1)S(1)} copy-done((bf16[1,4,128,128]{3,2,1,0:T(8,128)(2,1)S(1)}, bf16[1,4,128,128]{3,2,1,0:T(8,128)(2,1)}, u32[]{:S(2)}) %copy-start.1) | copy-done | bytes 131096
  14.5 4.5 %collective-permute-done.4.slab = bf16[4,128,128]{2,1,0:T(8,128)(2,1)S(1)} collective-permute-done((bf16[4,128,128]{2,1,0:T(8,128)(2,1)S(1)}, bf16[4,128,128]{2,1,0:T(8,128)(2,1)S(1)}, u32[]{:S(2)}, u32[]{:S(2)}) %collective-permute-start.4) | collective-permute-done | bytes 131104 | tf_op jit(solution)/shard_map/ppermute | solution.py:351
  19.7 2.9 %collective-permute-start.5 = (bf16[3,128,128]{2,1,0:T(8,128)(2,1)S(1)}, bf16[3,128,128]{2,1,0:T(8,128)(2,1)S(1)}, u32[]{:S(2)}, u32[]{:S(2)}) collective-permute-start(bf16[3,128,128]{2,1,0:T(8,128)(2,1)S(1)} %get-tuple-element.43), channel_id=1, source_target_pairs={{0,1},{2,3},{1,0},{3,2},{4,5},{6,7},{5,4},{7,6},{8,9},{10,11},{9,8... | collective-permute-start | bytes 294920 | tf_op jit(solution)/shard_map/ppermute | solution.py:21
  22.6 0.9 %copy-done.2 = bf16[1,4,128,128]{3,2,1,0:T(8,128)(2,1)S(1)} copy-done((bf16[1,4,128,128]{3,2,1,0:T(8,128)(2,1)S(1)}, bf16[1,4,128,128]{3,2,1,0:T(8,128)(2,1)}, u32[]{:S(2)}) %copy-start.2) | copy-done | bytes 131096
  23.5 1.0 %copy-done.3 = bf16[3,3,128,128]{3,2,1,0:T(8,128)(2,1)S(1)} copy-done((bf16[3,3,128,128]{3,2,1,0:T(8,128)(2,1)S(1)}, bf16[3,3,128,128]{3,2,1,0:T(8,128)(2,1)}, u32[]{:S(2)}) %copy-start.3) | copy-done | bytes 294936
  24.5 0.8 %copy-done.5 = bf16[128,128]{1,0:T(8,128)(2,1)S(1)} copy-done((bf16[128,128]{1,0:T(8,128)(2,1)S(1)}, bf16[128,128]{1,0:T(8,128)(2,1)}, u32[]{:S(2)}) %copy-start.5) | copy-done | bytes 32792
  25.3 0.8 %copy-done.7 = bf16[128,128]{1,0:T(8,128)(2,1)S(1)} copy-done((bf16[128,128]{1,0:T(8,128)(2,1)S(1)}, bf16[128,128]{1,0:T(8,128)(2,1)}, u32[]{:S(2)}) %copy-start.7) | copy-done | bytes 32792
  26.0 0.8 %copy-done.9 = bf16[128,128]{1,0:T(8,128)(2,1)S(1)} copy-done((bf16[128,128]{1,0:T(8,128)(2,1)S(1)}, bf16[128,128]{1,0:T(8,128)(2,1)}, u32[]{:S(2)}) %copy-start.9) | copy-done | bytes 32792
  26.8 0.9 %copy-done.11 = bf16[1,4,128,128]{3,2,1,0:T(8,128)(2,1)S(1)} copy-done((bf16[1,4,128,128]{3,2,1,0:T(8,128)(2,1)S(1)}, bf16[1,4,128,128]{3,2,1,0:T(8,128)(2,1)}, u32[]{:S(2)}) %copy-start.11) | copy-done | bytes 131096
  27.7 2.2 %shard_map.107 = (bf16[4,256,256]{2,1,0:T(8,128)(2,1)S(1)}, bf16[8,256,128]{2,1,0:T(8,128)(2,1)S(1)}, f32[4,384,128]{2,1,0:T(8,128)S(1)}, f32[4,384,128]{2,1,0:T(8,128)S(1)}) custom-call(s32[34]{0:T(128)S(1)} %shard_map.104.scalars, bf16[4,128,128]{2,1,0:T(8,128)(2,1)S(1)} %bitcast.15, bf16[4,128,128]{2,1,0:T(8,128)(2,1)S(1)} %get-tuple-element.22.slab, ...), custom_call_target="tpu_custom_call" | custom-call | flops 1000000 | bytes 1000 | tf_op jit(solution)/shard_map/pallas_call | solution.py:313
  30.0 3.7 %shard_map.108 = (bf16[4,128,128]{2,1,0:T(8,128)(2,1)S(1)}, bf16[4,128,128]{2,1,0:T(8,128)(2,1)S(1)}, f32[2,8,128,256]{3,2,1,0:T(8,128)S(1)}, bf16[4,768,128]{2,...) custom-call(s32[34]{0:T(128)S(1)} %shard_map.104.scalars, ...), custom_call_target="tpu_custom_call" | custom-call | flops 1500000000 | bytes 1500000 | tf_op jit(solution)/shard_map/pallas_call | solution.py:313
  34.4 1.3 %collective-permute-start.7 = (bf16[4,128,128]{2,1,0:T(8,128)(2,1)S(1)}, bf16[4,128,128]{2,1,0:T(8,128)(2,1)S(1)}, u32[]{:S(2)}, u32[]{:S(2)}) collective-permute-start(bf16[4,128,128]{2,1,0:T(8,128)(2,1)S(1)} %get-tuple-element.41), channel_id=1, source_target_pairs={{0,1},{2,3},{1,0},{3,2},{4,5},{6,7},{5,4},{7,6},{8,9},{10,11},{9,8... | collective-permute-start | bytes 393224 | tf_op jit(solution)/shard_map/ppermute | solution.py:21
  35.7 2.0 %shard_map.109 = (bf16[4,128,128]{2,1,0:T(8,128)(2,1)}, f32[2,4,128,128]{3,2,1,0:T(8,128)S(1)}, f32[4,128,128]{2,1,0:T(8,128)S(1)}) custom-call(s32[34]{0:T(128)S(1)} %shard_map.104.scalars, f32[2,8,128,256]{3,2,1,0:T(8,128)S(1)} %get-tuple-element.28.acc, bf16[4,768,128]{2,1,0:T(8,128)(2,1)S(1)} %get-tuple-element.29.probs, ...), custom_call_target="tpu_custom_call" | custom-call | flops 1000000 | bytes 1000 | tf_op jit(solution)/shard_map/pallas_call | solution.py:313
  38.3 2.9 %collective-permute-start.9 = (bf16[4,128,128]{2,1,0:T(8,128)(2,1)S(1)}, bf16[4,128,128]{2,1,0:T(8,128)(2,1)S(1)}, u32[]{:S(2)}, u32[]{:S(2)}) collective-permute-start(bf16[4,128,128]{2,1,0:T(8,128)(2,1)S(1)} %get-tuple-element.38), channel_id=1, source_target_pairs={{0,24},{4,12},{8,0},{12,20},{16,8},{20,28},{24,16},{28,4},{1,25},{... | collective-permute-start | bytes 393224 | tf_op jit(solution)/shard_map/ppermute | solution.py:351
  41.2 3.7 %collective-permute-done.9.from_second = bf16[4,128,128]{2,1,0:T(8,128)(2,1)S(1)} collective-permute-done((bf16[4,128,128]{2,1,0:T(8,128)(2,1)S(1)}, bf16[4,128,128]{2,1,0:T(8,128)(2,1)S(1)}, u32[]{:S(2)}, u32[]{:S(2)}) %collective-permute-start.9) | collective-permute-done | bytes 131104 | tf_op jit(solution)/shard_map/ppermute | solution.py:351
  45.6 2.6 %collective-permute-start.11 = (bf16[4,128,128]{2,1,0:T(8,128)(2,1)S(1)}, bf16[4,128,128]{2,1,0:T(8,128)(2,1)S(1)}, u32[]{:S(2)}, u32[]{:S(2)}) collective-permute-start(bf16[4,128,128]{2,1,0:T(8,128)(2,1)S(1)} %shard_map.111), channel_id=1, source_target_pairs={{0,4},{4,0},{8,12},{12,8},{16,20},{20,16},{24,28},{28,24},{1,5},{5... | collective-permute-start | bytes 393224 | tf_op jit(solution)/shard_map/ppermute | solution.py:351
  48.2 1.2 %collective-permute-done.10.from_first = bf16[4,128,128]{2,1,0:T(8,128)(2,1)S(1)} collective-permute-done((bf16[4,128,128]{2,1,0:T(8,128)(2,1)S(1)}, bf16[4,128,128]{2,1,0:T(8,128)(2,1)S(1)}, u32[]{:S(2)}, u32[]{:S(2)}) %collective-permute-start.10) | collective-permute-done | bytes 131104 | tf_op jit(solution)/shard_map/ppermute | solution.py:351
  49.3 2.6 %collective-permute-done.11.from_pair = bf16[4,128,128]{2,1,0:T(8,128)(2,1)S(1)} collective-permute-done((bf16[4,128,128]{2,1,0:T(8,128)(2,1)S(1)}, bf16[4,128,128]{2,1,0:T(8,128)(2,1)S(1)}, u32[]{:S(2)}, u32[]{:S(2)}) %collective-permute-start.11) | collective-permute-done | bytes 131104 | tf_op jit(solution)/shard_map/ppermute | solution.py:351
  52.0 1.3 %shard_map.112 = bf16[4,128,128]{2,1,0:T(8,128)(2,1)} custom-call(s32[34]{0:T(128)S(1)} %shard_map.104.scalars, f32[4,128,128]{2,1,0:T(8,128)S(1)} %get-tuple-element.34.grad_own, bf16[4,128,128]{2,1,0:T(8,128)(2,1)S(1)} %collective-permute-done.9.from_second, bf16[4,128,128]{2,1,0:T(8,128)(2,1)S(1)} %collective-permute-done.10.from_first, ...), custom_call_target="tpu_custom_call" | custom-call | flops 1000000 | bytes 1000 | tf_op jit(solution)/shard_map/pallas_call | solution.py:313
  (42 shorter events, 6.1 us)
Async XLA Ops:
  0.6 10.0 %collective-permute-start.1 = (bf16[4,128,128]{2,1,0:T(8,128)(2,1)}, bf16[4,128,128]{2,1,0:T(8,128)(2,1)S(1)}, u32[]{:S(2)}, u32[]{:S(2)}) collective-permute-start(bf16[4,128,128]{2,1,0:T(8,128)(2,1)} %bitcast.11), channel_id=1, source_target_pairs={{0,4},{4,0},{8,12},{12,8},{16,20},{20,16},{24,28},{28,24},{1,5},{5... | collective-permute-start | bytes 393224 | tf_op jit(solution)/shard_map/ppermute | solution.py:351
  3.6 8.6 %collective-permute-start = (bf16[4,128,128]{2,1,0:T(8,128)(2,1)}, bf16[4,128,128]{2,1,0:T(8,128)(2,1)S(1)}, u32[]{:S(2)}, u32[]{:S(2)}) collective-permute-start(bf16[4,128,128]{2,1,0:T(8,128)(2,1)} %bitcast.12), channel_id=1, source_target_pairs={{0,24},{4,12},{8,0},{12,20},{16,8},{20,28},{24,16},{28,4},{1,25},{... | collective-permute-start | bytes 393224 | tf_op jit(solution)/shard_map/ppermute | solution.py:351
  10.7 0.9 %copy-start = (bf16[1,4,128,128]{3,2,1,0:T(8,128)(2,1)S(1)}, bf16[1,4,128,128]{3,2,1,0:T(8,128)(2,1)}, u32[]{:S(2)}) copy-start(bf16[1,4,128,128]{3,2,1,0:T(8,128)(2,1)} %param.9) | copy-start | bytes 393220
  11.6 18.3 %copy-start.4 = (bf16[3,3,128,128]{3,2,1,0:T(8,128)(2,1)S(1)}, bf16[3,3,128,128]{3,2,1,0:T(8,128)(2,1)}, u32[]{:S(2)}) copy-start(bf16[3,3,128,128]{3,2,1,0:T(8,128)(2,1)} %conv_weight.3) | copy-start | bytes 884740
  11.6 18.4 %copy-start.8 = (bf16[128,128]{1,0:T(8,128)(2,1)S(1)}, bf16[128,128]{1,0:T(8,128)(2,1)}, u32[]{:S(2)}) copy-start(bf16[128,128]{1,0:T(8,128)(2,1)} %k_weight.5) | copy-start | bytes 98308
  11.6 18.4 %copy-start.10 = (bf16[128,128]{1,0:T(8,128)(2,1)S(1)}, bf16[128,128]{1,0:T(8,128)(2,1)}, u32[]{:S(2)}) copy-start(bf16[128,128]{1,0:T(8,128)(2,1)} %v_weight.5) | copy-start | bytes 98308
  12.2 6.8 %collective-permute-start.4 = (bf16[4,128,128]{2,1,0:T(8,128)(2,1)S(1)}, bf16[4,128,128]{2,1,0:T(8,128)(2,1)S(1)}, u32[]{:S(2)}, u32[]{:S(2)}) collective-permute-start(bf16[4,128,128]{2,1,0:T(8,128)(2,1)S(1)} %shard_map.105), channel_id=1, source_target_pairs={{0,8},{4,28},{8,16},{12,4},{16,24},{20,12},{24,0},{28,20},{1,9},{5... | collective-permute-start | bytes 393224 | tf_op jit(solution)/shard_map/ppermute | solution.py:351
  12.2 0.9 %copy-start.1 = (bf16[1,4,128,128]{3,2,1,0:T(8,128)(2,1)S(1)}, bf16[1,4,128,128]{3,2,1,0:T(8,128)(2,1)}, u32[]{:S(2)}) copy-start(bf16[1,4,128,128]{3,2,1,0:T(8,128)(2,1)} %param.9) | copy-start | bytes 393220
  13.8 8.9 %collective-permute-start.2 = (bf16[4,128,128]{2,1,0:T(8,128)(2,1)S(1)}, bf16[4,128,128]{2,1,0:T(8,128)(2,1)S(1)}, u32[]{:S(2)}, u32[]{:S(2)}) collective-permute-start(bf16[4,128,128]{2,1,0:T(8,128)(2,1)S(1)} %get-tuple-element.23), channel_id=1, source_target_pairs={{0,1},{2,3},{1,0},{3,2},{4,5},{6,7},{5,4},{7,6},{8,9},{10,11},{9,8... | collective-permute-start | bytes 393224 | tf_op jit(solution)/shard_map/ppermute | solution.py:21
  13.9 8.8 %collective-permute-start.3 = (bf16[4,128,128]{2,1,0:T(8,128)(2,1)S(1)}, bf16[4,128,128]{2,1,0:T(8,128)(2,1)S(1)}, u32[]{:S(2)}, u32[]{:S(2)}) collective-permute-start(bf16[4,128,128]{2,1,0:T(8,128)(2,1)S(1)} %get-tuple-element.24), channel_id=1, source_target_pairs={{1,2},{2,1},{5,6},{6,5},{9,10},{10,9},{13,14},{14,13},{17,18},{18,... | collective-permute-start | bytes 393224 | tf_op jit(solution)/shard_map/ppermute | solution.py:21
  19.0 10.9 %collective-permute-start.6 = (bf16[3,128,128]{2,1,0:T(8,128)(2,1)S(1)}, bf16[3,128,128]{2,1,0:T(8,128)(2,1)S(1)}, u32[]{:S(2)}, u32[]{:S(2)}) collective-permute-start(bf16[3,128,128]{2,1,0:T(8,128)(2,1)S(1)} %get-tuple-element.42), channel_id=1, source_target_pairs={{1,2},{2,1},{5,6},{6,5},{9,10},{10,9},{13,14},{14,13},{17,18},{18,... | collective-permute-start | bytes 294920 | tf_op jit(solution)/shard_map/ppermute | solution.py:21
  19.7 10.2 %collective-permute-start.5 = (bf16[3,128,128]{2,1,0:T(8,128)(2,1)S(1)}, bf16[3,128,128]{2,1,0:T(8,128)(2,1)S(1)}, u32[]{:S(2)}, u32[]{:S(2)}) collective-permute-start(bf16[3,128,128]{2,1,0:T(8,128)(2,1)S(1)} %get-tuple-element.43), channel_id=1, source_target_pairs={{0,1},{2,3},{1,0},{3,2},{4,5},{6,7},{5,4},{7,6},{8,9},{10,11},{9,8... | collective-permute-start | bytes 294920 | tf_op jit(solution)/shard_map/ppermute | solution.py:21
  22.6 0.9 %copy-start.2 = (bf16[1,4,128,128]{3,2,1,0:T(8,128)(2,1)S(1)}, bf16[1,4,128,128]{3,2,1,0:T(8,128)(2,1)}, u32[]{:S(2)}) copy-start(bf16[1,4,128,128]{3,2,1,0:T(8,128)(2,1)} %param.9) | copy-start | bytes 393220
  23.5 1.0 %copy-start.3 = (bf16[3,3,128,128]{3,2,1,0:T(8,128)(2,1)S(1)}, bf16[3,3,128,128]{3,2,1,0:T(8,128)(2,1)}, u32[]{:S(2)}) copy-start(bf16[3,3,128,128]{3,2,1,0:T(8,128)(2,1)} %conv_weight.3) | copy-start | bytes 884740
  24.5 0.8 %copy-start.5 = (bf16[128,128]{1,0:T(8,128)(2,1)S(1)}, bf16[128,128]{1,0:T(8,128)(2,1)}, u32[]{:S(2)}) copy-start(bf16[128,128]{1,0:T(8,128)(2,1)} %q_weight.3) | copy-start | bytes 98308
  25.3 0.8 %copy-start.7 = (bf16[128,128]{1,0:T(8,128)(2,1)S(1)}, bf16[128,128]{1,0:T(8,128)(2,1)}, u32[]{:S(2)}) copy-start(bf16[128,128]{1,0:T(8,128)(2,1)} %k_weight.5) | copy-start | bytes 98308
  26.0 0.8 %copy-start.9 = (bf16[128,128]{1,0:T(8,128)(2,1)S(1)}, bf16[128,128]{1,0:T(8,128)(2,1)}, u32[]{:S(2)}) copy-start(bf16[128,128]{1,0:T(8,128)(2,1)} %v_weight.5) | copy-start | bytes 98308
  26.8 0.9 %copy-start.11 = (bf16[1,4,128,128]{3,2,1,0:T(8,128)(2,1)S(1)}, bf16[1,4,128,128]{3,2,1,0:T(8,128)(2,1)}, u32[]{:S(2)}) copy-start(bf16[1,4,128,128]{3,2,1,0:T(8,128)(2,1)} %param.17) | copy-start | bytes 393220
  30.0 5.7 %copy-start.6 = (bf16[128,128]{1,0:T(8,128)(2,1)S(1)}, bf16[128,128]{1,0:T(8,128)(2,1)}, u32[]{:S(2)}) copy-start(bf16[128,128]{1,0:T(8,128)(2,1)} %q_weight.3) | copy-start | bytes 98308
  33.7 4.0 %collective-permute-start.8 = (bf16[4,128,128]{2,1,0:T(8,128)(2,1)S(1)}, bf16[4,128,128]{2,1,0:T(8,128)(2,1)S(1)}, u32[]{:S(2)}, u32[]{:S(2)}) collective-permute-start(bf16[4,128,128]{2,1,0:T(8,128)(2,1)S(1)} %get-tuple-element.40), channel_id=1, source_target_pairs={{1,2},{2,1},{5,6},{6,5},{9,10},{10,9},{13,14},{14,13},{17,18},{18,... | collective-permute-start | bytes 393224 | tf_op jit(solution)/shard_map/ppermute | solution.py:21
  34.4 3.3 %collective-permute-start.7 = (bf16[4,128,128]{2,1,0:T(8,128)(2,1)S(1)}, bf16[4,128,128]{2,1,0:T(8,128)(2,1)S(1)}, u32[]{:S(2)}, u32[]{:S(2)}) collective-permute-start(bf16[4,128,128]{2,1,0:T(8,128)(2,1)S(1)} %get-tuple-element.41), channel_id=1, source_target_pairs={{0,1},{2,3},{1,0},{3,2},{4,5},{6,7},{5,4},{7,6},{8,9},{10,11},{9,8... | collective-permute-start | bytes 393224 | tf_op jit(solution)/shard_map/ppermute | solution.py:21
  38.3 6.7 %collective-permute-start.9 = (bf16[4,128,128]{2,1,0:T(8,128)(2,1)S(1)}, bf16[4,128,128]{2,1,0:T(8,128)(2,1)S(1)}, u32[]{:S(2)}, u32[]{:S(2)}) collective-permute-start(bf16[4,128,128]{2,1,0:T(8,128)(2,1)S(1)} %get-tuple-element.38), channel_id=1, source_target_pairs={{0,24},{4,12},{8,0},{12,20},{16,8},{20,28},{24,16},{28,4},{1,25},{... | collective-permute-start | bytes 393224 | tf_op jit(solution)/shard_map/ppermute | solution.py:351
  41.2 8.1 %collective-permute-start.10 = (bf16[4,128,128]{2,1,0:T(8,128)(2,1)S(1)}, bf16[4,128,128]{2,1,0:T(8,128)(2,1)S(1)}, u32[]{:S(2)}, u32[]{:S(2)}) collective-permute-start(bf16[4,128,128]{2,1,0:T(8,128)(2,1)S(1)} %get-tuple-element.39.first), channel_id=1, source_target_pairs={{0,8},{4,28},{8,16},{12,4},{16,24},{20,12},{24,0},{28,20},{1,9},{5... | collective-permute-start | bytes 393224 | tf_op jit(solution)/shard_map/ppermute | solution.py:351
  45.6 6.4 %collective-permute-start.11 = (bf16[4,128,128]{2,1,0:T(8,128)(2,1)S(1)}, bf16[4,128,128]{2,1,0:T(8,128)(2,1)S(1)}, u32[]{:S(2)}, u32[]{:S(2)}) collective-permute-start(bf16[4,128,128]{2,1,0:T(8,128)(2,1)S(1)} %shard_map.111), channel_id=1, source_target_pairs={{0,4},{4,0},{8,12},{12,8},{16,20},{20,16},{24,28},{28,24},{1,5},{5... | collective-permute-start | bytes 393224 | tf_op jit(solution)/shard_map/ppermute | solution.py:351
  (3 other events, 2.0 us)

commit v7 on v6

--- a/solution.py
+++ b/solution.py
@@ -1,5 +1,3 @@
-import functools
-
 import jax
 import jax.numpy as jnp
 from jax import lax
@@ -10,7 +8,6 @@
 MARGIN = 2
 BAND = 3
 LOG2E = 1.4426950408889634
-FLAGS = 4
 
 
 def swap_parts(for_between, for_within, axis):
@@ -22,11 +19,8 @@
     return results
 
 
-def swapped(to_next, to_previous, axis):
-    odd = lax.rem(lax.axis_index(axis), 2) == 1
-    for_between = jnp.where(odd, to_next, to_previous)
-    for_within = jnp.where(odd, to_previous, to_next)
-    return swap_parts(for_between, for_within, axis)
+def parity_split(to_next, to_previous, odd):
+    return jnp.where(odd, to_next, to_previous), jnp.where(odd, to_previous, to_next)
 
 
 def margins_of(odd, between, within):
@@ -80,8 +74,8 @@
 def places_of(scalars, rows, b, side):
     return [
         (
-            scalars[FLAGS + (b * 2 + side) * BAND + s],
-            scalars[FLAGS + rows * 2 * BAND + side * BAND + s] == 1,
+            scalars[1 + (b * 2 + side) * BAND + s],
+            scalars[1 + rows * 2 * BAND + side * BAND + s] == 1,
         )
         for s in range(BAND)
     ]
@@ -236,77 +230,6 @@
         grad_own[b] = turned[:, b * width : (b + 1) * width].T
 
 
-def scalar_kernel(views, samples, where, partners, band_widths, bands, scalars):
-    camera, slab = where[0], where[1]
-    rows = bands.shape[2]
-    odd = lax.rem(lax.div(camera, samples), 2)
-
-    def is_near(steps, first):
-        other = lax.rem(camera + steps * samples + views, views)
-        side = jnp.where(odd == 1, 1 - first, first)
-        gap = jnp.where(side == 1, samples, views - samples)
-        return (partners[side, other] == lax.rem(other + gap, views)).astype(jnp.int32)
-
-    on = jnp.where(odd == 1, -2, 2)
-    scalars[0] = lax.rem(slab, 2)
-    scalars[1] = is_near(0, 1)
-    scalars[2] = is_near(on, 0)
-    scalars[3] = is_near(-on, 1)
-    top = slab * rows - MARGIN
-    last = rows + 2 * MARGIN - 1
-    for first in range(2):
-        side = jnp.where(odd == 1, 1 - first, first)
-        for s in range(BAND):
-            for b in range(rows):
-                at = jnp.clip(bands[s, side, b] - top, 0, last)
-                scalars[FLAGS + (b * 2 + first) * BAND + s] = at
-            live = (s < band_widths[side, camera]).astype(jnp.int32)
-            scalars[FLAGS + rows * 2 * BAND + first * BAND + s] = live
-
-
-def pass_kernel(scalars, pair_slab, own, passed_on):
-    passed_on[...] = jnp.where(scalars[2] == 1, pair_slab[...], own[...])
-
-
-def first_slab_kernel(scalars, far_slab, pair_slab, own, first_slab, for_within, for_between):
-    rows = own.shape[0]
-    halo = MARGIN + 1
-    odd = scalars[0] == 1
-    chosen = jnp.where(scalars[1] == 1, pair_slab[...], far_slab[...])
-    first_slab[...] = chosen
-    to_next, to_previous = chosen[rows - halo :], chosen[:halo]
-    for_within[:halo] = jnp.where(odd, to_previous, to_next)
-    for_between[:halo] = jnp.where(odd, to_next, to_previous)
-    for_within[halo] = jnp.where(odd, own[0], own[rows - 1])
-    for_between[halo] = jnp.where(odd, own[rows - 1], own[0])
-
-
-def pair_kernel(scalars, first, from_second, for_pair):
-    own = jnp.where(scalars[1] == 1, first[...].astype(jnp.float32), 0.0)
-    relayed = jnp.where(scalars[2] == 1, from_second[...].astype(jnp.float32), 0.0)
-    for_pair[...] = (own + relayed).astype(jnp.bfloat16)
-
-
-def sum_kernel(scalars, grad_own, from_second, from_first, from_pair, grad_features):
-    total = grad_own[...] + from_pair[...].astype(jnp.float32)
-    total = total + jnp.where(scalars[2] == 1, 0.0, from_second[...].astype(jnp.float32))
-    total = total + jnp.where(scalars[3] == 1, 0.0, from_first[...].astype(jnp.float32))
-    grad_features[...] = total.astype(jnp.bfloat16)
-
-
-def slab_kernel(scalars, center, within, between, left, right):
-    rows, width, channels = left.shape
-    above, below = margins_of(scalars[0] == 1, between[...], within[...])
-    for side, out in enumerate((left, right)):
-        for r in range(rows):
-            total = center[side, r]
-            if r < MARGIN:
-                total = total + above[side * MARGIN + r].astype(jnp.float32)
-            if r >= rows - MARGIN:
-                total = total + below[side * MARGIN + r - rows + MARGIN].astype(jnp.float32)
-            out[r] = total.astype(jnp.bfloat16)
-
-
 def on_device(kernel, out_shape, scratch, flops, *arrays):
     smem = pl.BlockSpec(memory_space=pltpu.SMEM)
     vmem = pl.BlockSpec(memory_space=pltpu.VMEM)
@@ -350,36 +273,45 @@
             pairs.append((c, (c // samples + step) % ring * samples + c % samples))
         return lax.ppermute(value, "cam", pairs)
 
+    camera = lax.axis_index("cam")
+    slab = lax.axis_index("row")
+    odd_place = lax.rem(lax.div(camera, samples), 2) == 1
+    odd_row = lax.rem(slab, 2) == 1
+    on = jnp.where(odd_place, -2, 2)
+
+    def is_near(steps, first):
+        other = lax.rem(camera + steps * samples + views, views)
+        side = jnp.where(odd_place, 1 - first, first)
+        gap = jnp.where(side == 1, samples, views - samples)
+        return partners[other, side] == lax.rem(other + gap, views)
+
+    first_near = is_near(0, 1)
+    second_near_on = is_near(on, 0)
+    first_near_back = is_near(-on, 1)
     pair_slab = routed(image, 1, -1)
     far_slab = routed(image, -2, 2)
-    where = jnp.stack([lax.axis_index("cam"), lax.axis_index("row")]).astype(jnp.int32)
-    (scalars,) = on_device(
-        functools.partial(scalar_kernel, views, samples),
-        [((FLAGS + (rows + 1) * 2 * BAND,), jnp.int32)],
-        [],
-        1_000_000,
-        where,
-        partners.T,
-        band_widths.T,
-        bands[0].transpose(2, 1, 0),
-    )
-    (passed_on,) = on_device(
-        pass_kernel, [(image.shape, half)], [], 1_000_000, scalars, pair_slab, image
-    )
+    passed_on = jnp.where(second_near_on, pair_slab, image)
     second_slab = routed(passed_on, 2, -2)
     far_slab, _ = lax.optimization_barrier((far_slab, passed_on))
-    edge = ((halo + 1, width, channels), half)
-    first_slab, for_within, for_between = on_device(
-        first_slab_kernel,
-        [(image.shape, half), edge, edge],
-        [],
-        1_000_000,
-        scalars,
-        far_slab,
-        pair_slab,
-        image,
-    )
+    first_slab = jnp.where(~first_near, far_slab, pair_slab)
+    to_next = jnp.concatenate([first_slab[rows - halo :], image[rows - 1 :]])
+    to_previous = jnp.concatenate([first_slab[:halo], image[:1]])
+    for_between, for_within = parity_split(to_next, to_previous, odd_row)
     between, within = swap_parts(for_between, for_within, "row")
+    bands, band_widths, _ = lax.optimization_barrier((bands, band_widths, for_between))
+
+    widths_here = lax.dynamic_index_in_dim(band_widths, camera, 0, keepdims=False)
+    live = jnp.arange(BAND, dtype=jnp.int32)[None, :] < widths_here[:, None]
+    places = jnp.clip(bands[0] - (slab * rows - MARGIN), 0, win - 1)
+    live = jnp.where(odd_place, live[::-1], live)
+    places = jnp.where(odd_place, places[:, ::-1], places)
+    scalars = jnp.concatenate(
+        [
+            odd_row.astype(jnp.int32).reshape(1),
+            places.reshape(-1),
+            live.reshape(-1).astype(jnp.int32),
+        ]
+    )
 
     conv_scratch = [
         (((win + 2) * width, channels), half),
@@ -407,7 +339,9 @@
         v_weight,
         grad_attended[0],
     )
-    between, within = swapped(second_slab[rows - halo :], second_slab[:halo], "row")
+    between, within = swap_parts(
+        *parity_split(second_slab[rows - halo :], second_slab[:halo], odd_row), "row"
+    )
     margins = ((2 * MARGIN, width, channels), half)
     weights = ((rows, 2 * BAND * width, width), half)
     top, bottom, acc, probs, grad_scores, kv_t = on_device(
@@ -433,7 +367,7 @@
         first_expo,
         first_grad_probs,
     )
-    between, within = swapped(bottom, top, "row")
+    between, within = swap_parts(*parity_split(bottom, top, odd_row), "row")
     attended, center, grad_own = on_device(
         third_kernel,
         [
@@ -453,34 +387,24 @@
         k_weight,
         v_weight,
     )
-    second, first = on_device(
-        slab_kernel,
-        [(image.shape, half)] * 2,
-        [],
-        1_000_000,
-        scalars,
-        center,
-        within,
-        between,
-    )
+    from_above, from_below = (
+        part.reshape(2, MARGIN, width, channels).astype(full)
+        for part in margins_of(~odd_row, within, between)
+    )
+    zeros = jnp.zeros((2, rows - MARGIN, width, channels), full)
+    total = center + jnp.concatenate([from_above, zeros], axis=1)
+    total = total + jnp.concatenate([zeros, from_below], axis=1)
+    second, first = total[0].astype(half), total[1].astype(half)
     from_second = routed(second, -2, 2)
     from_first = routed(first, 2, -2)
-    (for_pair,) = on_device(
-        pair_kernel, [(image.shape, half)], [], 1_000_000, scalars, first, from_second
-    )
-    from_pair = routed(for_pair, 1, -1)
-    (grad_features,) = on_device(
-        sum_kernel,
-        [(image.shape, half)],
-        [],
-        1_000_000,
-        scalars,
-        grad_own,
-        from_second,
-        from_first,
-        from_pair,
-    )
-    return (attended[None], grad_features[None])
+    for_pair = jnp.where(first_near, first.astype(full), 0.0) + jnp.where(
+        second_near_on, from_second.astype(full), 0.0
+    )
+    from_pair = routed(for_pair.astype(half), 1, -1)
+    summed = grad_own + from_pair.astype(full)
+    summed = summed + jnp.where(second_near_on, 0.0, from_second.astype(full))
+    summed = summed + jnp.where(first_near_back, 0.0, from_first.astype(full))
+    return (attended[None], summed.astype(half)[None])
 
 
 def solution(mesh):

time: 53.8 us -> 57.6 us (1.071)
  other arithmetic: 0.12 us -> 6.17 us
  waiting for transfers between devices: 12 us -> 6.7 us
  Pallas kernels: 12.8 us -> 7.83 us
  starting transfers between devices: 18.6 us -> 21.8 us
  local copies, waits for them, and re-layouts: 8.9 us -> 11.4 us
  between operations: 0.82 us -> 2.83 us
    ppermute x6, waiting for transfers between devices: 12 us -> 6.68 us  [routed(): return lax.ppermute(value, 'cam', pairs)]
    pallas_call x9 -> x3, Pallas kernels: 12.8 us -> 7.83 us  [on_device(): pl.pallas_call(kernel, out_shape=tuple((jax.ShapeDtypeStruct(*one) for on...]
    ppermute x6, starting transfers between devices: 6.36 us -> 10.7 us  [swap_parts(): results.append(lax.ppermute(part, axis, pairs + [(j, i) for i, j in pairs]))]
    select_n x2 -> x7, other arithmetic: 0.05 us -> 3.45 us  [the longest x1 1.03 us: margins_of(): return (jnp.where(odd, within, between), jnp.where(odd, between, within))]
    broadcast_in_dim x0 -> x1, other arithmetic: none -> 1.69 us  [local(): return (attended[None], summed.astype(half)[None])]
    dynamic_slice x0 -> x2, local copies, waits for them, and re-layouts: none -> 1.63 us  [the longest x1 1.45 us: is_near(): return partners[other, side] == lax.rem(other + gap, views)]
    ppermute x6, starting transfers between devices: 12.2 us -> 11.1 us  [routed(): return lax.ppermute(value, 'cam', pairs)]
    slice x0 -> x2, local copies, waits for them, and re-layouts: none -> 0.81 us  [local(): to_next = jnp.concatenate([first_slab[rows - halo:], image[rows - 1:]])]
  transfers between devices with their start and end apart: 12 -> 12, of which waited for: 4 -> 3; matrix products, arithmetic and copies ran while one was open for 0% -> 10% of each run, Pallas kernels for 14% -> 7%
where the time goes in v7:
time: 57.6 us; the launch traced here: 56.7 us
  starting transfers between devices  21.8 us (38%)
  local copies, waits for them, and re-layouts  11.4 us (20%)
  Pallas kernels  7.83 us (14%)
  waiting for transfers between devices  6.7 us (12%)
  other arithmetic  6.17 us (11%)
  between operations  2.83 us (5%)
    ppermute x6, starting transfers between devices, routed(): return lax.ppermute(value, 'cam', pairs)  11.1 us
    ppermute x6, starting transfers between devices, swap_parts(): results.append(lax.ppermute(part, axis, pairs + [(j, i) for i, j in pairs]))  10.7 us
    unnamed x36, local copies, waits for them, and re-layouts  8.64 us
    pallas_call x3, Pallas kernels, on_device(): pl.pallas_call(kernel, out_shape=tuple((jax.ShapeDtypeStruct(*one) for on...  7.83 us
    ppermute x6, waiting for transfers between devices, routed(): return lax.ppermute(value, 'cam', pairs)  6.68 us
    broadcast_in_dim x1, other arithmetic, local(): return (attended[None], summed.astype(half)[None])  1.69 us
    dynamic_slice x1, local copies, waits for them, and re-layouts, is_near(): return partners[other, side] == lax.rem(other + gap, views)  1.45 us
  transfers between devices with their start and end apart: 12, of which 3 were waited for; matrix products, arithmetic and copies ran while one was open for 10% of the time, Pallas kernels for 7%

profile of v7, /device:TPU:0, one launch (start us, length us, event | category | flops | bytes accessed | tf_op | source)
XLA Modules:
  0.0 56.7 jit_solution(12218969199245511155)
XLA Ops:
  0.7 3.0 %collective-permute-start.1 = (bf16[4,128,128]{2,1,0:T(8,128)(2,1)}, bf16[4,128,128]{2,1,0:T(8,128)(2,1)S(1)}, u32[]{:S(2)}, u32[]{:S(2)}) collective-permute-start(bf16[4,128,128]{2,1,0:T(8,128)(2,1)} %bitcast.26), channel_id=1, source_target_pairs={{0,4},{4,0},{8,12},{12,8},{16,20},{20,16},{24,28},{28,24},{1,5},{5... | collective-permute-start | bytes 393224 | tf_op jit(solution)/shard_map/ppermute | solution.py:274
  3.7 3.6 %collective-permute-start = (bf16[4,128,128]{2,1,0:T(8,128)(2,1)}, bf16[4,128,128]{2,1,0:T(8,128)(2,1)S(1)}, u32[]{:S(2)}, u32[]{:S(2)}) collective-permute-start(bf16[4,128,128]{2,1,0:T(8,128)(2,1)} %bitcast.27), channel_id=1, source_target_pairs={{0,24},{4,12},{8,0},{12,20},{16,8},{20,28},{24,16},{28,4},{1,25},{... | collective-permute-start | bytes 393224 | tf_op jit(solution)/shard_map/ppermute | solution.py:274
  7.3 1.4 %fusion.7 = (s32[1,1]{0,1:T(1,128)}, s32[1,1]{0,1:T(1,128)}, s32[1,1]{0,1:T(1,128)}) fusion(s32[8,2]{0,1:T(2,128)} %param.14, s32[]{:T(128)S(6)} %select_n.160, s32[]{:T(128)S(6)} %select_n.132, s32[]{:T(128)S(6)} %select_n.131, s32[]{:T(128)S(6)} %select_n.136, s32[]{:T(128)S(6)} %select_n.137), kind=kLoop, calls=%fused_computation.32 | loop fusion | bytes 44 | tf_op jit(solution)/shard_map/dynamic_slice | solution.py:286
  10.0 0.8 %slice_bitcast_fusion.3 = (bf16[1,128,128]{2,1,0:T(8,128)(2,1)S(1)}, bf16[1,128,128]{2,1,0:T(8,128)(2,1)S(1)}) fusion(bf16[1,4,128,128]{3,2,1,0:T(8,128)(2,1)} %param.9), kind=kLoop, calls=%fused_computation.24 | loop fusion | bytes 131072 | tf_op jit(solution)/shard_map/slice | solution.py:297
  10.8 0.9 %broadcast_select_fusion.2 = bf16[4,128,128]{2,1,0:T(8,128)(2,1)S(1)} fusion(bf16[4,128,128]{2,1,0:T(8,128)(2,1)S(1)} %collective-permute-done.1, pred[]{:T(512)S(6)} %eq.27, bf16[1,4,128,128]{3,2,1,0:T(8,128)(2,1)} %param.9), kind=kLoop, calls=%fused_computation.15 | loop fusion | flops 65536 | bytes 393217 | tf_op jit(solution)/shard_map/jit(_where)/select_n | solution.py:293
  14.6 2.9 %collective-permute-start.2 = (bf16[4,128,128]{2,1,0:T(8,128)(2,1)S(1)}, bf16[4,128,128]{2,1,0:T(8,128)(2,1)S(1)}, u32[]{:S(2)}, u32[]{:S(2)}) collective-permute-start(bf16[4,128,128]{2,1,0:T(8,128)(2,1)S(1)} %get-tuple-element.40), channel_id=1, source_target_pairs={{0,1},{2,3},{1,0},{3,2},{4,5},{6,7},{5,4},{7,6},{8,9},{10,11},{9,8... | collective-permute-start | bytes 393224 | tf_op jit(solution)/shard_map/ppermute | solution.py:18
  17.5 1.0 %collective-permute-done.4.slab = bf16[4,128,128]{2,1,0:T(8,128)(2,1)S(1)} collective-permute-done((bf16[4,128,128]{2,1,0:T(8,128)(2,1)S(1)}, bf16[4,128,128]{2,1,0:T(8,128)(2,1)S(1)}, u32[]{:S(2)}, u32[]{:S(2)}) %collective-permute-start.4) | collective-permute-done | bytes 131104 | tf_op jit(solution)/shard_map/ppermute | solution.py:274
  19.2 2.9 %collective-permute-start.5 = (bf16[3,128,128]{2,1,0:T(8,128)(2,1)S(1)}, bf16[3,128,128]{2,1,0:T(8,128)(2,1)S(1)}, u32[]{:S(2)}, u32[]{:S(2)}) collective-permute-start(bf16[3,128,128]{2,1,0:T(8,128)(2,1)S(1)} %get-tuple-element.43), channel_id=1, source_target_pairs={{0,1},{2,3},{1,0},{3,2},{4,5},{6,7},{5,4},{7,6},{8,9},{10,11},{9,8... | collective-permute-start | bytes 294920 | tf_op jit(solution)/shard_map/ppermute | solution.py:18
  22.3 2.2 %shard_map.104 = (bf16[4,256,256]{2,1,0:T(8,128)(2,1)S(1)}, bf16[8,256,128]{2,1,0:T(8,128)(2,1)S(1)}, f32[4,384,128]{2,1,0:T(8,128)S(1)}, f32[4,384,128]{2,1,0:T(8,128)S(1)}) custom-call(s32[31]{0:T(128)S(1)} %pad_add_fusion.scalars, bf16[4,128,128]{2,1,0:T(8,128)(2,1)S(1)} %bitcast.28, bf16[4,128,128]{2,1,0:T(8,128)(2,1)S(1)} %broadcast_select_fusion.3.slab, ...), custom_call_target="tpu_custom_call" | custom-call | flops 1000000 | bytes 1000 | tf_op jit(solution)/shard_map/pallas_call | solution.py:236
  24.6 1.0 %copy-done.7 = bf16[3,3,128,128]{3,2,1,0:T(8,128)(2,1)S(1)} copy-done((bf16[3,3,128,128]{3,2,1,0:T(8,128)(2,1)S(1)}, bf16[3,3,128,128]{3,2,1,0:T(8,128)(2,1)}, u32[]{:S(2)}) %copy-start.7) | copy-done | bytes 294936
  25.5 0.8 %copy-done.12 = bf16[128,128]{1,0:T(8,128)(2,1)S(1)} copy-done((bf16[128,128]{1,0:T(8,128)(2,1)S(1)}, bf16[128,128]{1,0:T(8,128)(2,1)}, u32[]{:S(2)}) %copy-start.12) | copy-done | bytes 32792
  27.0 3.7 %shard_map.105 = (bf16[4,128,128]{2,1,0:T(8,128)(2,1)S(1)}, bf16[4,128,128]{2,1,0:T(8,128)(2,1)S(1)}, f32[2,8,128,256]{3,2,1,0:T(8,128)S(1)}, bf16[4,768,128]{2,...) custom-call(s32[31]{0:T(128)S(1)} %pad_add_fusion.scalars, ...), custom_call_target="tpu_custom_call" | custom-call | flops 1500000000 | bytes 1500000 | tf_op jit(solution)/shard_map/pallas_call | solution.py:236
  30.7 0.9 %copy-done.2 = bf16[4,768,128]{2,1,0:T(8,128)(2,1)} copy-done((bf16[4,768,128]{2,1,0:T(8,128)(2,1)}, bf16[4,768,128]{2,1,0:T(8,128)(2,1)S(1)}, u32[]{:S(2)}) %copy-start.2) | copy-done | bytes 786456
  31.6 0.8 %copy-done.4 = bf16[8,256,128]{2,1,0:T(8,128)(2,1)} copy-done((bf16[8,256,128]{2,1,0:T(8,128)(2,1)}, bf16[8,256,128]{2,1,0:T(8,128)(2,1)S(1)}, u32[]{:S(2)}) %copy-start.4) | copy-done | bytes 524312
  33.8 2.9 %collective-permute-start.8 = (bf16[4,128,128]{2,1,0:T(8,128)(2,1)}, bf16[4,128,128]{2,1,0:T(8,128)(2,1)}, u32[]{:S(2)}, u32[]{:S(2)}) collective-permute-start(bf16[4,128,128]{2,1,0:T(8,128)(2,1)} %get-tuple-element.39), channel_id=1, source_target_pairs={{0,1},{2,3},{1,0},{3,2},{4,5},{6,7},{5,4},{7,6},{8,9},{10,11},{9,8... | collective-permute-start | bytes 393224 | tf_op jit(solution)/shard_map/ppermute | solution.py:18
  36.7 1.1 %copy-done.3 = bf16[4,768,128]{2,1,0:T(8,128)(2,1)S(1)} copy-done((bf16[4,768,128]{2,1,0:T(8,128)(2,1)S(1)}, bf16[4,768,128]{2,1,0:T(8,128)(2,1)}, u32[]{:S(2)}) %copy-start.3) | copy-done | bytes 786456
  37.8 1.0 %copy-done.5 = bf16[8,256,128]{2,1,0:T(8,128)(2,1)S(1)} copy-done((bf16[8,256,128]{2,1,0:T(8,128)(2,1)S(1)}, bf16[8,256,128]{2,1,0:T(8,128)(2,1)}, u32[]{:S(2)}) %copy-start.5) | copy-done | bytes 524312
  41.1 2.0 %shard_map.106 = (bf16[4,128,128]{2,1,0:T(8,128)(2,1)}, f32[2,4,128,128]{3,2,1,0:T(8,128)S(1)}, f32[4,128,128]{2,1,0:T(8,128)S(1)}) custom-call(s32[31]{0:T(128)S(1)} %pad_add_fusion.scalars, f32[2,8,128,256]{3,2,1,0:T(8,128)S(1)} %get-tuple-element.24.acc, bf16[4,768,128]{2,1,0:T(8,128)(2,1)S(1)} %get-tuple-element.25.probs, ...), custom_call_target="tpu_custom_call" | custom-call | flops 1000000 | bytes 1000 | tf_op jit(solution)/shard_map/pallas_call | solution.py:236
  43.1 1.0 %broadcast_select_fusion.1 = (bf16[4,128,128]{2,1,0:T(8,128)(2,1)S(1)}, bf16[4,128,128]{2,1,0:T(8,128)(2,1)S(1)}) fusion(bf16[4,128,128]{2,1,0:T(8,128)(2,1)S(1)} %collective-permute-done.7, bf16[4,128,128]{2,1,0:T(8,128)(2,1)} %collective-permute-done.8, pred[]{:T(512)S(6)} %not.7), kind=kLoop, calls=%fused_computation.14 | loop fusion | flops 131072 | bytes 524289 | tf_op jit(solution)/shard_map/jit(_where)/select_n | solution.py:27
  44.2 1.4 %collective-permute-start.9 = (bf16[4,128,128]{2,1,0:T(8,128)(2,1)S(1)}, bf16[4,128,128]{2,1,0:T(8,128)(2,1)S(1)}, u32[]{:S(2)}, u32[]{:S(2)}) collective-permute-start(bf16[4,128,128]{2,1,0:T(8,128)(2,1)S(1)} %get-tuple-element.34), channel_id=1, source_target_pairs={{0,24},{4,12},{8,0},{12,20},{16,8},{20,28},{24,16},{28,4},{1,25},{... | collective-permute-start | bytes 393224 | tf_op jit(solution)/shard_map/ppermute | solution.py:274
  46.3 3.4 %collective-permute-done.9 = bf16[4,128,128]{2,1,0:T(8,128)(2,1)S(1)} collective-permute-done((bf16[4,128,128]{2,1,0:T(8,128)(2,1)S(1)}, bf16[4,128,128]{2,1,0:T(8,128)(2,1)S(1)}, u32[]{:S(2)}, u32[]{:S(2)}) %collective-permute-start.9) | collective-permute-done | bytes 131104 | tf_op jit(solution)/shard_map/ppermute | solution.py:274
  49.7 2.4 %collective-permute-start.10 = (bf16[4,128,128]{2,1,0:T(8,128)(2,1)S(1)}, bf16[4,128,128]{2,1,0:T(8,128)(2,1)S(1)}, u32[]{:S(2)}, u32[]{:S(2)}) collective-permute-start(bf16[4,128,128]{2,1,0:T(8,128)(2,1)S(1)} %fusion.1), channel_id=1, source_target_pairs={{0,4},{4,0},{8,12},{12,8},{16,20},{20,16},{24,28},{28,24},{1,5},{5... | collective-permute-start | bytes 393224 | tf_op jit(solution)/shard_map/ppermute | solution.py:274
  52.8 2.3 %collective-permute-done.10 = bf16[4,128,128]{2,1,0:T(8,128)(2,1)S(1)} collective-permute-done((bf16[4,128,128]{2,1,0:T(8,128)(2,1)S(1)}, bf16[4,128,128]{2,1,0:T(8,128)(2,1)S(1)}, u32[]{:S(2)}, u32[]{:S(2)}) %collective-permute-start.10) | collective-permute-done | bytes 131104 | tf_op jit(solution)/shard_map/ppermute | solution.py:274
  55.1 1.7 %fusion.5 = bf16[1,4,128,128]{3,2,1,0:T(8,128)(2,1)} fusion(bf16[4,128,128]{2,1,0:T(8,128)(2,1)S(1)} %collective-permute-done.11, bf16[4,128,128]{2,1,0:T(8,128)(2,1)S(1)} %collective-permute-done.9, f32[4,128,128]{2,1,0:T(8,128)} %copy-done.8, bf16[4,128,128]{2,1,0:T(8,128)(2,1)S(1)} %collective-permute-done.10, pred[]{:T(512)S(6)} %eq.28, pred[]{:T(512)S(6)} %eq.27), kind=kLoop, calls=%fused_computation.8 | loop fusion | flops 589824 | bytes 786434 | tf_op jit(solution)/shard_map/broadcast_in_dim | solution.py:407
  (63 shorter events, 8.9 us)
Async XLA Ops:
  0.6 11.9 %copy-start = (s32[8,2]{0,1:T(2,128)S(1)}, s32[8,2]{0,1:T(2,128)}, u32[]{:S(2)}) copy-start(s32[8,2]{0,1:T(2,128)} %param.15) | copy-start | bytes 196
  0.6 21.6 %copy-start.1 = (bf16[1,4,128,128]{3,2,1,0:T(8,128)(2,1)S(1)}, bf16[1,4,128,128]{3,2,1,0:T(8,128)(2,1)}, u32[]{:S(2)}) copy-start(bf16[1,4,128,128]{3,2,1,0:T(8,128)(2,1)} %param.9) | copy-start | bytes 393220
  0.7 21.6 %copy-start.14 = (bf16[128,128]{1,0:T(8,128)(2,1)S(1)}, bf16[128,128]{1,0:T(8,128)(2,1)}, u32[]{:S(2)}) copy-start(bf16[128,128]{1,0:T(8,128)(2,1)} %v_weight.5) | copy-start | bytes 98308
  0.7 21.6 %copy-start.11 = (bf16[128,128]{1,0:T(8,128)(2,1)S(1)}, bf16[128,128]{1,0:T(8,128)(2,1)}, u32[]{:S(2)}) copy-start(bf16[128,128]{1,0:T(8,128)(2,1)} %k_weight.5) | copy-start | bytes 98308
  0.7 21.6 %copy-start.9 = (bf16[128,128]{1,0:T(8,128)(2,1)S(1)}, bf16[128,128]{1,0:T(8,128)(2,1)}, u32[]{:S(2)}) copy-start(bf16[128,128]{1,0:T(8,128)(2,1)} %q_weight.3) | copy-start | bytes 98308
  0.7 21.6 %copy-start.6 = (bf16[3,3,128,128]{3,2,1,0:T(8,128)(2,1)S(1)}, bf16[3,3,128,128]{3,2,1,0:T(8,128)(2,1)}, u32[]{:S(2)}) copy-start(bf16[3,3,128,128]{3,2,1,0:T(8,128)(2,1)} %conv_weight.3) | copy-start | bytes 884740
  0.7 21.6 %copy-start.17 = (bf16[1,4,128,128]{3,2,1,0:T(8,128)(2,1)S(1)}, bf16[1,4,128,128]{3,2,1,0:T(8,128)(2,1)}, u32[]{:S(2)}) copy-start(bf16[1,4,128,128]{3,2,1,0:T(8,128)(2,1)} %param.17) | copy-start | bytes 393220
  0.7 10.1 %collective-permute-start.1 = (bf16[4,128,128]{2,1,0:T(8,128)(2,1)}, bf16[4,128,128]{2,1,0:T(8,128)(2,1)S(1)}, u32[]{:S(2)}, u32[]{:S(2)}) collective-permute-start(bf16[4,128,128]{2,1,0:T(8,128)(2,1)} %bitcast.26), channel_id=1, source_target_pairs={{0,4},{4,0},{8,12},{12,8},{16,20},{20,16},{24,28},{28,24},{1,5},{5... | collective-permute-start | bytes 393224 | tf_op jit(solution)/shard_map/ppermute | solution.py:274
  3.7 8.1 %collective-permute-start = (bf16[4,128,128]{2,1,0:T(8,128)(2,1)}, bf16[4,128,128]{2,1,0:T(8,128)(2,1)S(1)}, u32[]{:S(2)}, u32[]{:S(2)}) collective-permute-start(bf16[4,128,128]{2,1,0:T(8,128)(2,1)} %bitcast.27), channel_id=1, source_target_pairs={{0,24},{4,12},{8,0},{12,20},{16,8},{20,28},{24,16},{28,4},{1,25},{... | collective-permute-start | bytes 393224 | tf_op jit(solution)/shard_map/ppermute | solution.py:274
  11.7 6.8 %collective-permute-start.4 = (bf16[4,128,128]{2,1,0:T(8,128)(2,1)S(1)}, bf16[4,128,128]{2,1,0:T(8,128)(2,1)S(1)}, u32[]{:S(2)}, u32[]{:S(2)}) collective-permute-start(bf16[4,128,128]{2,1,0:T(8,128)(2,1)S(1)} %broadcast_select_fusion.2), channel_id=1, source_target_pairs={{0,8},{4,28},{8,16},{12,4},{16,24},{20,12},{24,0},{28,20},{1,9},{5... | collective-permute-start | bytes 393224 | tf_op jit(solution)/shard_map/ppermute | solution.py:274
  11.9 10.4 %collective-permute-start.3 = (bf16[4,128,128]{2,1,0:T(8,128)(2,1)S(1)}, bf16[4,128,128]{2,1,0:T(8,128)(2,1)S(1)}, u32[]{:S(2)}, u32[]{:S(2)}) collective-permute-start(bf16[4,128,128]{2,1,0:T(8,128)(2,1)S(1)} %get-tuple-element.41), channel_id=1, source_target_pairs={{1,2},{2,1},{5,6},{6,5},{9,10},{10,9},{13,14},{14,13},{17,18},{18,... | collective-permute-start | bytes 393224 | tf_op jit(solution)/shard_map/ppermute | solution.py:18
  14.6 7.6 %collective-permute-start.2 = (bf16[4,128,128]{2,1,0:T(8,128)(2,1)S(1)}, bf16[4,128,128]{2,1,0:T(8,128)(2,1)S(1)}, u32[]{:S(2)}, u32[]{:S(2)}) collective-permute-start(bf16[4,128,128]{2,1,0:T(8,128)(2,1)S(1)} %get-tuple-element.40), channel_id=1, source_target_pairs={{0,1},{2,3},{1,0},{3,2},{4,5},{6,7},{5,4},{7,6},{8,9},{10,11},{9,8... | collective-permute-start | bytes 393224 | tf_op jit(solution)/shard_map/ppermute | solution.py:18
  18.6 6.0 %collective-permute-start.6 = (bf16[3,128,128]{2,1,0:T(8,128)(2,1)S(1)}, bf16[3,128,128]{2,1,0:T(8,128)(2,1)S(1)}, u32[]{:S(2)}, u32[]{:S(2)}) collective-permute-start(bf16[3,128,128]{2,1,0:T(8,128)(2,1)S(1)} %get-tuple-element.42), channel_id=1, source_target_pairs={{1,2},{2,1},{5,6},{6,5},{9,10},{10,9},{13,14},{14,13},{17,18},{18,... | collective-permute-start | bytes 294920 | tf_op jit(solution)/shard_map/ppermute | solution.py:18
  19.2 5.3 %collective-permute-start.5 = (bf16[3,128,128]{2,1,0:T(8,128)(2,1)S(1)}, bf16[3,128,128]{2,1,0:T(8,128)(2,1)S(1)}, u32[]{:S(2)}, u32[]{:S(2)}) collective-permute-start(bf16[3,128,128]{2,1,0:T(8,128)(2,1)S(1)} %get-tuple-element.43), channel_id=1, source_target_pairs={{0,1},{2,3},{1,0},{3,2},{4,5},{6,7},{5,4},{7,6},{8,9},{10,11},{9,8... | collective-permute-start | bytes 294920 | tf_op jit(solution)/shard_map/ppermute | solution.py:18
  24.6 1.0 %copy-start.7 = (bf16[3,3,128,128]{3,2,1,0:T(8,128)(2,1)S(1)}, bf16[3,3,128,128]{3,2,1,0:T(8,128)(2,1)}, u32[]{:S(2)}) copy-start(bf16[3,3,128,128]{3,2,1,0:T(8,128)(2,1)} %conv_weight.3) | copy-start | bytes 884740
  30.7 0.9 %copy-start.2 = (bf16[4,768,128]{2,1,0:T(8,128)(2,1)}, bf16[4,768,128]{2,1,0:T(8,128)(2,1)S(1)}, u32[]{:S(2)}) copy-start(bf16[4,768,128]{2,1,0:T(8,128)(2,1)S(1)} %get-tuple-element.26.grad_scores) | copy-start | bytes 2359300
  33.1 10.0 %collective-permute-start.7 = (bf16[4,128,128]{2,1,0:T(8,128)(2,1)}, bf16[4,128,128]{2,1,0:T(8,128)(2,1)S(1)}, u32[]{:S(2)}, u32[]{:S(2)}) collective-permute-start(bf16[4,128,128]{2,1,0:T(8,128)(2,1)} %get-tuple-element.38), channel_id=1, source_target_pairs={{1,2},{2,1},{5,6},{6,5},{9,10},{10,9},{13,14},{14,13},{17,18},{18,... | collective-permute-start | bytes 393224 | tf_op jit(solution)/shard_map/ppermute | solution.py:18
  33.8 9.3 %collective-permute-start.8 = (bf16[4,128,128]{2,1,0:T(8,128)(2,1)}, bf16[4,128,128]{2,1,0:T(8,128)(2,1)}, u32[]{:S(2)}, u32[]{:S(2)}) collective-permute-start(bf16[4,128,128]{2,1,0:T(8,128)(2,1)} %get-tuple-element.39), channel_id=1, source_target_pairs={{0,1},{2,3},{1,0},{3,2},{4,5},{6,7},{5,4},{7,6},{8,9},{10,11},{9,8... | collective-permute-start | bytes 393224 | tf_op jit(solution)/shard_map/ppermute | solution.py:18
  36.7 1.1 %copy-start.3 = (bf16[4,768,128]{2,1,0:T(8,128)(2,1)S(1)}, bf16[4,768,128]{2,1,0:T(8,128)(2,1)}, u32[]{:S(2)}) copy-start(bf16[4,768,128]{2,1,0:T(8,128)(2,1)} %copy-done.2) | copy-start | bytes 2359300
  37.8 1.0 %copy-start.5 = (bf16[8,256,128]{2,1,0:T(8,128)(2,1)S(1)}, bf16[8,256,128]{2,1,0:T(8,128)(2,1)}, u32[]{:S(2)}) copy-start(bf16[8,256,128]{2,1,0:T(8,128)(2,1)} %copy-done.4) | copy-start | bytes 1572868
  43.1 1.1 %copy-start.8 = (f32[4,128,128]{2,1,0:T(8,128)}, f32[4,128,128]{2,1,0:T(8,128)S(1)}, u32[]{:S(2)}) copy-start(f32[4,128,128]{2,1,0:T(8,128)S(1)} %get-tuple-element.30) | copy-start | bytes 786436
  44.2 5.5 %collective-permute-start.9 = (bf16[4,128,128]{2,1,0:T(8,128)(2,1)S(1)}, bf16[4,128,128]{2,1,0:T(8,128)(2,1)S(1)}, u32[]{:S(2)}, u32[]{:S(2)}) collective-permute-start(bf16[4,128,128]{2,1,0:T(8,128)(2,1)S(1)} %get-tuple-element.34), channel_id=1, source_target_pairs={{0,24},{4,12},{8,0},{12,20},{16,8},{20,28},{24,16},{28,4},{1,25},{... | collective-permute-start | bytes 393224 | tf_op jit(solution)/shard_map/ppermute | solution.py:274
  45.6 7.2 %collective-permute-start.11 = (bf16[4,128,128]{2,1,0:T(8,128)(2,1)S(1)}, bf16[4,128,128]{2,1,0:T(8,128)(2,1)S(1)}, u32[]{:S(2)}, u32[]{:S(2)}) collective-permute-start(bf16[4,128,128]{2,1,0:T(8,128)(2,1)S(1)} %get-tuple-element.35), channel_id=1, source_target_pairs={{0,8},{4,28},{8,16},{12,4},{16,24},{20,12},{24,0},{28,20},{1,9},{5... | collective-permute-start | bytes 393224 | tf_op jit(solution)/shard_map/ppermute | solution.py:274
  49.7 5.3 %collective-permute-start.10 = (bf16[4,128,128]{2,1,0:T(8,128)(2,1)S(1)}, bf16[4,128,128]{2,1,0:T(8,128)(2,1)S(1)}, u32[]{:S(2)}, u32[]{:S(2)}) collective-permute-start(bf16[4,128,128]{2,1,0:T(8,128)(2,1)S(1)} %fusion.1), channel_id=1, source_target_pairs={{0,4},{4,0},{8,12},{12,8},{16,20},{20,16},{24,28},{28,24},{1,5},{5... | collective-permute-start | bytes 393224 | tf_op jit(solution)/shard_map/ppermute | solution.py:274
  (6 other events, 4.6 us)

commit v8 on v7

--- a/solution.py
+++ b/solution.py
@@ -239,7 +239,7 @@
         in_specs=[smem if one.dtype == jnp.int32 else vmem for one in arrays],
         out_specs=tuple(smem if one[1] == jnp.int32 else vmem for one in out_shape),
         scratch_shapes=[pltpu.VMEM(*one) for one in scratch],
-        compiler_params=pltpu.CompilerParams(vmem_limit_bytes=32 * 1024 * 1024),
+        compiler_params=pltpu.CompilerParams(vmem_limit_bytes=14 * 1024 * 1024),
         cost_estimate=pl.CostEstimate(
             flops=flops, bytes_accessed=flops // 1000, transcendentals=0
         ),

time: 57.6 us -> 57.6 us (level)
  no operation moved by 1% of the time
where the time goes in v8:
time: 57.6 us; the launch traced here: 56.7 us
  starting transfers between devices  21.8 us (38%)
  local copies, waits for them, and re-layouts  11.4 us (20%)
  Pallas kernels  7.83 us (14%)
  waiting for transfers between devices  6.7 us (12%)
  other arithmetic  6.17 us (11%)
  between operations  2.83 us (5%)
    ppermute x6, starting transfers between devices, routed(): return lax.ppermute(value, 'cam', pairs)  11.1 us
    ppermute x6, starting transfers between devices, swap_parts(): results.append(lax.ppermute(part, axis, pairs + [(j, i) for i, j in pairs]))  10.7 us
    unnamed x36, local copies, waits for them, and re-layouts  8.64 us
    pallas_call x3, Pallas kernels, on_device(): pl.pallas_call(kernel, out_shape=tuple((jax.ShapeDtypeStruct(*one) for on...  7.83 us
    ppermute x6, waiting for transfers between devices, routed(): return lax.ppermute(value, 'cam', pairs)  6.68 us
    broadcast_in_dim x1, other arithmetic, local(): return (attended[None], summed.astype(half)[None])  1.69 us
    dynamic_slice x1, local copies, waits for them, and re-layouts, is_near(): return partners[other, side] == lax.rem(other + gap, views)  1.45 us
  transfers between devices with their start and end apart: 12, of which 3 were waited for; matrix products, arithmetic and copies ran while one was open for 10% of the time, Pallas kernels for 7%

profile of v8, /device:TPU:0, one launch (start us, length us, event | category | flops | bytes accessed | tf_op | source)
XLA Modules:
  0.0 56.7 jit_solution(15694938135004576529)
XLA Ops:
  0.7 3.0 %collective-permute-start.1 = (bf16[4,128,128]{2,1,0:T(8,128)(2,1)}, bf16[4,128,128]{2,1,0:T(8,128)(2,1)S(1)}, u32[]{:S(2)}, u32[]{:S(2)}) collective-permute-start(bf16[4,128,128]{2,1,0:T(8,128)(2,1)} %bitcast.26), channel_id=1, source_target_pairs={{0,4},{4,0},{8,12},{12,8},{16,20},{20,16},{24,28},{28,24},{1,5},{5... | collective-permute-start | bytes 393224 | tf_op jit(solution)/shard_map/ppermute | solution.py:274
  3.7 3.6 %collective-permute-start = (bf16[4,128,128]{2,1,0:T(8,128)(2,1)}, bf16[4,128,128]{2,1,0:T(8,128)(2,1)S(1)}, u32[]{:S(2)}, u32[]{:S(2)}) collective-permute-start(bf16[4,128,128]{2,1,0:T(8,128)(2,1)} %bitcast.27), channel_id=1, source_target_pairs={{0,24},{4,12},{8,0},{12,20},{16,8},{20,28},{24,16},{28,4},{1,25},{... | collective-permute-start | bytes 393224 | tf_op jit(solution)/shard_map/ppermute | solution.py:274
  7.3 1.4 %fusion.7 = (s32[1,1]{0,1:T(1,128)}, s32[1,1]{0,1:T(1,128)}, s32[1,1]{0,1:T(1,128)}) fusion(s32[8,2]{0,1:T(2,128)} %param.14, s32[]{:T(128)S(6)} %select_n.160, s32[]{:T(128)S(6)} %select_n.132, s32[]{:T(128)S(6)} %select_n.131, s32[]{:T(128)S(6)} %select_n.136, s32[]{:T(128)S(6)} %select_n.137), kind=kLoop, calls=%fused_computation.32 | loop fusion | bytes 44 | tf_op jit(solution)/shard_map/dynamic_slice | solution.py:286
  10.0 0.8 %slice_bitcast_fusion.3 = (bf16[1,128,128]{2,1,0:T(8,128)(2,1)S(1)}, bf16[1,128,128]{2,1,0:T(8,128)(2,1)S(1)}) fusion(bf16[1,4,128,128]{3,2,1,0:T(8,128)(2,1)} %param.9), kind=kLoop, calls=%fused_computation.24 | loop fusion | bytes 131072 | tf_op jit(solution)/shard_map/slice | solution.py:297
  10.8 0.9 %broadcast_select_fusion.2 = bf16[4,128,128]{2,1,0:T(8,128)(2,1)S(1)} fusion(bf16[4,128,128]{2,1,0:T(8,128)(2,1)S(1)} %collective-permute-done.1, pred[]{:T(512)S(6)} %eq.27, bf16[1,4,128,128]{3,2,1,0:T(8,128)(2,1)} %param.9), kind=kLoop, calls=%fused_computation.15 | loop fusion | flops 65536 | bytes 393217 | tf_op jit(solution)/shard_map/jit(_where)/select_n | solution.py:293
  14.6 2.9 %collective-permute-start.2 = (bf16[4,128,128]{2,1,0:T(8,128)(2,1)S(1)}, bf16[4,128,128]{2,1,0:T(8,128)(2,1)S(1)}, u32[]{:S(2)}, u32[]{:S(2)}) collective-permute-start(bf16[4,128,128]{2,1,0:T(8,128)(2,1)S(1)} %get-tuple-element.40), channel_id=1, source_target_pairs={{0,1},{2,3},{1,0},{3,2},{4,5},{6,7},{5,4},{7,6},{8,9},{10,11},{9,8... | collective-permute-start | bytes 393224 | tf_op jit(solution)/shard_map/ppermute | solution.py:18
  17.5 1.0 %collective-permute-done.4.slab = bf16[4,128,128]{2,1,0:T(8,128)(2,1)S(1)} collective-permute-done((bf16[4,128,128]{2,1,0:T(8,128)(2,1)S(1)}, bf16[4,128,128]{2,1,0:T(8,128)(2,1)S(1)}, u32[]{:S(2)}, u32[]{:S(2)}) %collective-permute-start.4) | collective-permute-done | bytes 131104 | tf_op jit(solution)/shard_map/ppermute | solution.py:274
  19.2 2.9 %collective-permute-start.5 = (bf16[3,128,128]{2,1,0:T(8,128)(2,1)S(1)}, bf16[3,128,128]{2,1,0:T(8,128)(2,1)S(1)}, u32[]{:S(2)}, u32[]{:S(2)}) collective-permute-start(bf16[3,128,128]{2,1,0:T(8,128)(2,1)S(1)} %get-tuple-element.43), channel_id=1, source_target_pairs={{0,1},{2,3},{1,0},{3,2},{4,5},{6,7},{5,4},{7,6},{8,9},{10,11},{9,8... | collective-permute-start | bytes 294920 | tf_op jit(solution)/shard_map/ppermute | solution.py:18
  22.3 2.2 %shard_map.104 = (bf16[4,256,256]{2,1,0:T(8,128)(2,1)S(1)}, bf16[8,256,128]{2,1,0:T(8,128)(2,1)S(1)}, f32[4,384,128]{2,1,0:T(8,128)S(1)}, f32[4,384,128]{2,1,0:T(8,128)S(1)}) custom-call(s32[31]{0:T(128)S(1)} %pad_add_fusion.scalars, bf16[4,128,128]{2,1,0:T(8,128)(2,1)S(1)} %bitcast.28, bf16[4,128,128]{2,1,0:T(8,128)(2,1)S(1)} %broadcast_select_fusion.3.slab, ...), custom_call_target="tpu_custom_call" | custom-call | flops 1000000 | bytes 1000 | tf_op jit(solution)/shard_map/pallas_call | solution.py:236
  24.6 1.0 %copy-done.7 = bf16[3,3,128,128]{3,2,1,0:T(8,128)(2,1)S(1)} copy-done((bf16[3,3,128,128]{3,2,1,0:T(8,128)(2,1)S(1)}, bf16[3,3,128,128]{3,2,1,0:T(8,128)(2,1)}, u32[]{:S(2)}) %copy-start.7) | copy-done | bytes 294936
  25.5 0.8 %copy-done.12 = bf16[128,128]{1,0:T(8,128)(2,1)S(1)} copy-done((bf16[128,128]{1,0:T(8,128)(2,1)S(1)}, bf16[128,128]{1,0:T(8,128)(2,1)}, u32[]{:S(2)}) %copy-start.12) | copy-done | bytes 32792
  27.0 3.7 %shard_map.105 = (bf16[4,128,128]{2,1,0:T(8,128)(2,1)S(1)}, bf16[4,128,128]{2,1,0:T(8,128)(2,1)S(1)}, f32[2,8,128,256]{3,2,1,0:T(8,128)S(1)}, bf16[4,768,128]{2,...) custom-call(s32[31]{0:T(128)S(1)} %pad_add_fusion.scalars, ...), custom_call_target="tpu_custom_call" | custom-call | flops 1500000000 | bytes 1500000 | tf_op jit(solution)/shard_map/pallas_call | solution.py:236
  30.7 0.9 %copy-done.2 = bf16[4,768,128]{2,1,0:T(8,128)(2,1)} copy-done((bf16[4,768,128]{2,1,0:T(8,128)(2,1)}, bf16[4,768,128]{2,1,0:T(8,128)(2,1)S(1)}, u32[]{:S(2)}) %copy-start.2) | copy-done | bytes 786456
  31.6 0.8 %copy-done.4 = bf16[8,256,128]{2,1,0:T(8,128)(2,1)} copy-done((bf16[8,256,128]{2,1,0:T(8,128)(2,1)}, bf16[8,256,128]{2,1,0:T(8,128)(2,1)S(1)}, u32[]{:S(2)}) %copy-start.4) | copy-done | bytes 524312
  33.8 2.9 %collective-permute-start.8 = (bf16[4,128,128]{2,1,0:T(8,128)(2,1)}, bf16[4,128,128]{2,1,0:T(8,128)(2,1)}, u32[]{:S(2)}, u32[]{:S(2)}) collective-permute-start(bf16[4,128,128]{2,1,0:T(8,128)(2,1)} %get-tuple-element.39), channel_id=1, source_target_pairs={{0,1},{2,3},{1,0},{3,2},{4,5},{6,7},{5,4},{7,6},{8,9},{10,11},{9,8... | collective-permute-start | bytes 393224 | tf_op jit(solution)/shard_map/ppermute | solution.py:18
  36.7 1.1 %copy-done.3 = bf16[4,768,128]{2,1,0:T(8,128)(2,1)S(1)} copy-done((bf16[4,768,128]{2,1,0:T(8,128)(2,1)S(1)}, bf16[4,768,128]{2,1,0:T(8,128)(2,1)}, u32[]{:S(2)}) %copy-start.3) | copy-done | bytes 786456
  37.8 1.0 %copy-done.5 = bf16[8,256,128]{2,1,0:T(8,128)(2,1)S(1)} copy-done((bf16[8,256,128]{2,1,0:T(8,128)(2,1)S(1)}, bf16[8,256,128]{2,1,0:T(8,128)(2,1)}, u32[]{:S(2)}) %copy-start.5) | copy-done | bytes 524312
  41.1 2.0 %shard_map.106 = (bf16[4,128,128]{2,1,0:T(8,128)(2,1)}, f32[2,4,128,128]{3,2,1,0:T(8,128)S(1)}, f32[4,128,128]{2,1,0:T(8,128)S(1)}) custom-call(s32[31]{0:T(128)S(1)} %pad_add_fusion.scalars, f32[2,8,128,256]{3,2,1,0:T(8,128)S(1)} %get-tuple-element.24.acc, bf16[4,768,128]{2,1,0:T(8,128)(2,1)S(1)} %get-tuple-element.25.probs, ...), custom_call_target="tpu_custom_call" | custom-call | flops 1000000 | bytes 1000 | tf_op jit(solution)/shard_map/pallas_call | solution.py:236
  43.1 1.0 %broadcast_select_fusion.1 = (bf16[4,128,128]{2,1,0:T(8,128)(2,1)S(1)}, bf16[4,128,128]{2,1,0:T(8,128)(2,1)S(1)}) fusion(bf16[4,128,128]{2,1,0:T(8,128)(2,1)S(1)} %collective-permute-done.7, bf16[4,128,128]{2,1,0:T(8,128)(2,1)} %collective-permute-done.8, pred[]{:T(512)S(6)} %not.7), kind=kLoop, calls=%fused_computation.14 | loop fusion | flops 131072 | bytes 524289 | tf_op jit(solution)/shard_map/jit(_where)/select_n | solution.py:27
  44.2 1.4 %collective-permute-start.9 = (bf16[4,128,128]{2,1,0:T(8,128)(2,1)S(1)}, bf16[4,128,128]{2,1,0:T(8,128)(2,1)S(1)}, u32[]{:S(2)}, u32[]{:S(2)}) collective-permute-start(bf16[4,128,128]{2,1,0:T(8,128)(2,1)S(1)} %get-tuple-element.34), channel_id=1, source_target_pairs={{0,24},{4,12},{8,0},{12,20},{16,8},{20,28},{24,16},{28,4},{1,25},{... | collective-permute-start | bytes 393224 | tf_op jit(solution)/shard_map/ppermute | solution.py:274
  46.3 3.4 %collective-permute-done.9 = bf16[4,128,128]{2,1,0:T(8,128)(2,1)S(1)} collective-permute-done((bf16[4,128,128]{2,1,0:T(8,128)(2,1)S(1)}, bf16[4,128,128]{2,1,0:T(8,128)(2,1)S(1)}, u32[]{:S(2)}, u32[]{:S(2)}) %collective-permute-start.9) | collective-permute-done | bytes 131104 | tf_op jit(solution)/shard_map/ppermute | solution.py:274
  49.7 2.4 %collective-permute-start.10 = (bf16[4,128,128]{2,1,0:T(8,128)(2,1)S(1)}, bf16[4,128,128]{2,1,0:T(8,128)(2,1)S(1)}, u32[]{:S(2)}, u32[]{:S(2)}) collective-permute-start(bf16[4,128,128]{2,1,0:T(8,128)(2,1)S(1)} %fusion.1), channel_id=1, source_target_pairs={{0,4},{4,0},{8,12},{12,8},{16,20},{20,16},{24,28},{28,24},{1,5},{5... | collective-permute-start | bytes 393224 | tf_op jit(solution)/shard_map/ppermute | solution.py:274
  52.8 2.3 %collective-permute-done.10 = bf16[4,128,128]{2,1,0:T(8,128)(2,1)S(1)} collective-permute-done((bf16[4,128,128]{2,1,0:T(8,128)(2,1)S(1)}, bf16[4,128,128]{2,1,0:T(8,128)(2,1)S(1)}, u32[]{:S(2)}, u32[]{:S(2)}) %collective-permute-start.10) | collective-permute-done | bytes 131104 | tf_op jit(solution)/shard_map/ppermute | solution.py:274
  55.1 1.7 %fusion.5 = bf16[1,4,128,128]{3,2,1,0:T(8,128)(2,1)} fusion(bf16[4,128,128]{2,1,0:T(8,128)(2,1)S(1)} %collective-permute-done.11, bf16[4,128,128]{2,1,0:T(8,128)(2,1)S(1)} %collective-permute-done.9, f32[4,128,128]{2,1,0:T(8,128)} %copy-done.8, bf16[4,128,128]{2,1,0:T(8,128)(2,1)S(1)} %collective-permute-done.10, pred[]{:T(512)S(6)} %eq.28, pred[]{:T(512)S(6)} %eq.27), kind=kLoop, calls=%fused_computation.8 | loop fusion | flops 589824 | bytes 786434 | tf_op jit(solution)/shard_map/broadcast_in_dim | solution.py:407
  (63 shorter events, 8.9 us)
Async XLA Ops:
  0.6 11.9 %copy-start = (s32[8,2]{0,1:T(2,128)S(1)}, s32[8,2]{0,1:T(2,128)}, u32[]{:S(2)}) copy-start(s32[8,2]{0,1:T(2,128)} %param.15) | copy-start | bytes 196
  0.6 21.6 %copy-start.1 = (bf16[1,4,128,128]{3,2,1,0:T(8,128)(2,1)S(1)}, bf16[1,4,128,128]{3,2,1,0:T(8,128)(2,1)}, u32[]{:S(2)}) copy-start(bf16[1,4,128,128]{3,2,1,0:T(8,128)(2,1)} %param.9) | copy-start | bytes 393220
  0.7 21.6 %copy-start.14 = (bf16[128,128]{1,0:T(8,128)(2,1)S(1)}, bf16[128,128]{1,0:T(8,128)(2,1)}, u32[]{:S(2)}) copy-start(bf16[128,128]{1,0:T(8,128)(2,1)} %v_weight.5) | copy-start | bytes 98308
  0.7 21.6 %copy-start.11 = (bf16[128,128]{1,0:T(8,128)(2,1)S(1)}, bf16[128,128]{1,0:T(8,128)(2,1)}, u32[]{:S(2)}) copy-start(bf16[128,128]{1,0:T(8,128)(2,1)} %k_weight.5) | copy-start | bytes 98308
  0.7 21.6 %copy-start.9 = (bf16[128,128]{1,0:T(8,128)(2,1)S(1)}, bf16[128,128]{1,0:T(8,128)(2,1)}, u32[]{:S(2)}) copy-start(bf16[128,128]{1,0:T(8,128)(2,1)} %q_weight.3) | copy-start | bytes 98308
  0.7 21.6 %copy-start.6 = (bf16[3,3,128,128]{3,2,1,0:T(8,128)(2,1)S(1)}, bf16[3,3,128,128]{3,2,1,0:T(8,128)(2,1)}, u32[]{:S(2)}) copy-start(bf16[3,3,128,128]{3,2,1,0:T(8,128)(2,1)} %conv_weight.3) | copy-start | bytes 884740
  0.7 21.6 %copy-start.17 = (bf16[1,4,128,128]{3,2,1,0:T(8,128)(2,1)S(1)}, bf16[1,4,128,128]{3,2,1,0:T(8,128)(2,1)}, u32[]{:S(2)}) copy-start(bf16[1,4,128,128]{3,2,1,0:T(8,128)(2,1)} %param.17) | copy-start | bytes 393220
  0.7 10.1 %collective-permute-start.1 = (bf16[4,128,128]{2,1,0:T(8,128)(2,1)}, bf16[4,128,128]{2,1,0:T(8,128)(2,1)S(1)}, u32[]{:S(2)}, u32[]{:S(2)}) collective-permute-start(bf16[4,128,128]{2,1,0:T(8,128)(2,1)} %bitcast.26), channel_id=1, source_target_pairs={{0,4},{4,0},{8,12},{12,8},{16,20},{20,16},{24,28},{28,24},{1,5},{5... | collective-permute-start | bytes 393224 | tf_op jit(solution)/shard_map/ppermute | solution.py:274
  3.7 8.1 %collective-permute-start = (bf16[4,128,128]{2,1,0:T(8,128)(2,1)}, bf16[4,128,128]{2,1,0:T(8,128)(2,1)S(1)}, u32[]{:S(2)}, u32[]{:S(2)}) collective-permute-start(bf16[4,128,128]{2,1,0:T(8,128)(2,1)} %bitcast.27), channel_id=1, source_target_pairs={{0,24},{4,12},{8,0},{12,20},{16,8},{20,28},{24,16},{28,4},{1,25},{... | collective-permute-start | bytes 393224 | tf_op jit(solution)/shard_map/ppermute | solution.py:274
  11.7 6.8 %collective-permute-start.4 = (bf16[4,128,128]{2,1,0:T(8,128)(2,1)S(1)}, bf16[4,128,128]{2,1,0:T(8,128)(2,1)S(1)}, u32[]{:S(2)}, u32[]{:S(2)}) collective-permute-start(bf16[4,128,128]{2,1,0:T(8,128)(2,1)S(1)} %broadcast_select_fusion.2), channel_id=1, source_target_pairs={{0,8},{4,28},{8,16},{12,4},{16,24},{20,12},{24,0},{28,20},{1,9},{5... | collective-permute-start | bytes 393224 | tf_op jit(solution)/shard_map/ppermute | solution.py:274
  11.9 10.4 %collective-permute-start.3 = (bf16[4,128,128]{2,1,0:T(8,128)(2,1)S(1)}, bf16[4,128,128]{2,1,0:T(8,128)(2,1)S(1)}, u32[]{:S(2)}, u32[]{:S(2)}) collective-permute-start(bf16[4,128,128]{2,1,0:T(8,128)(2,1)S(1)} %get-tuple-element.41), channel_id=1, source_target_pairs={{1,2},{2,1},{5,6},{6,5},{9,10},{10,9},{13,14},{14,13},{17,18},{18,... | collective-permute-start | bytes 393224 | tf_op jit(solution)/shard_map/ppermute | solution.py:18
  14.6 7.6 %collective-permute-start.2 = (bf16[4,128,128]{2,1,0:T(8,128)(2,1)S(1)}, bf16[4,128,128]{2,1,0:T(8,128)(2,1)S(1)}, u32[]{:S(2)}, u32[]{:S(2)}) collective-permute-start(bf16[4,128,128]{2,1,0:T(8,128)(2,1)S(1)} %get-tuple-element.40), channel_id=1, source_target_pairs={{0,1},{2,3},{1,0},{3,2},{4,5},{6,7},{5,4},{7,6},{8,9},{10,11},{9,8... | collective-permute-start | bytes 393224 | tf_op jit(solution)/shard_map/ppermute | solution.py:18
  18.6 6.0 %collective-permute-start.6 = (bf16[3,128,128]{2,1,0:T(8,128)(2,1)S(1)}, bf16[3,128,128]{2,1,0:T(8,128)(2,1)S(1)}, u32[]{:S(2)}, u32[]{:S(2)}) collective-permute-start(bf16[3,128,128]{2,1,0:T(8,128)(2,1)S(1)} %get-tuple-element.42), channel_id=1, source_target_pairs={{1,2},{2,1},{5,6},{6,5},{9,10},{10,9},{13,14},{14,13},{17,18},{18,... | collective-permute-start | bytes 294920 | tf_op jit(solution)/shard_map/ppermute | solution.py:18
  19.2 5.3 %collective-permute-start.5 = (bf16[3,128,128]{2,1,0:T(8,128)(2,1)S(1)}, bf16[3,128,128]{2,1,0:T(8,128)(2,1)S(1)}, u32[]{:S(2)}, u32[]{:S(2)}) collective-permute-start(bf16[3,128,128]{2,1,0:T(8,128)(2,1)S(1)} %get-tuple-element.43), channel_id=1, source_target_pairs={{0,1},{2,3},{1,0},{3,2},{4,5},{6,7},{5,4},{7,6},{8,9},{10,11},{9,8... | collective-permute-start | bytes 294920 | tf_op jit(solution)/shard_map/ppermute | solution.py:18
  24.6 1.0 %copy-start.7 = (bf16[3,3,128,128]{3,2,1,0:T(8,128)(2,1)S(1)}, bf16[3,3,128,128]{3,2,1,0:T(8,128)(2,1)}, u32[]{:S(2)}) copy-start(bf16[3,3,128,128]{3,2,1,0:T(8,128)(2,1)} %conv_weight.3) | copy-start | bytes 884740
  30.7 0.9 %copy-start.2 = (bf16[4,768,128]{2,1,0:T(8,128)(2,1)}, bf16[4,768,128]{2,1,0:T(8,128)(2,1)S(1)}, u32[]{:S(2)}) copy-start(bf16[4,768,128]{2,1,0:T(8,128)(2,1)S(1)} %get-tuple-element.26.grad_scores) | copy-start | bytes 2359300
  33.1 10.0 %collective-permute-start.7 = (bf16[4,128,128]{2,1,0:T(8,128)(2,1)}, bf16[4,128,128]{2,1,0:T(8,128)(2,1)S(1)}, u32[]{:S(2)}, u32[]{:S(2)}) collective-permute-start(bf16[4,128,128]{2,1,0:T(8,128)(2,1)} %get-tuple-element.38), channel_id=1, source_target_pairs={{1,2},{2,1},{5,6},{6,5},{9,10},{10,9},{13,14},{14,13},{17,18},{18,... | collective-permute-start | bytes 393224 | tf_op jit(solution)/shard_map/ppermute | solution.py:18
  33.8 9.3 %collective-permute-start.8 = (bf16[4,128,128]{2,1,0:T(8,128)(2,1)}, bf16[4,128,128]{2,1,0:T(8,128)(2,1)}, u32[]{:S(2)}, u32[]{:S(2)}) collective-permute-start(bf16[4,128,128]{2,1,0:T(8,128)(2,1)} %get-tuple-element.39), channel_id=1, source_target_pairs={{0,1},{2,3},{1,0},{3,2},{4,5},{6,7},{5,4},{7,6},{8,9},{10,11},{9,8... | collective-permute-start | bytes 393224 | tf_op jit(solution)/shard_map/ppermute | solution.py:18
  36.7 1.1 %copy-start.3 = (bf16[4,768,128]{2,1,0:T(8,128)(2,1)S(1)}, bf16[4,768,128]{2,1,0:T(8,128)(2,1)}, u32[]{:S(2)}) copy-start(bf16[4,768,128]{2,1,0:T(8,128)(2,1)} %copy-done.2) | copy-start | bytes 2359300
  37.8 1.0 %copy-start.5 = (bf16[8,256,128]{2,1,0:T(8,128)(2,1)S(1)}, bf16[8,256,128]{2,1,0:T(8,128)(2,1)}, u32[]{:S(2)}) copy-start(bf16[8,256,128]{2,1,0:T(8,128)(2,1)} %copy-done.4) | copy-start | bytes 1572868
  43.1 1.1 %copy-start.8 = (f32[4,128,128]{2,1,0:T(8,128)}, f32[4,128,128]{2,1,0:T(8,128)S(1)}, u32[]{:S(2)}) copy-start(f32[4,128,128]{2,1,0:T(8,128)S(1)} %get-tuple-element.30) | copy-start | bytes 786436
  44.2 5.5 %collective-permute-start.9 = (bf16[4,128,128]{2,1,0:T(8,128)(2,1)S(1)}, bf16[4,128,128]{2,1,0:T(8,128)(2,1)S(1)}, u32[]{:S(2)}, u32[]{:S(2)}) collective-permute-start(bf16[4,128,128]{2,1,0:T(8,128)(2,1)S(1)} %get-tuple-element.34), channel_id=1, source_target_pairs={{0,24},{4,12},{8,0},{12,20},{16,8},{20,28},{24,16},{28,4},{1,25},{... | collective-permute-start | bytes 393224 | tf_op jit(solution)/shard_map/ppermute | solution.py:274
  45.6 7.2 %collective-permute-start.11 = (bf16[4,128,128]{2,1,0:T(8,128)(2,1)S(1)}, bf16[4,128,128]{2,1,0:T(8,128)(2,1)S(1)}, u32[]{:S(2)}, u32[]{:S(2)}) collective-permute-start(bf16[4,128,128]{2,1,0:T(8,128)(2,1)S(1)} %get-tuple-element.35), channel_id=1, source_target_pairs={{0,8},{4,28},{8,16},{12,4},{16,24},{20,12},{24,0},{28,20},{1,9},{5... | collective-permute-start | bytes 393224 | tf_op jit(solution)/shard_map/ppermute | solution.py:274
  49.7 5.3 %collective-permute-start.10 = (bf16[4,128,128]{2,1,0:T(8,128)(2,1)S(1)}, bf16[4,128,128]{2,1,0:T(8,128)(2,1)S(1)}, u32[]{:S(2)}, u32[]{:S(2)}) collective-permute-start(bf16[4,128,128]{2,1,0:T(8,128)(2,1)S(1)} %fusion.1), channel_id=1, source_target_pairs={{0,4},{4,0},{8,12},{12,8},{16,20},{20,16},{24,28},{28,24},{1,5},{5... | collective-permute-start | bytes 393224 | tf_op jit(solution)/shard_map/ppermute | solution.py:274
  (6 other events, 4.6 us)

commit v9 on v8

--- a/solution.py
+++ b/solution.py
@@ -95,6 +95,13 @@
     return expo, both[:, width:]
 
 
+def squared(queries_b, cotangent_b, square):
+    width, channels = queries_b.shape
+    square[...] = jnp.zeros_like(square)
+    square[:width, :channels] = queries_b
+    square[width:, channels:] = cotangent_b
+
+
 def first_kernel(
     scalars,
     own,
@@ -106,68 +113,72 @@
     k_weight,
     v_weight,
     cotangent,
-    pair,
+    queries,
     kv_t,
     expo,
     grad_probs,
+    taps,
+    wkv,
     image,
     work,
     kv,
+    square,
 ):
     rows, width, channels = own.shape
     halo = MARGIN + 1
-    taps = stacked_taps(conv_weight)
-    wkv = jnp.concatenate([k_weight[...], v_weight[...]], axis=1)
-
     odd = scalars[0] == 1
+    taps[...] = stacked_taps(conv_weight)
+    wkv[...] = jnp.concatenate([k_weight[...], v_weight[...]], axis=1)
+
     above, below = margins_of(odd, between[halo], within[halo])
     image[0:width, :] = above
     image[width : (rows + 1) * width, :] = own[...].reshape(rows * width, channels)
     image[(rows + 1) * width : (rows + 2) * width, :] = below
-    hidden = conv_rows(image, work, rows, width, taps)
-    queries = dot_nn(hidden, q_weight[...]).astype(jnp.bfloat16)
-    pair[...] = jnp.zeros_like(pair)
+    hidden = conv_rows(image, work, rows, width, taps[...])
+    queries[...] = (
+        dot_nn(hidden, q_weight[...]).astype(jnp.bfloat16).reshape(rows, width, channels)
+    )
+
+    side_keys(slab[...], odd, between, within, image, work, taps[...], wkv[...], kv, kv_t)
     for b in range(rows):
-        pair[b, 0:width, 0:channels] = queries[b * width : (b + 1) * width, :]
-        pair[b, width : 2 * width, channels : 2 * channels] = cotangent[b]
-
-    side_keys(slab[...], odd, between, within, image, work, taps, wkv, kv, kv_t)
-    for b in range(rows):
+        squared(queries[b], cotangent[b], square.at[b])
         expo[b], grad_probs[b] = side_scores(
-            places_of(scalars, rows, b, 1), kv, pair[b], width, channels
+            places_of(scalars, rows, b, 1), kv, square[b], width, channels
         )
 
 
 def second_kernel(
     scalars,
-    pair,
+    queries,
+    cotangent,
     slab,
     within,
     between,
-    conv_weight,
-    k_weight,
-    v_weight,
+    taps,
+    wkv,
     first_expo,
     first_grad_probs,
-    top,
-    bottom,
-    acc,
+    for_within,
+    for_between,
+    middle,
     probs_out,
     grad_scores_out,
     kv_t,
     image,
     work,
     kv,
+    square,
+    acc,
 ):
     rows, width, channels = slab.shape
-    taps = stacked_taps(conv_weight)
-    wkv = jnp.concatenate([k_weight[...], v_weight[...]], axis=1)
+    odd = scalars[0] == 1
     acc[...] = jnp.zeros_like(acc)
-    side_keys(slab[...], scalars[0] == 1, between, within, image, work, taps, wkv, kv, kv_t)
+    side_keys(slab[...], odd, between, within, image, work, taps[...], wkv[...], kv, kv_t)
 
     for b in range(rows):
+        squared(queries[b], cotangent[b], square.at[b])
         places = [places_of(scalars, rows, b, side) for side in range(2)]
-        expo, grad_probs = side_scores(places[0], kv, pair[b], width, channels)
+        expo, grad_probs = side_scores(places[0], kv, square[b], width, channels)
         expo = jnp.concatenate([expo, first_expo[b]], axis=0)
         grad_probs = jnp.concatenate([grad_probs, first_grad_probs[b]], axis=0)
         probs = expo * (1.0 / jnp.sum(expo, axis=0, keepdims=True))
@@ -176,7 +187,7 @@
         grad_scores = (probs * (grad_probs - delta)).astype(jnp.bfloat16)
         probs_out[b] = probs_bf
         grad_scores_out[b] = grad_scores
-        terms = dot_nn(jnp.concatenate([grad_scores, probs_bf], axis=1), pair[b])
+        terms = dot_nn(jnp.concatenate([grad_scores, probs_bf], axis=1), square[b])
         for side in range(2):
             for s, (at, _) in enumerate(places[side]):
                 i = side * BAND + s
@@ -184,38 +195,41 @@
 
     for side in range(2):
         span = slice(side * MARGIN, (side + 1) * MARGIN)
-        top[span] = back_projected(acc[side, :MARGIN], wkv).astype(jnp.bfloat16)
-        bottom[span] = back_projected(acc[side, MARGIN + rows :], wkv).astype(jnp.bfloat16)
+        top = back_projected(scaled(acc[side, :MARGIN]), wkv[...])
+        bottom = back_projected(scaled(acc[side, MARGIN + rows :]), wkv[...])
+        for_within[span] = jnp.where(odd, top, bottom).astype(jnp.bfloat16)
+        for_between[span] = jnp.where(odd, bottom, top).astype(jnp.bfloat16)
+        middle[side] = scaled(acc[side, MARGIN : MARGIN + rows])
+
+
+def scaled(grads):
+    channels = grads.shape[2] // 2
+    return jnp.concatenate(
+        [grads[:, :, :channels] * channels**-0.5, grads[:, :, channels:]], axis=2
+    ).astype(jnp.bfloat16)
 
 
 def back_projected(grads, wkv):
     rows, width, both = grads.shape
-    channels = both // 2
-    grads = grads.reshape(rows * width, both)
-    grads = jnp.concatenate(
-        [grads[:, :channels] * channels**-0.5, grads[:, channels:]], axis=1
-    )
-    return dot_nt(grads.astype(jnp.bfloat16), wkv).reshape(rows, width, channels)
+    return dot_nt(grads.reshape(rows * width, both), wkv).reshape(rows, width, both // 2)
 
 
 def third_kernel(
     scalars,
-    acc,
+    middle,
     probs,
     grad_scores,
     kv_t,
     first_kv_t,
     q_weight,
-    k_weight,
-    v_weight,
+    wkv,
     attended,
     center,
     grad_own,
 ):
     rows, width, channels = attended.shape
-    wkv = jnp.concatenate([k_weight[...], v_weight[...]], axis=1)
     for side in range(2):
-        center[side] = back_projected(acc[side, MARGIN : MARGIN + rows], wkv)
+        center[side] = back_projected(middle[side], wkv[...])
     grad_q = []
     for b in range(rows):
         places = [places_of(scalars, rows, b, side) for side in range(2)]
@@ -317,14 +331,17 @@
         (((win + 2) * width, channels), half),
         ((win * width + 16, 3 * channels), full),
         ((win, width, 2 * channels), half),
+        ((rows, 2 * width, 2 * channels), half),
     ]
-    pair, first_kv_t, first_expo, first_grad_probs = on_device(
+    queries, first_kv_t, first_expo, first_grad_probs, taps, wkv = on_device(
         first_kernel,
         [
-            ((rows, 2 * width, 2 * channels), half),
+            (image.shape, half),
             ((win, 2 * channels, width), half),
             ((rows, BAND * width, width), full),
             ((rows, BAND * width, width), full),
+            ((3 * channels, 3 * channels), half),
+            ((channels, 2 * channels), half),
         ],
         conv_scratch,
         1_000_000,
@@ -344,30 +361,30 @@
     )
     margins = ((2 * MARGIN, width, channels), half)
     weights = ((rows, 2 * BAND * width, width), half)
-    top, bottom, acc, probs, grad_scores, kv_t = on_device(
+    for_within, for_between, middle, probs, grad_scores, kv_t = on_device(
         second_kernel,
         [
             margins,
             margins,
-            ((2, win, width, 2 * channels), full),
+            ((2, rows, width, 2 * channels), half),
             weights,
             weights,
             ((win, 2 * channels, width), half),
         ],
-        conv_scratch,
+        conv_scratch + [((2, win, width, 2 * channels), full)],
         1_500_000_000,
         scalars,
-        pair,
+        queries,
+        grad_attended[0],
         second_slab,
         within,
         between,
-        conv_weight,
-        k_weight,
-        v_weight,
+        taps,
+        wkv,
         first_expo,
         first_grad_probs,
     )
-    between, within = swap_parts(*parity_split(bottom, top, odd_row), "row")
+    between, within = swap_parts(for_between, for_within, "row")
     attended, center, grad_own = on_device(
         third_kernel,
         [
@@ -378,14 +395,13 @@
         [],
         1_000_000,
         scalars,
-        acc,
+        middle,
         probs,
         grad_scores,
         kv_t,
         first_kv_t,
         q_weight,
-        k_weight,
-        v_weight,
+        wkv,
     )
     from_above, from_below = (
         part.reshape(2, MARGIN, width, channels).astype(full)

time: 57.6 us -> 47.5 us (0.82)
  the two profiles are of different devices: /device:TPU:0 before, /device:TPU:1 now
where the time goes in v9:
time: 47.5 us; the launch traced here: 47.2 us
  starting transfers between devices  21 us (44%)
  waiting for transfers between devices  10.4 us (22%)
  Pallas kernels  8.72 us (18%)
  between operations  2.91 us (6%)
  other arithmetic  2.16 us (5%)
  local copies, waits for them, and re-layouts  1.96 us (4%)
    ppermute x6, starting transfers between devices, swap_parts(): results.append(lax.ppermute(part, axis, pairs + [(j, i) for i, j in pairs]))  13.6 us
    ppermute x6, waiting for transfers between devices, routed(): return lax.ppermute(value, 'cam', pairs)  9.28 us
    pallas_call x3, Pallas kernels, on_device(): pl.pallas_call(kernel, out_shape=tuple((jax.ShapeDtypeStruct(*one) for on...  8.72 us
    ppermute x6, starting transfers between devices, routed(): return lax.ppermute(value, 'cam', pairs)  7.43 us
    ppermute x6, waiting for transfers between devices, swap_parts(): results.append(lax.ppermute(part, axis, pairs + [(j, i) for i, j in pairs]))  1.15 us
    select_n x1, other arithmetic, margins_of(): return (jnp.where(odd, within, between), jnp.where(odd, between, within))  0.99 us
  transfers between devices with their start and end apart: 12, of which 4 were waited for; matrix products, arithmetic and copies ran while one was open for 3% of the time, Pallas kernels for 9%

profile of v9, /device:TPU:1, one launch (start us, length us, event | category | flops | bytes accessed | tf_op | source)
XLA Modules:
  0.0 47.2 jit_solution(11730739060980776889)
XLA Ops:
  0.7 2.1 %collective-permute-start.1 = (bf16[4,128,128]{2,1,0:T(8,128)(2,1)}, bf16[4,128,128]{2,1,0:T(8,128)(2,1)S(1)}, u32[]{:S(2)}, u32[]{:S(2)}) collective-permute-start(bf16[4,128,128]{2,1,0:T(8,128)(2,1)} %bitcast.26), channel_id=1, source_target_pairs={{0,4},{4,0},{8,12},{12,8},{16,20},{20,16},{24,28},{28,24},{1,5},{5... | collective-permute-start | bytes 393224 | tf_op jit(solution)/shard_map/ppermute | solution.py:288
  2.8 3.3 %collective-permute-start = (bf16[4,128,128]{2,1,0:T(8,128)(2,1)}, bf16[4,128,128]{2,1,0:T(8,128)(2,1)S(1)}, u32[]{:S(2)}, u32[]{:S(2)}) collective-permute-start(bf16[4,128,128]{2,1,0:T(8,128)(2,1)} %bitcast.27), channel_id=1, source_target_pairs={{0,24},{4,12},{8,0},{12,20},{16,8},{20,28},{24,16},{28,4},{1,25},{... | collective-permute-start | bytes 393224 | tf_op jit(solution)/shard_map/ppermute | solution.py:288
  6.1 0.7 %copy-done.8 = s32[8,2]{0,1:T(2,128)S(1)} copy-done((s32[8,2]{0,1:T(2,128)S(1)}, s32[8,2]{0,1:T(2,128)}, u32[]{:S(2)}) %copy-start.8) | copy-done | bytes 88
  6.8 0.7 %fusion.7 = (s32[1,1]{0,1:T(1,128)}, s32[1,1]{0,1:T(1,128)}, s32[1,1]{0,1:T(1,128)}) fusion(s32[8,2]{0,1:T(2,128)S(1)} %copy-done.8, s32[]{:T(128)S(6)} %select_n.150, s32[]{:T(128)S(6)} %select_n.124, s32[]{:T(128)S(6)} %select_n.123, s32[]{:T(128)S(6)} %select_n.128, s32[]{:T(128)S(6)} %select_n.129), kind=kLoop, calls=%fused_computation.30 | loop fusion | bytes 44 | tf_op jit(solution)/shard_map/dynamic_slice | solution.py:300
  9.0 4.6 %collective-permute-start.3 = (bf16[4,128,128]{2,1,0:T(8,128)(2,1)S(1)}, bf16[4,128,128]{2,1,0:T(8,128)(2,1)S(1)}, u32[]{:S(2)}, u32[]{:S(2)}) collective-permute-start(bf16[4,128,128]{2,1,0:T(8,128)(2,1)S(1)} %get-tuple-element.43), channel_id=1, source_target_pairs={{1,2},{2,1},{5,6},{6,5},{9,10},{10,9},{13,14},{14,13},{17,18},{18,... | collective-permute-start | bytes 393224 | tf_op jit(solution)/shard_map/ppermute | solution.py:18
  13.6 0.2 dynamic-slice_reduce_fusion
  13.8 0.1 iota_compare_fusion
  13.9 0.1 select_convert_fusion
  14.0 0.1 reshape.38
  14.1 0.1 copy.12
  14.2 0.1 reshape.35
  14.4 0.1 collective-permute-done.4.slab
  14.5 5.4 %collective-permute-start.6 = (bf16[3,128,128]{2,1,0:T(8,128)(2,1)S(1)}, bf16[3,128,128]{2,1,0:T(8,128)(2,1)S(1)}, u32[]{:S(2)}, u32[]{:S(2)}) collective-permute-start(bf16[3,128,128]{2,1,0:T(8,128)(2,1)S(1)} %get-tuple-element.44), channel_id=1, source_target_pairs={{1,2},{2,1},{5,6},{6,5},{9,10},{10,9},{13,14},{14,13},{17,18},{18,... | collective-permute-start | bytes 294920 | tf_op jit(solution)/shard_map/ppermute | solution.py:18
  20.0 0.1 pad_add_fusion.scalars
  20.2 2.3 %shard_map.104 = (bf16[4,128,128]{2,1,0:T(8,128)(2,1)S(1)}, bf16[8,256,128]{2,1,0:T(8,128)(2,1)S(1)}, f32[4,384,128]{2,1,0:T(8,128)S(1)}, f32[4,384,128]{2,1,0:T...) custom-call(s32[31]{0:T(128)S(1)} %pad_add_fusion.scalars, bf16[4,128,128]{2,1,0:T(8,128)(2,1)S(1)} %bitcast.28, ...), custom_call_target="tpu_custom_call" | custom-call | flops 1000000 | bytes 1000 | tf_op jit(solution)/shard_map/pallas_call | solution.py:250
  22.5 4.5 %shard_map.105 = (bf16[4,128,128]{2,1,0:T(8,128)(2,1)}, bf16[4,128,128]{2,1,0:T(8,128)(2,1)}, bf16[2,4,128,256]{3,2,1,0:T(8,128)(2,1)S(1)}, bf16[4,768,128]{2,1,...) custom-call(s32[31]{0:T(128)S(1)} %pad_add_fusion.scalars, ...), custom_call_target="tpu_custom_call" | custom-call | flops 1500000000 | bytes 1500000 | tf_op jit(solution)/shard_map/pallas_call | solution.py:250
  27.0 3.4 %collective-permute-start.7 = (bf16[4,128,128]{2,1,0:T(8,128)(2,1)}, bf16[4,128,128]{2,1,0:T(8,128)(2,1)}, u32[]{:S(2)}, u32[]{:S(2)}) collective-permute-start(bf16[4,128,128]{2,1,0:T(8,128)(2,1)} %get-tuple-element.36), channel_id=1, source_target_pairs={{1,2},{2,1},{5,6},{6,5},{9,10},{10,9},{13,14},{14,13},{17,18},{18,... | collective-permute-start | bytes 393224 | tf_op jit(solution)/shard_map/ppermute | solution.py:18
  30.4 2.0 %shard_map.106 = (bf16[4,128,128]{2,1,0:T(8,128)(2,1)}, f32[2,4,128,128]{3,2,1,0:T(8,128)S(1)}, f32[4,128,128]{2,1,0:T(8,128)S(1)}) custom-call(s32[31]{0:T(128)S(1)} %pad_add_fusion.scalars, bf16[2,4,128,256]{3,2,1,0:T(8,128)(2,1)S(1)} %get-tuple-element.28.middle, bf16[4,768,128]{2,1,0:T(8,128)(2,1)S(1)} %get-tuple-element.29.probs, ...), custom_call_target="tpu_custom_call" | custom-call | flops 1000000 | bytes 1000 | tf_op jit(solution)/shard_map/pallas_call | solution.py:250
  32.4 1.1 %collective-permute-done.7 = bf16[4,128,128]{2,1,0:T(8,128)(2,1)} collective-permute-done((bf16[4,128,128]{2,1,0:T(8,128)(2,1)}, bf16[4,128,128]{2,1,0:T(8,128)(2,1)}, u32[]{:S(2)}, u32[]{:S(2)}) %collective-permute-start.7) | collective-permute-done | bytes 131104 | tf_op jit(solution)/shard_map/ppermute | solution.py:18
  33.5 1.0 %broadcast_select_fusion.1 = (bf16[4,128,128]{2,1,0:T(8,128)(2,1)S(1)}, bf16[4,128,128]{2,1,0:T(8,128)(2,1)S(1)}) fusion(bf16[4,128,128]{2,1,0:T(8,128)(2,1)} %collective-permute-done.7, bf16[4,128,128]{2,1,0:T(8,128)(2,1)} %collective-permute-done.8, pred[]{:T(512)S(6)} %not.7), kind=kLoop, calls=%fused_computation.14 | loop fusion | flops 131072 | bytes 524289 | tf_op jit(solution)/shard_map/jit(_where)/select_n | solution.py:27
  34.6 1.9 %collective-permute-start.9 = (bf16[4,128,128]{2,1,0:T(8,128)(2,1)S(1)}, bf16[4,128,128]{2,1,0:T(8,128)(2,1)S(1)}, u32[]{:S(2)}, u32[]{:S(2)}) collective-permute-start(bf16[4,128,128]{2,1,0:T(8,128)(2,1)S(1)} %get-tuple-element.38), channel_id=1, source_target_pairs={{0,24},{4,12},{8,0},{12,20},{16,8},{20,28},{24,16},{28,4},{1,25},{... | collective-permute-start | bytes 393224 | tf_op jit(solution)/shard_map/ppermute | solution.py:288
  36.5 6.0 %collective-permute-done.9 = bf16[4,128,128]{2,1,0:T(8,128)(2,1)S(1)} collective-permute-done((bf16[4,128,128]{2,1,0:T(8,128)(2,1)S(1)}, bf16[4,128,128]{2,1,0:T(8,128)(2,1)S(1)}, u32[]{:S(2)}, u32[]{:S(2)}) %collective-permute-start.9) | collective-permute-done | bytes 131104 | tf_op jit(solution)/shard_map/ppermute | solution.py:288
  43.3 3.2 %collective-permute-done.10 = bf16[4,128,128]{2,1,0:T(8,128)(2,1)S(1)} collective-permute-done((bf16[4,128,128]{2,1,0:T(8,128)(2,1)S(1)}, bf16[4,128,128]{2,1,0:T(8,128)(2,1)S(1)}, u32[]{:S(2)}, u32[]{:S(2)}) %collective-permute-start.10) | collective-permute-done | bytes 131104 | tf_op jit(solution)/shard_map/ppermute | solution.py:288
  46.5 0.7 %fusion.5 = bf16[1,4,128,128]{3,2,1,0:T(8,128)(2,1)} fusion(bf16[4,128,128]{2,1,0:T(8,128)(2,1)S(1)} %collective-permute-done.11, bf16[4,128,128]{2,1,0:T(8,128)(2,1)S(1)} %collective-permute-done.9, f32[4,128,128]{2,1,0:T(8,128)S(1)} %get-tuple-element.34, bf16[4,128,128]{2,1,0:T(8,128)(2,1)S(1)} %collective-permute-done.10, pred[]{:T(512)S(6)} %eq.28, ...), kind=kLoop, calls=%fused_computation.8 | loop fusion | flops 589824 | bytes 786434 | tf_op jit(solution)/shard_map/broadcast_in_dim | solution.py:423
  (44 shorter events, 0.7 us)
Async XLA Ops:
  0.6 13.0 %copy-start = (s32[8,2]{0,1:T(2,128)S(1)}, s32[8,2]{0,1:T(2,128)}, u32[]{:S(2)}) copy-start(s32[8,2]{0,1:T(2,128)} %param.15) | copy-start | bytes 196
  0.6 8.1 %copy-start.1 = (bf16[1,4,128,128]{3,2,1,0:T(8,128)(2,1)S(1)}, bf16[1,4,128,128]{3,2,1,0:T(8,128)(2,1)}, u32[]{:S(2)}) copy-start(bf16[1,4,128,128]{3,2,1,0:T(8,128)(2,1)} %param.9) | copy-start | bytes 393220
  0.7 8.1 %collective-permute-start.1 = (bf16[4,128,128]{2,1,0:T(8,128)(2,1)}, bf16[4,128,128]{2,1,0:T(8,128)(2,1)S(1)}, u32[]{:S(2)}, u32[]{:S(2)}) collective-permute-start(bf16[4,128,128]{2,1,0:T(8,128)(2,1)} %bitcast.26), channel_id=1, source_target_pairs={{0,4},{4,0},{8,12},{12,8},{16,20},{20,16},{24,28},{28,24},{1,5},{5... | collective-permute-start | bytes 393224 | tf_op jit(solution)/shard_map/ppermute | solution.py:288
  2.8 6.1 %collective-permute-start = (bf16[4,128,128]{2,1,0:T(8,128)(2,1)}, bf16[4,128,128]{2,1,0:T(8,128)(2,1)S(1)}, u32[]{:S(2)}, u32[]{:S(2)}) collective-permute-start(bf16[4,128,128]{2,1,0:T(8,128)(2,1)} %bitcast.27), channel_id=1, source_target_pairs={{0,24},{4,12},{8,0},{12,20},{16,8},{20,28},{24,16},{28,4},{1,25},{... | collective-permute-start | bytes 393224 | tf_op jit(solution)/shard_map/ppermute | solution.py:288
  6.1 0.7 %copy-start.8 = (s32[8,2]{0,1:T(2,128)S(1)}, s32[8,2]{0,1:T(2,128)}, u32[]{:S(2)}) copy-start(s32[8,2]{0,1:T(2,128)} %param.14) | copy-start | bytes 196
  8.8 5.7 %collective-permute-start.4 = (bf16[4,128,128]{2,1,0:T(8,128)(2,1)S(1)}, bf16[4,128,128]{2,1,0:T(8,128)(2,1)S(1)}, u32[]{:S(2)}, u32[]{:S(2)}) collective-permute-start(bf16[4,128,128]{2,1,0:T(8,128)(2,1)S(1)} %broadcast_select_fusion.2), channel_id=1, source_target_pairs={{0,8},{4,28},{8,16},{12,4},{16,24},{20,12},{24,0},{28,20},{1,9},{5... | collective-permute-start | bytes 393224 | tf_op jit(solution)/shard_map/ppermute | solution.py:288
  9.0 5.1 %copy-start.7 = (s32[1,4,2,3]{1,2,3,0:T(2,128)S(1)}, s32[1,4,2,3]{1,2,3,0:T(2,128)}, u32[]{:S(2)}) copy-start(s32[1,4,2,3]{1,2,3,0:T(2,128)} %param.16) | copy-start | bytes 292
  9.0 11.1 %copy-start.4 = (bf16[1,4,128,128]{3,2,1,0:T(8,128)(2,1)S(1)}, bf16[1,4,128,128]{3,2,1,0:T(8,128)(2,1)}, u32[]{:S(2)}) copy-start(bf16[1,4,128,128]{3,2,1,0:T(8,128)(2,1)} %param.17) | copy-start | bytes 393220
  9.0 11.1 %copy-start.2 = (bf16[3,3,128,128]{3,2,1,0:T(8,128)(2,1)S(1)}, bf16[3,3,128,128]{3,2,1,0:T(8,128)(2,1)}, u32[]{:S(2)}) copy-start(bf16[3,3,128,128]{3,2,1,0:T(8,128)(2,1)} %conv_weight.1) | copy-start | bytes 884740
  9.0 11.1 %collective-permute-start.3 = (bf16[4,128,128]{2,1,0:T(8,128)(2,1)S(1)}, bf16[4,128,128]{2,1,0:T(8,128)(2,1)S(1)}, u32[]{:S(2)}, u32[]{:S(2)}) collective-permute-start(bf16[4,128,128]{2,1,0:T(8,128)(2,1)S(1)} %get-tuple-element.43), channel_id=1, source_target_pairs={{1,2},{2,1},{5,6},{6,5},{9,10},{10,9},{13,14},{14,13},{17,18},{18,... | collective-permute-start | bytes 393224 | tf_op jit(solution)/shard_map/ppermute | solution.py:18
  14.3 5.8 %copy-start.3 = (bf16[128,128]{1,0:T(8,128)(2,1)S(1)}, bf16[128,128]{1,0:T(8,128)(2,1)}, u32[]{:S(2)}) copy-start(bf16[128,128]{1,0:T(8,128)(2,1)} %q_weight.3) | copy-start | bytes 98308
  14.3 5.8 %copy-start.5 = (bf16[128,128]{1,0:T(8,128)(2,1)S(1)}, bf16[128,128]{1,0:T(8,128)(2,1)}, u32[]{:S(2)}) copy-start(bf16[128,128]{1,0:T(8,128)(2,1)} %k_weight.1) | copy-start | bytes 98308
  14.3 5.8 %copy-start.6 = (bf16[128,128]{1,0:T(8,128)(2,1)S(1)}, bf16[128,128]{1,0:T(8,128)(2,1)}, u32[]{:S(2)}) copy-start(bf16[128,128]{1,0:T(8,128)(2,1)} %v_weight.1) | copy-start | bytes 98308
  14.3 5.8 %collective-permute-start.2 = (bf16[4,128,128]{2,1,0:T(8,128)(2,1)S(1)}, bf16[4,128,128]{2,1,0:T(8,128)(2,1)S(1)}, u32[]{:S(2)}, u32[]{:S(2)}) collective-permute-start(bf16[4,128,128]{2,1,0:T(8,128)(2,1)S(1)} %get-tuple-element.42), channel_id=1, source_target_pairs={{0,1},{2,3},{1,0},{3,2},{4,5},{6,7},{5,4},{7,6},{8,9},{10,11},{9,8... | collective-permute-start | bytes 393224 | tf_op jit(solution)/shard_map/ppermute | solution.py:18
  14.5 7.9 %collective-permute-start.6 = (bf16[3,128,128]{2,1,0:T(8,128)(2,1)S(1)}, bf16[3,128,128]{2,1,0:T(8,128)(2,1)S(1)}, u32[]{:S(2)}, u32[]{:S(2)}) collective-permute-start(bf16[3,128,128]{2,1,0:T(8,128)(2,1)S(1)} %get-tuple-element.44), channel_id=1, source_target_pairs={{1,2},{2,1},{5,6},{6,5},{9,10},{10,9},{13,14},{14,13},{17,18},{18,... | collective-permute-start | bytes 294920 | tf_op jit(solution)/shard_map/ppermute | solution.py:18
  19.9 2.5 %collective-permute-start.5 = (bf16[3,128,128]{2,1,0:T(8,128)(2,1)S(1)}, bf16[3,128,128]{2,1,0:T(8,128)(2,1)S(1)}, u32[]{:S(2)}, u32[]{:S(2)}) collective-permute-start(bf16[3,128,128]{2,1,0:T(8,128)(2,1)S(1)} %get-tuple-element.45), channel_id=1, source_target_pairs={{0,1},{2,3},{1,0},{3,2},{4,5},{6,7},{5,4},{7,6},{8,9},{10,11},{9,8... | collective-permute-start | bytes 294920 | tf_op jit(solution)/shard_map/ppermute | solution.py:18
  27.0 6.6 %collective-permute-start.7 = (bf16[4,128,128]{2,1,0:T(8,128)(2,1)}, bf16[4,128,128]{2,1,0:T(8,128)(2,1)}, u32[]{:S(2)}, u32[]{:S(2)}) collective-permute-start(bf16[4,128,128]{2,1,0:T(8,128)(2,1)} %get-tuple-element.36), channel_id=1, source_target_pairs={{1,2},{2,1},{5,6},{6,5},{9,10},{10,9},{13,14},{14,13},{17,18},{18,... | collective-permute-start | bytes 393224 | tf_op jit(solution)/shard_map/ppermute | solution.py:18
  30.4 3.2 %collective-permute-start.8 = (bf16[4,128,128]{2,1,0:T(8,128)(2,1)}, bf16[4,128,128]{2,1,0:T(8,128)(2,1)}, u32[]{:S(2)}, u32[]{:S(2)}) collective-permute-start(bf16[4,128,128]{2,1,0:T(8,128)(2,1)} %get-tuple-element.37), channel_id=1, source_target_pairs={{0,1},{2,3},{1,0},{3,2},{4,5},{6,7},{5,4},{7,6},{8,9},{10,11},{9,8... | collective-permute-start | bytes 393224 | tf_op jit(solution)/shard_map/ppermute | solution.py:18
  34.6 7.9 %collective-permute-start.9 = (bf16[4,128,128]{2,1,0:T(8,128)(2,1)S(1)}, bf16[4,128,128]{2,1,0:T(8,128)(2,1)S(1)}, u32[]{:S(2)}, u32[]{:S(2)}) collective-permute-start(bf16[4,128,128]{2,1,0:T(8,128)(2,1)S(1)} %get-tuple-element.38), channel_id=1, source_target_pairs={{0,24},{4,12},{8,0},{12,20},{16,8},{20,28},{24,16},{28,4},{1,25},{... | collective-permute-start | bytes 393224 | tf_op jit(solution)/shard_map/ppermute | solution.py:288
  36.5 6.8 %collective-permute-start.11 = (bf16[4,128,128]{2,1,0:T(8,128)(2,1)S(1)}, bf16[4,128,128]{2,1,0:T(8,128)(2,1)S(1)}, u32[]{:S(2)}, u32[]{:S(2)}) collective-permute-start(bf16[4,128,128]{2,1,0:T(8,128)(2,1)S(1)} %get-tuple-element.39), channel_id=1, source_target_pairs={{0,8},{4,28},{8,16},{12,4},{16,24},{20,12},{24,0},{28,20},{1,9},{5... | collective-permute-start | bytes 393224 | tf_op jit(solution)/shard_map/ppermute | solution.py:288
  42.6 3.9 %collective-permute-start.10 = (bf16[4,128,128]{2,1,0:T(8,128)(2,1)S(1)}, bf16[4,128,128]{2,1,0:T(8,128)(2,1)S(1)}, u32[]{:S(2)}, u32[]{:S(2)}) collective-permute-start(bf16[4,128,128]{2,1,0:T(8,128)(2,1)S(1)} %fusion.1), channel_id=1, source_target_pairs={{0,4},{4,0},{8,12},{12,8},{16,20},{20,16},{24,28},{28,24},{1,5},{5... | collective-permute-start | bytes 393224 | tf_op jit(solution)/shard_map/ppermute | solution.py:288

commit v10 on v9

--- a/solution.py
+++ b/solution.py
@@ -289,36 +289,55 @@
 
     camera = lax.axis_index("cam")
     slab = lax.axis_index("row")
-    odd_place = lax.rem(lax.div(camera, samples), 2) == 1
-    odd_row = lax.rem(slab, 2) == 1
-    on = jnp.where(odd_place, -2, 2)
-
-    def is_near(steps, first):
-        other = lax.rem(camera + steps * samples + views, views)
-        side = jnp.where(odd_place, 1 - first, first)
-        gap = jnp.where(side == 1, samples, views - samples)
-        return partners[other, side] == lax.rem(other + gap, views)
-
-    first_near = is_near(0, 1)
-    second_near_on = is_near(on, 0)
-    first_near_back = is_near(-on, 1)
+    odd_place = (camera if samples == 1 else lax.div(camera, samples)) & 1
+    odd_row = (slab & 1) == 1
+    even_row = (slab & 1) == 0
+    on = (2 - 4 * odd_place) * samples
+    to_pair = (1 - 2 * odd_place) * samples
+
+    def around(place):
+        return place & (views - 1) if views & (views - 1) == 0 else lax.rem(place + views, views)
+
+    def is_near(other, side, gap):
+        partner = lax.dynamic_slice(
+            partners, (other, side), (1, 1), allow_negative_indices=False
+        )
+        return partner[0, 0] == around(other + gap)
+
+    second_near_on = is_near(around(camera + on), odd_place, -to_pair)
+    first_near = is_near(camera, odd_place ^ 1, to_pair)
+    first_near_back = is_near(around(camera - on), odd_place ^ 1, to_pair)
     pair_slab = routed(image, 1, -1)
     far_slab = routed(image, -2, 2)
     passed_on = jnp.where(second_near_on, pair_slab, image)
     second_slab = routed(passed_on, 2, -2)
-    far_slab, _ = lax.optimization_barrier((far_slab, passed_on))
+    far_slab, image, _ = lax.optimization_barrier((far_slab, image, passed_on))
     first_slab = jnp.where(~first_near, far_slab, pair_slab)
     to_next = jnp.concatenate([first_slab[rows - halo :], image[rows - 1 :]])
     to_previous = jnp.concatenate([first_slab[:halo], image[:1]])
     for_between, for_within = parity_split(to_next, to_previous, odd_row)
     between, within = swap_parts(for_between, for_within, "row")
-    bands, band_widths, _ = lax.optimization_barrier((bands, band_widths, for_between))
-
-    widths_here = lax.dynamic_index_in_dim(band_widths, camera, 0, keepdims=False)
+    bands, band_widths, even_row, second_near, first_near, first_near_back, _ = (
+        lax.optimization_barrier(
+            (
+                bands,
+                band_widths,
+                even_row,
+                second_near_on,
+                first_near,
+                first_near_back,
+                for_between,
+            )
+        )
+    )
+
+    widths_here = lax.dynamic_slice(
+        band_widths, (camera, 0), (1, 2), allow_negative_indices=False
+    )[0]
     live = jnp.arange(BAND, dtype=jnp.int32)[None, :] < widths_here[:, None]
     places = jnp.clip(bands[0] - (slab * rows - MARGIN), 0, win - 1)
-    live = jnp.where(odd_place, live[::-1], live)
-    places = jnp.where(odd_place, places[:, ::-1], places)
+    live = jnp.where(odd_place == 1, live[::-1], live)
+    places = jnp.where(odd_place == 1, places[:, ::-1], places)
     scalars = jnp.concatenate(
         [
             odd_row.astype(jnp.int32).reshape(1),
@@ -405,7 +424,7 @@
     )
     from_above, from_below = (
         part.reshape(2, MARGIN, width, channels).astype(full)
-        for part in margins_of(~odd_row, within, between)
+        for part in margins_of(even_row, within, between)
     )
     zeros = jnp.zeros((2, rows - MARGIN, width, channels), full)
     total = center + jnp.concatenate([from_above, zeros], axis=1)
@@ -414,11 +433,11 @@
     from_second = routed(second, -2, 2)
     from_first = routed(first, 2, -2)
     for_pair = jnp.where(first_near, first.astype(full), 0.0) + jnp.where(
-        second_near_on, from_second.astype(full), 0.0
+        second_near, from_second.astype(full), 0.0
     )
     from_pair = routed(for_pair.astype(half), 1, -1)
     summed = grad_own + from_pair.astype(full)
-    summed = summed + jnp.where(second_near_on, 0.0, from_second.astype(full))
+    summed = summed + jnp.where(second_near, 0.0, from_second.astype(full))
     summed = summed + jnp.where(first_near_back, 0.0, from_first.astype(full))
     return (attended[None], summed.astype(half)[None])
 

time: 47.5 us -> 49.5 us (1.042)
  the two profiles are of different devices: /device:TPU:1 before, /device:TPU:0 now
where the time goes in v10:
time: 49.5 us; the launch traced here: 49.2 us
  starting transfers between devices  19.6 us (40%)
  waiting for transfers between devices  14.5 us (29%)
  Pallas kernels  8.01 us (16%)
  between operations  2.89 us (6%)
  other arithmetic  2.16 us (4%)
  local copies, waits for them, and re-layouts  1.96 us (4%)
    ppermute x6, waiting for transfers between devices, routed(): return lax.ppermute(value, 'cam', pairs)  14.5 us
    ppermute x6, starting transfers between devices, swap_parts(): results.append(lax.ppermute(part, axis, pairs + [(j, i) for i, j in pairs]))  10.8 us
    ppermute x6, starting transfers between devices, routed(): return lax.ppermute(value, 'cam', pairs)  8.81 us
    pallas_call x3, Pallas kernels, on_device(): pl.pallas_call(kernel, out_shape=tuple((jax.ShapeDtypeStruct(*one) for on...  8.01 us
  transfers between devices with their start and end apart: 12, of which 3 were waited for; matrix products, arithmetic and copies ran while one was open for 5% of the time, Pallas kernels for 9%

profile of v10, /device:TPU:0, one launch (start us, length us, event | category | flops | bytes accessed | tf_op | source)
XLA Modules:
  0.0 49.2 jit_solution(14649404685895933567)
XLA Ops:
  0.6 3.0 %collective-permute-start.1 = (bf16[4,128,128]{2,1,0:T(8,128)(2,1)}, bf16[4,128,128]{2,1,0:T(8,128)(2,1)S(1)}, u32[]{:S(2)}, u32[]{:S(2)}) collective-permute-start(bf16[4,128,128]{2,1,0:T(8,128)(2,1)} %bitcast.22), channel_id=1, source_target_pairs={{0,4},{4,0},{8,12},{12,8},{16,20},{20,16},{24,28},{28,24},{1,5},{5... | collective-permute-start | bytes 393224 | tf_op jit(solution)/shard_map/ppermute | solution.py:288
  3.6 3.6 %collective-permute-start = (bf16[4,128,128]{2,1,0:T(8,128)(2,1)}, bf16[4,128,128]{2,1,0:T(8,128)(2,1)S(1)}, u32[]{:S(2)}, u32[]{:S(2)}) collective-permute-start(bf16[4,128,128]{2,1,0:T(8,128)(2,1)} %bitcast.23), channel_id=1, source_target_pairs={{0,24},{4,12},{8,0},{12,20},{16,8},{20,28},{24,16},{28,4},{1,25},{... | collective-permute-start | bytes 393224 | tf_op jit(solution)/shard_map/ppermute | solution.py:288
  7.3 0.7 %copy-done.8 = s32[8,2]{0,1:T(2,128)S(1)} copy-done((s32[8,2]{0,1:T(2,128)S(1)}, s32[8,2]{0,1:T(2,128)}, u32[]{:S(2)}) %copy-start.8) | copy-done | bytes 88
  7.9 0.7 %fusion.8 = (s32[1,1]{0,1:T(1,128)}, s32[1,1]{0,1:T(1,128)}, s32[1,1]{0,1:T(1,128)}) fusion(s32[8,2]{0,1:T(2,128)S(1)} %copy-done.8, s32[]{:T(128)S(6)} %and.29, s32[]{:T(128)S(6)} %xor.4, s32[]{:T(128)S(6)} %and.26, s32[]{:T(128)S(6)} %and.25, s32[]{:T(128)S(6)} %axis_index.25), kind=kLoop, calls=%fused_computation.29 | loop fusion | bytes 44 | tf_op jit(solution)/shard_map/dynamic_slice | solution.py:302
  10.6 1.0 %broadcast_select_fusion.2 = bf16[4,128,128]{2,1,0:T(8,128)(2,1)S(1)} fusion(bf16[4,128,128]{2,1,0:T(8,128)(2,1)S(1)} %collective-permute-done.1, pred[]{:T(512)S(6)} %eq.22, bf16[1,4,128,128]{3,2,1,0:T(8,128)(2,1)} %param.9), kind=kLoop, calls=%fused_computation.15 | loop fusion | flops 65536 | bytes 393217 | tf_op jit(solution)/shard_map/jit(_where)/select_n | solution.py:312
  11.8 0.8 %collective-permute-start.3 = (bf16[4,128,128]{2,1,0:T(8,128)(2,1)S(1)}, bf16[4,128,128]{2,1,0:T(8,128)(2,1)S(1)}, u32[]{:S(2)}, u32[]{:S(2)}) collective-permute-start(bf16[4,128,128]{2,1,0:T(8,128)(2,1)S(1)} %get-tuple-element.53), channel_id=1, source_target_pairs={{1,2},{2,1},{5,6},{6,5},{9,10},{10,9},{13,14},{14,13},{17,18},{18,... | collective-permute-start | bytes 393224 | tf_op jit(solution)/shard_map/ppermute | solution.py:18
  12.6 0.2 dynamic-slice_reduce_fusion
  13.0 0.1 reshape.35
  13.1 0.1 copy.12
  13.2 0.1 reshape.32
  13.3 2.9 %collective-permute-start.2 = (bf16[4,128,128]{2,1,0:T(8,128)(2,1)S(1)}, bf16[4,128,128]{2,1,0:T(8,128)(2,1)S(1)}, u32[]{:S(2)}, u32[]{:S(2)}) collective-permute-start(bf16[4,128,128]{2,1,0:T(8,128)(2,1)S(1)} %get-tuple-element.52), channel_id=1, source_target_pairs={{0,1},{2,3},{1,0},{3,2},{4,5},{6,7},{5,4},{7,6},{8,9},{10,11},{9,8... | collective-permute-start | bytes 393224 | tf_op jit(solution)/shard_map/ppermute | solution.py:18
  16.3 2.1 %collective-permute-done.4.slab = bf16[4,128,128]{2,1,0:T(8,128)(2,1)S(1)} collective-permute-done((bf16[4,128,128]{2,1,0:T(8,128)(2,1)S(1)}, bf16[4,128,128]{2,1,0:T(8,128)(2,1)S(1)}, u32[]{:S(2)}, u32[]{:S(2)}) %collective-permute-start.4) | collective-permute-done | bytes 131104 | tf_op jit(solution)/shard_map/ppermute | solution.py:288
  18.4 0.7 %collective-permute-start.6 = (bf16[3,128,128]{2,1,0:T(8,128)(2,1)S(1)}, bf16[3,128,128]{2,1,0:T(8,128)(2,1)S(1)}, u32[]{:S(2)}, u32[]{:S(2)}) collective-permute-start(bf16[3,128,128]{2,1,0:T(8,128)(2,1)S(1)} %get-tuple-element.54), channel_id=1, source_target_pairs={{1,2},{2,1},{5,6},{6,5},{9,10},{10,9},{13,14},{14,13},{17,18},{18,... | collective-permute-start | bytes 294920 | tf_op jit(solution)/shard_map/ppermute | solution.py:18
  19.1 2.9 %collective-permute-start.5 = (bf16[3,128,128]{2,1,0:T(8,128)(2,1)S(1)}, bf16[3,128,128]{2,1,0:T(8,128)(2,1)S(1)}, u32[]{:S(2)}, u32[]{:S(2)}) collective-permute-start(bf16[3,128,128]{2,1,0:T(8,128)(2,1)S(1)} %get-tuple-element.55), channel_id=1, source_target_pairs={{0,1},{2,3},{1,0},{3,2},{4,5},{6,7},{5,4},{7,6},{8,9},{10,11},{9,8... | collective-permute-start | bytes 294920 | tf_op jit(solution)/shard_map/ppermute | solution.py:18
  22.2 2.3 %shard_map.104 = (bf16[4,128,128]{2,1,0:T(8,128)(2,1)S(1)}, bf16[8,256,128]{2,1,0:T(8,128)(2,1)S(1)}, f32[4,384,128]{2,1,0:T(8,128)S(1)}, f32[4,384,128]{2,1,0:T...) custom-call(s32[31]{0:T(128)S(1)} %pad_add_fusion.scalars, bf16[4,128,128]{2,1,0:T(8,128)(2,1)S(1)} %bitcast.25, ...), custom_call_target="tpu_custom_call" | custom-call | flops 1000000 | bytes 1000 | tf_op jit(solution)/shard_map/pallas_call | solution.py:250
  24.5 3.8 %shard_map.105 = (bf16[4,128,128]{2,1,0:T(8,128)(2,1)S(1)}, bf16[4,128,128]{2,1,0:T(8,128)(2,1)S(1)}, bf16[2,4,128,256]{3,2,1,0:T(8,128)(2,1)S(1)}, bf16[4,768,1...) custom-call(s32[31]{0:T(128)S(1)} %pad_add_fusion.scalars, ...), custom_call_target="tpu_custom_call" | custom-call | flops 1500000000 | bytes 1500000 | tf_op jit(solution)/shard_map/pallas_call | solution.py:250
  28.2 0.7 %collective-permute-start.7 = (bf16[4,128,128]{2,1,0:T(8,128)(2,1)S(1)}, bf16[4,128,128]{2,1,0:T(8,128)(2,1)S(1)}, u32[]{:S(2)}, u32[]{:S(2)}) collective-permute-start(bf16[4,128,128]{2,1,0:T(8,128)(2,1)S(1)} %get-tuple-element.44), channel_id=1, source_target_pairs={{1,2},{2,1},{5,6},{6,5},{9,10},{10,9},{13,14},{14,13},{17,18},{18,... | collective-permute-start | bytes 393224 | tf_op jit(solution)/shard_map/ppermute | solution.py:18
  28.9 2.8 %collective-permute-start.8 = (bf16[4,128,128]{2,1,0:T(8,128)(2,1)S(1)}, bf16[4,128,128]{2,1,0:T(8,128)(2,1)S(1)}, u32[]{:S(2)}, u32[]{:S(2)}) collective-permute-start(bf16[4,128,128]{2,1,0:T(8,128)(2,1)S(1)} %get-tuple-element.45), channel_id=1, source_target_pairs={{0,1},{2,3},{1,0},{3,2},{4,5},{6,7},{5,4},{7,6},{8,9},{10,11},{9,8... | collective-permute-start | bytes 393224 | tf_op jit(solution)/shard_map/ppermute | solution.py:18
  31.7 2.0 %shard_map.106 = (bf16[4,128,128]{2,1,0:T(8,128)(2,1)}, f32[2,4,128,128]{3,2,1,0:T(8,128)S(1)}, f32[4,128,128]{2,1,0:T(8,128)S(1)}) custom-call(s32[31]{0:T(128)S(1)} %pad_add_fusion.scalars, bf16[2,4,128,256]{3,2,1,0:T(8,128)(2,1)S(1)} %get-tuple-element.34.middle, bf16[4,768,128]{2,1,0:T(8,128)(2,1)S(1)} %get-tuple-element.35.probs, ...), custom_call_target="tpu_custom_call" | custom-call | flops 1000000 | bytes 1000 | tf_op jit(solution)/shard_map/pallas_call | solution.py:250
  33.8 0.4 collective-permute-start.9
  34.2 1.7 %collective-permute-start.11 = (bf16[4,128,128]{2,1,0:T(8,128)(2,1)S(1)}, bf16[4,128,128]{2,1,0:T(8,128)(2,1)S(1)}, u32[]{:S(2)}, u32[]{:S(2)}) collective-permute-start(bf16[4,128,128]{2,1,0:T(8,128)(2,1)S(1)} %get-tuple-element.49), channel_id=1, source_target_pairs={{0,8},{4,28},{8,16},{12,4},{16,24},{20,12},{24,0},{28,20},{1,9},{5... | collective-permute-start | bytes 393224 | tf_op jit(solution)/shard_map/ppermute | solution.py:288
  35.9 7.0 %collective-permute-done.9 = bf16[4,128,128]{2,1,0:T(8,128)(2,1)S(1)} collective-permute-done((bf16[4,128,128]{2,1,0:T(8,128)(2,1)S(1)}, bf16[4,128,128]{2,1,0:T(8,128)(2,1)S(1)}, u32[]{:S(2)}, u32[]{:S(2)}) %collective-permute-start.9) | collective-permute-done | bytes 131104 | tf_op jit(solution)/shard_map/ppermute | solution.py:288
  43.1 5.4 %collective-permute-done.10 = bf16[4,128,128]{2,1,0:T(8,128)(2,1)S(1)} collective-permute-done((bf16[4,128,128]{2,1,0:T(8,128)(2,1)S(1)}, bf16[4,128,128]{2,1,0:T(8,128)(2,1)S(1)}, u32[]{:S(2)}, u32[]{:S(2)}) %collective-permute-start.10) | collective-permute-done | bytes 131104 | tf_op jit(solution)/shard_map/ppermute | solution.py:288
  48.5 0.7 %fusion.5 = bf16[1,4,128,128]{3,2,1,0:T(8,128)(2,1)} fusion(bf16[4,128,128]{2,1,0:T(8,128)(2,1)S(1)} %collective-permute-done.11, bf16[4,128,128]{2,1,0:T(8,128)(2,1)S(1)} %collective-permute-done.9, f32[4,128,128]{2,1,0:T(8,128)S(1)} %get-tuple-element.40, bf16[4,128,128]{2,1,0:T(8,128)(2,1)S(1)} %collective-permute-done.10, pred[]{:T(512)S(6)} %eq.24, ...), kind=kLoop, calls=%fused_computation.8 | loop fusion | flops 589824 | bytes 786434 | tf_op jit(solution)/shard_map/broadcast_in_dim | solution.py:442
  (44 shorter events, 0.8 us)
Async XLA Ops:
  0.6 12.0 %copy-start = (s32[8,2]{0,1:T(2,128)S(1)}, s32[8,2]{0,1:T(2,128)}, u32[]{:S(2)}) copy-start(s32[8,2]{0,1:T(2,128)} %param.15) | copy-start | bytes 196
  0.6 9.9 %collective-permute-start.1 = (bf16[4,128,128]{2,1,0:T(8,128)(2,1)}, bf16[4,128,128]{2,1,0:T(8,128)(2,1)S(1)}, u32[]{:S(2)}, u32[]{:S(2)}) collective-permute-start(bf16[4,128,128]{2,1,0:T(8,128)(2,1)} %bitcast.22), channel_id=1, source_target_pairs={{0,4},{4,0},{8,12},{12,8},{16,20},{20,16},{24,28},{28,24},{1,5},{5... | collective-permute-start | bytes 393224 | tf_op jit(solution)/shard_map/ppermute | solution.py:288
  3.6 8.0 %collective-permute-start = (bf16[4,128,128]{2,1,0:T(8,128)(2,1)}, bf16[4,128,128]{2,1,0:T(8,128)(2,1)S(1)}, u32[]{:S(2)}, u32[]{:S(2)}) collective-permute-start(bf16[4,128,128]{2,1,0:T(8,128)(2,1)} %bitcast.23), channel_id=1, source_target_pairs={{0,24},{4,12},{8,0},{12,20},{16,8},{20,28},{24,16},{28,4},{1,25},{... | collective-permute-start | bytes 393224 | tf_op jit(solution)/shard_map/ppermute | solution.py:288
  7.3 0.7 %copy-start.8 = (s32[8,2]{0,1:T(2,128)S(1)}, s32[8,2]{0,1:T(2,128)}, u32[]{:S(2)}) copy-start(s32[8,2]{0,1:T(2,128)} %param.14) | copy-start | bytes 196
  10.6 1.1 %copy-start.1 = (bf16[1,4,128,128]{3,2,1,0:T(8,128)(2,1)S(1)}, bf16[1,4,128,128]{3,2,1,0:T(8,128)(2,1)}, u32[]{:S(2)}) copy-start(bf16[1,4,128,128]{3,2,1,0:T(8,128)(2,1)} %param.9) | copy-start | bytes 393220
  11.6 6.8 %collective-permute-start.4 = (bf16[4,128,128]{2,1,0:T(8,128)(2,1)S(1)}, bf16[4,128,128]{2,1,0:T(8,128)(2,1)S(1)}, u32[]{:S(2)}, u32[]{:S(2)}) collective-permute-start(bf16[4,128,128]{2,1,0:T(8,128)(2,1)S(1)} %broadcast_select_fusion.2), channel_id=1, source_target_pairs={{0,8},{4,28},{8,16},{12,4},{16,24},{20,12},{24,0},{28,20},{1,9},{5... | collective-permute-start | bytes 393224 | tf_op jit(solution)/shard_map/ppermute | solution.py:288
  11.7 1.3 %copy-start.7 = (s32[1,4,2,3]{1,2,3,0:T(2,128)S(1)}, s32[1,4,2,3]{1,2,3,0:T(2,128)}, u32[]{:S(2)}) copy-start(s32[1,4,2,3]{1,2,3,0:T(2,128)} %param.16) | copy-start | bytes 292
  11.8 10.4 %copy-start.4 = (bf16[1,4,128,128]{3,2,1,0:T(8,128)(2,1)S(1)}, bf16[1,4,128,128]{3,2,1,0:T(8,128)(2,1)}, u32[]{:S(2)}) copy-start(bf16[1,4,128,128]{3,2,1,0:T(8,128)(2,1)} %param.17) | copy-start | bytes 393220
  11.8 10.3 %copy-start.2 = (bf16[3,3,128,128]{3,2,1,0:T(8,128)(2,1)S(1)}, bf16[3,3,128,128]{3,2,1,0:T(8,128)(2,1)}, u32[]{:S(2)}) copy-start(bf16[3,3,128,128]{3,2,1,0:T(8,128)(2,1)} %conv_weight.1) | copy-start | bytes 884740
  11.8 10.3 %collective-permute-start.3 = (bf16[4,128,128]{2,1,0:T(8,128)(2,1)S(1)}, bf16[4,128,128]{2,1,0:T(8,128)(2,1)S(1)}, u32[]{:S(2)}, u32[]{:S(2)}) collective-permute-start(bf16[4,128,128]{2,1,0:T(8,128)(2,1)S(1)} %get-tuple-element.53), channel_id=1, source_target_pairs={{1,2},{2,1},{5,6},{6,5},{9,10},{10,9},{13,14},{14,13},{17,18},{18,... | collective-permute-start | bytes 393224 | tf_op jit(solution)/shard_map/ppermute | solution.py:18
  13.3 8.8 %copy-start.3 = (bf16[128,128]{1,0:T(8,128)(2,1)S(1)}, bf16[128,128]{1,0:T(8,128)(2,1)}, u32[]{:S(2)}) copy-start(bf16[128,128]{1,0:T(8,128)(2,1)} %q_weight.3) | copy-start | bytes 98308
  13.3 8.8 %copy-start.5 = (bf16[128,128]{1,0:T(8,128)(2,1)S(1)}, bf16[128,128]{1,0:T(8,128)(2,1)}, u32[]{:S(2)}) copy-start(bf16[128,128]{1,0:T(8,128)(2,1)} %k_weight.1) | copy-start | bytes 98308
  13.3 8.8 %copy-start.6 = (bf16[128,128]{1,0:T(8,128)(2,1)S(1)}, bf16[128,128]{1,0:T(8,128)(2,1)}, u32[]{:S(2)}) copy-start(bf16[128,128]{1,0:T(8,128)(2,1)} %v_weight.1) | copy-start | bytes 98308
  13.3 8.8 %collective-permute-start.2 = (bf16[4,128,128]{2,1,0:T(8,128)(2,1)S(1)}, bf16[4,128,128]{2,1,0:T(8,128)(2,1)S(1)}, u32[]{:S(2)}, u32[]{:S(2)}) collective-permute-start(bf16[4,128,128]{2,1,0:T(8,128)(2,1)S(1)} %get-tuple-element.52), channel_id=1, source_target_pairs={{0,1},{2,3},{1,0},{3,2},{4,5},{6,7},{5,4},{7,6},{8,9},{10,11},{9,8... | collective-permute-start | bytes 393224 | tf_op jit(solution)/shard_map/ppermute | solution.py:18
  18.4 6.0 %collective-permute-start.6 = (bf16[3,128,128]{2,1,0:T(8,128)(2,1)S(1)}, bf16[3,128,128]{2,1,0:T(8,128)(2,1)S(1)}, u32[]{:S(2)}, u32[]{:S(2)}) collective-permute-start(bf16[3,128,128]{2,1,0:T(8,128)(2,1)S(1)} %get-tuple-element.54), channel_id=1, source_target_pairs={{1,2},{2,1},{5,6},{6,5},{9,10},{10,9},{13,14},{14,13},{17,18},{18,... | collective-permute-start | bytes 294920 | tf_op jit(solution)/shard_map/ppermute | solution.py:18
  19.1 5.4 %collective-permute-start.5 = (bf16[3,128,128]{2,1,0:T(8,128)(2,1)S(1)}, bf16[3,128,128]{2,1,0:T(8,128)(2,1)S(1)}, u32[]{:S(2)}, u32[]{:S(2)}) collective-permute-start(bf16[3,128,128]{2,1,0:T(8,128)(2,1)S(1)} %get-tuple-element.55), channel_id=1, source_target_pairs={{0,1},{2,3},{1,0},{3,2},{4,5},{6,7},{5,4},{7,6},{8,9},{10,11},{9,8... | collective-permute-start | bytes 294920 | tf_op jit(solution)/shard_map/ppermute | solution.py:18
  28.2 5.5 %collective-permute-start.7 = (bf16[4,128,128]{2,1,0:T(8,128)(2,1)S(1)}, bf16[4,128,128]{2,1,0:T(8,128)(2,1)S(1)}, u32[]{:S(2)}, u32[]{:S(2)}) collective-permute-start(bf16[4,128,128]{2,1,0:T(8,128)(2,1)S(1)} %get-tuple-element.44), channel_id=1, source_target_pairs={{1,2},{2,1},{5,6},{6,5},{9,10},{10,9},{13,14},{14,13},{17,18},{18,... | collective-permute-start | bytes 393224 | tf_op jit(solution)/shard_map/ppermute | solution.py:18
  28.9 4.8 %collective-permute-start.8 = (bf16[4,128,128]{2,1,0:T(8,128)(2,1)S(1)}, bf16[4,128,128]{2,1,0:T(8,128)(2,1)S(1)}, u32[]{:S(2)}, u32[]{:S(2)}) collective-permute-start(bf16[4,128,128]{2,1,0:T(8,128)(2,1)S(1)} %get-tuple-element.45), channel_id=1, source_target_pairs={{0,1},{2,3},{1,0},{3,2},{4,5},{6,7},{5,4},{7,6},{8,9},{10,11},{9,8... | collective-permute-start | bytes 393224 | tf_op jit(solution)/shard_map/ppermute | solution.py:18
  33.8 9.1 %collective-permute-start.9 = (bf16[4,128,128]{2,1,0:T(8,128)(2,1)S(1)}, bf16[4,128,128]{2,1,0:T(8,128)(2,1)S(1)}, u32[]{:S(2)}, u32[]{:S(2)}) collective-permute-start(bf16[4,128,128]{2,1,0:T(8,128)(2,1)S(1)} %get-tuple-element.48), channel_id=1, source_target_pairs={{0,24},{4,12},{8,0},{12,20},{16,8},{20,28},{24,16},{28,4},{1,25},{... | collective-permute-start | bytes 393224 | tf_op jit(solution)/shard_map/ppermute | solution.py:288
  34.2 8.9 %collective-permute-start.11 = (bf16[4,128,128]{2,1,0:T(8,128)(2,1)S(1)}, bf16[4,128,128]{2,1,0:T(8,128)(2,1)S(1)}, u32[]{:S(2)}, u32[]{:S(2)}) collective-permute-start(bf16[4,128,128]{2,1,0:T(8,128)(2,1)S(1)} %get-tuple-element.49), channel_id=1, source_target_pairs={{0,8},{4,28},{8,16},{12,4},{16,24},{20,12},{24,0},{28,20},{1,9},{5... | collective-permute-start | bytes 393224 | tf_op jit(solution)/shard_map/ppermute | solution.py:288
  43.0 5.5 %collective-permute-start.10 = (bf16[4,128,128]{2,1,0:T(8,128)(2,1)S(1)}, bf16[4,128,128]{2,1,0:T(8,128)(2,1)S(1)}, u32[]{:S(2)}, u32[]{:S(2)}) collective-permute-start(bf16[4,128,128]{2,1,0:T(8,128)(2,1)S(1)} %fusion.1), channel_id=1, source_target_pairs={{0,4},{4,0},{8,12},{12,8},{16,20},{20,16},{24,28},{28,24},{1,5},{5... | collective-permute-start | bytes 393224 | tf_op jit(solution)/shard_map/ppermute | solution.py:288

commit v11 on v10

--- a/solution.py
+++ b/solution.py
@@ -1,5 +1,6 @@
 import jax
 import jax.numpy as jnp
+import numpy as np
 from jax import lax
 from jax.experimental import pallas as pl
 from jax.experimental.pallas import tpu as pltpu
@@ -10,13 +11,14 @@
 LOG2E = 1.4426950408889634
 
 
-def swap_parts(for_between, for_within, axis):
-    count = lax.axis_size(axis)
-    results = []
-    for first, part in ((1, for_between), (0, for_within)):
-        pairs = [(i, i + 1) for i in range(first, count - 1, 2)]
-        results.append(lax.ppermute(part, axis, pairs + [(j, i) for i, j in pairs]))
-    return results
+def swap_within(value):
+    pairs = [(i, i + 1) for i in range(0, lax.axis_size("row") - 1, 2)]
+    return lax.ppermute(value, "row", pairs + [(j, i) for i, j in pairs])
+
+
+def swap_between(value):
+    pairs = [(i, i + 1) for i in range(1, lax.axis_size("row") - 1, 2)]
+    return lax.ppermute(value, "row", pairs + [(j, i) for i, j in pairs])
 
 
 def parity_split(to_next, to_previous, odd):
@@ -159,8 +161,9 @@
     first_expo,
     first_grad_probs,
     for_within,
-    for_between,
-    middle,
+    second_for_between,
+    first_for_between,
+    center,
     probs_out,
     grad_scores_out,
     kv_t,
@@ -193,43 +196,35 @@
                 i = side * BAND + s
                 acc[side, at] += terms[i * width : (i + 1) * width]
 
-    for side in range(2):
+    for side, for_between in enumerate((second_for_between, first_for_between)):
+        back = back_projected(acc[side], wkv[...])
+        top, bottom = back[:MARGIN], back[MARGIN + rows :]
         span = slice(side * MARGIN, (side + 1) * MARGIN)
-        top = back_projected(scaled(acc[side, :MARGIN]), wkv[...])
-        bottom = back_projected(scaled(acc[side, MARGIN + rows :]), wkv[...])
         for_within[span] = jnp.where(odd, top, bottom).astype(jnp.bfloat16)
-        for_between[span] = jnp.where(odd, bottom, top).astype(jnp.bfloat16)
-        middle[side] = scaled(acc[side, MARGIN : MARGIN + rows])
-
-
-def scaled(grads):
-    channels = grads.shape[2] // 2
-    return jnp.concatenate(
+        for_between[...] = jnp.where(odd, bottom, top).astype(jnp.bfloat16)
+        center[side] = back[MARGIN : MARGIN + rows]
+
+
+def back_projected(grads, wkv):
+    rows, width, both = grads.shape
+    channels = both // 2
+    grads = jnp.concatenate(
         [grads[:, :, :channels] * channels**-0.5, grads[:, :, channels:]], axis=2
     ).astype(jnp.bfloat16)
-
-
-def back_projected(grads, wkv):
-    rows, width, both = grads.shape
-    return dot_nt(grads.reshape(rows * width, both), wkv).reshape(rows, width, both // 2)
+    return dot_nt(grads.reshape(rows * width, both), wkv).reshape(rows, width, channels)
 
 
 def third_kernel(
     scalars,
-    middle,
     probs,
     grad_scores,
     kv_t,
     first_kv_t,
     q_weight,
-    wkv,
     attended,
-    center,
     grad_own,
 ):
     rows, width, channels = attended.shape
-    for side in range(2):
-        center[side] = back_projected(middle[side], wkv[...])
     grad_q = []
     for b in range(rows):
         places = [places_of(scalars, rows, b, side) for side in range(2)]
@@ -279,6 +274,7 @@
     views = lax.axis_size("cam")
     samples = views // min(16, views)
     ring = views // samples
+    count = lax.axis_size("row")
 
     def routed(value, evens, odds):
         pairs = []
@@ -293,42 +289,47 @@
     odd_row = (slab & 1) == 1
     even_row = (slab & 1) == 0
     on = (2 - 4 * odd_place) * samples
-    to_pair = (1 - 2 * odd_place) * samples
 
     def around(place):
         return place & (views - 1) if views & (views - 1) == 0 else lax.rem(place + views, views)
 
-    def is_near(other, side, gap):
-        partner = lax.dynamic_slice(
-            partners, (other, side), (1, 1), allow_negative_indices=False
-        )
-        return partner[0, 0] == around(other + gap)
-
-    second_near_on = is_near(around(camera + on), odd_place, -to_pair)
-    first_near = is_near(camera, odd_place ^ 1, to_pair)
-    first_near_back = is_near(around(camera - on), odd_place ^ 1, to_pair)
+    near_partner = np.arange(views)[:, None] + samples * np.array([[-1, 1]])
+    near = (partners == np.mod(near_partner, views).astype(np.int32)).astype(full)
+    near = jnp.broadcast_to(near.reshape(2 * views, 1), (2 * views, channels))
+    near = lax.optimization_barrier(near)
+
+    def is_near(other, side):
+        place = (2 * other + side, jnp.int32(0))
+        row = lax.dynamic_slice(near, place, (1, channels), allow_negative_indices=False)
+        return row[None] > 0.5
+
+    def across(value, evens, odds):
+        pairs = []
+        for c in range(views):
+            step = odds if (c // samples) % 2 else evens
+            to = (c // samples + step) % ring * samples + c % samples
+            for r in range(1, count - 1, 2):
+                pairs += [(c * count + r, to * count + r + 1), (c * count + r + 1, to * count + r)]
+        return lax.ppermute(value, ("cam", "row"), pairs)
+
+    second_near = is_near(around(camera + on), odd_place)
+    first_near = is_near(camera, odd_place ^ 1)
+    first_near_back = is_near(around(camera - on), odd_place ^ 1)
     pair_slab = routed(image, 1, -1)
     far_slab = routed(image, -2, 2)
-    passed_on = jnp.where(second_near_on, pair_slab, image)
+    passed_on = jnp.where(second_near, pair_slab, image)
     second_slab = routed(passed_on, 2, -2)
-    far_slab, image, _ = lax.optimization_barrier((far_slab, image, passed_on))
+    second_between = across(
+        jnp.where(odd_row, passed_on[rows - halo :], passed_on[:halo]), 2, -2
+    )
+    far_slab, _ = lax.optimization_barrier((far_slab, passed_on))
     first_slab = jnp.where(~first_near, far_slab, pair_slab)
     to_next = jnp.concatenate([first_slab[rows - halo :], image[rows - 1 :]])
     to_previous = jnp.concatenate([first_slab[:halo], image[:1]])
     for_between, for_within = parity_split(to_next, to_previous, odd_row)
-    between, within = swap_parts(for_between, for_within, "row")
-    bands, band_widths, even_row, second_near, first_near, first_near_back, _ = (
-        lax.optimization_barrier(
-            (
-                bands,
-                band_widths,
-                even_row,
-                second_near_on,
-                first_near,
-                first_near_back,
-                for_between,
-            )
-        )
+    between, within = swap_between(for_between), swap_within(for_within)
+    bands, band_widths, even_row, _ = lax.optimization_barrier(
+        (bands, band_widths, even_row, for_between)
     )
 
     widths_here = lax.dynamic_slice(
@@ -375,17 +376,18 @@
         v_weight,
         grad_attended[0],
     )
-    between, within = swap_parts(
-        *parity_split(second_slab[rows - halo :], second_slab[:halo], odd_row), "row"
-    )
-    margins = ((2 * MARGIN, width, channels), half)
+    second_within = swap_within(
+        jnp.where(odd_row, second_slab[:halo], second_slab[rows - halo :])
+    )
+    margins = ((MARGIN, width, channels), half)
     weights = ((rows, 2 * BAND * width, width), half)
-    for_within, for_between, middle, probs, grad_scores, kv_t = on_device(
+    for_within, second_for_between, first_for_between, center, probs, grad_scores, kv_t = on_device(
         second_kernel,
         [
+            ((2 * MARGIN, width, channels), half),
             margins,
             margins,
-            ((2, rows, width, 2 * channels), half),
+            ((2, rows, width, channels), full),
             weights,
             weights,
             ((win, 2 * channels, width), half),
@@ -396,48 +398,52 @@
         queries,
         grad_attended[0],
         second_slab,
-        within,
-        between,
+        second_within,
+        second_between,
         taps,
         wkv,
         first_expo,
         first_grad_probs,
     )
-    between, within = swap_parts(for_between, for_within, "row")
-    attended, center, grad_own = on_device(
+    within = swap_within(for_within)
+    second_between = across(second_for_between, -2, 2)
+
+    def spread(part, onto_first):
+        part = part.astype(full)
+        none = jnp.zeros((rows - 2 * MARGIN, width, channels), full)
+        return jnp.concatenate(
+            [jnp.where(onto_first, part, 0.0), none, jnp.where(onto_first, 0.0, part)], axis=0
+        )
+
+    second = (center[0] + spread(within[:MARGIN], odd_row)).astype(half)
+    from_second = routed(second, -2, 2)
+    first_for_between, _ = lax.optimization_barrier((first_for_between, second))
+    first_between = swap_between(first_for_between)
+    attended, grad_own = on_device(
         third_kernel,
-        [
-            (image.shape, half),
-            ((2, rows, width, channels), full),
-            (image.shape, full),
-        ],
+        [(image.shape, half), (image.shape, full)],
         [],
         1_000_000,
         scalars,
-        middle,
         probs,
         grad_scores,
         kv_t,
         first_kv_t,
         q_weight,
-        wkv,
-    )
-    from_above, from_below = (
-        part.reshape(2, MARGIN, width, channels).astype(full)
-        for part in margins_of(even_row, within, between)
-    )
-    zeros = jnp.zeros((2, rows - MARGIN, width, channels), full)
-    total = center + jnp.concatenate([from_above, zeros], axis=1)
-    total = total + jnp.concatenate([zeros, from_below], axis=1)
-    second, first = total[0].astype(half), total[1].astype(half)
-    from_second = routed(second, -2, 2)
+    )
+    first = center[1] + spread(within[MARGIN:], odd_row) + spread(first_between, even_row)
+    first = first.astype(half)
     from_first = routed(first, 2, -2)
+    from_second, second_between, _ = lax.optimization_barrier(
+        (from_second, second_between, first)
+    )
+    from_second = from_second.astype(full) + spread(second_between, even_row)
     for_pair = jnp.where(first_near, first.astype(full), 0.0) + jnp.where(
-        second_near, from_second.astype(full), 0.0
+        second_near, from_second, 0.0
     )
     from_pair = routed(for_pair.astype(half), 1, -1)
     summed = grad_own + from_pair.astype(full)
-    summed = summed + jnp.where(second_near, 0.0, from_second.astype(full))
+    summed = summed + jnp.where(second_near, 0.0, from_second)
     summed = summed + jnp.where(first_near_back, 0.0, from_first.astype(full))
     return (attended[None], summed.astype(half)[None])
 

time: 49.5 us -> 45.8 us (0.925)
  the two profiles are of different devices: /device:TPU:0 before, /device:TPU:1 now
where the time goes in v11:
time: 45.8 us; the launch traced here: 45.5 us
  starting transfers between devices  25.7 us (56%)
  Pallas kernels  7.98 us (17%)
  waiting for transfers between devices  7.24 us (16%)
  local copies, waits for them, and re-layouts  2.31 us (5%)
  other arithmetic  1.34 us (3%)
  between operations  0.98 us (2%)
    ppermute x6, starting transfers between devices, routed(): return lax.ppermute(value, 'cam', pairs)  10.3 us
    ppermute x2, starting transfers between devices, across(): return lax.ppermute(value, ('cam', 'row'), pairs)  10.2 us
    pallas_call x3, Pallas kernels, on_device(): pl.pallas_call(kernel, out_shape=tuple((jax.ShapeDtypeStruct(*one) for on...  7.98 us
    ppermute x2, starting transfers between devices, swap_between(): return lax.ppermute(value, 'row', pairs + [(j, i) for i, j in pairs])  4.49 us
    ppermute x2, waiting for transfers between devices, swap_between(): return lax.ppermute(value, 'row', pairs + [(j, i) for i, j in pairs])  2.26 us
    ppermute x3, waiting for transfers between devices, swap_within(): return lax.ppermute(value, 'row', pairs + [(j, i) for i, j in pairs])  2.01 us
    ppermute x6, waiting for transfers between devices, routed(): return lax.ppermute(value, 'cam', pairs)  1.61 us
    ppermute x2, waiting for transfers between devices, across(): return lax.ppermute(value, ('cam', 'row'), pairs)  1.36 us
  transfers between devices with their start and end apart: 13, of which 6 were waited for; matrix products, arithmetic and copies ran while one was open for 5% of the time, Pallas kernels for 9%

profile of v11, /device:TPU:1, one launch (start us, length us, event | category | flops | bytes accessed | tf_op | source)
XLA Modules:
  0.0 45.5 jit_solution(17193643420761609224)
XLA Ops:
  0.7 2.1 %collective-permute-start.1 = (bf16[4,128,128]{2,1,0:T(8,128)(2,1)}, bf16[4,128,128]{2,1,0:T(8,128)(2,1)S(1)}, u32[]{:S(2)}, u32[]{:S(2)}) collective-permute-start(bf16[4,128,128]{2,1,0:T(8,128)(2,1)} %bitcast.26), channel_id=1, source_target_pairs={{0,4},{4,0},{8,12},{12,8},{16,20},{20,16},{24,28},{28,24},{1,5},{5... | collective-permute-start | bytes 393224 | tf_op jit(solution)/shard_map/ppermute | solution.py:284
  2.8 3.3 %collective-permute-start = (bf16[4,128,128]{2,1,0:T(8,128)(2,1)}, bf16[4,128,128]{2,1,0:T(8,128)(2,1)S(1)}, u32[]{:S(2)}, u32[]{:S(2)}) collective-permute-start(bf16[4,128,128]{2,1,0:T(8,128)(2,1)} %bitcast.27), channel_id=1, source_target_pairs={{0,24},{4,12},{8,0},{12,20},{16,8},{20,28},{24,16},{28,4},{1,25},{... | collective-permute-start | bytes 393224 | tf_op jit(solution)/shard_map/ppermute | solution.py:284
  6.1 0.8 %slice_bitcast_fusion.1 = (bf16[1,128,128]{2,1,0:T(8,128)(2,1)S(1)}, bf16[1,128,128]{2,1,0:T(8,128)(2,1)S(1)}) fusion(bf16[1,4,128,128]{3,2,1,0:T(8,128)(2,1)} %param.10), kind=kLoop, calls=%fused_computation.26 | loop fusion | bytes 131072 | tf_op jit(solution)/shard_map/slice | solution.py:327
  6.9 0.7 %copy-done.9 = s32[8,2]{0,1:T(2,128)S(1)} copy-done((s32[8,2]{0,1:T(2,128)S(1)}, s32[8,2]{0,1:T(2,128)}, u32[]{:S(2)}) %copy-start.9) | copy-done | bytes 88
  8.0 5.4 %collective-permute-start.6 = (bf16[3,128,128]{2,1,0:T(8,128)(2,1)S(1)}, bf16[3,128,128]{2,1,0:T(8,128)(2,1)S(1)}, u32[]{:S(2)}, u32[]{:S(2)}) collective-permute-start(bf16[3,128,128]{2,1,0:T(8,128)(2,1)S(1)} %slice_select_fusion), channel_id=1, source_target_pairs={{1,10},{2,9},{5,30},{6,29},{9,18},{10,17},{13,6},{14,5},{17,26},{1... | collective-permute-start | bytes 294920 | tf_op jit(solution)/shard_map/ppermute | solution.py:313
  13.6 2.1 %collective-permute-start.3 = (bf16[4,128,128]{2,1,0:T(8,128)(2,1)S(1)}, bf16[4,128,128]{2,1,0:T(8,128)(2,1)S(1)}, u32[]{:S(2)}, u32[]{:S(2)}) collective-permute-start(bf16[4,128,128]{2,1,0:T(8,128)(2,1)S(1)} %get-tuple-element.49), channel_id=1, source_target_pairs={{1,2},{2,1},{5,6},{6,5},{9,10},{10,9},{13,14},{14,13},{17,18},{18,... | collective-permute-start | bytes 393224 | tf_op jit(solution)/shard_map/ppermute | solution.py:21
  15.6 0.2 dynamic-slice_reduce_fusion
  16.1 0.1 copy.15
  16.2 0.1 reshape.60
  16.4 0.5 %collective-permute-start.5 = (bf16[3,128,128]{2,1,0:T(8,128)(2,1)S(1)}, bf16[3,128,128]{2,1,0:T(8,128)(2,1)S(1)}, u32[]{:S(2)}, u32[]{:S(2)}) collective-permute-start(bf16[3,128,128]{2,1,0:T(8,128)(2,1)S(1)} %slice_select_fusion.1), channel_id=1, source_target_pairs={{0,1},{2,3},{1,0},{3,2},{4,5},{6,7},{5,4},{7,6},{8,9},{10,11},{9,8... | collective-permute-start | bytes 294920 | tf_op jit(solution)/shard_map/ppermute | solution.py:16
  17.0 0.7 %collective-permute-done.2.within = bf16[4,128,128]{2,1,0:T(8,128)(2,1)S(1)} collective-permute-done((bf16[4,128,128]{2,1,0:T(8,128)(2,1)S(1)}, bf16[4,128,128]{2,1,0:T(8,128)(2,1)S(1)}, u32[]{:S(2)}, u32[]{:S(2)}) %collective-permute-start.2) | collective-permute-done | bytes 131104 | tf_op jit(solution)/shard_map/ppermute | solution.py:16
  17.7 2.3 %collective-permute-done.3.between = bf16[4,128,128]{2,1,0:T(8,128)(2,1)S(1)} collective-permute-done((bf16[4,128,128]{2,1,0:T(8,128)(2,1)S(1)}, bf16[4,128,128]{2,1,0:T(8,128)(2,1)S(1)}, u32[]{:S(2)}, u32[]{:S(2)}) %collective-permute-start.3) | collective-permute-done | bytes 131104 | tf_op jit(solution)/shard_map/ppermute | solution.py:21
  20.0 2.3 %shard_map.113 = (bf16[4,128,128]{2,1,0:T(8,128)(2,1)S(1)}, bf16[8,256,128]{2,1,0:T(8,128)(2,1)S(1)}, f32[4,384,128]{2,1,0:T(8,128)S(1)}, f32[4,384,128]{2,1,0:T...) custom-call(s32[31]{0:T(128)S(1)} %pad_add_fusion.scalars, bf16[4,128,128]{2,1,0:T(8,128)(2,1)S(1)} %bitcast.28, ...), custom_call_target="tpu_custom_call" | custom-call | flops 1000000 | bytes 1000 | tf_op jit(solution)/shard_map/pallas_call | solution.py:245
  22.3 3.9 %shard_map.114 = (bf16[4,128,128]{2,1,0:T(8,128)(2,1)S(1)}, bf16[2,128,128]{2,1,0:T(8,128)(2,1)S(1)}, bf16[2,128,128]{2,1,0:T(8,128)(2,1)S(1)}, f32[2,4,128,128]...) custom-call(s32[31]{0:T(128)S(1)} %pad_add_fusion.scalars, ...), custom_call_target="tpu_custom_call" | custom-call | flops 1500000000 | bytes 1500000 | tf_op jit(solution)/shard_map/pallas_call | solution.py:245
  26.3 1.3 %collective-permute-done.7 = bf16[4,128,128]{2,1,0:T(8,128)(2,1)S(1)} collective-permute-done((bf16[4,128,128]{2,1,0:T(8,128)(2,1)S(1)}, bf16[4,128,128]{2,1,0:T(8,128)(2,1)S(1)}, u32[]{:S(2)}, u32[]{:S(2)}) %collective-permute-start.7) | collective-permute-done | bytes 131104 | tf_op jit(solution)/shard_map/ppermute | solution.py:16
  27.7 2.4 %collective-permute-start.8 = (bf16[2,128,128]{2,1,0:T(8,128)(2,1)S(1)}, bf16[2,128,128]{2,1,0:T(8,128)(2,1)S(1)}, u32[]{:S(2)}, u32[]{:S(2)}) collective-permute-start(bf16[2,128,128]{2,1,0:T(8,128)(2,1)S(1)} %get-tuple-element.42), channel_id=1, source_target_pairs={{1,2},{2,1},{5,6},{6,5},{9,10},{10,9},{13,14},{14,13},{17,18},{18,... | collective-permute-start | bytes 196616 | tf_op jit(solution)/shard_map/ppermute | solution.py:21
  30.1 4.8 %collective-permute-start.10 = (bf16[2,128,128]{2,1,0:T(8,128)(2,1)S(1)}, bf16[2,128,128]{2,1,0:T(8,128)(2,1)S(1)}, u32[]{:S(2)}, u32[]{:S(2)}) collective-permute-start(bf16[2,128,128]{2,1,0:T(8,128)(2,1)S(1)} %get-tuple-element.43), channel_id=1, source_target_pairs={{1,26},{2,25},{5,14},{6,13},{9,2},{10,1},{13,22},{14,21},{17,10},{... | collective-permute-start | bytes 196616 | tf_op jit(solution)/shard_map/ppermute | solution.py:313
  35.0 1.7 %collective-permute-start.9 = (bf16[4,128,128]{2,1,0:T(8,128)(2,1)S(1)}, bf16[4,128,128]{2,1,0:T(8,128)(2,1)S(1)}, u32[]{:S(2)}, u32[]{:S(2)}) collective-permute-start(bf16[4,128,128]{2,1,0:T(8,128)(2,1)S(1)} %fusion.2), channel_id=1, source_target_pairs={{0,24},{4,12},{8,0},{12,20},{16,8},{20,28},{24,16},{28,4},{1,25},{... | collective-permute-start | bytes 393224 | tf_op jit(solution)/shard_map/ppermute | solution.py:284
  36.8 1.4 %collective-permute-done.10 = bf16[2,128,128]{2,1,0:T(8,128)(2,1)S(1)} collective-permute-done((bf16[2,128,128]{2,1,0:T(8,128)(2,1)S(1)}, bf16[2,128,128]{2,1,0:T(8,128)(2,1)S(1)}, u32[]{:S(2)}, u32[]{:S(2)}) %collective-permute-start.10) | collective-permute-done | bytes 65568 | tf_op jit(solution)/shard_map/ppermute | solution.py:313
  38.2 1.1 %collective-permute-done.9 = bf16[4,128,128]{2,1,0:T(8,128)(2,1)S(1)} collective-permute-done((bf16[4,128,128]{2,1,0:T(8,128)(2,1)S(1)}, bf16[4,128,128]{2,1,0:T(8,128)(2,1)S(1)}, u32[]{:S(2)}, u32[]{:S(2)}) %collective-permute-start.9) | collective-permute-done | bytes 131104 | tf_op jit(solution)/shard_map/ppermute | solution.py:284
  39.3 3.1 %collective-permute-start.11 = (bf16[4,128,128]{2,1,0:T(8,128)(2,1)S(1)}, bf16[4,128,128]{2,1,0:T(8,128)(2,1)S(1)}, u32[]{:S(2)}, u32[]{:S(2)}) collective-permute-start(bf16[4,128,128]{2,1,0:T(8,128)(2,1)S(1)} %add_convert_fusion.1), channel_id=1, source_target_pairs={{0,4},{4,0},{8,12},{12,8},{16,20},{20,16},{24,28},{28,24},{1,5},{5... | collective-permute-start | bytes 393224 | tf_op jit(solution)/shard_map/ppermute | solution.py:284
  42.4 1.8 %shard_map.115 = (bf16[4,128,128]{2,1,0:T(8,128)(2,1)}, f32[4,128,128]{2,1,0:T(8,128)S(1)}) custom-call(s32[31]{0:T(128)S(1)} %pad_add_fusion.scalars, bf16[4,768,128]{2,1,0:T(8,128)(2,1)S(1)} %get-tuple-element.32.probs, bf16[4,768,128]{2,1,0:T(8,128)(2,1)S(1)} %get-tuple-element.33.grad_scores, bf16[8,256,128]{2,1,0:T(8,128)(2,1)S(1)} %get-tuple-element.34.kv_t, ...), custom_call_target="tpu_custom_call" | custom-call | flops 1000000 | bytes 1000 | tf_op jit(solution)/shard_map/pallas_call | solution.py:245
  44.2 0.5 %collective-permute-done.11 = bf16[4,128,128]{2,1,0:T(8,128)(2,1)S(1)} collective-permute-done((bf16[4,128,128]{2,1,0:T(8,128)(2,1)S(1)}, bf16[4,128,128]{2,1,0:T(8,128)(2,1)S(1)}, u32[]{:S(2)}, u32[]{:S(2)}) %collective-permute-start.11) | collective-permute-done | bytes 131104 | tf_op jit(solution)/shard_map/ppermute | solution.py:284
  44.8 0.7 %fusion.3 = bf16[1,4,128,128]{3,2,1,0:T(8,128)(2,1)} fusion(bf16[4,128,128]{2,1,0:T(8,128)(2,1)S(1)} %collective-permute-done.12, f32[2,128,128]{2,1,0:T(8,128)S(1)} %get-tuple-element.59, f32[2,128,128]{2,1,0:T(8,128)S(1)} %get-tuple-element.58, bf16[4,128,128]{2,1,0:T(8,128)(2,1)S(1)} %collective-permute-done.9, f32[4,128,128]{2,1,0:T(8,128)S(1)} %get-tuple-element.37, ...), kind=kLoop, calls=%fused_computation.18 | loop fusion | flops 720896 | bytes 1048832 | tf_op jit(solution)/shard_map/broadcast_in_dim | solution.py:448
  (56 shorter events, 1.3 us)
Async XLA Ops:
  0.6 15.0 %copy-start = (s32[8,2]{0,1:T(2,128)S(1)}, s32[8,2]{0,1:T(2,128)}, u32[]{:S(2)}) copy-start(s32[8,2]{0,1:T(2,128)} %param.16) | copy-start | bytes 196
  0.6 7.2 %copy-start.1 = (bf16[1,4,128,128]{3,2,1,0:T(8,128)(2,1)S(1)}, bf16[1,4,128,128]{3,2,1,0:T(8,128)(2,1)}, u32[]{:S(2)}) copy-start(bf16[1,4,128,128]{3,2,1,0:T(8,128)(2,1)} %param.10) | copy-start | bytes 393220
  0.7 7.2 %collective-permute-start.1 = (bf16[4,128,128]{2,1,0:T(8,128)(2,1)}, bf16[4,128,128]{2,1,0:T(8,128)(2,1)S(1)}, u32[]{:S(2)}, u32[]{:S(2)}) collective-permute-start(bf16[4,128,128]{2,1,0:T(8,128)(2,1)} %bitcast.26), channel_id=1, source_target_pairs={{0,4},{4,0},{8,12},{12,8},{16,20},{20,16},{24,28},{28,24},{1,5},{5... | collective-permute-start | bytes 393224 | tf_op jit(solution)/shard_map/ppermute | solution.py:284
  2.8 10.6 %collective-permute-start = (bf16[4,128,128]{2,1,0:T(8,128)(2,1)}, bf16[4,128,128]{2,1,0:T(8,128)(2,1)S(1)}, u32[]{:S(2)}, u32[]{:S(2)}) collective-permute-start(bf16[4,128,128]{2,1,0:T(8,128)(2,1)} %bitcast.27), channel_id=1, source_target_pairs={{0,24},{4,12},{8,0},{12,20},{16,8},{20,28},{24,16},{28,4},{1,25},{... | collective-permute-start | bytes 393224 | tf_op jit(solution)/shard_map/ppermute | solution.py:284
  6.9 0.7 %copy-start.9 = (s32[8,2]{0,1:T(2,128)S(1)}, s32[8,2]{0,1:T(2,128)}, u32[]{:S(2)}) copy-start(s32[8,2]{0,1:T(2,128)} %constant.27.clone) | copy-start | bytes 196
  6.9 0.7 %copy-start.8 = (s32[8,2]{0,1:T(2,128)S(1)}, s32[8,2]{0,1:T(2,128)}, u32[]{:S(2)}) copy-start(s32[8,2]{0,1:T(2,128)} %param.15) | copy-start | bytes 196
  7.9 8.5 %collective-permute-start.4 = (bf16[4,128,128]{2,1,0:T(8,128)(2,1)S(1)}, bf16[4,128,128]{2,1,0:T(8,128)(2,1)S(1)}, u32[]{:S(2)}, u32[]{:S(2)}) collective-permute-start(bf16[4,128,128]{2,1,0:T(8,128)(2,1)S(1)} %broadcast_select_fusion), channel_id=1, source_target_pairs={{0,8},{4,28},{8,16},{12,4},{16,24},{20,12},{24,0},{28,20},{1,9},{5... | collective-permute-start | bytes 393224 | tf_op jit(solution)/shard_map/ppermute | solution.py:284
  8.0 14.3 %collective-permute-start.6 = (bf16[3,128,128]{2,1,0:T(8,128)(2,1)S(1)}, bf16[3,128,128]{2,1,0:T(8,128)(2,1)S(1)}, u32[]{:S(2)}, u32[]{:S(2)}) collective-permute-start(bf16[3,128,128]{2,1,0:T(8,128)(2,1)S(1)} %slice_select_fusion), channel_id=1, source_target_pairs={{1,10},{2,9},{5,30},{6,29},{9,18},{10,17},{13,6},{14,5},{17,26},{1... | collective-permute-start | bytes 294920 | tf_op jit(solution)/shard_map/ppermute | solution.py:313
  13.5 2.6 %copy-start.7 = (s32[1,4,2,3]{1,2,3,0:T(2,128)S(1)}, s32[1,4,2,3]{1,2,3,0:T(2,128)}, u32[]{:S(2)}) copy-start(s32[1,4,2,3]{1,2,3,0:T(2,128)} %param.17) | copy-start | bytes 292
  13.5 6.5 %copy-start.4 = (bf16[1,4,128,128]{3,2,1,0:T(8,128)(2,1)S(1)}, bf16[1,4,128,128]{3,2,1,0:T(8,128)(2,1)}, u32[]{:S(2)}) copy-start(bf16[1,4,128,128]{3,2,1,0:T(8,128)(2,1)} %param.18) | copy-start | bytes 393220
  13.5 6.5 %copy-start.5 = (bf16[128,128]{1,0:T(8,128)(2,1)S(1)}, bf16[128,128]{1,0:T(8,128)(2,1)}, u32[]{:S(2)}) copy-start(bf16[128,128]{1,0:T(8,128)(2,1)} %k_weight.1) | copy-start | bytes 98308
  13.5 6.5 %copy-start.6 = (bf16[128,128]{1,0:T(8,128)(2,1)S(1)}, bf16[128,128]{1,0:T(8,128)(2,1)}, u32[]{:S(2)}) copy-start(bf16[128,128]{1,0:T(8,128)(2,1)} %v_weight.1) | copy-start | bytes 98308
  13.5 6.4 %copy-start.2 = (bf16[3,3,128,128]{3,2,1,0:T(8,128)(2,1)S(1)}, bf16[3,3,128,128]{3,2,1,0:T(8,128)(2,1)}, u32[]{:S(2)}) copy-start(bf16[3,3,128,128]{3,2,1,0:T(8,128)(2,1)} %conv_weight.1) | copy-start | bytes 884740
  13.6 6.4 %collective-permute-start.3 = (bf16[4,128,128]{2,1,0:T(8,128)(2,1)S(1)}, bf16[4,128,128]{2,1,0:T(8,128)(2,1)S(1)}, u32[]{:S(2)}, u32[]{:S(2)}) collective-permute-start(bf16[4,128,128]{2,1,0:T(8,128)(2,1)S(1)} %get-tuple-element.49), channel_id=1, source_target_pairs={{1,2},{2,1},{5,6},{6,5},{9,10},{10,9},{13,14},{14,13},{17,18},{18,... | collective-permute-start | bytes 393224 | tf_op jit(solution)/shard_map/ppermute | solution.py:21
  16.3 3.7 %copy-start.3 = (bf16[128,128]{1,0:T(8,128)(2,1)S(1)}, bf16[128,128]{1,0:T(8,128)(2,1)}, u32[]{:S(2)}) copy-start(bf16[128,128]{1,0:T(8,128)(2,1)} %q_weight.3) | copy-start | bytes 98308
  16.3 1.4 %collective-permute-start.2 = (bf16[4,128,128]{2,1,0:T(8,128)(2,1)S(1)}, bf16[4,128,128]{2,1,0:T(8,128)(2,1)S(1)}, u32[]{:S(2)}, u32[]{:S(2)}) collective-permute-start(bf16[4,128,128]{2,1,0:T(8,128)(2,1)S(1)} %get-tuple-element.48), channel_id=1, source_target_pairs={{0,1},{2,3},{1,0},{3,2},{4,5},{6,7},{5,4},{7,6},{8,9},{10,11},{9,8... | collective-permute-start | bytes 393224 | tf_op jit(solution)/shard_map/ppermute | solution.py:16
  16.4 5.9 %collective-permute-start.5 = (bf16[3,128,128]{2,1,0:T(8,128)(2,1)S(1)}, bf16[3,128,128]{2,1,0:T(8,128)(2,1)S(1)}, u32[]{:S(2)}, u32[]{:S(2)}) collective-permute-start(bf16[3,128,128]{2,1,0:T(8,128)(2,1)S(1)} %slice_select_fusion.1), channel_id=1, source_target_pairs={{0,1},{2,3},{1,0},{3,2},{4,5},{6,7},{5,4},{7,6},{8,9},{10,11},{9,8... | collective-permute-start | bytes 294920 | tf_op jit(solution)/shard_map/ppermute | solution.py:16
  26.2 1.4 %collective-permute-start.7 = (bf16[4,128,128]{2,1,0:T(8,128)(2,1)S(1)}, bf16[4,128,128]{2,1,0:T(8,128)(2,1)S(1)}, u32[]{:S(2)}, u32[]{:S(2)}) collective-permute-start(bf16[4,128,128]{2,1,0:T(8,128)(2,1)S(1)} %get-tuple-element.39), channel_id=1, source_target_pairs={{0,1},{2,3},{1,0},{3,2},{4,5},{6,7},{5,4},{7,6},{8,9},{10,11},{9,8... | collective-permute-start | bytes 393224 | tf_op jit(solution)/shard_map/ppermute | solution.py:16
  27.7 9.0 %collective-permute-start.8 = (bf16[2,128,128]{2,1,0:T(8,128)(2,1)S(1)}, bf16[2,128,128]{2,1,0:T(8,128)(2,1)S(1)}, u32[]{:S(2)}, u32[]{:S(2)}) collective-permute-start(bf16[2,128,128]{2,1,0:T(8,128)(2,1)S(1)} %get-tuple-element.42), channel_id=1, source_target_pairs={{1,2},{2,1},{5,6},{6,5},{9,10},{10,9},{13,14},{14,13},{17,18},{18,... | collective-permute-start | bytes 196616 | tf_op jit(solution)/shard_map/ppermute | solution.py:21
  30.1 8.0 %collective-permute-start.10 = (bf16[2,128,128]{2,1,0:T(8,128)(2,1)S(1)}, bf16[2,128,128]{2,1,0:T(8,128)(2,1)S(1)}, u32[]{:S(2)}, u32[]{:S(2)}) collective-permute-start(bf16[2,128,128]{2,1,0:T(8,128)(2,1)S(1)} %get-tuple-element.43), channel_id=1, source_target_pairs={{1,26},{2,25},{5,14},{6,13},{9,2},{10,1},{13,22},{14,21},{17,10},{... | collective-permute-start | bytes 196616 | tf_op jit(solution)/shard_map/ppermute | solution.py:313
  35.0 4.2 %collective-permute-start.9 = (bf16[4,128,128]{2,1,0:T(8,128)(2,1)S(1)}, bf16[4,128,128]{2,1,0:T(8,128)(2,1)S(1)}, u32[]{:S(2)}, u32[]{:S(2)}) collective-permute-start(bf16[4,128,128]{2,1,0:T(8,128)(2,1)S(1)} %fusion.2), channel_id=1, source_target_pairs={{0,24},{4,12},{8,0},{12,20},{16,8},{20,28},{24,16},{28,4},{1,25},{... | collective-permute-start | bytes 393224 | tf_op jit(solution)/shard_map/ppermute | solution.py:284
  36.7 7.5 %collective-permute-start.12 = (bf16[4,128,128]{2,1,0:T(8,128)(2,1)S(1)}, bf16[4,128,128]{2,1,0:T(8,128)(2,1)S(1)}, u32[]{:S(2)}, u32[]{:S(2)}) collective-permute-start(bf16[4,128,128]{2,1,0:T(8,128)(2,1)S(1)} %fusion.1), channel_id=1, source_target_pairs={{0,8},{4,28},{8,16},{12,4},{16,24},{20,12},{24,0},{28,20},{1,9},{5... | collective-permute-start | bytes 393224 | tf_op jit(solution)/shard_map/ppermute | solution.py:284
  39.3 5.4 %collective-permute-start.11 = (bf16[4,128,128]{2,1,0:T(8,128)(2,1)S(1)}, bf16[4,128,128]{2,1,0:T(8,128)(2,1)S(1)}, u32[]{:S(2)}, u32[]{:S(2)}) collective-permute-start(bf16[4,128,128]{2,1,0:T(8,128)(2,1)S(1)} %add_convert_fusion.1), channel_id=1, source_target_pairs={{0,4},{4,0},{8,12},{12,8},{16,20},{20,16},{24,28},{28,24},{1,5},{5... | collective-permute-start | bytes 393224 | tf_op jit(solution)/shard_map/ppermute | solution.py:284

commit v12 on v11

--- a/solution.py
+++ b/solution.py
@@ -161,8 +161,8 @@
     first_expo,
     first_grad_probs,
     for_within,
-    second_for_between,
-    first_for_between,
+    second_edges,
+    first_edges,
     center,
     probs_out,
     grad_scores_out,
@@ -196,12 +196,13 @@
                 i = side * BAND + s
                 acc[side, at] += terms[i * width : (i + 1) * width]
 
-    for side, for_between in enumerate((second_for_between, first_for_between)):
+    for side, edges in enumerate((second_edges, first_edges)):
         back = back_projected(acc[side], wkv[...])
         top, bottom = back[:MARGIN], back[MARGIN + rows :]
         span = slice(side * MARGIN, (side + 1) * MARGIN)
         for_within[span] = jnp.where(odd, top, bottom).astype(jnp.bfloat16)
-        for_between[...] = jnp.where(odd, bottom, top).astype(jnp.bfloat16)
+        edges[:MARGIN] = top.astype(jnp.bfloat16)
+        edges[MARGIN:] = bottom.astype(jnp.bfloat16)
         center[side] = back[MARGIN : MARGIN + rows]
 
 
@@ -379,9 +380,9 @@
     second_within = swap_within(
         jnp.where(odd_row, second_slab[:halo], second_slab[rows - halo :])
     )
-    margins = ((MARGIN, width, channels), half)
+    margins = ((2 * MARGIN, width, channels), half)
     weights = ((rows, 2 * BAND * width, width), half)
-    for_within, second_for_between, first_for_between, center, probs, grad_scores, kv_t = on_device(
+    for_within, second_edges, first_edges, center, probs, grad_scores, kv_t = on_device(
         second_kernel,
         [
             ((2 * MARGIN, width, channels), half),
@@ -406,7 +407,6 @@
         first_grad_probs,
     )
     within = swap_within(for_within)
-    second_between = across(second_for_between, -2, 2)
 
     def spread(part, onto_first):
         part = part.astype(full)
@@ -417,8 +417,13 @@
 
     second = (center[0] + spread(within[:MARGIN], odd_row)).astype(half)
     from_second = routed(second, -2, 2)
-    first_for_between, _ = lax.optimization_barrier((first_for_between, second))
-    first_between = swap_between(first_for_between)
+    second_edges, first_edges, _ = lax.optimization_barrier((second_edges, first_edges, second))
+    second_between = across(
+        jnp.where(odd_row, second_edges[MARGIN:], second_edges[:MARGIN]), -2, 2
+    )
+    first_between = swap_between(
+        jnp.where(odd_row, first_edges[MARGIN:], first_edges[:MARGIN])
+    )
     attended, grad_own = on_device(
         third_kernel,
         [(image.shape, half), (image.shape, full)],

time: 45.8 us -> 45.6 us (level)
  starting transfers between devices: 25.7 us -> 25.2 us
    ppermute x2, waiting for transfers between devices: 1.36 us -> 2.48 us  [across(): return lax.ppermute(value, ('cam', 'row'), pairs)]
    ppermute x6, waiting for transfers between devices: 1.61 us -> 0.55 us  [routed(): return lax.ppermute(value, 'cam', pairs)]
    ppermute x2, starting transfers between devices: 10.2 us -> 9.21 us  [across(): return lax.ppermute(value, ('cam', 'row'), pairs)]
    ppermute x2, starting transfers between devices: 4.49 us -> 5.13 us  [swap_between(): return lax.ppermute(value, 'row', pairs + [(j, i) for i, j in pairs])]
  transfers between devices with their start and end apart: 13 -> 13, of which waited for: 6 -> 5; matrix products, arithmetic and copies ran while one was open for 5% -> 5% of each run, Pallas kernels for 9% -> 9%
where the time goes in v12:
time: 45.6 us; the launch traced here: 45.1 us
  starting transfers between devices  25.2 us (55%)
  Pallas kernels  7.98 us (18%)
  waiting for transfers between devices  7.31 us (16%)
  local copies, waits for them, and re-layouts  2.31 us (5%)
  other arithmetic  1.36 us (3%)
  between operations  1 us (2%)
    ppermute x6, starting transfers between devices, routed(): return lax.ppermute(value, 'cam', pairs)  10.1 us
    ppermute x2, starting transfers between devices, across(): return lax.ppermute(value, ('cam', 'row'), pairs)  9.21 us
    pallas_call x3, Pallas kernels, on_device(): pl.pallas_call(kernel, out_shape=tuple((jax.ShapeDtypeStruct(*one) for on...  7.98 us
    ppermute x2, starting transfers between devices, swap_between(): return lax.ppermute(value, 'row', pairs + [(j, i) for i, j in pairs])  5.13 us
    ppermute x2, waiting for transfers between devices, across(): return lax.ppermute(value, ('cam', 'row'), pairs)  2.48 us
    ppermute x2, waiting for transfers between devices, swap_between(): return lax.ppermute(value, 'row', pairs + [(j, i) for i, j in pairs])  2.26 us
    ppermute x3, waiting for transfers between devices, swap_within(): return lax.ppermute(value, 'row', pairs + [(j, i) for i, j in pairs])  2.01 us
  transfers between devices with their start and end apart: 13, of which 5 were waited for; matrix products, arithmetic and copies ran while one was open for 5% of the time, Pallas kernels for 9%

profile of v12, /device:TPU:1, one launch (start us, length us, event | category | flops | bytes accessed | tf_op | source)
XLA Modules:
  0.0 45.1 jit_solution(9700911455750061533)
XLA Ops:
  0.7 2.1 %collective-permute-start.1 = (bf16[4,128,128]{2,1,0:T(8,128)(2,1)}, bf16[4,128,128]{2,1,0:T(8,128)(2,1)S(1)}, u32[]{:S(2)}, u32[]{:S(2)}) collective-permute-start(bf16[4,128,128]{2,1,0:T(8,128)(2,1)} %bitcast.26), channel_id=1, source_target_pairs={{0,4},{4,0},{8,12},{12,8},{16,20},{20,16},{24,28},{28,24},{1,5},{5... | collective-permute-start | bytes 393224 | tf_op jit(solution)/shard_map/ppermute | solution.py:285
  2.8 3.3 %collective-permute-start = (bf16[4,128,128]{2,1,0:T(8,128)(2,1)}, bf16[4,128,128]{2,1,0:T(8,128)(2,1)S(1)}, u32[]{:S(2)}, u32[]{:S(2)}) collective-permute-start(bf16[4,128,128]{2,1,0:T(8,128)(2,1)} %bitcast.27), channel_id=1, source_target_pairs={{0,24},{4,12},{8,0},{12,20},{16,8},{20,28},{24,16},{28,4},{1,25},{... | collective-permute-start | bytes 393224 | tf_op jit(solution)/shard_map/ppermute | solution.py:285
  6.1 0.8 %slice_bitcast_fusion.1 = (bf16[1,128,128]{2,1,0:T(8,128)(2,1)S(1)}, bf16[1,128,128]{2,1,0:T(8,128)(2,1)S(1)}) fusion(bf16[1,4,128,128]{3,2,1,0:T(8,128)(2,1)} %param.10), kind=kLoop, calls=%fused_computation.28 | loop fusion | bytes 131072 | tf_op jit(solution)/shard_map/slice | solution.py:328
  6.9 0.7 %copy-done.9 = s32[8,2]{0,1:T(2,128)S(1)} copy-done((s32[8,2]{0,1:T(2,128)S(1)}, s32[8,2]{0,1:T(2,128)}, u32[]{:S(2)}) %copy-start.9) | copy-done | bytes 88
  8.0 5.4 %collective-permute-start.6 = (bf16[3,128,128]{2,1,0:T(8,128)(2,1)S(1)}, bf16[3,128,128]{2,1,0:T(8,128)(2,1)S(1)}, u32[]{:S(2)}, u32[]{:S(2)}) collective-permute-start(bf16[3,128,128]{2,1,0:T(8,128)(2,1)S(1)} %slice_select_fusion), channel_id=1, source_target_pairs={{1,10},{2,9},{5,30},{6,29},{9,18},{10,17},{13,6},{14,5},{17,26},{1... | collective-permute-start | bytes 294920 | tf_op jit(solution)/shard_map/ppermute | solution.py:314
  13.6 2.1 %collective-permute-start.3 = (bf16[4,128,128]{2,1,0:T(8,128)(2,1)S(1)}, bf16[4,128,128]{2,1,0:T(8,128)(2,1)S(1)}, u32[]{:S(2)}, u32[]{:S(2)}) collective-permute-start(bf16[4,128,128]{2,1,0:T(8,128)(2,1)S(1)} %get-tuple-element.51), channel_id=1, source_target_pairs={{1,2},{2,1},{5,6},{6,5},{9,10},{10,9},{13,14},{14,13},{17,18},{18,... | collective-permute-start | bytes 393224 | tf_op jit(solution)/shard_map/ppermute | solution.py:21
  15.6 0.2 dynamic-slice_reduce_fusion
  16.0 0.1 reshape.64
  16.1 0.1 copy.15
  16.2 0.1 reshape.60
  16.4 0.5 %collective-permute-start.5 = (bf16[3,128,128]{2,1,0:T(8,128)(2,1)S(1)}, bf16[3,128,128]{2,1,0:T(8,128)(2,1)S(1)}, u32[]{:S(2)}, u32[]{:S(2)}) collective-permute-start(bf16[3,128,128]{2,1,0:T(8,128)(2,1)S(1)} %slice_select_fusion.1), channel_id=1, source_target_pairs={{0,1},{2,3},{1,0},{3,2},{4,5},{6,7},{5,4},{7,6},{8,9},{10,11},{9,8... | collective-permute-start | bytes 294920 | tf_op jit(solution)/shard_map/ppermute | solution.py:16
  17.0 0.7 %collective-permute-done.2.within = bf16[4,128,128]{2,1,0:T(8,128)(2,1)S(1)} collective-permute-done((bf16[4,128,128]{2,1,0:T(8,128)(2,1)S(1)}, bf16[4,128,128]{2,1,0:T(8,128)(2,1)S(1)}, u32[]{:S(2)}, u32[]{:S(2)}) %collective-permute-start.2) | collective-permute-done | bytes 131104 | tf_op jit(solution)/shard_map/ppermute | solution.py:16
  17.7 2.3 %collective-permute-done.3.between = bf16[4,128,128]{2,1,0:T(8,128)(2,1)S(1)} collective-permute-done((bf16[4,128,128]{2,1,0:T(8,128)(2,1)S(1)}, bf16[4,128,128]{2,1,0:T(8,128)(2,1)S(1)}, u32[]{:S(2)}, u32[]{:S(2)}) %collective-permute-start.3) | collective-permute-done | bytes 131104 | tf_op jit(solution)/shard_map/ppermute | solution.py:21
  20.0 2.3 %shard_map.113 = (bf16[4,128,128]{2,1,0:T(8,128)(2,1)S(1)}, bf16[8,256,128]{2,1,0:T(8,128)(2,1)S(1)}, f32[4,384,128]{2,1,0:T(8,128)S(1)}, f32[4,384,128]{2,1,0:T...) custom-call(s32[31]{0:T(128)S(1)} %pad_add_fusion.scalars, bf16[4,128,128]{2,1,0:T(8,128)(2,1)S(1)} %bitcast.28, ...), custom_call_target="tpu_custom_call" | custom-call | flops 1000000 | bytes 1000 | tf_op jit(solution)/shard_map/pallas_call | solution.py:246
  22.3 3.9 %shard_map.114 = (bf16[4,128,128]{2,1,0:T(8,128)(2,1)S(1)}, bf16[4,128,128]{2,1,0:T(8,128)(2,1)S(1)}, bf16[4,128,128]{2,1,0:T(8,128)(2,1)S(1)}, f32[2,4,128,128]...) custom-call(s32[31]{0:T(128)S(1)} %pad_add_fusion.scalars, ...), custom_call_target="tpu_custom_call" | custom-call | flops 1500000000 | bytes 1500000 | tf_op jit(solution)/shard_map/pallas_call | solution.py:246
  26.3 1.3 %collective-permute-done.7 = bf16[4,128,128]{2,1,0:T(8,128)(2,1)S(1)} collective-permute-done((bf16[4,128,128]{2,1,0:T(8,128)(2,1)S(1)}, bf16[4,128,128]{2,1,0:T(8,128)(2,1)S(1)}, u32[]{:S(2)}, u32[]{:S(2)}) %collective-permute-start.7) | collective-permute-done | bytes 131104 | tf_op jit(solution)/shard_map/ppermute | solution.py:16
  27.7 2.0 %collective-permute-start.9 = (bf16[4,128,128]{2,1,0:T(8,128)(2,1)S(1)}, bf16[4,128,128]{2,1,0:T(8,128)(2,1)S(1)}, u32[]{:S(2)}, u32[]{:S(2)}) collective-permute-start(bf16[4,128,128]{2,1,0:T(8,128)(2,1)S(1)} %fusion.2), channel_id=1, source_target_pairs={{0,24},{4,12},{8,0},{12,20},{16,8},{20,28},{24,16},{28,4},{1,25},{... | collective-permute-start | bytes 393224 | tf_op jit(solution)/shard_map/ppermute | solution.py:285
  29.7 3.1 %collective-permute-start.8 = (bf16[2,128,128]{2,1,0:T(8,128)(2,1)S(1)}, bf16[2,128,128]{2,1,0:T(8,128)(2,1)S(1)}, u32[]{:S(2)}, u32[]{:S(2)}) collective-permute-start(bf16[2,128,128]{2,1,0:T(8,128)(2,1)S(1)} %slice_select_fusion.3), channel_id=1, source_target_pairs={{1,2},{2,1},{5,6},{6,5},{9,10},{10,9},{13,14},{14,13},{17,18},{18,... | collective-permute-start | bytes 196616 | tf_op jit(solution)/shard_map/ppermute | solution.py:21
  32.8 3.8 %collective-permute-start.10 = (bf16[2,128,128]{2,1,0:T(8,128)(2,1)S(1)}, bf16[2,128,128]{2,1,0:T(8,128)(2,1)S(1)}, u32[]{:S(2)}, u32[]{:S(2)}) collective-permute-start(bf16[2,128,128]{2,1,0:T(8,128)(2,1)S(1)} %slice_select_fusion.2), channel_id=1, source_target_pairs={{1,26},{2,25},{5,14},{6,13},{9,2},{10,1},{13,22},{14,21},{17,10},{... | collective-permute-start | bytes 196616 | tf_op jit(solution)/shard_map/ppermute | solution.py:314
  36.8 2.5 %collective-permute-done.10 = bf16[2,128,128]{2,1,0:T(8,128)(2,1)S(1)} collective-permute-done((bf16[2,128,128]{2,1,0:T(8,128)(2,1)S(1)}, bf16[2,128,128]{2,1,0:T(8,128)(2,1)S(1)}, u32[]{:S(2)}, u32[]{:S(2)}) %collective-permute-start.10) | collective-permute-done | bytes 65568 | tf_op jit(solution)/shard_map/ppermute | solution.py:314
  39.4 2.6 %collective-permute-start.11 = (bf16[4,128,128]{2,1,0:T(8,128)(2,1)S(1)}, bf16[4,128,128]{2,1,0:T(8,128)(2,1)S(1)}, u32[]{:S(2)}, u32[]{:S(2)}) collective-permute-start(bf16[4,128,128]{2,1,0:T(8,128)(2,1)S(1)} %add_convert_fusion.1), channel_id=1, source_target_pairs={{0,4},{4,0},{8,12},{12,8},{16,20},{20,16},{24,28},{28,24},{1,5},{5... | collective-permute-start | bytes 393224 | tf_op jit(solution)/shard_map/ppermute | solution.py:285
  42.0 1.8 %shard_map.115 = (bf16[4,128,128]{2,1,0:T(8,128)(2,1)}, f32[4,128,128]{2,1,0:T(8,128)S(1)}) custom-call(s32[31]{0:T(128)S(1)} %pad_add_fusion.scalars, bf16[4,768,128]{2,1,0:T(8,128)(2,1)S(1)} %get-tuple-element.33.probs, bf16[4,768,128]{2,1,0:T(8,128)(2,1)S(1)} %get-tuple-element.34.grad_scores, bf16[8,256,128]{2,1,0:T(8,128)(2,1)S(1)} %get-tuple-element.35.kv_t, ...), custom_call_target="tpu_custom_call" | custom-call | flops 1000000 | bytes 1000 | tf_op jit(solution)/shard_map/pallas_call | solution.py:246
  43.8 0.5 %collective-permute-done.11 = bf16[4,128,128]{2,1,0:T(8,128)(2,1)S(1)} collective-permute-done((bf16[4,128,128]{2,1,0:T(8,128)(2,1)S(1)}, bf16[4,128,128]{2,1,0:T(8,128)(2,1)S(1)}, u32[]{:S(2)}, u32[]{:S(2)}) %collective-permute-start.11) | collective-permute-done | bytes 131104 | tf_op jit(solution)/shard_map/ppermute | solution.py:285
  44.4 0.7 %fusion.3 = bf16[1,4,128,128]{3,2,1,0:T(8,128)(2,1)} fusion(bf16[4,128,128]{2,1,0:T(8,128)(2,1)S(1)} %collective-permute-done.12, f32[2,128,128]{2,1,0:T(8,128)S(1)} %get-tuple-element.61, f32[2,128,128]{2,1,0:T(8,128)S(1)} %get-tuple-element.60, bf16[4,128,128]{2,1,0:T(8,128)(2,1)S(1)} %collective-permute-done.9, f32[4,128,128]{2,1,0:T(8,128)S(1)} %get-tuple-element.38, ...), kind=kLoop, calls=%fused_computation.18 | loop fusion | flops 720896 | bytes 1048832 | tf_op jit(solution)/shard_map/broadcast_in_dim | solution.py:453
  (58 shorter events, 1.3 us)
Async XLA Ops:
  0.6 15.0 %copy-start = (s32[8,2]{0,1:T(2,128)S(1)}, s32[8,2]{0,1:T(2,128)}, u32[]{:S(2)}) copy-start(s32[8,2]{0,1:T(2,128)} %param.16) | copy-start | bytes 196
  0.6 7.2 %copy-start.1 = (bf16[1,4,128,128]{3,2,1,0:T(8,128)(2,1)S(1)}, bf16[1,4,128,128]{3,2,1,0:T(8,128)(2,1)}, u32[]{:S(2)}) copy-start(bf16[1,4,128,128]{3,2,1,0:T(8,128)(2,1)} %param.10) | copy-start | bytes 393220
  0.7 7.2 %collective-permute-start.1 = (bf16[4,128,128]{2,1,0:T(8,128)(2,1)}, bf16[4,128,128]{2,1,0:T(8,128)(2,1)S(1)}, u32[]{:S(2)}, u32[]{:S(2)}) collective-permute-start(bf16[4,128,128]{2,1,0:T(8,128)(2,1)} %bitcast.26), channel_id=1, source_target_pairs={{0,4},{4,0},{8,12},{12,8},{16,20},{20,16},{24,28},{28,24},{1,5},{5... | collective-permute-start | bytes 393224 | tf_op jit(solution)/shard_map/ppermute | solution.py:285
  2.8 10.6 %collective-permute-start = (bf16[4,128,128]{2,1,0:T(8,128)(2,1)}, bf16[4,128,128]{2,1,0:T(8,128)(2,1)S(1)}, u32[]{:S(2)}, u32[]{:S(2)}) collective-permute-start(bf16[4,128,128]{2,1,0:T(8,128)(2,1)} %bitcast.27), channel_id=1, source_target_pairs={{0,24},{4,12},{8,0},{12,20},{16,8},{20,28},{24,16},{28,4},{1,25},{... | collective-permute-start | bytes 393224 | tf_op jit(solution)/shard_map/ppermute | solution.py:285
  6.9 0.7 %copy-start.9 = (s32[8,2]{0,1:T(2,128)S(1)}, s32[8,2]{0,1:T(2,128)}, u32[]{:S(2)}) copy-start(s32[8,2]{0,1:T(2,128)} %constant.27.clone) | copy-start | bytes 196
  6.9 0.7 %copy-start.8 = (s32[8,2]{0,1:T(2,128)S(1)}, s32[8,2]{0,1:T(2,128)}, u32[]{:S(2)}) copy-start(s32[8,2]{0,1:T(2,128)} %param.15) | copy-start | bytes 196
  7.9 8.5 %collective-permute-start.4 = (bf16[4,128,128]{2,1,0:T(8,128)(2,1)S(1)}, bf16[4,128,128]{2,1,0:T(8,128)(2,1)S(1)}, u32[]{:S(2)}, u32[]{:S(2)}) collective-permute-start(bf16[4,128,128]{2,1,0:T(8,128)(2,1)S(1)} %broadcast_select_fusion), channel_id=1, source_target_pairs={{0,8},{4,28},{8,16},{12,4},{16,24},{20,12},{24,0},{28,20},{1,9},{5... | collective-permute-start | bytes 393224 | tf_op jit(solution)/shard_map/ppermute | solution.py:285
  8.0 14.3 %collective-permute-start.6 = (bf16[3,128,128]{2,1,0:T(8,128)(2,1)S(1)}, bf16[3,128,128]{2,1,0:T(8,128)(2,1)S(1)}, u32[]{:S(2)}, u32[]{:S(2)}) collective-permute-start(bf16[3,128,128]{2,1,0:T(8,128)(2,1)S(1)} %slice_select_fusion), channel_id=1, source_target_pairs={{1,10},{2,9},{5,30},{6,29},{9,18},{10,17},{13,6},{14,5},{17,26},{1... | collective-permute-start | bytes 294920 | tf_op jit(solution)/shard_map/ppermute | solution.py:314
  13.5 2.6 %copy-start.7 = (s32[1,4,2,3]{1,2,3,0:T(2,128)S(1)}, s32[1,4,2,3]{1,2,3,0:T(2,128)}, u32[]{:S(2)}) copy-start(s32[1,4,2,3]{1,2,3,0:T(2,128)} %param.17) | copy-start | bytes 292
  13.5 6.5 %copy-start.4 = (bf16[1,4,128,128]{3,2,1,0:T(8,128)(2,1)S(1)}, bf16[1,4,128,128]{3,2,1,0:T(8,128)(2,1)}, u32[]{:S(2)}) copy-start(bf16[1,4,128,128]{3,2,1,0:T(8,128)(2,1)} %param.18) | copy-start | bytes 393220
  13.5 6.5 %copy-start.5 = (bf16[128,128]{1,0:T(8,128)(2,1)S(1)}, bf16[128,128]{1,0:T(8,128)(2,1)}, u32[]{:S(2)}) copy-start(bf16[128,128]{1,0:T(8,128)(2,1)} %k_weight.1) | copy-start | bytes 98308
  13.5 6.5 %copy-start.6 = (bf16[128,128]{1,0:T(8,128)(2,1)S(1)}, bf16[128,128]{1,0:T(8,128)(2,1)}, u32[]{:S(2)}) copy-start(bf16[128,128]{1,0:T(8,128)(2,1)} %v_weight.1) | copy-start | bytes 98308
  13.5 6.4 %copy-start.2 = (bf16[3,3,128,128]{3,2,1,0:T(8,128)(2,1)S(1)}, bf16[3,3,128,128]{3,2,1,0:T(8,128)(2,1)}, u32[]{:S(2)}) copy-start(bf16[3,3,128,128]{3,2,1,0:T(8,128)(2,1)} %conv_weight.1) | copy-start | bytes 884740
  13.6 6.4 %collective-permute-start.3 = (bf16[4,128,128]{2,1,0:T(8,128)(2,1)S(1)}, bf16[4,128,128]{2,1,0:T(8,128)(2,1)S(1)}, u32[]{:S(2)}, u32[]{:S(2)}) collective-permute-start(bf16[4,128,128]{2,1,0:T(8,128)(2,1)S(1)} %get-tuple-element.51), channel_id=1, source_target_pairs={{1,2},{2,1},{5,6},{6,5},{9,10},{10,9},{13,14},{14,13},{17,18},{18,... | collective-permute-start | bytes 393224 | tf_op jit(solution)/shard_map/ppermute | solution.py:21
  16.3 3.7 %copy-start.3 = (bf16[128,128]{1,0:T(8,128)(2,1)S(1)}, bf16[128,128]{1,0:T(8,128)(2,1)}, u32[]{:S(2)}) copy-start(bf16[128,128]{1,0:T(8,128)(2,1)} %q_weight.3) | copy-start | bytes 98308
  16.3 1.4 %collective-permute-start.2 = (bf16[4,128,128]{2,1,0:T(8,128)(2,1)S(1)}, bf16[4,128,128]{2,1,0:T(8,128)(2,1)S(1)}, u32[]{:S(2)}, u32[]{:S(2)}) collective-permute-start(bf16[4,128,128]{2,1,0:T(8,128)(2,1)S(1)} %get-tuple-element.50), channel_id=1, source_target_pairs={{0,1},{2,3},{1,0},{3,2},{4,5},{6,7},{5,4},{7,6},{8,9},{10,11},{9,8... | collective-permute-start | bytes 393224 | tf_op jit(solution)/shard_map/ppermute | solution.py:16
  16.4 5.9 %collective-permute-start.5 = (bf16[3,128,128]{2,1,0:T(8,128)(2,1)S(1)}, bf16[3,128,128]{2,1,0:T(8,128)(2,1)S(1)}, u32[]{:S(2)}, u32[]{:S(2)}) collective-permute-start(bf16[3,128,128]{2,1,0:T(8,128)(2,1)S(1)} %slice_select_fusion.1), channel_id=1, source_target_pairs={{0,1},{2,3},{1,0},{3,2},{4,5},{6,7},{5,4},{7,6},{8,9},{10,11},{9,8... | collective-permute-start | bytes 294920 | tf_op jit(solution)/shard_map/ppermute | solution.py:16
  26.2 1.4 %collective-permute-start.7 = (bf16[4,128,128]{2,1,0:T(8,128)(2,1)S(1)}, bf16[4,128,128]{2,1,0:T(8,128)(2,1)S(1)}, u32[]{:S(2)}, u32[]{:S(2)}) collective-permute-start(bf16[4,128,128]{2,1,0:T(8,128)(2,1)S(1)} %get-tuple-element.40), channel_id=1, source_target_pairs={{0,1},{2,3},{1,0},{3,2},{4,5},{6,7},{5,4},{7,6},{8,9},{10,11},{9,8... | collective-permute-start | bytes 393224 | tf_op jit(solution)/shard_map/ppermute | solution.py:16
  27.7 11.6 %collective-permute-start.9 = (bf16[4,128,128]{2,1,0:T(8,128)(2,1)S(1)}, bf16[4,128,128]{2,1,0:T(8,128)(2,1)S(1)}, u32[]{:S(2)}, u32[]{:S(2)}) collective-permute-start(bf16[4,128,128]{2,1,0:T(8,128)(2,1)S(1)} %fusion.2), channel_id=1, source_target_pairs={{0,24},{4,12},{8,0},{12,20},{16,8},{20,28},{24,16},{28,4},{1,25},{... | collective-permute-start | bytes 393224 | tf_op jit(solution)/shard_map/ppermute | solution.py:285
  29.7 7.0 %collective-permute-start.8 = (bf16[2,128,128]{2,1,0:T(8,128)(2,1)S(1)}, bf16[2,128,128]{2,1,0:T(8,128)(2,1)S(1)}, u32[]{:S(2)}, u32[]{:S(2)}) collective-permute-start(bf16[2,128,128]{2,1,0:T(8,128)(2,1)S(1)} %slice_select_fusion.3), channel_id=1, source_target_pairs={{1,2},{2,1},{5,6},{6,5},{9,10},{10,9},{13,14},{14,13},{17,18},{18,... | collective-permute-start | bytes 196616 | tf_op jit(solution)/shard_map/ppermute | solution.py:21
  32.8 6.5 %collective-permute-start.10 = (bf16[2,128,128]{2,1,0:T(8,128)(2,1)S(1)}, bf16[2,128,128]{2,1,0:T(8,128)(2,1)S(1)}, u32[]{:S(2)}, u32[]{:S(2)}) collective-permute-start(bf16[2,128,128]{2,1,0:T(8,128)(2,1)S(1)} %slice_select_fusion.2), channel_id=1, source_target_pairs={{1,26},{2,25},{5,14},{6,13},{9,2},{10,1},{13,22},{14,21},{17,10},{... | collective-permute-start | bytes 196616 | tf_op jit(solution)/shard_map/ppermute | solution.py:314
  36.8 7.0 %collective-permute-start.12 = (bf16[4,128,128]{2,1,0:T(8,128)(2,1)S(1)}, bf16[4,128,128]{2,1,0:T(8,128)(2,1)S(1)}, u32[]{:S(2)}, u32[]{:S(2)}) collective-permute-start(bf16[4,128,128]{2,1,0:T(8,128)(2,1)S(1)} %fusion.1), channel_id=1, source_target_pairs={{0,8},{4,28},{8,16},{12,4},{16,24},{20,12},{24,0},{28,20},{1,9},{5... | collective-permute-start | bytes 393224 | tf_op jit(solution)/shard_map/ppermute | solution.py:285
  39.4 4.9 %collective-permute-start.11 = (bf16[4,128,128]{2,1,0:T(8,128)(2,1)S(1)}, bf16[4,128,128]{2,1,0:T(8,128)(2,1)S(1)}, u32[]{:S(2)}, u32[]{:S(2)}) collective-permute-start(bf16[4,128,128]{2,1,0:T(8,128)(2,1)S(1)} %add_convert_fusion.1), channel_id=1, source_target_pairs={{0,4},{4,0},{8,12},{12,8},{16,20},{20,16},{24,28},{28,24},{1,5},{5... | collective-permute-start | bytes 393224 | tf_op jit(solution)/shard_map/ppermute | solution.py:285

commit v13 on v12

--- a/solution.py
+++ b/solution.py
@@ -320,18 +320,16 @@
     far_slab = routed(image, -2, 2)
     passed_on = jnp.where(second_near, pair_slab, image)
     second_slab = routed(passed_on, 2, -2)
-    second_between = across(
-        jnp.where(odd_row, passed_on[rows - halo :], passed_on[:halo]), 2, -2
-    )
     far_slab, _ = lax.optimization_barrier((far_slab, passed_on))
     first_slab = jnp.where(~first_near, far_slab, pair_slab)
     to_next = jnp.concatenate([first_slab[rows - halo :], image[rows - 1 :]])
     to_previous = jnp.concatenate([first_slab[:halo], image[:1]])
     for_between, for_within = parity_split(to_next, to_previous, odd_row)
     between, within = swap_between(for_between), swap_within(for_within)
-    bands, band_widths, even_row, _ = lax.optimization_barrier(
-        (bands, band_widths, even_row, for_between)
-    )
+    _, bands, band_widths, even_row, edge = lax.optimization_barrier(
+        (for_between, bands, band_widths, even_row, passed_on)
+    )
+    second_between = across(jnp.where(odd_row, edge[rows - halo :], edge[:halo]), 2, -2)
 
     widths_here = lax.dynamic_slice(
         band_widths, (camera, 0), (1, 2), allow_negative_indices=False

time: 45.6 us -> 46.3 us (1.015)
  waiting for transfers between devices: 7.31 us -> 8.46 us
  starting transfers between devices: 25.2 us -> 24.1 us
  local copies, waits for them, and re-layouts: 2.31 us -> 2.8 us
    ppermute x2, starting transfers between devices: 9.21 us -> 5.51 us  [across(): return lax.ppermute(value, ('cam', 'row'), pairs)]
    ppermute x2, starting transfers between devices: 5.13 us -> 8.13 us  [swap_between(): return lax.ppermute(value, 'row', pairs + [(j, i) for i, j in pairs])]
    ppermute x2, waiting for transfers between devices: 2.48 us -> 4.99 us  [across(): return lax.ppermute(value, ('cam', 'row'), pairs)]
    ppermute x2, waiting for transfers between devices: 2.26 us -> 0.01 us  [swap_between(): return lax.ppermute(value, 'row', pairs + [(j, i) for i, j in pairs])]
    ppermute x6, waiting for transfers between devices: 0.55 us -> 1.46 us  [routed(): return lax.ppermute(value, 'cam', pairs)]
    unnamed x20, local copies, waits for them, and re-layouts: 0.73 us -> 1.22 us
  transfers between devices with their start and end apart: 13 -> 13, of which waited for: 5 -> 6; matrix products, arithmetic and copies ran while one was open for 5% -> 5% of each run, Pallas kernels for 9% -> 9%
where the time goes in v13:
time: 46.3 us; the launch traced here: 45.6 us
  starting transfers between devices  24.1 us (52%)
  waiting for transfers between devices  8.46 us (18%)
  Pallas kernels  7.97 us (17%)
  local copies, waits for them, and re-layouts  2.8 us (6%)
  other arithmetic  1.36 us (3%)
  between operations  0.96 us (2%)
    ppermute x6, starting transfers between devices, routed(): return lax.ppermute(value, 'cam', pairs)  9.75 us
    ppermute x2, starting transfers between devices, swap_between(): return lax.ppermute(value, 'row', pairs + [(j, i) for i, j in pairs])  8.13 us
    pallas_call x3, Pallas kernels, on_device(): pl.pallas_call(kernel, out_shape=tuple((jax.ShapeDtypeStruct(*one) for on...  7.97 us
    ppermute x2, starting transfers between devices, across(): return lax.ppermute(value, ('cam', 'row'), pairs)  5.51 us
    ppermute x2, waiting for transfers between devices, across(): return lax.ppermute(value, ('cam', 'row'), pairs)  4.99 us
    ppermute x3, waiting for transfers between devices, swap_within(): return lax.ppermute(value, 'row', pairs + [(j, i) for i, j in pairs])  2.01 us
    ppermute x6, waiting for transfers between devices, routed(): return lax.ppermute(value, 'cam', pairs)  1.46 us
    unnamed x20, local copies, waits for them, and re-layouts  1.22 us
  transfers between devices with their start and end apart: 13, of which 6 were waited for; matrix products, arithmetic and copies ran while one was open for 5% of the time, Pallas kernels for 9%

profile of v13, /device:TPU:1, one launch (start us, length us, event | category | flops | bytes accessed | tf_op | source)
XLA Modules:
  0.0 45.6 jit_solution(16747714405393044657)
XLA Ops:
  0.7 2.1 %collective-permute-start.1 = (bf16[4,128,128]{2,1,0:T(8,128)(2,1)}, bf16[4,128,128]{2,1,0:T(8,128)(2,1)S(1)}, u32[]{:S(2)}, u32[]{:S(2)}) collective-permute-start(bf16[4,128,128]{2,1,0:T(8,128)(2,1)} %bitcast.26), channel_id=1, source_target_pairs={{0,4},{4,0},{8,12},{12,8},{16,20},{20,16},{24,28},{28,24},{1,5},{5... | collective-permute-start | bytes 393224 | tf_op jit(solution)/shard_map/ppermute | solution.py:285
  2.8 3.3 %collective-permute-start = (bf16[4,128,128]{2,1,0:T(8,128)(2,1)}, bf16[4,128,128]{2,1,0:T(8,128)(2,1)S(1)}, u32[]{:S(2)}, u32[]{:S(2)}) collective-permute-start(bf16[4,128,128]{2,1,0:T(8,128)(2,1)} %bitcast.27), channel_id=1, source_target_pairs={{0,24},{4,12},{8,0},{12,20},{16,8},{20,28},{24,16},{28,4},{1,25},{... | collective-permute-start | bytes 393224 | tf_op jit(solution)/shard_map/ppermute | solution.py:285
  6.1 0.8 %slice_bitcast_fusion.1 = (bf16[1,128,128]{2,1,0:T(8,128)(2,1)S(1)}, bf16[1,128,128]{2,1,0:T(8,128)(2,1)S(1)}) fusion(bf16[1,4,128,128]{3,2,1,0:T(8,128)(2,1)} %param.10), kind=kLoop, calls=%fused_computation.28 | loop fusion | bytes 131072 | tf_op jit(solution)/shard_map/slice | solution.py:325
  6.9 0.7 %copy-done.9 = s32[8,2]{0,1:T(2,128)S(1)} copy-done((s32[8,2]{0,1:T(2,128)S(1)}, s32[8,2]{0,1:T(2,128)}, u32[]{:S(2)}) %copy-start.9) | copy-done | bytes 88
  8.0 0.4 collective-permute-done
  8.4 5.9 %collective-permute-start.3 = (bf16[4,128,128]{2,1,0:T(8,128)(2,1)S(1)}, bf16[4,128,128]{2,1,0:T(8,128)(2,1)S(1)}, u32[]{:S(2)}, u32[]{:S(2)}) collective-permute-start(bf16[4,128,128]{2,1,0:T(8,128)(2,1)S(1)} %get-tuple-element.53), channel_id=1, source_target_pairs={{1,2},{2,1},{5,6},{6,5},{9,10},{10,9},{13,14},{14,13},{17,18},{18,... | collective-permute-start | bytes 393224 | tf_op jit(solution)/shard_map/ppermute | solution.py:21
  14.4 0.2 dynamic-slice_reduce_fusion
  14.8 0.5 %copy-done.7 = s32[1,4,2,3]{1,2,3,0:T(2,128)S(1)} copy-done((s32[1,4,2,3]{1,2,3,0:T(2,128)S(1)}, s32[1,4,2,3]{1,2,3,0:T(2,128)}, u32[]{:S(2)}) %copy-start.7) | copy-done | bytes 120
  15.6 2.1 %collective-permute-start.6 = (bf16[3,128,128]{2,1,0:T(8,128)(2,1)S(1)}, bf16[3,128,128]{2,1,0:T(8,128)(2,1)S(1)}, u32[]{:S(2)}, u32[]{:S(2)}) collective-permute-start(bf16[3,128,128]{2,1,0:T(8,128)(2,1)S(1)} %slice_select_fusion.1), channel_id=1, source_target_pairs={{1,10},{2,9},{5,30},{6,29},{9,18},{10,17},{13,6},{14,5},{17,26},{1... | collective-permute-start | bytes 294920 | tf_op jit(solution)/shard_map/ppermute | solution.py:314
  17.8 0.5 %collective-permute-start.5 = (bf16[3,128,128]{2,1,0:T(8,128)(2,1)S(1)}, bf16[3,128,128]{2,1,0:T(8,128)(2,1)S(1)}, u32[]{:S(2)}, u32[]{:S(2)}) collective-permute-start(bf16[3,128,128]{2,1,0:T(8,128)(2,1)S(1)} %slice_select_fusion), channel_id=1, source_target_pairs={{0,1},{2,3},{1,0},{3,2},{4,5},{6,7},{5,4},{7,6},{8,9},{10,11},{9,8... | collective-permute-start | bytes 294920 | tf_op jit(solution)/shard_map/ppermute | solution.py:16
  18.4 0.7 %collective-permute-done.2.within = bf16[4,128,128]{2,1,0:T(8,128)(2,1)S(1)} collective-permute-done((bf16[4,128,128]{2,1,0:T(8,128)(2,1)S(1)}, bf16[4,128,128]{2,1,0:T(8,128)(2,1)S(1)}, u32[]{:S(2)}, u32[]{:S(2)}) %collective-permute-start.2) | collective-permute-done | bytes 131104 | tf_op jit(solution)/shard_map/ppermute | solution.py:16
  19.2 2.3 %shard_map.113 = (bf16[4,128,128]{2,1,0:T(8,128)(2,1)S(1)}, bf16[8,256,128]{2,1,0:T(8,128)(2,1)S(1)}, f32[4,384,128]{2,1,0:T(8,128)S(1)}, f32[4,384,128]{2,1,0:T...) custom-call(s32[31]{0:T(128)S(1)} %pad_add_fusion.scalars, bf16[4,128,128]{2,1,0:T(8,128)(2,1)S(1)} %bitcast.28, ...), custom_call_target="tpu_custom_call" | custom-call | flops 1000000 | bytes 1000 | tf_op jit(solution)/shard_map/pallas_call | solution.py:246
  21.4 2.9 %collective-permute-done.6.between = bf16[3,128,128]{2,1,0:T(8,128)(2,1)S(1)} collective-permute-done((bf16[3,128,128]{2,1,0:T(8,128)(2,1)S(1)}, bf16[3,128,128]{2,1,0:T(8,128)(2,1)S(1)}, u32[]{:S(2)}, u32[]{:S(2)}) %collective-permute-start.6) | collective-permute-done | bytes 98336 | tf_op jit(solution)/shard_map/ppermute | solution.py:314
  24.4 3.9 %shard_map.114 = (bf16[4,128,128]{2,1,0:T(8,128)(2,1)S(1)}, bf16[4,128,128]{2,1,0:T(8,128)(2,1)S(1)}, bf16[4,128,128]{2,1,0:T(8,128)(2,1)S(1)}, f32[2,4,128,128]...) custom-call(s32[31]{0:T(128)S(1)} %pad_add_fusion.scalars, ...), custom_call_target="tpu_custom_call" | custom-call | flops 1500000000 | bytes 1500000 | tf_op jit(solution)/shard_map/pallas_call | solution.py:246
  28.3 1.3 %collective-permute-done.7 = bf16[4,128,128]{2,1,0:T(8,128)(2,1)S(1)} collective-permute-done((bf16[4,128,128]{2,1,0:T(8,128)(2,1)S(1)}, bf16[4,128,128]{2,1,0:T(8,128)(2,1)S(1)}, u32[]{:S(2)}, u32[]{:S(2)}) %collective-permute-start.7) | collective-permute-done | bytes 131104 | tf_op jit(solution)/shard_map/ppermute | solution.py:16
  29.7 2.1 %collective-permute-start.9 = (bf16[4,128,128]{2,1,0:T(8,128)(2,1)S(1)}, bf16[4,128,128]{2,1,0:T(8,128)(2,1)S(1)}, u32[]{:S(2)}, u32[]{:S(2)}) collective-permute-start(bf16[4,128,128]{2,1,0:T(8,128)(2,1)S(1)} %fusion.2), channel_id=1, source_target_pairs={{0,24},{4,12},{8,0},{12,20},{16,8},{20,28},{24,16},{28,4},{1,25},{... | collective-permute-start | bytes 393224 | tf_op jit(solution)/shard_map/ppermute | solution.py:285
  31.9 2.2 %collective-permute-start.8 = (bf16[2,128,128]{2,1,0:T(8,128)(2,1)S(1)}, bf16[2,128,128]{2,1,0:T(8,128)(2,1)S(1)}, u32[]{:S(2)}, u32[]{:S(2)}) collective-permute-start(bf16[2,128,128]{2,1,0:T(8,128)(2,1)S(1)} %slice_select_fusion.3), channel_id=1, source_target_pairs={{1,2},{2,1},{5,6},{6,5},{9,10},{10,9},{13,14},{14,13},{17,18},{18,... | collective-permute-start | bytes 196616 | tf_op jit(solution)/shard_map/ppermute | solution.py:21
  34.1 3.5 %collective-permute-start.10 = (bf16[2,128,128]{2,1,0:T(8,128)(2,1)S(1)}, bf16[2,128,128]{2,1,0:T(8,128)(2,1)S(1)}, u32[]{:S(2)}, u32[]{:S(2)}) collective-permute-start(bf16[2,128,128]{2,1,0:T(8,128)(2,1)S(1)} %slice_select_fusion.2), channel_id=1, source_target_pairs={{1,26},{2,25},{5,14},{6,13},{9,2},{10,1},{13,22},{14,21},{17,10},{... | collective-permute-start | bytes 196616 | tf_op jit(solution)/shard_map/ppermute | solution.py:314
  37.7 1.1 %collective-permute-start.12 = (bf16[4,128,128]{2,1,0:T(8,128)(2,1)S(1)}, bf16[4,128,128]{2,1,0:T(8,128)(2,1)S(1)}, u32[]{:S(2)}, u32[]{:S(2)}) collective-permute-start(bf16[4,128,128]{2,1,0:T(8,128)(2,1)S(1)} %fusion.1), channel_id=1, source_target_pairs={{0,8},{4,28},{8,16},{12,4},{16,24},{20,12},{24,0},{28,20},{1,9},{5... | collective-permute-start | bytes 393224 | tf_op jit(solution)/shard_map/ppermute | solution.py:285
  38.8 2.1 %collective-permute-done.10 = bf16[2,128,128]{2,1,0:T(8,128)(2,1)S(1)} collective-permute-done((bf16[2,128,128]{2,1,0:T(8,128)(2,1)S(1)}, bf16[2,128,128]{2,1,0:T(8,128)(2,1)S(1)}, u32[]{:S(2)}, u32[]{:S(2)}) %collective-permute-start.10) | collective-permute-done | bytes 65568 | tf_op jit(solution)/shard_map/ppermute | solution.py:314
  41.0 1.0 %collective-permute-start.11 = (bf16[4,128,128]{2,1,0:T(8,128)(2,1)S(1)}, bf16[4,128,128]{2,1,0:T(8,128)(2,1)S(1)}, u32[]{:S(2)}, u32[]{:S(2)}) collective-permute-start(bf16[4,128,128]{2,1,0:T(8,128)(2,1)S(1)} %add_convert_fusion.1), channel_id=1, source_target_pairs={{0,4},{4,0},{8,12},{12,8},{16,20},{20,16},{24,28},{28,24},{1,5},{5... | collective-permute-start | bytes 393224 | tf_op jit(solution)/shard_map/ppermute | solution.py:285
  42.0 1.8 %shard_map.115 = (bf16[4,128,128]{2,1,0:T(8,128)(2,1)}, f32[4,128,128]{2,1,0:T(8,128)S(1)}) custom-call(s32[31]{0:T(128)S(1)} %pad_add_fusion.scalars, bf16[4,768,128]{2,1,0:T(8,128)(2,1)S(1)} %get-tuple-element.35.probs, bf16[4,768,128]{2,1,0:T(8,128)(2,1)S(1)} %get-tuple-element.36.grad_scores, bf16[8,256,128]{2,1,0:T(8,128)(2,1)S(1)} %get-tuple-element.37.kv_t, ...), custom_call_target="tpu_custom_call" | custom-call | flops 1000000 | bytes 1000 | tf_op jit(solution)/shard_map/pallas_call | solution.py:246
  43.8 1.1 %collective-permute-done.11 = bf16[4,128,128]{2,1,0:T(8,128)(2,1)S(1)} collective-permute-done((bf16[4,128,128]{2,1,0:T(8,128)(2,1)S(1)}, bf16[4,128,128]{2,1,0:T(8,128)(2,1)S(1)}, u32[]{:S(2)}, u32[]{:S(2)}) %collective-permute-start.11) | collective-permute-done | bytes 131104 | tf_op jit(solution)/shard_map/ppermute | solution.py:285
  44.9 0.7 %fusion.3 = bf16[1,4,128,128]{3,2,1,0:T(8,128)(2,1)} fusion(bf16[4,128,128]{2,1,0:T(8,128)(2,1)S(1)} %collective-permute-done.12, f32[2,128,128]{2,1,0:T(8,128)S(1)} %get-tuple-element.63, f32[2,128,128]{2,1,0:T(8,128)S(1)} %get-tuple-element.62, bf16[4,128,128]{2,1,0:T(8,128)(2,1)S(1)} %collective-permute-done.9, f32[4,128,128]{2,1,0:T(8,128)S(1)} %get-tuple-element.40, ...), kind=kLoop, calls=%fused_computation.18 | loop fusion | flops 720896 | bytes 1048832 | tf_op jit(solution)/shard_map/broadcast_in_dim | solution.py:451
  (58 shorter events, 1.5 us)
Async XLA Ops:
  0.6 13.7 %copy-start = (s32[8,2]{0,1:T(2,128)S(1)}, s32[8,2]{0,1:T(2,128)}, u32[]{:S(2)}) copy-start(s32[8,2]{0,1:T(2,128)} %param.16) | copy-start | bytes 196
  0.6 7.2 %copy-start.1 = (bf16[1,4,128,128]{3,2,1,0:T(8,128)(2,1)S(1)}, bf16[1,4,128,128]{3,2,1,0:T(8,128)(2,1)}, u32[]{:S(2)}) copy-start(bf16[1,4,128,128]{3,2,1,0:T(8,128)(2,1)} %param.10) | copy-start | bytes 393220
  0.7 7.2 %collective-permute-start.1 = (bf16[4,128,128]{2,1,0:T(8,128)(2,1)}, bf16[4,128,128]{2,1,0:T(8,128)(2,1)S(1)}, u32[]{:S(2)}, u32[]{:S(2)}) collective-permute-start(bf16[4,128,128]{2,1,0:T(8,128)(2,1)} %bitcast.26), channel_id=1, source_target_pairs={{0,4},{4,0},{8,12},{12,8},{16,20},{20,16},{24,28},{28,24},{1,5},{5... | collective-permute-start | bytes 393224 | tf_op jit(solution)/shard_map/ppermute | solution.py:285
  2.8 5.6 %collective-permute-start = (bf16[4,128,128]{2,1,0:T(8,128)(2,1)}, bf16[4,128,128]{2,1,0:T(8,128)(2,1)S(1)}, u32[]{:S(2)}, u32[]{:S(2)}) collective-permute-start(bf16[4,128,128]{2,1,0:T(8,128)(2,1)} %bitcast.27), channel_id=1, source_target_pairs={{0,24},{4,12},{8,0},{12,20},{16,8},{20,28},{24,16},{28,4},{1,25},{... | collective-permute-start | bytes 393224 | tf_op jit(solution)/shard_map/ppermute | solution.py:285
  6.9 0.7 %copy-start.9 = (s32[8,2]{0,1:T(2,128)S(1)}, s32[8,2]{0,1:T(2,128)}, u32[]{:S(2)}) copy-start(s32[8,2]{0,1:T(2,128)} %constant.27.clone) | copy-start | bytes 196
  6.9 0.7 %copy-start.8 = (s32[8,2]{0,1:T(2,128)S(1)}, s32[8,2]{0,1:T(2,128)}, u32[]{:S(2)}) copy-start(s32[8,2]{0,1:T(2,128)} %param.15) | copy-start | bytes 196
  7.9 9.9 %collective-permute-start.4 = (bf16[4,128,128]{2,1,0:T(8,128)(2,1)S(1)}, bf16[4,128,128]{2,1,0:T(8,128)(2,1)S(1)}, u32[]{:S(2)}, u32[]{:S(2)}) collective-permute-start(bf16[4,128,128]{2,1,0:T(8,128)(2,1)S(1)} %broadcast_select_fusion), channel_id=1, source_target_pairs={{0,8},{4,28},{8,16},{12,4},{16,24},{20,12},{24,0},{28,20},{1,9},{5... | collective-permute-start | bytes 393224 | tf_op jit(solution)/shard_map/ppermute | solution.py:285
  8.4 10.7 %collective-permute-start.3 = (bf16[4,128,128]{2,1,0:T(8,128)(2,1)S(1)}, bf16[4,128,128]{2,1,0:T(8,128)(2,1)S(1)}, u32[]{:S(2)}, u32[]{:S(2)}) collective-permute-start(bf16[4,128,128]{2,1,0:T(8,128)(2,1)S(1)} %get-tuple-element.53), channel_id=1, source_target_pairs={{1,2},{2,1},{5,6},{6,5},{9,10},{10,9},{13,14},{14,13},{17,18},{18,... | collective-permute-start | bytes 393224 | tf_op jit(solution)/shard_map/ppermute | solution.py:21
  14.6 0.7 %copy-start.7 = (s32[1,4,2,3]{1,2,3,0:T(2,128)S(1)}, s32[1,4,2,3]{1,2,3,0:T(2,128)}, u32[]{:S(2)}) copy-start(s32[1,4,2,3]{1,2,3,0:T(2,128)} %param.17) | copy-start | bytes 292
  15.6 3.5 %copy-start.2 = (bf16[3,3,128,128]{3,2,1,0:T(8,128)(2,1)S(1)}, bf16[3,3,128,128]{3,2,1,0:T(8,128)(2,1)}, u32[]{:S(2)}) copy-start(bf16[3,3,128,128]{3,2,1,0:T(8,128)(2,1)} %conv_weight.1) | copy-start | bytes 884740
  15.6 8.8 %collective-permute-start.6 = (bf16[3,128,128]{2,1,0:T(8,128)(2,1)S(1)}, bf16[3,128,128]{2,1,0:T(8,128)(2,1)S(1)}, u32[]{:S(2)}, u32[]{:S(2)}) collective-permute-start(bf16[3,128,128]{2,1,0:T(8,128)(2,1)S(1)} %slice_select_fusion.1), channel_id=1, source_target_pairs={{1,10},{2,9},{5,30},{6,29},{9,18},{10,17},{13,6},{14,5},{17,26},{1... | collective-permute-start | bytes 294920 | tf_op jit(solution)/shard_map/ppermute | solution.py:314
  17.6 1.5 %copy-start.3 = (bf16[128,128]{1,0:T(8,128)(2,1)S(1)}, bf16[128,128]{1,0:T(8,128)(2,1)}, u32[]{:S(2)}) copy-start(bf16[128,128]{1,0:T(8,128)(2,1)} %q_weight.3) | copy-start | bytes 98308
  17.7 1.5 %copy-start.4 = (bf16[1,4,128,128]{3,2,1,0:T(8,128)(2,1)S(1)}, bf16[1,4,128,128]{3,2,1,0:T(8,128)(2,1)}, u32[]{:S(2)}) copy-start(bf16[1,4,128,128]{3,2,1,0:T(8,128)(2,1)} %param.18) | copy-start | bytes 393220
  17.7 1.5 %copy-start.5 = (bf16[128,128]{1,0:T(8,128)(2,1)S(1)}, bf16[128,128]{1,0:T(8,128)(2,1)}, u32[]{:S(2)}) copy-start(bf16[128,128]{1,0:T(8,128)(2,1)} %k_weight.1) | copy-start | bytes 98308
  17.7 1.5 %copy-start.6 = (bf16[128,128]{1,0:T(8,128)(2,1)S(1)}, bf16[128,128]{1,0:T(8,128)(2,1)}, u32[]{:S(2)}) copy-start(bf16[128,128]{1,0:T(8,128)(2,1)} %v_weight.1) | copy-start | bytes 98308
  17.7 1.4 %collective-permute-start.2 = (bf16[4,128,128]{2,1,0:T(8,128)(2,1)S(1)}, bf16[4,128,128]{2,1,0:T(8,128)(2,1)S(1)}, u32[]{:S(2)}, u32[]{:S(2)}) collective-permute-start(bf16[4,128,128]{2,1,0:T(8,128)(2,1)S(1)} %get-tuple-element.52), channel_id=1, source_target_pairs={{0,1},{2,3},{1,0},{3,2},{4,5},{6,7},{5,4},{7,6},{8,9},{10,11},{9,8... | collective-permute-start | bytes 393224 | tf_op jit(solution)/shard_map/ppermute | solution.py:16
  17.8 6.5 %collective-permute-start.5 = (bf16[3,128,128]{2,1,0:T(8,128)(2,1)S(1)}, bf16[3,128,128]{2,1,0:T(8,128)(2,1)S(1)}, u32[]{:S(2)}, u32[]{:S(2)}) collective-permute-start(bf16[3,128,128]{2,1,0:T(8,128)(2,1)S(1)} %slice_select_fusion), channel_id=1, source_target_pairs={{0,1},{2,3},{1,0},{3,2},{4,5},{6,7},{5,4},{7,6},{8,9},{10,11},{9,8... | collective-permute-start | bytes 294920 | tf_op jit(solution)/shard_map/ppermute | solution.py:16
  28.2 1.4 %collective-permute-start.7 = (bf16[4,128,128]{2,1,0:T(8,128)(2,1)S(1)}, bf16[4,128,128]{2,1,0:T(8,128)(2,1)S(1)}, u32[]{:S(2)}, u32[]{:S(2)}) collective-permute-start(bf16[4,128,128]{2,1,0:T(8,128)(2,1)S(1)} %get-tuple-element.42), channel_id=1, source_target_pairs={{0,1},{2,3},{1,0},{3,2},{4,5},{6,7},{5,4},{7,6},{8,9},{10,11},{9,8... | collective-permute-start | bytes 393224 | tf_op jit(solution)/shard_map/ppermute | solution.py:16
  29.7 11.2 %collective-permute-start.9 = (bf16[4,128,128]{2,1,0:T(8,128)(2,1)S(1)}, bf16[4,128,128]{2,1,0:T(8,128)(2,1)S(1)}, u32[]{:S(2)}, u32[]{:S(2)}) collective-permute-start(bf16[4,128,128]{2,1,0:T(8,128)(2,1)S(1)} %fusion.2), channel_id=1, source_target_pairs={{0,24},{4,12},{8,0},{12,20},{16,8},{20,28},{24,16},{28,4},{1,25},{... | collective-permute-start | bytes 393224 | tf_op jit(solution)/shard_map/ppermute | solution.py:285
  31.9 5.7 %collective-permute-start.8 = (bf16[2,128,128]{2,1,0:T(8,128)(2,1)S(1)}, bf16[2,128,128]{2,1,0:T(8,128)(2,1)S(1)}, u32[]{:S(2)}, u32[]{:S(2)}) collective-permute-start(bf16[2,128,128]{2,1,0:T(8,128)(2,1)S(1)} %slice_select_fusion.3), channel_id=1, source_target_pairs={{1,2},{2,1},{5,6},{6,5},{9,10},{10,9},{13,14},{14,13},{17,18},{18,... | collective-permute-start | bytes 196616 | tf_op jit(solution)/shard_map/ppermute | solution.py:21
  34.1 6.8 %collective-permute-start.10 = (bf16[2,128,128]{2,1,0:T(8,128)(2,1)S(1)}, bf16[2,128,128]{2,1,0:T(8,128)(2,1)S(1)}, u32[]{:S(2)}, u32[]{:S(2)}) collective-permute-start(bf16[2,128,128]{2,1,0:T(8,128)(2,1)S(1)} %slice_select_fusion.2), channel_id=1, source_target_pairs={{1,26},{2,25},{5,14},{6,13},{9,2},{10,1},{13,22},{14,21},{17,10},{... | collective-permute-start | bytes 196616 | tf_op jit(solution)/shard_map/ppermute | solution.py:314
  37.7 6.1 %collective-permute-start.12 = (bf16[4,128,128]{2,1,0:T(8,128)(2,1)S(1)}, bf16[4,128,128]{2,1,0:T(8,128)(2,1)S(1)}, u32[]{:S(2)}, u32[]{:S(2)}) collective-permute-start(bf16[4,128,128]{2,1,0:T(8,128)(2,1)S(1)} %fusion.1), channel_id=1, source_target_pairs={{0,8},{4,28},{8,16},{12,4},{16,24},{20,12},{24,0},{28,20},{1,9},{5... | collective-permute-start | bytes 393224 | tf_op jit(solution)/shard_map/ppermute | solution.py:285
  41.0 3.9 %collective-permute-start.11 = (bf16[4,128,128]{2,1,0:T(8,128)(2,1)S(1)}, bf16[4,128,128]{2,1,0:T(8,128)(2,1)S(1)}, u32[]{:S(2)}, u32[]{:S(2)}) collective-permute-start(bf16[4,128,128]{2,1,0:T(8,128)(2,1)S(1)} %add_convert_fusion.1), channel_id=1, source_target_pairs={{0,4},{4,0},{8,12},{12,8},{16,20},{20,16},{24,28},{28,24},{1,5},{5... | collective-permute-start | bytes 393224 | tf_op jit(solution)/shard_map/ppermute | solution.py:285

commit v14 on v12

--- a/solution.py
+++ b/solution.py
@@ -436,15 +436,14 @@
         first_kv_t,
         q_weight,
     )
+    from_second, second_between = lax.optimization_barrier((from_second, second_between))
+    from_second = from_second.astype(full) + spread(second_between, even_row)
+    first_between, _ = lax.optimization_barrier((first_between, from_second))
     first = center[1] + spread(within[MARGIN:], odd_row) + spread(first_between, even_row)
     first = first.astype(half)
     from_first = routed(first, 2, -2)
-    from_second, second_between, _ = lax.optimization_barrier(
-        (from_second, second_between, first)
-    )
-    from_second = from_second.astype(full) + spread(second_between, even_row)
-    for_pair = jnp.where(first_near, first.astype(full), 0.0) + jnp.where(
-        second_near, from_second, 0.0
+    for_pair = jnp.where(second_near, from_second, 0.0) + jnp.where(
+        first_near, first.astype(full), 0.0
     )
     from_pair = routed(for_pair.astype(half), 1, -1)
     summed = grad_own + from_pair.astype(full)

time: 45.6 us -> 46.6 us (1.022)
  waiting for transfers between devices: 7.31 us -> 10 us
  starting transfers between devices: 25.2 us -> 23.6 us
    ppermute x6, waiting for transfers between devices: 0.55 us -> 3.64 us  [routed(): return lax.ppermute(value, 'cam', pairs)]
    ppermute x2, waiting for transfers between devices: 2.48 us -> 0.01 us  [across(): return lax.ppermute(value, ('cam', 'row'), pairs)]
    ppermute x2, waiting for transfers between devices: 2.26 us -> 4.38 us  [swap_between(): return lax.ppermute(value, 'row', pairs + [(j, i) for i, j in pairs])]
    ppermute x6, starting transfers between devices: 10.1 us -> 8.64 us  [routed(): return lax.ppermute(value, 'cam', pairs)]
  transfers between devices with their start and end apart: 13 -> 13, of which waited for: 5 -> 6; matrix products, arithmetic and copies ran while one was open for 5% -> 4% of each run, Pallas kernels for 9% -> 9%
where the time goes in v14:
time: 46.6 us; the launch traced here: 46.3 us
  starting transfers between devices  23.6 us (51%)
  waiting for transfers between devices  10 us (21%)
  Pallas kernels  7.98 us (17%)
  local copies, waits for them, and re-layouts  2.31 us (5%)
  other arithmetic  1.33 us (3%)
  between operations  1 us (2%)
    ppermute x2, starting transfers between devices, across(): return lax.ppermute(value, ('cam', 'row'), pairs)  8.92 us
    ppermute x6, starting transfers between devices, routed(): return lax.ppermute(value, 'cam', pairs)  8.64 us
    pallas_call x3, Pallas kernels, on_device(): pl.pallas_call(kernel, out_shape=tuple((jax.ShapeDtypeStruct(*one) for on...  7.98 us
    ppermute x2, starting transfers between devices, swap_between(): return lax.ppermute(value, 'row', pairs + [(j, i) for i, j in pairs])  5.41 us
    ppermute x2, waiting for transfers between devices, swap_between(): return lax.ppermute(value, 'row', pairs + [(j, i) for i, j in pairs])  4.38 us
    ppermute x6, waiting for transfers between devices, routed(): return lax.ppermute(value, 'cam', pairs)  3.64 us
    ppermute x3, waiting for transfers between devices, swap_within(): return lax.ppermute(value, 'row', pairs + [(j, i) for i, j in pairs])  2.01 us
  transfers between devices with their start and end apart: 13, of which 6 were waited for; matrix products, arithmetic and copies ran while one was open for 4% of the time, Pallas kernels for 9%

profile of v14, /device:TPU:1, one launch (start us, length us, event | category | flops | bytes accessed | tf_op | source)
XLA Modules:
  0.0 46.3 jit_solution(3639994270583767841)
XLA Ops:
  0.7 2.1 %collective-permute-start.1 = (bf16[4,128,128]{2,1,0:T(8,128)(2,1)}, bf16[4,128,128]{2,1,0:T(8,128)(2,1)S(1)}, u32[]{:S(2)}, u32[]{:S(2)}) collective-permute-start(bf16[4,128,128]{2,1,0:T(8,128)(2,1)} %bitcast.27), channel_id=1, source_target_pairs={{0,4},{4,0},{8,12},{12,8},{16,20},{20,16},{24,28},{28,24},{1,5},{5... | collective-permute-start | bytes 393224 | tf_op jit(solution)/shard_map/ppermute | solution.py:285
  2.8 3.3 %collective-permute-start = (bf16[4,128,128]{2,1,0:T(8,128)(2,1)}, bf16[4,128,128]{2,1,0:T(8,128)(2,1)S(1)}, u32[]{:S(2)}, u32[]{:S(2)}) collective-permute-start(bf16[4,128,128]{2,1,0:T(8,128)(2,1)} %bitcast.28), channel_id=1, source_target_pairs={{0,24},{4,12},{8,0},{12,20},{16,8},{20,28},{24,16},{28,4},{1,25},{... | collective-permute-start | bytes 393224 | tf_op jit(solution)/shard_map/ppermute | solution.py:285
  6.1 0.8 %slice_bitcast_fusion.1 = (bf16[1,128,128]{2,1,0:T(8,128)(2,1)S(1)}, bf16[1,128,128]{2,1,0:T(8,128)(2,1)S(1)}) fusion(bf16[1,4,128,128]{3,2,1,0:T(8,128)(2,1)} %param.10), kind=kLoop, calls=%fused_computation.28 | loop fusion | bytes 131072 | tf_op jit(solution)/shard_map/slice | solution.py:328
  6.9 0.7 %copy-done.9 = s32[8,2]{0,1:T(2,128)S(1)} copy-done((s32[8,2]{0,1:T(2,128)S(1)}, s32[8,2]{0,1:T(2,128)}, u32[]{:S(2)}) %copy-start.9) | copy-done | bytes 88
  8.0 5.4 %collective-permute-start.6 = (bf16[3,128,128]{2,1,0:T(8,128)(2,1)S(1)}, bf16[3,128,128]{2,1,0:T(8,128)(2,1)S(1)}, u32[]{:S(2)}, u32[]{:S(2)}) collective-permute-start(bf16[3,128,128]{2,1,0:T(8,128)(2,1)S(1)} %slice_select_fusion), channel_id=1, source_target_pairs={{1,10},{2,9},{5,30},{6,29},{9,18},{10,17},{13,6},{14,5},{17,26},{1... | collective-permute-start | bytes 294920 | tf_op jit(solution)/shard_map/ppermute | solution.py:314
  13.6 2.1 %collective-permute-start.3 = (bf16[4,128,128]{2,1,0:T(8,128)(2,1)S(1)}, bf16[4,128,128]{2,1,0:T(8,128)(2,1)S(1)}, u32[]{:S(2)}, u32[]{:S(2)}) collective-permute-start(bf16[4,128,128]{2,1,0:T(8,128)(2,1)S(1)} %get-tuple-element.55), channel_id=1, source_target_pairs={{1,2},{2,1},{5,6},{6,5},{9,10},{10,9},{13,14},{14,13},{17,18},{18,... | collective-permute-start | bytes 393224 | tf_op jit(solution)/shard_map/ppermute | solution.py:21
  15.6 0.2 dynamic-slice_reduce_fusion
  16.1 0.1 copy.15
  16.4 0.5 %collective-permute-start.5 = (bf16[3,128,128]{2,1,0:T(8,128)(2,1)S(1)}, bf16[3,128,128]{2,1,0:T(8,128)(2,1)S(1)}, u32[]{:S(2)}, u32[]{:S(2)}) collective-permute-start(bf16[3,128,128]{2,1,0:T(8,128)(2,1)S(1)} %slice_select_fusion.1), channel_id=1, source_target_pairs={{0,1},{2,3},{1,0},{3,2},{4,5},{6,7},{5,4},{7,6},{8,9},{10,11},{9,8... | collective-permute-start | bytes 294920 | tf_op jit(solution)/shard_map/ppermute | solution.py:16
  17.0 0.7 %collective-permute-done.2.within = bf16[4,128,128]{2,1,0:T(8,128)(2,1)S(1)} collective-permute-done((bf16[4,128,128]{2,1,0:T(8,128)(2,1)S(1)}, bf16[4,128,128]{2,1,0:T(8,128)(2,1)S(1)}, u32[]{:S(2)}, u32[]{:S(2)}) %collective-permute-start.2) | collective-permute-done | bytes 131104 | tf_op jit(solution)/shard_map/ppermute | solution.py:16
  17.7 2.3 %collective-permute-done.3.between = bf16[4,128,128]{2,1,0:T(8,128)(2,1)S(1)} collective-permute-done((bf16[4,128,128]{2,1,0:T(8,128)(2,1)S(1)}, bf16[4,128,128]{2,1,0:T(8,128)(2,1)S(1)}, u32[]{:S(2)}, u32[]{:S(2)}) %collective-permute-start.3) | collective-permute-done | bytes 131104 | tf_op jit(solution)/shard_map/ppermute | solution.py:21
  20.0 2.3 %shard_map.113 = (bf16[4,128,128]{2,1,0:T(8,128)(2,1)S(1)}, bf16[8,256,128]{2,1,0:T(8,128)(2,1)S(1)}, f32[4,384,128]{2,1,0:T(8,128)S(1)}, f32[4,384,128]{2,1,0:T...) custom-call(s32[31]{0:T(128)S(1)} %pad_add_fusion.scalars, bf16[4,128,128]{2,1,0:T(8,128)(2,1)S(1)} %bitcast.29, ...), custom_call_target="tpu_custom_call" | custom-call | flops 1000000 | bytes 1000 | tf_op jit(solution)/shard_map/pallas_call | solution.py:246
  22.3 3.9 %shard_map.114 = (bf16[4,128,128]{2,1,0:T(8,128)(2,1)S(1)}, bf16[4,128,128]{2,1,0:T(8,128)(2,1)S(1)}, bf16[4,128,128]{2,1,0:T(8,128)(2,1)S(1)}, f32[2,4,128,128]...) custom-call(s32[31]{0:T(128)S(1)} %pad_add_fusion.scalars, ...), custom_call_target="tpu_custom_call" | custom-call | flops 1500000000 | bytes 1500000 | tf_op jit(solution)/shard_map/pallas_call | solution.py:246
  26.3 1.3 %collective-permute-done.7 = bf16[4,128,128]{2,1,0:T(8,128)(2,1)S(1)} collective-permute-done((bf16[4,128,128]{2,1,0:T(8,128)(2,1)S(1)}, bf16[4,128,128]{2,1,0:T(8,128)(2,1)S(1)}, u32[]{:S(2)}, u32[]{:S(2)}) %collective-permute-start.7) | collective-permute-done | bytes 131104 | tf_op jit(solution)/shard_map/ppermute | solution.py:16
  27.7 2.0 %collective-permute-start.8 = (bf16[4,128,128]{2,1,0:T(8,128)(2,1)S(1)}, bf16[4,128,128]{2,1,0:T(8,128)(2,1)S(1)}, u32[]{:S(2)}, u32[]{:S(2)}) collective-permute-start(bf16[4,128,128]{2,1,0:T(8,128)(2,1)S(1)} %fusion), channel_id=1, source_target_pairs={{0,24},{4,12},{8,0},{12,20},{16,8},{20,28},{24,16},{28,4},{1,25},{... | collective-permute-start | bytes 393224 | tf_op jit(solution)/shard_map/ppermute | solution.py:285
  29.7 3.6 %collective-permute-start.9 = (bf16[2,128,128]{2,1,0:T(8,128)(2,1)S(1)}, bf16[2,128,128]{2,1,0:T(8,128)(2,1)S(1)}, u32[]{:S(2)}, u32[]{:S(2)}) collective-permute-start(bf16[2,128,128]{2,1,0:T(8,128)(2,1)S(1)} %slice_select_fusion.3), channel_id=1, source_target_pairs={{1,26},{2,25},{5,14},{6,13},{9,2},{10,1},{13,22},{14,21},{17,10},{... | collective-permute-start | bytes 196616 | tf_op jit(solution)/shard_map/ppermute | solution.py:314
  33.3 3.4 %collective-permute-start.10 = (bf16[2,128,128]{2,1,0:T(8,128)(2,1)S(1)}, bf16[2,128,128]{2,1,0:T(8,128)(2,1)S(1)}, u32[]{:S(2)}, u32[]{:S(2)}) collective-permute-start(bf16[2,128,128]{2,1,0:T(8,128)(2,1)S(1)} %slice_select_fusion.2), channel_id=1, source_target_pairs={{1,2},{2,1},{5,6},{6,5},{9,10},{10,9},{13,14},{14,13},{17,18},{18,... | collective-permute-start | bytes 196616 | tf_op jit(solution)/shard_map/ppermute | solution.py:21
  36.8 2.1 %collective-permute-done.10 = bf16[2,128,128]{2,1,0:T(8,128)(2,1)S(1)} collective-permute-done((bf16[2,128,128]{2,1,0:T(8,128)(2,1)S(1)}, bf16[2,128,128]{2,1,0:T(8,128)(2,1)S(1)}, u32[]{:S(2)}, u32[]{:S(2)}) %collective-permute-start.10) | collective-permute-done | bytes 65568 | tf_op jit(solution)/shard_map/ppermute | solution.py:21
  39.0 1.0 %collective-permute-start.11 = (bf16[4,128,128]{2,1,0:T(8,128)(2,1)S(1)}, bf16[4,128,128]{2,1,0:T(8,128)(2,1)S(1)}, u32[]{:S(2)}, u32[]{:S(2)}) collective-permute-start(bf16[4,128,128]{2,1,0:T(8,128)(2,1)S(1)} %get-tuple-element.50), channel_id=1, source_target_pairs={{0,4},{4,0},{8,12},{12,8},{16,20},{20,16},{24,28},{28,24},{1,5},{5... | collective-permute-start | bytes 393224 | tf_op jit(solution)/shard_map/ppermute | solution.py:285
  40.0 0.2 collective-permute-start.12
  40.1 1.8 %shard_map.115 = (bf16[4,128,128]{2,1,0:T(8,128)(2,1)}, f32[4,128,128]{2,1,0:T(8,128)S(1)}) custom-call(s32[31]{0:T(128)S(1)} %pad_add_fusion.scalars, bf16[4,768,128]{2,1,0:T(8,128)(2,1)S(1)} %get-tuple-element.34.probs, bf16[4,768,128]{2,1,0:T(8,128)(2,1)S(1)} %get-tuple-element.35.grad_scores, bf16[8,256,128]{2,1,0:T(8,128)(2,1)S(1)} %get-tuple-element.36.kv_t, ...), custom_call_target="tpu_custom_call" | custom-call | flops 1000000 | bytes 1000 | tf_op jit(solution)/shard_map/pallas_call | solution.py:246
  42.0 1.2 %collective-permute-done.11 = bf16[4,128,128]{2,1,0:T(8,128)(2,1)S(1)} collective-permute-done((bf16[4,128,128]{2,1,0:T(8,128)(2,1)S(1)}, bf16[4,128,128]{2,1,0:T(8,128)(2,1)S(1)}, u32[]{:S(2)}, u32[]{:S(2)}) %collective-permute-start.11) | collective-permute-done | bytes 131104 | tf_op jit(solution)/shard_map/ppermute | solution.py:285
  43.2 2.4 %collective-permute-done.12 = bf16[4,128,128]{2,1,0:T(8,128)(2,1)S(1)} collective-permute-done((bf16[4,128,128]{2,1,0:T(8,128)(2,1)S(1)}, bf16[4,128,128]{2,1,0:T(8,128)(2,1)S(1)}, u32[]{:S(2)}, u32[]{:S(2)}) %collective-permute-start.12) | collective-permute-done | bytes 131104 | tf_op jit(solution)/shard_map/ppermute | solution.py:285
  45.6 0.7 %fusion.3 = bf16[1,4,128,128]{3,2,1,0:T(8,128)(2,1)} fusion(bf16[4,128,128]{2,1,0:T(8,128)(2,1)S(1)} %collective-permute-done.12, f32[4,128,128]{2,1,0:T(8,128)S(1)} %maximum_add_fusion.1, f32[4,128,128]{2,1,0:T(8,128)S(1)} %get-tuple-element.39, bf16[4,128,128]{2,1,0:T(8,128)(2,1)S(1)} %collective-permute-done.11, pred[128]{0:T(512)(128)(4,1)S(1)} %get-tuple-element.68, ...), kind=kLoop, calls=%fused_computation.16 | loop fusion | flops 524288 | bytes 917760 | tf_op jit(solution)/shard_map/broadcast_in_dim | solution.py:452
  (58 shorter events, 1.4 us)
Async XLA Ops:
  0.6 15.0 %copy-start = (s32[8,2]{0,1:T(2,128)S(1)}, s32[8,2]{0,1:T(2,128)}, u32[]{:S(2)}) copy-start(s32[8,2]{0,1:T(2,128)} %param.16) | copy-start | bytes 196
  0.6 7.2 %copy-start.1 = (bf16[1,4,128,128]{3,2,1,0:T(8,128)(2,1)S(1)}, bf16[1,4,128,128]{3,2,1,0:T(8,128)(2,1)}, u32[]{:S(2)}) copy-start(bf16[1,4,128,128]{3,2,1,0:T(8,128)(2,1)} %param.10) | copy-start | bytes 393220
  0.7 7.2 %collective-permute-start.1 = (bf16[4,128,128]{2,1,0:T(8,128)(2,1)}, bf16[4,128,128]{2,1,0:T(8,128)(2,1)S(1)}, u32[]{:S(2)}, u32[]{:S(2)}) collective-permute-start(bf16[4,128,128]{2,1,0:T(8,128)(2,1)} %bitcast.27), channel_id=1, source_target_pairs={{0,4},{4,0},{8,12},{12,8},{16,20},{20,16},{24,28},{28,24},{1,5},{5... | collective-permute-start | bytes 393224 | tf_op jit(solution)/shard_map/ppermute | solution.py:285
  2.8 10.6 %collective-permute-start = (bf16[4,128,128]{2,1,0:T(8,128)(2,1)}, bf16[4,128,128]{2,1,0:T(8,128)(2,1)S(1)}, u32[]{:S(2)}, u32[]{:S(2)}) collective-permute-start(bf16[4,128,128]{2,1,0:T(8,128)(2,1)} %bitcast.28), channel_id=1, source_target_pairs={{0,24},{4,12},{8,0},{12,20},{16,8},{20,28},{24,16},{28,4},{1,25},{... | collective-permute-start | bytes 393224 | tf_op jit(solution)/shard_map/ppermute | solution.py:285
  6.9 0.7 %copy-start.9 = (s32[8,2]{0,1:T(2,128)S(1)}, s32[8,2]{0,1:T(2,128)}, u32[]{:S(2)}) copy-start(s32[8,2]{0,1:T(2,128)} %constant.27.clone) | copy-start | bytes 196
  6.9 0.7 %copy-start.8 = (s32[8,2]{0,1:T(2,128)S(1)}, s32[8,2]{0,1:T(2,128)}, u32[]{:S(2)}) copy-start(s32[8,2]{0,1:T(2,128)} %param.15) | copy-start | bytes 196
  7.9 8.5 %collective-permute-start.4 = (bf16[4,128,128]{2,1,0:T(8,128)(2,1)S(1)}, bf16[4,128,128]{2,1,0:T(8,128)(2,1)S(1)}, u32[]{:S(2)}, u32[]{:S(2)}) collective-permute-start(bf16[4,128,128]{2,1,0:T(8,128)(2,1)S(1)} %broadcast_select_fusion), channel_id=1, source_target_pairs={{0,8},{4,28},{8,16},{12,4},{16,24},{20,12},{24,0},{28,20},{1,9},{5... | collective-permute-start | bytes 393224 | tf_op jit(solution)/shard_map/ppermute | solution.py:285
  8.0 14.3 %collective-permute-start.6 = (bf16[3,128,128]{2,1,0:T(8,128)(2,1)S(1)}, bf16[3,128,128]{2,1,0:T(8,128)(2,1)S(1)}, u32[]{:S(2)}, u32[]{:S(2)}) collective-permute-start(bf16[3,128,128]{2,1,0:T(8,128)(2,1)S(1)} %slice_select_fusion), channel_id=1, source_target_pairs={{1,10},{2,9},{5,30},{6,29},{9,18},{10,17},{13,6},{14,5},{17,26},{1... | collective-permute-start | bytes 294920 | tf_op jit(solution)/shard_map/ppermute | solution.py:314
  13.5 2.6 %copy-start.7 = (s32[1,4,2,3]{1,2,3,0:T(2,128)S(1)}, s32[1,4,2,3]{1,2,3,0:T(2,128)}, u32[]{:S(2)}) copy-start(s32[1,4,2,3]{1,2,3,0:T(2,128)} %param.17) | copy-start | bytes 292
  13.5 6.5 %copy-start.4 = (bf16[1,4,128,128]{3,2,1,0:T(8,128)(2,1)S(1)}, bf16[1,4,128,128]{3,2,1,0:T(8,128)(2,1)}, u32[]{:S(2)}) copy-start(bf16[1,4,128,128]{3,2,1,0:T(8,128)(2,1)} %param.18) | copy-start | bytes 393220
  13.5 6.5 %copy-start.5 = (bf16[128,128]{1,0:T(8,128)(2,1)S(1)}, bf16[128,128]{1,0:T(8,128)(2,1)}, u32[]{:S(2)}) copy-start(bf16[128,128]{1,0:T(8,128)(2,1)} %k_weight.1) | copy-start | bytes 98308
  13.5 6.5 %copy-start.6 = (bf16[128,128]{1,0:T(8,128)(2,1)S(1)}, bf16[128,128]{1,0:T(8,128)(2,1)}, u32[]{:S(2)}) copy-start(bf16[128,128]{1,0:T(8,128)(2,1)} %v_weight.1) | copy-start | bytes 98308
  13.5 6.4 %copy-start.2 = (bf16[3,3,128,128]{3,2,1,0:T(8,128)(2,1)S(1)}, bf16[3,3,128,128]{3,2,1,0:T(8,128)(2,1)}, u32[]{:S(2)}) copy-start(bf16[3,3,128,128]{3,2,1,0:T(8,128)(2,1)} %conv_weight.1) | copy-start | bytes 884740
  13.6 6.4 %collective-permute-start.3 = (bf16[4,128,128]{2,1,0:T(8,128)(2,1)S(1)}, bf16[4,128,128]{2,1,0:T(8,128)(2,1)S(1)}, u32[]{:S(2)}, u32[]{:S(2)}) collective-permute-start(bf16[4,128,128]{2,1,0:T(8,128)(2,1)S(1)} %get-tuple-element.55), channel_id=1, source_target_pairs={{1,2},{2,1},{5,6},{6,5},{9,10},{10,9},{13,14},{14,13},{17,18},{18,... | collective-permute-start | bytes 393224 | tf_op jit(solution)/shard_map/ppermute | solution.py:21
  16.3 3.7 %copy-start.3 = (bf16[128,128]{1,0:T(8,128)(2,1)S(1)}, bf16[128,128]{1,0:T(8,128)(2,1)}, u32[]{:S(2)}) copy-start(bf16[128,128]{1,0:T(8,128)(2,1)} %q_weight.3) | copy-start | bytes 98308
  16.3 1.4 %collective-permute-start.2 = (bf16[4,128,128]{2,1,0:T(8,128)(2,1)S(1)}, bf16[4,128,128]{2,1,0:T(8,128)(2,1)S(1)}, u32[]{:S(2)}, u32[]{:S(2)}) collective-permute-start(bf16[4,128,128]{2,1,0:T(8,128)(2,1)S(1)} %get-tuple-element.54), channel_id=1, source_target_pairs={{0,1},{2,3},{1,0},{3,2},{4,5},{6,7},{5,4},{7,6},{8,9},{10,11},{9,8... | collective-permute-start | bytes 393224 | tf_op jit(solution)/shard_map/ppermute | solution.py:16
  16.4 5.9 %collective-permute-start.5 = (bf16[3,128,128]{2,1,0:T(8,128)(2,1)S(1)}, bf16[3,128,128]{2,1,0:T(8,128)(2,1)S(1)}, u32[]{:S(2)}, u32[]{:S(2)}) collective-permute-start(bf16[3,128,128]{2,1,0:T(8,128)(2,1)S(1)} %slice_select_fusion.1), channel_id=1, source_target_pairs={{0,1},{2,3},{1,0},{3,2},{4,5},{6,7},{5,4},{7,6},{8,9},{10,11},{9,8... | collective-permute-start | bytes 294920 | tf_op jit(solution)/shard_map/ppermute | solution.py:16
  26.2 1.4 %collective-permute-start.7 = (bf16[4,128,128]{2,1,0:T(8,128)(2,1)S(1)}, bf16[4,128,128]{2,1,0:T(8,128)(2,1)S(1)}, u32[]{:S(2)}, u32[]{:S(2)}) collective-permute-start(bf16[4,128,128]{2,1,0:T(8,128)(2,1)S(1)} %get-tuple-element.41), channel_id=1, source_target_pairs={{0,1},{2,3},{1,0},{3,2},{4,5},{6,7},{5,4},{7,6},{8,9},{10,11},{9,8... | collective-permute-start | bytes 393224 | tf_op jit(solution)/shard_map/ppermute | solution.py:16
  27.7 9.0 %collective-permute-start.8 = (bf16[4,128,128]{2,1,0:T(8,128)(2,1)S(1)}, bf16[4,128,128]{2,1,0:T(8,128)(2,1)S(1)}, u32[]{:S(2)}, u32[]{:S(2)}) collective-permute-start(bf16[4,128,128]{2,1,0:T(8,128)(2,1)S(1)} %fusion), channel_id=1, source_target_pairs={{0,24},{4,12},{8,0},{12,20},{16,8},{20,28},{24,16},{28,4},{1,25},{... | collective-permute-start | bytes 393224 | tf_op jit(solution)/shard_map/ppermute | solution.py:285
  29.7 7.0 %collective-permute-start.9 = (bf16[2,128,128]{2,1,0:T(8,128)(2,1)S(1)}, bf16[2,128,128]{2,1,0:T(8,128)(2,1)S(1)}, u32[]{:S(2)}, u32[]{:S(2)}) collective-permute-start(bf16[2,128,128]{2,1,0:T(8,128)(2,1)S(1)} %slice_select_fusion.3), channel_id=1, source_target_pairs={{1,26},{2,25},{5,14},{6,13},{9,2},{10,1},{13,22},{14,21},{17,10},{... | collective-permute-start | bytes 196616 | tf_op jit(solution)/shard_map/ppermute | solution.py:314
  33.3 5.6 %collective-permute-start.10 = (bf16[2,128,128]{2,1,0:T(8,128)(2,1)S(1)}, bf16[2,128,128]{2,1,0:T(8,128)(2,1)S(1)}, u32[]{:S(2)}, u32[]{:S(2)}) collective-permute-start(bf16[2,128,128]{2,1,0:T(8,128)(2,1)S(1)} %slice_select_fusion.2), channel_id=1, source_target_pairs={{1,2},{2,1},{5,6},{6,5},{9,10},{10,9},{13,14},{14,13},{17,18},{18,... | collective-permute-start | bytes 196616 | tf_op jit(solution)/shard_map/ppermute | solution.py:21
  39.0 4.2 %collective-permute-start.11 = (bf16[4,128,128]{2,1,0:T(8,128)(2,1)S(1)}, bf16[4,128,128]{2,1,0:T(8,128)(2,1)S(1)}, u32[]{:S(2)}, u32[]{:S(2)}) collective-permute-start(bf16[4,128,128]{2,1,0:T(8,128)(2,1)S(1)} %get-tuple-element.50), channel_id=1, source_target_pairs={{0,4},{4,0},{8,12},{12,8},{16,20},{20,16},{24,28},{28,24},{1,5},{5... | collective-permute-start | bytes 393224 | tf_op jit(solution)/shard_map/ppermute | solution.py:285
  40.0 5.6 %collective-permute-start.12 = (bf16[4,128,128]{2,1,0:T(8,128)(2,1)S(1)}, bf16[4,128,128]{2,1,0:T(8,128)(2,1)S(1)}, u32[]{:S(2)}, u32[]{:S(2)}) collective-permute-start(bf16[4,128,128]{2,1,0:T(8,128)(2,1)S(1)} %get-tuple-element.51), channel_id=1, source_target_pairs={{0,8},{4,28},{8,16},{12,4},{16,24},{20,12},{24,0},{28,20},{1,9},{5... | collective-permute-start | bytes 393224 | tf_op jit(solution)/shard_map/ppermute | solution.py:285

commit v15 on v12

--- a/solution.py
+++ b/solution.py
@@ -43,22 +43,19 @@
     )
 
 
-def conv_rows(image, work, out_rows, width, taps):
+def conv_rows(image, out_rows, width, taps):
     count = out_rows * width
     channels = taps.shape[1] // 3
     stacked = jnp.concatenate([image[i * width : i * width + count, :] for i in range(3)], axis=1)
-    work[8 : 8 + count, :] = dot_nn(stacked, taps)
-    none = jnp.zeros((1, channels), jnp.float32)
-    for i in range(out_rows + 1):
-        work[7 + i * width : 8 + i * width, :channels] = none
-        work[8 + i * width : 9 + i * width, 2 * channels :] = none
-    total = work[8 : 8 + count, channels : 2 * channels]
-    total = total + work[7 : 7 + count, :channels]
-    total = total + work[9 : 9 + count, 2 * channels :]
+    parts = dot_nn(stacked, taps)
+    left, middle, right = (parts[:, i * channels : (i + 1) * channels] for i in range(3))
+    column = lax.broadcasted_iota(jnp.int32, (count, channels), 0) & (width - 1)
+    total = middle + jnp.where(column == 0, 0.0, pltpu.roll(left, 1, 0))
+    total = total + jnp.where(column == width - 1, 0.0, pltpu.roll(right, count - 1, 0))
     return total.astype(jnp.bfloat16)
 
 
-def side_keys(slab, odd, between, within, image, work, taps, wkv, kv, kv_t):
+def side_keys(slab, odd, between, within, image, taps, wkv, kv, kv_t):
     rows, width, channels = slab.shape
     halo = MARGIN + 1
     win = rows + 2 * MARGIN
@@ -66,7 +63,7 @@
     image[0 : halo * width, :] = above.reshape(halo * width, channels)
     image[halo * width : (halo + rows) * width, :] = slab.reshape(rows * width, channels)
     image[(halo + rows) * width :, :] = below.reshape(halo * width, channels)
-    hidden = conv_rows(image, work, win, width, taps)
+    hidden = conv_rows(image, win, width, taps)
     kv[...] = dot_nn(hidden, wkv).astype(jnp.bfloat16).reshape(win, width, 2 * channels)
     turned = dot_nt(wkv.T, hidden).astype(jnp.bfloat16)
     for r in range(win):
@@ -122,7 +119,6 @@
     taps,
     wkv,
     image,
-    work,
     kv,
     square,
 ):
@@ -136,12 +132,12 @@
     image[0:width, :] = above
     image[width : (rows + 1) * width, :] = own[...].reshape(rows * width, channels)
     image[(rows + 1) * width : (rows + 2) * width, :] = below
-    hidden = conv_rows(image, work, rows, width, taps[...])
+    hidden = conv_rows(image, rows, width, taps[...])
     queries[...] = (
         dot_nn(hidden, q_weight[...]).astype(jnp.bfloat16).reshape(rows, width, channels)
     )
 
-    side_keys(slab[...], odd, between, within, image, work, taps[...], wkv[...], kv, kv_t)
+    side_keys(slab[...], odd, between, within, image, taps[...], wkv[...], kv, kv_t)
     for b in range(rows):
         squared(queries[b], cotangent[b], square.at[b])
         expo[b], grad_probs[b] = side_scores(
@@ -168,7 +164,6 @@
     grad_scores_out,
     kv_t,
     image,
-    work,
     kv,
     square,
     acc,
@@ -176,7 +171,7 @@
     rows, width, channels = slab.shape
     odd = scalars[0] == 1
     acc[...] = jnp.zeros_like(acc)
-    side_keys(slab[...], odd, between, within, image, work, taps[...], wkv[...], kv, kv_t)
+    side_keys(slab[...], odd, between, within, image, taps[...], wkv[...], kv, kv_t)
 
     for b in range(rows):
         squared(queries[b], cotangent[b], square.at[b])
@@ -350,7 +345,6 @@
 
     conv_scratch = [
         (((win + 2) * width, channels), half),
-        ((win * width + 16, 3 * channels), full),
         ((win, width, 2 * channels), half),
         ((rows, 2 * width, 2 * channels), half),
     ]

time: 45.6 us -> 45.7 us (level)
  no operation moved by 1% of the time
where the time goes in v15:
time: 45.7 us; the launch traced here: 45.2 us
  starting transfers between devices  25.2 us (55%)
  Pallas kernels  8.04 us (18%)
  waiting for transfers between devices  7.3 us (16%)
  local copies, waits for them, and re-layouts  2.31 us (5%)
  other arithmetic  1.36 us (3%)
  between operations  1 us (2%)
    ppermute x6, starting transfers between devices, routed(): return lax.ppermute(value, 'cam', pairs)  10.1 us
    ppermute x2, starting transfers between devices, across(): return lax.ppermute(value, ('cam', 'row'), pairs)  9.21 us
    pallas_call x3, Pallas kernels, on_device(): pl.pallas_call(kernel, out_shape=tuple((jax.ShapeDtypeStruct(*one) for on...  8.04 us
    ppermute x2, starting transfers between devices, swap_between(): return lax.ppermute(value, 'row', pairs + [(j, i) for i, j in pairs])  5.13 us
    ppermute x2, waiting for transfers between devices, across(): return lax.ppermute(value, ('cam', 'row'), pairs)  2.47 us
    ppermute x2, waiting for transfers between devices, swap_between(): return lax.ppermute(value, 'row', pairs + [(j, i) for i, j in pairs])  2.26 us
    ppermute x3, waiting for transfers between devices, swap_within(): return lax.ppermute(value, 'row', pairs + [(j, i) for i, j in pairs])  2.01 us
  transfers between devices with their start and end apart: 13, of which 5 were waited for; matrix products, arithmetic and copies ran while one was open for 5% of the time, Pallas kernels for 9%

profile of v15, /device:TPU:1, one launch (start us, length us, event | category | flops | bytes accessed | tf_op | source)
XLA Modules:
  0.0 45.2 jit_solution(2492898076794301109)
XLA Ops:
  0.7 2.1 %collective-permute-start.1 = (bf16[4,128,128]{2,1,0:T(8,128)(2,1)}, bf16[4,128,128]{2,1,0:T(8,128)(2,1)S(1)}, u32[]{:S(2)}, u32[]{:S(2)}) collective-permute-start(bf16[4,128,128]{2,1,0:T(8,128)(2,1)} %bitcast.26), channel_id=1, source_target_pairs={{0,4},{4,0},{8,12},{12,8},{16,20},{20,16},{24,28},{28,24},{1,5},{5... | collective-permute-start | bytes 393224 | tf_op jit(solution)/shard_map/ppermute | solution.py:280
  2.8 3.3 %collective-permute-start = (bf16[4,128,128]{2,1,0:T(8,128)(2,1)}, bf16[4,128,128]{2,1,0:T(8,128)(2,1)S(1)}, u32[]{:S(2)}, u32[]{:S(2)}) collective-permute-start(bf16[4,128,128]{2,1,0:T(8,128)(2,1)} %bitcast.27), channel_id=1, source_target_pairs={{0,24},{4,12},{8,0},{12,20},{16,8},{20,28},{24,16},{28,4},{1,25},{... | collective-permute-start | bytes 393224 | tf_op jit(solution)/shard_map/ppermute | solution.py:280
  6.1 0.8 %slice_bitcast_fusion.1 = (bf16[1,128,128]{2,1,0:T(8,128)(2,1)S(1)}, bf16[1,128,128]{2,1,0:T(8,128)(2,1)S(1)}) fusion(bf16[1,4,128,128]{3,2,1,0:T(8,128)(2,1)} %param.10), kind=kLoop, calls=%fused_computation.28 | loop fusion | bytes 131072 | tf_op jit(solution)/shard_map/slice | solution.py:323
  6.9 0.7 %copy-done.9 = s32[8,2]{0,1:T(2,128)S(1)} copy-done((s32[8,2]{0,1:T(2,128)S(1)}, s32[8,2]{0,1:T(2,128)}, u32[]{:S(2)}) %copy-start.9) | copy-done | bytes 88
  8.0 5.4 %collective-permute-start.6 = (bf16[3,128,128]{2,1,0:T(8,128)(2,1)S(1)}, bf16[3,128,128]{2,1,0:T(8,128)(2,1)S(1)}, u32[]{:S(2)}, u32[]{:S(2)}) collective-permute-start(bf16[3,128,128]{2,1,0:T(8,128)(2,1)S(1)} %slice_select_fusion), channel_id=1, source_target_pairs={{1,10},{2,9},{5,30},{6,29},{9,18},{10,17},{13,6},{14,5},{17,26},{1... | collective-permute-start | bytes 294920 | tf_op jit(solution)/shard_map/ppermute | solution.py:309
  13.6 2.1 %collective-permute-start.3 = (bf16[4,128,128]{2,1,0:T(8,128)(2,1)S(1)}, bf16[4,128,128]{2,1,0:T(8,128)(2,1)S(1)}, u32[]{:S(2)}, u32[]{:S(2)}) collective-permute-start(bf16[4,128,128]{2,1,0:T(8,128)(2,1)S(1)} %get-tuple-element.51), channel_id=1, source_target_pairs={{1,2},{2,1},{5,6},{6,5},{9,10},{10,9},{13,14},{14,13},{17,18},{18,... | collective-permute-start | bytes 393224 | tf_op jit(solution)/shard_map/ppermute | solution.py:21
  15.6 0.2 dynamic-slice_reduce_fusion
  16.0 0.1 reshape.64
  16.1 0.1 copy.15
  16.2 0.1 reshape.60
  16.4 0.5 %collective-permute-start.5 = (bf16[3,128,128]{2,1,0:T(8,128)(2,1)S(1)}, bf16[3,128,128]{2,1,0:T(8,128)(2,1)S(1)}, u32[]{:S(2)}, u32[]{:S(2)}) collective-permute-start(bf16[3,128,128]{2,1,0:T(8,128)(2,1)S(1)} %slice_select_fusion.1), channel_id=1, source_target_pairs={{0,1},{2,3},{1,0},{3,2},{4,5},{6,7},{5,4},{7,6},{8,9},{10,11},{9,8... | collective-permute-start | bytes 294920 | tf_op jit(solution)/shard_map/ppermute | solution.py:16
  17.0 0.7 %collective-permute-done.2.within = bf16[4,128,128]{2,1,0:T(8,128)(2,1)S(1)} collective-permute-done((bf16[4,128,128]{2,1,0:T(8,128)(2,1)S(1)}, bf16[4,128,128]{2,1,0:T(8,128)(2,1)S(1)}, u32[]{:S(2)}, u32[]{:S(2)}) %collective-permute-start.2) | collective-permute-done | bytes 131104 | tf_op jit(solution)/shard_map/ppermute | solution.py:16
  17.7 2.3 %collective-permute-done.3.between = bf16[4,128,128]{2,1,0:T(8,128)(2,1)S(1)} collective-permute-done((bf16[4,128,128]{2,1,0:T(8,128)(2,1)S(1)}, bf16[4,128,128]{2,1,0:T(8,128)(2,1)S(1)}, u32[]{:S(2)}, u32[]{:S(2)}) %collective-permute-start.3) | collective-permute-done | bytes 131104 | tf_op jit(solution)/shard_map/ppermute | solution.py:21
  20.0 2.4 %shard_map.113 = (bf16[4,128,128]{2,1,0:T(8,128)(2,1)S(1)}, bf16[8,256,128]{2,1,0:T(8,128)(2,1)S(1)}, f32[4,384,128]{2,1,0:T(8,128)S(1)}, f32[4,384,128]{2,1,0:T...) custom-call(s32[31]{0:T(128)S(1)} %pad_add_fusion.scalars, bf16[4,128,128]{2,1,0:T(8,128)(2,1)S(1)} %bitcast.28, ...), custom_call_target="tpu_custom_call" | custom-call | flops 1000000 | bytes 1000 | tf_op jit(solution)/shard_map/pallas_call | solution.py:241
  22.4 3.8 %shard_map.114 = (bf16[4,128,128]{2,1,0:T(8,128)(2,1)S(1)}, bf16[4,128,128]{2,1,0:T(8,128)(2,1)S(1)}, bf16[4,128,128]{2,1,0:T(8,128)(2,1)S(1)}, f32[2,4,128,128]...) custom-call(s32[31]{0:T(128)S(1)} %pad_add_fusion.scalars, ...), custom_call_target="tpu_custom_call" | custom-call | flops 1500000000 | bytes 1500000 | tf_op jit(solution)/shard_map/pallas_call | solution.py:241
  26.3 1.3 %collective-permute-done.7 = bf16[4,128,128]{2,1,0:T(8,128)(2,1)S(1)} collective-permute-done((bf16[4,128,128]{2,1,0:T(8,128)(2,1)S(1)}, bf16[4,128,128]{2,1,0:T(8,128)(2,1)S(1)}, u32[]{:S(2)}, u32[]{:S(2)}) %collective-permute-start.7) | collective-permute-done | bytes 131104 | tf_op jit(solution)/shard_map/ppermute | solution.py:16
  27.8 2.0 %collective-permute-start.9 = (bf16[4,128,128]{2,1,0:T(8,128)(2,1)S(1)}, bf16[4,128,128]{2,1,0:T(8,128)(2,1)S(1)}, u32[]{:S(2)}, u32[]{:S(2)}) collective-permute-start(bf16[4,128,128]{2,1,0:T(8,128)(2,1)S(1)} %fusion.2), channel_id=1, source_target_pairs={{0,24},{4,12},{8,0},{12,20},{16,8},{20,28},{24,16},{28,4},{1,25},{... | collective-permute-start | bytes 393224 | tf_op jit(solution)/shard_map/ppermute | solution.py:280
  29.8 3.1 %collective-permute-start.8 = (bf16[2,128,128]{2,1,0:T(8,128)(2,1)S(1)}, bf16[2,128,128]{2,1,0:T(8,128)(2,1)S(1)}, u32[]{:S(2)}, u32[]{:S(2)}) collective-permute-start(bf16[2,128,128]{2,1,0:T(8,128)(2,1)S(1)} %slice_select_fusion.3), channel_id=1, source_target_pairs={{1,2},{2,1},{5,6},{6,5},{9,10},{10,9},{13,14},{14,13},{17,18},{18,... | collective-permute-start | bytes 196616 | tf_op jit(solution)/shard_map/ppermute | solution.py:21
  32.9 3.8 %collective-permute-start.10 = (bf16[2,128,128]{2,1,0:T(8,128)(2,1)S(1)}, bf16[2,128,128]{2,1,0:T(8,128)(2,1)S(1)}, u32[]{:S(2)}, u32[]{:S(2)}) collective-permute-start(bf16[2,128,128]{2,1,0:T(8,128)(2,1)S(1)} %slice_select_fusion.2), channel_id=1, source_target_pairs={{1,26},{2,25},{5,14},{6,13},{9,2},{10,1},{13,22},{14,21},{17,10},{... | collective-permute-start | bytes 196616 | tf_op jit(solution)/shard_map/ppermute | solution.py:309
  36.9 2.5 %collective-permute-done.10 = bf16[2,128,128]{2,1,0:T(8,128)(2,1)S(1)} collective-permute-done((bf16[2,128,128]{2,1,0:T(8,128)(2,1)S(1)}, bf16[2,128,128]{2,1,0:T(8,128)(2,1)S(1)}, u32[]{:S(2)}, u32[]{:S(2)}) %collective-permute-start.10) | collective-permute-done | bytes 65568 | tf_op jit(solution)/shard_map/ppermute | solution.py:309
  39.5 2.6 %collective-permute-start.11 = (bf16[4,128,128]{2,1,0:T(8,128)(2,1)S(1)}, bf16[4,128,128]{2,1,0:T(8,128)(2,1)S(1)}, u32[]{:S(2)}, u32[]{:S(2)}) collective-permute-start(bf16[4,128,128]{2,1,0:T(8,128)(2,1)S(1)} %add_convert_fusion.1), channel_id=1, source_target_pairs={{0,4},{4,0},{8,12},{12,8},{16,20},{20,16},{24,28},{28,24},{1,5},{5... | collective-permute-start | bytes 393224 | tf_op jit(solution)/shard_map/ppermute | solution.py:280
  42.1 1.8 %shard_map.115 = (bf16[4,128,128]{2,1,0:T(8,128)(2,1)}, f32[4,128,128]{2,1,0:T(8,128)S(1)}) custom-call(s32[31]{0:T(128)S(1)} %pad_add_fusion.scalars, bf16[4,768,128]{2,1,0:T(8,128)(2,1)S(1)} %get-tuple-element.33.probs, bf16[4,768,128]{2,1,0:T(8,128)(2,1)S(1)} %get-tuple-element.34.grad_scores, bf16[8,256,128]{2,1,0:T(8,128)(2,1)S(1)} %get-tuple-element.35.kv_t, ...), custom_call_target="tpu_custom_call" | custom-call | flops 1000000 | bytes 1000 | tf_op jit(solution)/shard_map/pallas_call | solution.py:241
  43.9 0.5 %collective-permute-done.11 = bf16[4,128,128]{2,1,0:T(8,128)(2,1)S(1)} collective-permute-done((bf16[4,128,128]{2,1,0:T(8,128)(2,1)S(1)}, bf16[4,128,128]{2,1,0:T(8,128)(2,1)S(1)}, u32[]{:S(2)}, u32[]{:S(2)}) %collective-permute-start.11) | collective-permute-done | bytes 131104 | tf_op jit(solution)/shard_map/ppermute | solution.py:280
  44.4 0.7 %fusion.3 = bf16[1,4,128,128]{3,2,1,0:T(8,128)(2,1)} fusion(bf16[4,128,128]{2,1,0:T(8,128)(2,1)S(1)} %collective-permute-done.12, f32[2,128,128]{2,1,0:T(8,128)S(1)} %get-tuple-element.61, f32[2,128,128]{2,1,0:T(8,128)S(1)} %get-tuple-element.60, bf16[4,128,128]{2,1,0:T(8,128)(2,1)S(1)} %collective-permute-done.9, f32[4,128,128]{2,1,0:T(8,128)S(1)} %get-tuple-element.38, ...), kind=kLoop, calls=%fused_computation.18 | loop fusion | flops 720896 | bytes 1048832 | tf_op jit(solution)/shard_map/broadcast_in_dim | solution.py:447
  (58 shorter events, 1.3 us)
Async XLA Ops:
  0.6 15.0 %copy-start = (s32[8,2]{0,1:T(2,128)S(1)}, s32[8,2]{0,1:T(2,128)}, u32[]{:S(2)}) copy-start(s32[8,2]{0,1:T(2,128)} %param.16) | copy-start | bytes 196
  0.6 7.2 %copy-start.1 = (bf16[1,4,128,128]{3,2,1,0:T(8,128)(2,1)S(1)}, bf16[1,4,128,128]{3,2,1,0:T(8,128)(2,1)}, u32[]{:S(2)}) copy-start(bf16[1,4,128,128]{3,2,1,0:T(8,128)(2,1)} %param.10) | copy-start | bytes 393220
  0.7 7.2 %collective-permute-start.1 = (bf16[4,128,128]{2,1,0:T(8,128)(2,1)}, bf16[4,128,128]{2,1,0:T(8,128)(2,1)S(1)}, u32[]{:S(2)}, u32[]{:S(2)}) collective-permute-start(bf16[4,128,128]{2,1,0:T(8,128)(2,1)} %bitcast.26), channel_id=1, source_target_pairs={{0,4},{4,0},{8,12},{12,8},{16,20},{20,16},{24,28},{28,24},{1,5},{5... | collective-permute-start | bytes 393224 | tf_op jit(solution)/shard_map/ppermute | solution.py:280
  2.8 10.6 %collective-permute-start = (bf16[4,128,128]{2,1,0:T(8,128)(2,1)}, bf16[4,128,128]{2,1,0:T(8,128)(2,1)S(1)}, u32[]{:S(2)}, u32[]{:S(2)}) collective-permute-start(bf16[4,128,128]{2,1,0:T(8,128)(2,1)} %bitcast.27), channel_id=1, source_target_pairs={{0,24},{4,12},{8,0},{12,20},{16,8},{20,28},{24,16},{28,4},{1,25},{... | collective-permute-start | bytes 393224 | tf_op jit(solution)/shard_map/ppermute | solution.py:280
  6.9 0.7 %copy-start.9 = (s32[8,2]{0,1:T(2,128)S(1)}, s32[8,2]{0,1:T(2,128)}, u32[]{:S(2)}) copy-start(s32[8,2]{0,1:T(2,128)} %constant.27.clone) | copy-start | bytes 196
  6.9 0.7 %copy-start.8 = (s32[8,2]{0,1:T(2,128)S(1)}, s32[8,2]{0,1:T(2,128)}, u32[]{:S(2)}) copy-start(s32[8,2]{0,1:T(2,128)} %param.15) | copy-start | bytes 196
  7.9 8.5 %collective-permute-start.4 = (bf16[4,128,128]{2,1,0:T(8,128)(2,1)S(1)}, bf16[4,128,128]{2,1,0:T(8,128)(2,1)S(1)}, u32[]{:S(2)}, u32[]{:S(2)}) collective-permute-start(bf16[4,128,128]{2,1,0:T(8,128)(2,1)S(1)} %broadcast_select_fusion), channel_id=1, source_target_pairs={{0,8},{4,28},{8,16},{12,4},{16,24},{20,12},{24,0},{28,20},{1,9},{5... | collective-permute-start | bytes 393224 | tf_op jit(solution)/shard_map/ppermute | solution.py:280
  8.0 14.4 %collective-permute-start.6 = (bf16[3,128,128]{2,1,0:T(8,128)(2,1)S(1)}, bf16[3,128,128]{2,1,0:T(8,128)(2,1)S(1)}, u32[]{:S(2)}, u32[]{:S(2)}) collective-permute-start(bf16[3,128,128]{2,1,0:T(8,128)(2,1)S(1)} %slice_select_fusion), channel_id=1, source_target_pairs={{1,10},{2,9},{5,30},{6,29},{9,18},{10,17},{13,6},{14,5},{17,26},{1... | collective-permute-start | bytes 294920 | tf_op jit(solution)/shard_map/ppermute | solution.py:309
  13.5 2.6 %copy-start.7 = (s32[1,4,2,3]{1,2,3,0:T(2,128)S(1)}, s32[1,4,2,3]{1,2,3,0:T(2,128)}, u32[]{:S(2)}) copy-start(s32[1,4,2,3]{1,2,3,0:T(2,128)} %param.17) | copy-start | bytes 292
  13.5 6.5 %copy-start.4 = (bf16[1,4,128,128]{3,2,1,0:T(8,128)(2,1)S(1)}, bf16[1,4,128,128]{3,2,1,0:T(8,128)(2,1)}, u32[]{:S(2)}) copy-start(bf16[1,4,128,128]{3,2,1,0:T(8,128)(2,1)} %param.18) | copy-start | bytes 393220
  13.5 6.5 %copy-start.5 = (bf16[128,128]{1,0:T(8,128)(2,1)S(1)}, bf16[128,128]{1,0:T(8,128)(2,1)}, u32[]{:S(2)}) copy-start(bf16[128,128]{1,0:T(8,128)(2,1)} %k_weight.1) | copy-start | bytes 98308
  13.5 6.5 %copy-start.6 = (bf16[128,128]{1,0:T(8,128)(2,1)S(1)}, bf16[128,128]{1,0:T(8,128)(2,1)}, u32[]{:S(2)}) copy-start(bf16[128,128]{1,0:T(8,128)(2,1)} %v_weight.1) | copy-start | bytes 98308
  13.5 6.4 %copy-start.2 = (bf16[3,3,128,128]{3,2,1,0:T(8,128)(2,1)S(1)}, bf16[3,3,128,128]{3,2,1,0:T(8,128)(2,1)}, u32[]{:S(2)}) copy-start(bf16[3,3,128,128]{3,2,1,0:T(8,128)(2,1)} %conv_weight.1) | copy-start | bytes 884740
  13.6 6.4 %collective-permute-start.3 = (bf16[4,128,128]{2,1,0:T(8,128)(2,1)S(1)}, bf16[4,128,128]{2,1,0:T(8,128)(2,1)S(1)}, u32[]{:S(2)}, u32[]{:S(2)}) collective-permute-start(bf16[4,128,128]{2,1,0:T(8,128)(2,1)S(1)} %get-tuple-element.51), channel_id=1, source_target_pairs={{1,2},{2,1},{5,6},{6,5},{9,10},{10,9},{13,14},{14,13},{17,18},{18,... | collective-permute-start | bytes 393224 | tf_op jit(solution)/shard_map/ppermute | solution.py:21
  16.3 3.7 %copy-start.3 = (bf16[128,128]{1,0:T(8,128)(2,1)S(1)}, bf16[128,128]{1,0:T(8,128)(2,1)}, u32[]{:S(2)}) copy-start(bf16[128,128]{1,0:T(8,128)(2,1)} %q_weight.3) | copy-start | bytes 98308
  16.3 1.4 %collective-permute-start.2 = (bf16[4,128,128]{2,1,0:T(8,128)(2,1)S(1)}, bf16[4,128,128]{2,1,0:T(8,128)(2,1)S(1)}, u32[]{:S(2)}, u32[]{:S(2)}) collective-permute-start(bf16[4,128,128]{2,1,0:T(8,128)(2,1)S(1)} %get-tuple-element.50), channel_id=1, source_target_pairs={{0,1},{2,3},{1,0},{3,2},{4,5},{6,7},{5,4},{7,6},{8,9},{10,11},{9,8... | collective-permute-start | bytes 393224 | tf_op jit(solution)/shard_map/ppermute | solution.py:16
  16.4 6.0 %collective-permute-start.5 = (bf16[3,128,128]{2,1,0:T(8,128)(2,1)S(1)}, bf16[3,128,128]{2,1,0:T(8,128)(2,1)S(1)}, u32[]{:S(2)}, u32[]{:S(2)}) collective-permute-start(bf16[3,128,128]{2,1,0:T(8,128)(2,1)S(1)} %slice_select_fusion.1), channel_id=1, source_target_pairs={{0,1},{2,3},{1,0},{3,2},{4,5},{6,7},{5,4},{7,6},{8,9},{10,11},{9,8... | collective-permute-start | bytes 294920 | tf_op jit(solution)/shard_map/ppermute | solution.py:16
  26.3 1.4 %collective-permute-start.7 = (bf16[4,128,128]{2,1,0:T(8,128)(2,1)S(1)}, bf16[4,128,128]{2,1,0:T(8,128)(2,1)S(1)}, u32[]{:S(2)}, u32[]{:S(2)}) collective-permute-start(bf16[4,128,128]{2,1,0:T(8,128)(2,1)S(1)} %get-tuple-element.40), channel_id=1, source_target_pairs={{0,1},{2,3},{1,0},{3,2},{4,5},{6,7},{5,4},{7,6},{8,9},{10,11},{9,8... | collective-permute-start | bytes 393224 | tf_op jit(solution)/shard_map/ppermute | solution.py:16
  27.8 11.6 %collective-permute-start.9 = (bf16[4,128,128]{2,1,0:T(8,128)(2,1)S(1)}, bf16[4,128,128]{2,1,0:T(8,128)(2,1)S(1)}, u32[]{:S(2)}, u32[]{:S(2)}) collective-permute-start(bf16[4,128,128]{2,1,0:T(8,128)(2,1)S(1)} %fusion.2), channel_id=1, source_target_pairs={{0,24},{4,12},{8,0},{12,20},{16,8},{20,28},{24,16},{28,4},{1,25},{... | collective-permute-start | bytes 393224 | tf_op jit(solution)/shard_map/ppermute | solution.py:280
  29.8 7.0 %collective-permute-start.8 = (bf16[2,128,128]{2,1,0:T(8,128)(2,1)S(1)}, bf16[2,128,128]{2,1,0:T(8,128)(2,1)S(1)}, u32[]{:S(2)}, u32[]{:S(2)}) collective-permute-start(bf16[2,128,128]{2,1,0:T(8,128)(2,1)S(1)} %slice_select_fusion.3), channel_id=1, source_target_pairs={{1,2},{2,1},{5,6},{6,5},{9,10},{10,9},{13,14},{14,13},{17,18},{18,... | collective-permute-start | bytes 196616 | tf_op jit(solution)/shard_map/ppermute | solution.py:21
  32.9 6.5 %collective-permute-start.10 = (bf16[2,128,128]{2,1,0:T(8,128)(2,1)S(1)}, bf16[2,128,128]{2,1,0:T(8,128)(2,1)S(1)}, u32[]{:S(2)}, u32[]{:S(2)}) collective-permute-start(bf16[2,128,128]{2,1,0:T(8,128)(2,1)S(1)} %slice_select_fusion.2), channel_id=1, source_target_pairs={{1,26},{2,25},{5,14},{6,13},{9,2},{10,1},{13,22},{14,21},{17,10},{... | collective-permute-start | bytes 196616 | tf_op jit(solution)/shard_map/ppermute | solution.py:309
  36.8 7.0 %collective-permute-start.12 = (bf16[4,128,128]{2,1,0:T(8,128)(2,1)S(1)}, bf16[4,128,128]{2,1,0:T(8,128)(2,1)S(1)}, u32[]{:S(2)}, u32[]{:S(2)}) collective-permute-start(bf16[4,128,128]{2,1,0:T(8,128)(2,1)S(1)} %fusion.1), channel_id=1, source_target_pairs={{0,8},{4,28},{8,16},{12,4},{16,24},{20,12},{24,0},{28,20},{1,9},{5... | collective-permute-start | bytes 393224 | tf_op jit(solution)/shard_map/ppermute | solution.py:280
  39.5 4.9 %collective-permute-start.11 = (bf16[4,128,128]{2,1,0:T(8,128)(2,1)S(1)}, bf16[4,128,128]{2,1,0:T(8,128)(2,1)S(1)}, u32[]{:S(2)}, u32[]{:S(2)}) collective-permute-start(bf16[4,128,128]{2,1,0:T(8,128)(2,1)S(1)} %add_convert_fusion.1), channel_id=1, source_target_pairs={{0,4},{4,0},{8,12},{12,8},{16,20},{20,16},{24,28},{28,24},{1,5},{5... | collective-permute-start | bytes 393224 | tf_op jit(solution)/shard_map/ppermute | solution.py:280

commit v16 on v12

--- a/solution.py
+++ b/solution.py
@@ -1,6 +1,5 @@
 import jax
 import jax.numpy as jnp
-import numpy as np
 from jax import lax
 from jax.experimental import pallas as pl
 from jax.experimental.pallas import tpu as pltpu
@@ -294,8 +293,8 @@
     def around(place):
         return place & (views - 1) if views & (views - 1) == 0 else lax.rem(place + views, views)
 
-    near_partner = np.arange(views)[:, None] + samples * np.array([[-1, 1]])
-    near = (partners == np.mod(near_partner, views).astype(np.int32)).astype(full)
+    place, side = (lax.broadcasted_iota(jnp.int32, (views, 2), dim) for dim in range(2))
+    near = (partners == around(place + (2 * side - 1) * samples)).astype(full)
     near = jnp.broadcast_to(near.reshape(2 * views, 1), (2 * views, channels))
     near = lax.optimization_barrier(near)
 

time: 45.6 us -> 45.6 us (level)
  no operation moved by 1% of the time
where the time goes in v16:
time: 45.6 us; the launch traced here: 45.1 us
  starting transfers between devices  25.2 us (55%)
  Pallas kernels  7.97 us (17%)
  waiting for transfers between devices  7.2 us (16%)
  local copies, waits for them, and re-layouts  2.3 us (5%)
  other arithmetic  1.44 us (3%)
  between operations  0.99 us (2%)
    ppermute x6, starting transfers between devices, routed(): return lax.ppermute(value, 'cam', pairs)  10.2 us
    ppermute x2, starting transfers between devices, across(): return lax.ppermute(value, ('cam', 'row'), pairs)  9.26 us
    pallas_call x3, Pallas kernels, on_device(): pl.pallas_call(kernel, out_shape=tuple((jax.ShapeDtypeStruct(*one) for on...  7.97 us
    ppermute x2, starting transfers between devices, swap_between(): return lax.ppermute(value, 'row', pairs + [(j, i) for i, j in pairs])  5.08 us
    ppermute x2, waiting for transfers between devices, across(): return lax.ppermute(value, ('cam', 'row'), pairs)  2.37 us
    ppermute x2, waiting for transfers between devices, swap_between(): return lax.ppermute(value, 'row', pairs + [(j, i) for i, j in pairs])  2.26 us
    ppermute x3, waiting for transfers between devices, swap_within(): return lax.ppermute(value, 'row', pairs + [(j, i) for i, j in pairs])  2.01 us
  transfers between devices with their start and end apart: 13, of which 5 were waited for; matrix products, arithmetic and copies ran while one was open for 5% of the time, Pallas kernels for 9%

profile of v16, /device:TPU:1, one launch (start us, length us, event | category | flops | bytes accessed | tf_op | source)
XLA Modules:
  0.0 45.1 jit_solution(13037196838108914387)
XLA Ops:
  0.7 2.1 %collective-permute-start.1 = (bf16[4,128,128]{2,1,0:T(8,128)(2,1)}, bf16[4,128,128]{2,1,0:T(8,128)(2,1)S(1)}, u32[]{:S(2)}, u32[]{:S(2)}) collective-permute-start(bf16[4,128,128]{2,1,0:T(8,128)(2,1)} %bitcast.26), channel_id=1, source_target_pairs={{0,4},{4,0},{8,12},{12,8},{16,20},{20,16},{24,28},{28,24},{1,5},{5... | collective-permute-start | bytes 393224 | tf_op jit(solution)/shard_map/ppermute | solution.py:284
  2.8 3.3 %collective-permute-start = (bf16[4,128,128]{2,1,0:T(8,128)(2,1)}, bf16[4,128,128]{2,1,0:T(8,128)(2,1)S(1)}, u32[]{:S(2)}, u32[]{:S(2)}) collective-permute-start(bf16[4,128,128]{2,1,0:T(8,128)(2,1)} %bitcast.27), channel_id=1, source_target_pairs={{0,24},{4,12},{8,0},{12,20},{16,8},{20,28},{24,16},{28,4},{1,25},{... | collective-permute-start | bytes 393224 | tf_op jit(solution)/shard_map/ppermute | solution.py:284
  6.1 0.8 %slice_bitcast_fusion.1 = (bf16[1,128,128]{2,1,0:T(8,128)(2,1)S(1)}, bf16[1,128,128]{2,1,0:T(8,128)(2,1)S(1)}) fusion(bf16[1,4,128,128]{3,2,1,0:T(8,128)(2,1)} %param.9), kind=kLoop, calls=%fused_computation.28 | loop fusion | bytes 131072 | tf_op jit(solution)/shard_map/slice | solution.py:327
  6.9 0.7 %copy-done.8 = s32[8,2]{0,1:T(2,128)S(1)} copy-done((s32[8,2]{0,1:T(2,128)S(1)}, s32[8,2]{0,1:T(2,128)}, u32[]{:S(2)}) %copy-start.8) | copy-done | bytes 88
  8.1 5.3 %collective-permute-start.6 = (bf16[3,128,128]{2,1,0:T(8,128)(2,1)S(1)}, bf16[3,128,128]{2,1,0:T(8,128)(2,1)S(1)}, u32[]{:S(2)}, u32[]{:S(2)}) collective-permute-start(bf16[3,128,128]{2,1,0:T(8,128)(2,1)S(1)} %slice_select_fusion), channel_id=1, source_target_pairs={{1,10},{2,9},{5,30},{6,29},{9,18},{10,17},{13,6},{14,5},{17,26},{1... | collective-permute-start | bytes 294920 | tf_op jit(solution)/shard_map/ppermute | solution.py:313
  13.6 2.1 %collective-permute-start.3 = (bf16[4,128,128]{2,1,0:T(8,128)(2,1)S(1)}, bf16[4,128,128]{2,1,0:T(8,128)(2,1)S(1)}, u32[]{:S(2)}, u32[]{:S(2)}) collective-permute-start(bf16[4,128,128]{2,1,0:T(8,128)(2,1)S(1)} %get-tuple-element.51), channel_id=1, source_target_pairs={{1,2},{2,1},{5,6},{6,5},{9,10},{10,9},{13,14},{14,13},{17,18},{18,... | collective-permute-start | bytes 393224 | tf_op jit(solution)/shard_map/ppermute | solution.py:20
  15.6 0.2 dynamic-slice_reduce_fusion
  16.0 0.1 reshape.64
  16.1 0.1 copy.14
  16.2 0.1 reshape.60
  16.4 0.5 %collective-permute-start.5 = (bf16[3,128,128]{2,1,0:T(8,128)(2,1)S(1)}, bf16[3,128,128]{2,1,0:T(8,128)(2,1)S(1)}, u32[]{:S(2)}, u32[]{:S(2)}) collective-permute-start(bf16[3,128,128]{2,1,0:T(8,128)(2,1)S(1)} %slice_select_fusion.1), channel_id=1, source_target_pairs={{0,1},{2,3},{1,0},{3,2},{4,5},{6,7},{5,4},{7,6},{8,9},{10,11},{9,8... | collective-permute-start | bytes 294920 | tf_op jit(solution)/shard_map/ppermute | solution.py:15
  17.0 0.7 %collective-permute-done.2.within = bf16[4,128,128]{2,1,0:T(8,128)(2,1)S(1)} collective-permute-done((bf16[4,128,128]{2,1,0:T(8,128)(2,1)S(1)}, bf16[4,128,128]{2,1,0:T(8,128)(2,1)S(1)}, u32[]{:S(2)}, u32[]{:S(2)}) %collective-permute-start.2) | collective-permute-done | bytes 131104 | tf_op jit(solution)/shard_map/ppermute | solution.py:15
  17.7 2.3 %collective-permute-done.3.between = bf16[4,128,128]{2,1,0:T(8,128)(2,1)S(1)} collective-permute-done((bf16[4,128,128]{2,1,0:T(8,128)(2,1)S(1)}, bf16[4,128,128]{2,1,0:T(8,128)(2,1)S(1)}, u32[]{:S(2)}, u32[]{:S(2)}) %collective-permute-start.3) | collective-permute-done | bytes 131104 | tf_op jit(solution)/shard_map/ppermute | solution.py:20
  20.0 2.3 %shard_map.104 = (bf16[4,128,128]{2,1,0:T(8,128)(2,1)S(1)}, bf16[8,256,128]{2,1,0:T(8,128)(2,1)S(1)}, f32[4,384,128]{2,1,0:T(8,128)S(1)}, f32[4,384,128]{2,1,0:T...) custom-call(s32[31]{0:T(128)S(1)} %pad_add_fusion.scalars, bf16[4,128,128]{2,1,0:T(8,128)(2,1)S(1)} %bitcast.28, ...), custom_call_target="tpu_custom_call" | custom-call | flops 1000000 | bytes 1000 | tf_op jit(solution)/shard_map/pallas_call | solution.py:245
  22.3 3.9 %shard_map.105 = (bf16[4,128,128]{2,1,0:T(8,128)(2,1)S(1)}, bf16[4,128,128]{2,1,0:T(8,128)(2,1)S(1)}, bf16[4,128,128]{2,1,0:T(8,128)(2,1)S(1)}, f32[2,4,128,128]...) custom-call(s32[31]{0:T(128)S(1)} %pad_add_fusion.scalars, ...), custom_call_target="tpu_custom_call" | custom-call | flops 1500000000 | bytes 1500000 | tf_op jit(solution)/shard_map/pallas_call | solution.py:245
  26.3 1.3 %collective-permute-done.7 = bf16[4,128,128]{2,1,0:T(8,128)(2,1)S(1)} collective-permute-done((bf16[4,128,128]{2,1,0:T(8,128)(2,1)S(1)}, bf16[4,128,128]{2,1,0:T(8,128)(2,1)S(1)}, u32[]{:S(2)}, u32[]{:S(2)}) %collective-permute-start.7) | collective-permute-done | bytes 131104 | tf_op jit(solution)/shard_map/ppermute | solution.py:15
  27.7 2.0 %collective-permute-start.9 = (bf16[4,128,128]{2,1,0:T(8,128)(2,1)S(1)}, bf16[4,128,128]{2,1,0:T(8,128)(2,1)S(1)}, u32[]{:S(2)}, u32[]{:S(2)}) collective-permute-start(bf16[4,128,128]{2,1,0:T(8,128)(2,1)S(1)} %fusion.2), channel_id=1, source_target_pairs={{0,24},{4,12},{8,0},{12,20},{16,8},{20,28},{24,16},{28,4},{1,25},{... | collective-permute-start | bytes 393224 | tf_op jit(solution)/shard_map/ppermute | solution.py:284
  29.7 3.0 %collective-permute-start.8 = (bf16[2,128,128]{2,1,0:T(8,128)(2,1)S(1)}, bf16[2,128,128]{2,1,0:T(8,128)(2,1)S(1)}, u32[]{:S(2)}, u32[]{:S(2)}) collective-permute-start(bf16[2,128,128]{2,1,0:T(8,128)(2,1)S(1)} %slice_select_fusion.3), channel_id=1, source_target_pairs={{1,2},{2,1},{5,6},{6,5},{9,10},{10,9},{13,14},{14,13},{17,18},{18,... | collective-permute-start | bytes 196616 | tf_op jit(solution)/shard_map/ppermute | solution.py:20
  32.8 3.9 %collective-permute-start.10 = (bf16[2,128,128]{2,1,0:T(8,128)(2,1)S(1)}, bf16[2,128,128]{2,1,0:T(8,128)(2,1)S(1)}, u32[]{:S(2)}, u32[]{:S(2)}) collective-permute-start(bf16[2,128,128]{2,1,0:T(8,128)(2,1)S(1)} %slice_select_fusion.2), channel_id=1, source_target_pairs={{1,26},{2,25},{5,14},{6,13},{9,2},{10,1},{13,22},{14,21},{17,10},{... | collective-permute-start | bytes 196616 | tf_op jit(solution)/shard_map/ppermute | solution.py:313
  36.9 2.4 %collective-permute-done.10 = bf16[2,128,128]{2,1,0:T(8,128)(2,1)S(1)} collective-permute-done((bf16[2,128,128]{2,1,0:T(8,128)(2,1)S(1)}, bf16[2,128,128]{2,1,0:T(8,128)(2,1)S(1)}, u32[]{:S(2)}, u32[]{:S(2)}) %collective-permute-start.10) | collective-permute-done | bytes 65568 | tf_op jit(solution)/shard_map/ppermute | solution.py:313
  39.4 2.6 %collective-permute-start.11 = (bf16[4,128,128]{2,1,0:T(8,128)(2,1)S(1)}, bf16[4,128,128]{2,1,0:T(8,128)(2,1)S(1)}, u32[]{:S(2)}, u32[]{:S(2)}) collective-permute-start(bf16[4,128,128]{2,1,0:T(8,128)(2,1)S(1)} %add_convert_fusion.1), channel_id=1, source_target_pairs={{0,4},{4,0},{8,12},{12,8},{16,20},{20,16},{24,28},{28,24},{1,5},{5... | collective-permute-start | bytes 393224 | tf_op jit(solution)/shard_map/ppermute | solution.py:284
  42.0 1.8 %shard_map.106 = (bf16[4,128,128]{2,1,0:T(8,128)(2,1)}, f32[4,128,128]{2,1,0:T(8,128)S(1)}) custom-call(s32[31]{0:T(128)S(1)} %pad_add_fusion.scalars, bf16[4,768,128]{2,1,0:T(8,128)(2,1)S(1)} %get-tuple-element.33.probs, bf16[4,768,128]{2,1,0:T(8,128)(2,1)S(1)} %get-tuple-element.34.grad_scores, bf16[8,256,128]{2,1,0:T(8,128)(2,1)S(1)} %get-tuple-element.35.kv_t, ...), custom_call_target="tpu_custom_call" | custom-call | flops 1000000 | bytes 1000 | tf_op jit(solution)/shard_map/pallas_call | solution.py:245
  43.8 0.5 %collective-permute-done.11 = bf16[4,128,128]{2,1,0:T(8,128)(2,1)S(1)} collective-permute-done((bf16[4,128,128]{2,1,0:T(8,128)(2,1)S(1)}, bf16[4,128,128]{2,1,0:T(8,128)(2,1)S(1)}, u32[]{:S(2)}, u32[]{:S(2)}) %collective-permute-start.11) | collective-permute-done | bytes 131104 | tf_op jit(solution)/shard_map/ppermute | solution.py:284
  44.4 0.7 %fusion.3 = bf16[1,4,128,128]{3,2,1,0:T(8,128)(2,1)} fusion(bf16[4,128,128]{2,1,0:T(8,128)(2,1)S(1)} %collective-permute-done.12, f32[2,128,128]{2,1,0:T(8,128)S(1)} %get-tuple-element.61, f32[2,128,128]{2,1,0:T(8,128)S(1)} %get-tuple-element.60, bf16[4,128,128]{2,1,0:T(8,128)(2,1)S(1)} %collective-permute-done.9, f32[4,128,128]{2,1,0:T(8,128)S(1)} %get-tuple-element.38, ...), kind=kLoop, calls=%fused_computation.18 | loop fusion | flops 720896 | bytes 1048832 | tf_op jit(solution)/shard_map/broadcast_in_dim | solution.py:452
  (57 shorter events, 1.3 us)
Async XLA Ops:
  0.6 15.0 %copy-start = (s32[8,2]{0,1:T(2,128)S(1)}, s32[8,2]{0,1:T(2,128)}, u32[]{:S(2)}) copy-start(s32[8,2]{0,1:T(2,128)} %param.15) | copy-start | bytes 196
  0.6 7.3 %copy-start.1 = (bf16[1,4,128,128]{3,2,1,0:T(8,128)(2,1)S(1)}, bf16[1,4,128,128]{3,2,1,0:T(8,128)(2,1)}, u32[]{:S(2)}) copy-start(bf16[1,4,128,128]{3,2,1,0:T(8,128)(2,1)} %param.9) | copy-start | bytes 393220
  0.7 7.3 %collective-permute-start.1 = (bf16[4,128,128]{2,1,0:T(8,128)(2,1)}, bf16[4,128,128]{2,1,0:T(8,128)(2,1)S(1)}, u32[]{:S(2)}, u32[]{:S(2)}) collective-permute-start(bf16[4,128,128]{2,1,0:T(8,128)(2,1)} %bitcast.26), channel_id=1, source_target_pairs={{0,4},{4,0},{8,12},{12,8},{16,20},{20,16},{24,28},{28,24},{1,5},{5... | collective-permute-start | bytes 393224 | tf_op jit(solution)/shard_map/ppermute | solution.py:284
  2.8 10.6 %collective-permute-start = (bf16[4,128,128]{2,1,0:T(8,128)(2,1)}, bf16[4,128,128]{2,1,0:T(8,128)(2,1)S(1)}, u32[]{:S(2)}, u32[]{:S(2)}) collective-permute-start(bf16[4,128,128]{2,1,0:T(8,128)(2,1)} %bitcast.27), channel_id=1, source_target_pairs={{0,24},{4,12},{8,0},{12,20},{16,8},{20,28},{24,16},{28,4},{1,25},{... | collective-permute-start | bytes 393224 | tf_op jit(solution)/shard_map/ppermute | solution.py:284
  6.9 0.7 %copy-start.8 = (s32[8,2]{0,1:T(2,128)S(1)}, s32[8,2]{0,1:T(2,128)}, u32[]{:S(2)}) copy-start(s32[8,2]{0,1:T(2,128)} %param.14) | copy-start | bytes 196
  8.0 8.4 %collective-permute-start.4 = (bf16[4,128,128]{2,1,0:T(8,128)(2,1)S(1)}, bf16[4,128,128]{2,1,0:T(8,128)(2,1)S(1)}, u32[]{:S(2)}, u32[]{:S(2)}) collective-permute-start(bf16[4,128,128]{2,1,0:T(8,128)(2,1)S(1)} %broadcast_select_fusion), channel_id=1, source_target_pairs={{0,8},{4,28},{8,16},{12,4},{16,24},{20,12},{24,0},{28,20},{1,9},{5... | collective-permute-start | bytes 393224 | tf_op jit(solution)/shard_map/ppermute | solution.py:284
  8.1 14.2 %collective-permute-start.6 = (bf16[3,128,128]{2,1,0:T(8,128)(2,1)S(1)}, bf16[3,128,128]{2,1,0:T(8,128)(2,1)S(1)}, u32[]{:S(2)}, u32[]{:S(2)}) collective-permute-start(bf16[3,128,128]{2,1,0:T(8,128)(2,1)S(1)} %slice_select_fusion), channel_id=1, source_target_pairs={{1,10},{2,9},{5,30},{6,29},{9,18},{10,17},{13,6},{14,5},{17,26},{1... | collective-permute-start | bytes 294920 | tf_op jit(solution)/shard_map/ppermute | solution.py:313
  13.5 2.6 %copy-start.7 = (s32[1,4,2,3]{1,2,3,0:T(2,128)S(1)}, s32[1,4,2,3]{1,2,3,0:T(2,128)}, u32[]{:S(2)}) copy-start(s32[1,4,2,3]{1,2,3,0:T(2,128)} %param.16) | copy-start | bytes 292
  13.5 6.5 %copy-start.4 = (bf16[1,4,128,128]{3,2,1,0:T(8,128)(2,1)S(1)}, bf16[1,4,128,128]{3,2,1,0:T(8,128)(2,1)}, u32[]{:S(2)}) copy-start(bf16[1,4,128,128]{3,2,1,0:T(8,128)(2,1)} %param.17) | copy-start | bytes 393220
  13.5 6.5 %copy-start.5 = (bf16[128,128]{1,0:T(8,128)(2,1)S(1)}, bf16[128,128]{1,0:T(8,128)(2,1)}, u32[]{:S(2)}) copy-start(bf16[128,128]{1,0:T(8,128)(2,1)} %k_weight.1) | copy-start | bytes 98308
  13.5 6.5 %copy-start.6 = (bf16[128,128]{1,0:T(8,128)(2,1)S(1)}, bf16[128,128]{1,0:T(8,128)(2,1)}, u32[]{:S(2)}) copy-start(bf16[128,128]{1,0:T(8,128)(2,1)} %v_weight.1) | copy-start | bytes 98308
  13.5 6.4 %copy-start.2 = (bf16[3,3,128,128]{3,2,1,0:T(8,128)(2,1)S(1)}, bf16[3,3,128,128]{3,2,1,0:T(8,128)(2,1)}, u32[]{:S(2)}) copy-start(bf16[3,3,128,128]{3,2,1,0:T(8,128)(2,1)} %conv_weight.1) | copy-start | bytes 884740
  13.6 6.4 %collective-permute-start.3 = (bf16[4,128,128]{2,1,0:T(8,128)(2,1)S(1)}, bf16[4,128,128]{2,1,0:T(8,128)(2,1)S(1)}, u32[]{:S(2)}, u32[]{:S(2)}) collective-permute-start(bf16[4,128,128]{2,1,0:T(8,128)(2,1)S(1)} %get-tuple-element.51), channel_id=1, source_target_pairs={{1,2},{2,1},{5,6},{6,5},{9,10},{10,9},{13,14},{14,13},{17,18},{18,... | collective-permute-start | bytes 393224 | tf_op jit(solution)/shard_map/ppermute | solution.py:20
  16.3 3.7 %copy-start.3 = (bf16[128,128]{1,0:T(8,128)(2,1)S(1)}, bf16[128,128]{1,0:T(8,128)(2,1)}, u32[]{:S(2)}) copy-start(bf16[128,128]{1,0:T(8,128)(2,1)} %q_weight.3) | copy-start | bytes 98308
  16.3 1.4 %collective-permute-start.2 = (bf16[4,128,128]{2,1,0:T(8,128)(2,1)S(1)}, bf16[4,128,128]{2,1,0:T(8,128)(2,1)S(1)}, u32[]{:S(2)}, u32[]{:S(2)}) collective-permute-start(bf16[4,128,128]{2,1,0:T(8,128)(2,1)S(1)} %get-tuple-element.50), channel_id=1, source_target_pairs={{0,1},{2,3},{1,0},{3,2},{4,5},{6,7},{5,4},{7,6},{8,9},{10,11},{9,8... | collective-permute-start | bytes 393224 | tf_op jit(solution)/shard_map/ppermute | solution.py:15
  16.4 5.9 %collective-permute-start.5 = (bf16[3,128,128]{2,1,0:T(8,128)(2,1)S(1)}, bf16[3,128,128]{2,1,0:T(8,128)(2,1)S(1)}, u32[]{:S(2)}, u32[]{:S(2)}) collective-permute-start(bf16[3,128,128]{2,1,0:T(8,128)(2,1)S(1)} %slice_select_fusion.1), channel_id=1, source_target_pairs={{0,1},{2,3},{1,0},{3,2},{4,5},{6,7},{5,4},{7,6},{8,9},{10,11},{9,8... | collective-permute-start | bytes 294920 | tf_op jit(solution)/shard_map/ppermute | solution.py:15
  26.2 1.4 %collective-permute-start.7 = (bf16[4,128,128]{2,1,0:T(8,128)(2,1)S(1)}, bf16[4,128,128]{2,1,0:T(8,128)(2,1)S(1)}, u32[]{:S(2)}, u32[]{:S(2)}) collective-permute-start(bf16[4,128,128]{2,1,0:T(8,128)(2,1)S(1)} %get-tuple-element.40), channel_id=1, source_target_pairs={{0,1},{2,3},{1,0},{3,2},{4,5},{6,7},{5,4},{7,6},{8,9},{10,11},{9,8... | collective-permute-start | bytes 393224 | tf_op jit(solution)/shard_map/ppermute | solution.py:15
  27.7 11.6 %collective-permute-start.9 = (bf16[4,128,128]{2,1,0:T(8,128)(2,1)S(1)}, bf16[4,128,128]{2,1,0:T(8,128)(2,1)S(1)}, u32[]{:S(2)}, u32[]{:S(2)}) collective-permute-start(bf16[4,128,128]{2,1,0:T(8,128)(2,1)S(1)} %fusion.2), channel_id=1, source_target_pairs={{0,24},{4,12},{8,0},{12,20},{16,8},{20,28},{24,16},{28,4},{1,25},{... | collective-permute-start | bytes 393224 | tf_op jit(solution)/shard_map/ppermute | solution.py:284
  29.7 7.0 %collective-permute-start.8 = (bf16[2,128,128]{2,1,0:T(8,128)(2,1)S(1)}, bf16[2,128,128]{2,1,0:T(8,128)(2,1)S(1)}, u32[]{:S(2)}, u32[]{:S(2)}) collective-permute-start(bf16[2,128,128]{2,1,0:T(8,128)(2,1)S(1)} %slice_select_fusion.3), channel_id=1, source_target_pairs={{1,2},{2,1},{5,6},{6,5},{9,10},{10,9},{13,14},{14,13},{17,18},{18,... | collective-permute-start | bytes 196616 | tf_op jit(solution)/shard_map/ppermute | solution.py:20
  32.8 6.5 %collective-permute-start.10 = (bf16[2,128,128]{2,1,0:T(8,128)(2,1)S(1)}, bf16[2,128,128]{2,1,0:T(8,128)(2,1)S(1)}, u32[]{:S(2)}, u32[]{:S(2)}) collective-permute-start(bf16[2,128,128]{2,1,0:T(8,128)(2,1)S(1)} %slice_select_fusion.2), channel_id=1, source_target_pairs={{1,26},{2,25},{5,14},{6,13},{9,2},{10,1},{13,22},{14,21},{17,10},{... | collective-permute-start | bytes 196616 | tf_op jit(solution)/shard_map/ppermute | solution.py:313
  36.8 7.0 %collective-permute-start.12 = (bf16[4,128,128]{2,1,0:T(8,128)(2,1)S(1)}, bf16[4,128,128]{2,1,0:T(8,128)(2,1)S(1)}, u32[]{:S(2)}, u32[]{:S(2)}) collective-permute-start(bf16[4,128,128]{2,1,0:T(8,128)(2,1)S(1)} %fusion.1), channel_id=1, source_target_pairs={{0,8},{4,28},{8,16},{12,4},{16,24},{20,12},{24,0},{28,20},{1,9},{5... | collective-permute-start | bytes 393224 | tf_op jit(solution)/shard_map/ppermute | solution.py:284
  39.4 5.0 %collective-permute-start.11 = (bf16[4,128,128]{2,1,0:T(8,128)(2,1)S(1)}, bf16[4,128,128]{2,1,0:T(8,128)(2,1)S(1)}, u32[]{:S(2)}, u32[]{:S(2)}) collective-permute-start(bf16[4,128,128]{2,1,0:T(8,128)(2,1)S(1)} %add_convert_fusion.1), channel_id=1, source_target_pairs={{0,4},{4,0},{8,12},{12,8},{16,20},{20,16},{24,28},{28,24},{1,5},{5... | collective-permute-start | bytes 393224 | tf_op jit(solution)/shard_map/ppermute | solution.py:284

commit v17 on v16

--- a/solution.py
+++ b/solution.py
@@ -438,8 +438,8 @@
     first = center[1] + spread(within[MARGIN:], odd_row) + spread(first_between, even_row)
     first = first.astype(half)
     from_first = routed(first, 2, -2)
-    from_second, second_between, _ = lax.optimization_barrier(
-        (from_second, second_between, first)
+    from_second, second_between, _, grad_own = lax.optimization_barrier(
+        (from_second, second_between, first, grad_own)
     )
     from_second = from_second.astype(full) + spread(second_between, even_row)
     for_pair = jnp.where(first_near, first.astype(full), 0.0) + jnp.where(

time: 45.6 us -> 46.1 us (1.011)
  waiting for transfers between devices: 7.2 us -> 7.68 us
    ppermute x6, waiting for transfers between devices: 0.55 us -> 2.37 us  [routed(): return lax.ppermute(value, 'cam', pairs)]
    ppermute x3, waiting for transfers between devices: 2.01 us -> 0.68 us  [swap_within(): return lax.ppermute(value, 'row', pairs + [(j, i) for i, j in pairs])]
where the time goes in v17:
time: 46.1 us; the launch traced here: 45.6 us
  starting transfers between devices  25.2 us (55%)
  Pallas kernels  7.98 us (17%)
  waiting for transfers between devices  7.68 us (17%)
  local copies, waits for them, and re-layouts  2.3 us (5%)
  other arithmetic  1.42 us (3%)
  between operations  1 us (2%)
    ppermute x6, starting transfers between devices, routed(): return lax.ppermute(value, 'cam', pairs)  10.2 us
    ppermute x2, starting transfers between devices, across(): return lax.ppermute(value, ('cam', 'row'), pairs)  9.26 us
    pallas_call x3, Pallas kernels, on_device(): pl.pallas_call(kernel, out_shape=tuple((jax.ShapeDtypeStruct(*one) for on...  7.98 us
    ppermute x2, starting transfers between devices, swap_between(): return lax.ppermute(value, 'row', pairs + [(j, i) for i, j in pairs])  5.08 us
    ppermute x2, waiting for transfers between devices, across(): return lax.ppermute(value, ('cam', 'row'), pairs)  2.37 us
    ppermute x6, waiting for transfers between devices, routed(): return lax.ppermute(value, 'cam', pairs)  2.37 us
    ppermute x2, waiting for transfers between devices, swap_between(): return lax.ppermute(value, 'row', pairs + [(j, i) for i, j in pairs])  2.26 us
  transfers between devices with their start and end apart: 13, of which 5 were waited for; matrix products, arithmetic and copies ran while one was open for 5% of the time, Pallas kernels for 9%

profile of v17, /device:TPU:1, one launch (start us, length us, event | category | flops | bytes accessed | tf_op | source)
XLA Modules:
  0.0 45.6 jit_solution(17979906279613836886)
XLA Ops:
  0.7 2.1 %collective-permute-start.1 = (bf16[4,128,128]{2,1,0:T(8,128)(2,1)}, bf16[4,128,128]{2,1,0:T(8,128)(2,1)S(1)}, u32[]{:S(2)}, u32[]{:S(2)}) collective-permute-start(bf16[4,128,128]{2,1,0:T(8,128)(2,1)} %bitcast.26), channel_id=1, source_target_pairs={{0,4},{4,0},{8,12},{12,8},{16,20},{20,16},{24,28},{28,24},{1,5},{5... | collective-permute-start | bytes 393224 | tf_op jit(solution)/shard_map/ppermute | solution.py:284
  2.8 3.3 %collective-permute-start = (bf16[4,128,128]{2,1,0:T(8,128)(2,1)}, bf16[4,128,128]{2,1,0:T(8,128)(2,1)S(1)}, u32[]{:S(2)}, u32[]{:S(2)}) collective-permute-start(bf16[4,128,128]{2,1,0:T(8,128)(2,1)} %bitcast.27), channel_id=1, source_target_pairs={{0,24},{4,12},{8,0},{12,20},{16,8},{20,28},{24,16},{28,4},{1,25},{... | collective-permute-start | bytes 393224 | tf_op jit(solution)/shard_map/ppermute | solution.py:284
  6.1 0.8 %slice_bitcast_fusion.1 = (bf16[1,128,128]{2,1,0:T(8,128)(2,1)S(1)}, bf16[1,128,128]{2,1,0:T(8,128)(2,1)S(1)}) fusion(bf16[1,4,128,128]{3,2,1,0:T(8,128)(2,1)} %param.9), kind=kLoop, calls=%fused_computation.28 | loop fusion | bytes 131072 | tf_op jit(solution)/shard_map/slice | solution.py:327
  6.9 0.7 %copy-done.8 = s32[8,2]{0,1:T(2,128)S(1)} copy-done((s32[8,2]{0,1:T(2,128)S(1)}, s32[8,2]{0,1:T(2,128)}, u32[]{:S(2)}) %copy-start.8) | copy-done | bytes 88
  8.1 5.3 %collective-permute-start.6 = (bf16[3,128,128]{2,1,0:T(8,128)(2,1)S(1)}, bf16[3,128,128]{2,1,0:T(8,128)(2,1)S(1)}, u32[]{:S(2)}, u32[]{:S(2)}) collective-permute-start(bf16[3,128,128]{2,1,0:T(8,128)(2,1)S(1)} %slice_select_fusion), channel_id=1, source_target_pairs={{1,10},{2,9},{5,30},{6,29},{9,18},{10,17},{13,6},{14,5},{17,26},{1... | collective-permute-start | bytes 294920 | tf_op jit(solution)/shard_map/ppermute | solution.py:313
  13.6 2.1 %collective-permute-start.3 = (bf16[4,128,128]{2,1,0:T(8,128)(2,1)S(1)}, bf16[4,128,128]{2,1,0:T(8,128)(2,1)S(1)}, u32[]{:S(2)}, u32[]{:S(2)}) collective-permute-start(bf16[4,128,128]{2,1,0:T(8,128)(2,1)S(1)} %get-tuple-element.53), channel_id=1, source_target_pairs={{1,2},{2,1},{5,6},{6,5},{9,10},{10,9},{13,14},{14,13},{17,18},{18,... | collective-permute-start | bytes 393224 | tf_op jit(solution)/shard_map/ppermute | solution.py:20
  15.6 0.2 dynamic-slice_reduce_fusion
  16.0 0.1 reshape.64
  16.1 0.1 copy.14
  16.2 0.1 reshape.60
  16.4 0.5 %collective-permute-start.5 = (bf16[3,128,128]{2,1,0:T(8,128)(2,1)S(1)}, bf16[3,128,128]{2,1,0:T(8,128)(2,1)S(1)}, u32[]{:S(2)}, u32[]{:S(2)}) collective-permute-start(bf16[3,128,128]{2,1,0:T(8,128)(2,1)S(1)} %slice_select_fusion.1), channel_id=1, source_target_pairs={{0,1},{2,3},{1,0},{3,2},{4,5},{6,7},{5,4},{7,6},{8,9},{10,11},{9,8... | collective-permute-start | bytes 294920 | tf_op jit(solution)/shard_map/ppermute | solution.py:15
  17.0 0.7 %collective-permute-done.2.within = bf16[4,128,128]{2,1,0:T(8,128)(2,1)S(1)} collective-permute-done((bf16[4,128,128]{2,1,0:T(8,128)(2,1)S(1)}, bf16[4,128,128]{2,1,0:T(8,128)(2,1)S(1)}, u32[]{:S(2)}, u32[]{:S(2)}) %collective-permute-start.2) | collective-permute-done | bytes 131104 | tf_op jit(solution)/shard_map/ppermute | solution.py:15
  17.7 2.3 %collective-permute-done.3.between = bf16[4,128,128]{2,1,0:T(8,128)(2,1)S(1)} collective-permute-done((bf16[4,128,128]{2,1,0:T(8,128)(2,1)S(1)}, bf16[4,128,128]{2,1,0:T(8,128)(2,1)S(1)}, u32[]{:S(2)}, u32[]{:S(2)}) %collective-permute-start.3) | collective-permute-done | bytes 131104 | tf_op jit(solution)/shard_map/ppermute | solution.py:20
  20.0 2.3 %shard_map.104 = (bf16[4,128,128]{2,1,0:T(8,128)(2,1)S(1)}, bf16[8,256,128]{2,1,0:T(8,128)(2,1)S(1)}, f32[4,384,128]{2,1,0:T(8,128)S(1)}, f32[4,384,128]{2,1,0:T...) custom-call(s32[31]{0:T(128)S(1)} %pad_add_fusion.scalars, bf16[4,128,128]{2,1,0:T(8,128)(2,1)S(1)} %bitcast.28, ...), custom_call_target="tpu_custom_call" | custom-call | flops 1000000 | bytes 1000 | tf_op jit(solution)/shard_map/pallas_call | solution.py:245
  22.3 3.9 %shard_map.105 = (bf16[4,128,128]{2,1,0:T(8,128)(2,1)S(1)}, bf16[4,128,128]{2,1,0:T(8,128)(2,1)S(1)}, bf16[4,128,128]{2,1,0:T(8,128)(2,1)S(1)}, f32[2,4,128,128]...) custom-call(s32[31]{0:T(128)S(1)} %pad_add_fusion.scalars, ...), custom_call_target="tpu_custom_call" | custom-call | flops 1500000000 | bytes 1500000 | tf_op jit(solution)/shard_map/pallas_call | solution.py:245
  26.3 1.8 %shard_map.106 = (bf16[4,128,128]{2,1,0:T(8,128)(2,1)}, f32[4,128,128]{2,1,0:T(8,128)S(1)}) custom-call(s32[31]{0:T(128)S(1)} %pad_add_fusion.scalars, bf16[4,768,128]{2,1,0:T(8,128)(2,1)S(1)} %get-tuple-element.34.probs, bf16[4,768,128]{2,1,0:T(8,128)(2,1)S(1)} %get-tuple-element.35.grad_scores, bf16[8,256,128]{2,1,0:T(8,128)(2,1)S(1)} %get-tuple-element.36.kv_t, ...), custom_call_target="tpu_custom_call" | custom-call | flops 1000000 | bytes 1000 | tf_op jit(solution)/shard_map/pallas_call | solution.py:245
  28.2 2.0 %collective-permute-start.8 = (bf16[4,128,128]{2,1,0:T(8,128)(2,1)S(1)}, bf16[4,128,128]{2,1,0:T(8,128)(2,1)S(1)}, u32[]{:S(2)}, u32[]{:S(2)}) collective-permute-start(bf16[4,128,128]{2,1,0:T(8,128)(2,1)S(1)} %fusion), channel_id=1, source_target_pairs={{0,24},{4,12},{8,0},{12,20},{16,8},{20,28},{24,16},{28,4},{1,25},{... | collective-permute-start | bytes 393224 | tf_op jit(solution)/shard_map/ppermute | solution.py:284
  30.2 3.0 %collective-permute-start.10 = (bf16[2,128,128]{2,1,0:T(8,128)(2,1)S(1)}, bf16[2,128,128]{2,1,0:T(8,128)(2,1)S(1)}, u32[]{:S(2)}, u32[]{:S(2)}) collective-permute-start(bf16[2,128,128]{2,1,0:T(8,128)(2,1)S(1)} %slice_select_fusion.2), channel_id=1, source_target_pairs={{1,2},{2,1},{5,6},{6,5},{9,10},{10,9},{13,14},{14,13},{17,18},{18,... | collective-permute-start | bytes 196616 | tf_op jit(solution)/shard_map/ppermute | solution.py:20
  33.3 3.9 %collective-permute-start.9 = (bf16[2,128,128]{2,1,0:T(8,128)(2,1)S(1)}, bf16[2,128,128]{2,1,0:T(8,128)(2,1)S(1)}, u32[]{:S(2)}, u32[]{:S(2)}) collective-permute-start(bf16[2,128,128]{2,1,0:T(8,128)(2,1)S(1)} %slice_select_fusion.3), channel_id=1, source_target_pairs={{1,26},{2,25},{5,14},{6,13},{9,2},{10,1},{13,22},{14,21},{17,10},{... | collective-permute-start | bytes 196616 | tf_op jit(solution)/shard_map/ppermute | solution.py:313
  37.4 2.4 %collective-permute-done.9 = bf16[2,128,128]{2,1,0:T(8,128)(2,1)S(1)} collective-permute-done((bf16[2,128,128]{2,1,0:T(8,128)(2,1)S(1)}, bf16[2,128,128]{2,1,0:T(8,128)(2,1)S(1)}, u32[]{:S(2)}, u32[]{:S(2)}) %collective-permute-start.9) | collective-permute-done | bytes 65568 | tf_op jit(solution)/shard_map/ppermute | solution.py:313
  39.9 2.6 %collective-permute-start.11 = (bf16[4,128,128]{2,1,0:T(8,128)(2,1)S(1)}, bf16[4,128,128]{2,1,0:T(8,128)(2,1)S(1)}, u32[]{:S(2)}, u32[]{:S(2)}) collective-permute-start(bf16[4,128,128]{2,1,0:T(8,128)(2,1)S(1)} %add_convert_fusion.1), channel_id=1, source_target_pairs={{0,4},{4,0},{8,12},{12,8},{16,20},{20,16},{24,28},{28,24},{1,5},{5... | collective-permute-start | bytes 393224 | tf_op jit(solution)/shard_map/ppermute | solution.py:284
  42.5 0.5 %collective-permute-done.12 = bf16[4,128,128]{2,1,0:T(8,128)(2,1)S(1)} collective-permute-done((bf16[4,128,128]{2,1,0:T(8,128)(2,1)S(1)}, bf16[4,128,128]{2,1,0:T(8,128)(2,1)S(1)}, u32[]{:S(2)}, u32[]{:S(2)}) %collective-permute-start.12) | collective-permute-done | bytes 131104 | tf_op jit(solution)/shard_map/ppermute | solution.py:284
  43.0 1.9 %collective-permute-done.11 = bf16[4,128,128]{2,1,0:T(8,128)(2,1)S(1)} collective-permute-done((bf16[4,128,128]{2,1,0:T(8,128)(2,1)S(1)}, bf16[4,128,128]{2,1,0:T(8,128)(2,1)S(1)}, u32[]{:S(2)}, u32[]{:S(2)}) %collective-permute-start.11) | collective-permute-done | bytes 131104 | tf_op jit(solution)/shard_map/ppermute | solution.py:284
  44.9 0.7 %fusion.3 = bf16[1,4,128,128]{3,2,1,0:T(8,128)(2,1)} fusion(bf16[4,128,128]{2,1,0:T(8,128)(2,1)S(1)} %collective-permute-done.12, f32[2,128,128]{2,1,0:T(8,128)S(1)} %get-tuple-element.63, f32[2,128,128]{2,1,0:T(8,128)S(1)} %get-tuple-element.62, bf16[4,128,128]{2,1,0:T(8,128)(2,1)S(1)} %collective-permute-done.8, f32[4,128,128]{2,1,0:T(8,128)S(1)} %get-tuple-element.47, ...), kind=kLoop, calls=%fused_computation.18 | loop fusion | flops 720896 | bytes 1048832 | tf_op jit(solution)/shard_map/broadcast_in_dim | solution.py:452
  (57 shorter events, 1.3 us)
Async XLA Ops:
  0.6 15.0 %copy-start = (s32[8,2]{0,1:T(2,128)S(1)}, s32[8,2]{0,1:T(2,128)}, u32[]{:S(2)}) copy-start(s32[8,2]{0,1:T(2,128)} %param.15) | copy-start | bytes 196
  0.6 7.3 %copy-start.1 = (bf16[1,4,128,128]{3,2,1,0:T(8,128)(2,1)S(1)}, bf16[1,4,128,128]{3,2,1,0:T(8,128)(2,1)}, u32[]{:S(2)}) copy-start(bf16[1,4,128,128]{3,2,1,0:T(8,128)(2,1)} %param.9) | copy-start | bytes 393220
  0.7 7.3 %collective-permute-start.1 = (bf16[4,128,128]{2,1,0:T(8,128)(2,1)}, bf16[4,128,128]{2,1,0:T(8,128)(2,1)S(1)}, u32[]{:S(2)}, u32[]{:S(2)}) collective-permute-start(bf16[4,128,128]{2,1,0:T(8,128)(2,1)} %bitcast.26), channel_id=1, source_target_pairs={{0,4},{4,0},{8,12},{12,8},{16,20},{20,16},{24,28},{28,24},{1,5},{5... | collective-permute-start | bytes 393224 | tf_op jit(solution)/shard_map/ppermute | solution.py:284
  2.8 10.6 %collective-permute-start = (bf16[4,128,128]{2,1,0:T(8,128)(2,1)}, bf16[4,128,128]{2,1,0:T(8,128)(2,1)S(1)}, u32[]{:S(2)}, u32[]{:S(2)}) collective-permute-start(bf16[4,128,128]{2,1,0:T(8,128)(2,1)} %bitcast.27), channel_id=1, source_target_pairs={{0,24},{4,12},{8,0},{12,20},{16,8},{20,28},{24,16},{28,4},{1,25},{... | collective-permute-start | bytes 393224 | tf_op jit(solution)/shard_map/ppermute | solution.py:284
  6.9 0.7 %copy-start.8 = (s32[8,2]{0,1:T(2,128)S(1)}, s32[8,2]{0,1:T(2,128)}, u32[]{:S(2)}) copy-start(s32[8,2]{0,1:T(2,128)} %param.14) | copy-start | bytes 196
  8.0 8.4 %collective-permute-start.4 = (bf16[4,128,128]{2,1,0:T(8,128)(2,1)S(1)}, bf16[4,128,128]{2,1,0:T(8,128)(2,1)S(1)}, u32[]{:S(2)}, u32[]{:S(2)}) collective-permute-start(bf16[4,128,128]{2,1,0:T(8,128)(2,1)S(1)} %broadcast_select_fusion), channel_id=1, source_target_pairs={{0,8},{4,28},{8,16},{12,4},{16,24},{20,12},{24,0},{28,20},{1,9},{5... | collective-permute-start | bytes 393224 | tf_op jit(solution)/shard_map/ppermute | solution.py:284
  8.1 14.2 %collective-permute-start.6 = (bf16[3,128,128]{2,1,0:T(8,128)(2,1)S(1)}, bf16[3,128,128]{2,1,0:T(8,128)(2,1)S(1)}, u32[]{:S(2)}, u32[]{:S(2)}) collective-permute-start(bf16[3,128,128]{2,1,0:T(8,128)(2,1)S(1)} %slice_select_fusion), channel_id=1, source_target_pairs={{1,10},{2,9},{5,30},{6,29},{9,18},{10,17},{13,6},{14,5},{17,26},{1... | collective-permute-start | bytes 294920 | tf_op jit(solution)/shard_map/ppermute | solution.py:313
  13.5 2.6 %copy-start.7 = (s32[1,4,2,3]{1,2,3,0:T(2,128)S(1)}, s32[1,4,2,3]{1,2,3,0:T(2,128)}, u32[]{:S(2)}) copy-start(s32[1,4,2,3]{1,2,3,0:T(2,128)} %param.16) | copy-start | bytes 292
  13.5 6.5 %copy-start.4 = (bf16[1,4,128,128]{3,2,1,0:T(8,128)(2,1)S(1)}, bf16[1,4,128,128]{3,2,1,0:T(8,128)(2,1)}, u32[]{:S(2)}) copy-start(bf16[1,4,128,128]{3,2,1,0:T(8,128)(2,1)} %param.17) | copy-start | bytes 393220
  13.5 6.5 %copy-start.5 = (bf16[128,128]{1,0:T(8,128)(2,1)S(1)}, bf16[128,128]{1,0:T(8,128)(2,1)}, u32[]{:S(2)}) copy-start(bf16[128,128]{1,0:T(8,128)(2,1)} %k_weight.1) | copy-start | bytes 98308
  13.5 6.5 %copy-start.6 = (bf16[128,128]{1,0:T(8,128)(2,1)S(1)}, bf16[128,128]{1,0:T(8,128)(2,1)}, u32[]{:S(2)}) copy-start(bf16[128,128]{1,0:T(8,128)(2,1)} %v_weight.1) | copy-start | bytes 98308
  13.5 6.4 %copy-start.2 = (bf16[3,3,128,128]{3,2,1,0:T(8,128)(2,1)S(1)}, bf16[3,3,128,128]{3,2,1,0:T(8,128)(2,1)}, u32[]{:S(2)}) copy-start(bf16[3,3,128,128]{3,2,1,0:T(8,128)(2,1)} %conv_weight.1) | copy-start | bytes 884740
  13.6 6.4 %collective-permute-start.3 = (bf16[4,128,128]{2,1,0:T(8,128)(2,1)S(1)}, bf16[4,128,128]{2,1,0:T(8,128)(2,1)S(1)}, u32[]{:S(2)}, u32[]{:S(2)}) collective-permute-start(bf16[4,128,128]{2,1,0:T(8,128)(2,1)S(1)} %get-tuple-element.53), channel_id=1, source_target_pairs={{1,2},{2,1},{5,6},{6,5},{9,10},{10,9},{13,14},{14,13},{17,18},{18,... | collective-permute-start | bytes 393224 | tf_op jit(solution)/shard_map/ppermute | solution.py:20
  16.3 3.7 %copy-start.3 = (bf16[128,128]{1,0:T(8,128)(2,1)S(1)}, bf16[128,128]{1,0:T(8,128)(2,1)}, u32[]{:S(2)}) copy-start(bf16[128,128]{1,0:T(8,128)(2,1)} %q_weight.3) | copy-start | bytes 98308
  16.3 1.4 %collective-permute-start.2 = (bf16[4,128,128]{2,1,0:T(8,128)(2,1)S(1)}, bf16[4,128,128]{2,1,0:T(8,128)(2,1)S(1)}, u32[]{:S(2)}, u32[]{:S(2)}) collective-permute-start(bf16[4,128,128]{2,1,0:T(8,128)(2,1)S(1)} %get-tuple-element.52), channel_id=1, source_target_pairs={{0,1},{2,3},{1,0},{3,2},{4,5},{6,7},{5,4},{7,6},{8,9},{10,11},{9,8... | collective-permute-start | bytes 393224 | tf_op jit(solution)/shard_map/ppermute | solution.py:15
  16.4 5.9 %collective-permute-start.5 = (bf16[3,128,128]{2,1,0:T(8,128)(2,1)S(1)}, bf16[3,128,128]{2,1,0:T(8,128)(2,1)S(1)}, u32[]{:S(2)}, u32[]{:S(2)}) collective-permute-start(bf16[3,128,128]{2,1,0:T(8,128)(2,1)S(1)} %slice_select_fusion.1), channel_id=1, source_target_pairs={{0,1},{2,3},{1,0},{3,2},{4,5},{6,7},{5,4},{7,6},{8,9},{10,11},{9,8... | collective-permute-start | bytes 294920 | tf_op jit(solution)/shard_map/ppermute | solution.py:15
  26.2 1.9 %collective-permute-start.7 = (bf16[4,128,128]{2,1,0:T(8,128)(2,1)S(1)}, bf16[4,128,128]{2,1,0:T(8,128)(2,1)S(1)}, u32[]{:S(2)}, u32[]{:S(2)}) collective-permute-start(bf16[4,128,128]{2,1,0:T(8,128)(2,1)S(1)} %get-tuple-element.40), channel_id=1, source_target_pairs={{0,1},{2,3},{1,0},{3,2},{4,5},{6,7},{5,4},{7,6},{8,9},{10,11},{9,8... | collective-permute-start | bytes 393224 | tf_op jit(solution)/shard_map/ppermute | solution.py:15
  28.2 11.6 %collective-permute-start.8 = (bf16[4,128,128]{2,1,0:T(8,128)(2,1)S(1)}, bf16[4,128,128]{2,1,0:T(8,128)(2,1)S(1)}, u32[]{:S(2)}, u32[]{:S(2)}) collective-permute-start(bf16[4,128,128]{2,1,0:T(8,128)(2,1)S(1)} %fusion), channel_id=1, source_target_pairs={{0,24},{4,12},{8,0},{12,20},{16,8},{20,28},{24,16},{28,4},{1,25},{... | collective-permute-start | bytes 393224 | tf_op jit(solution)/shard_map/ppermute | solution.py:284
  30.2 7.0 %collective-permute-start.10 = (bf16[2,128,128]{2,1,0:T(8,128)(2,1)S(1)}, bf16[2,128,128]{2,1,0:T(8,128)(2,1)S(1)}, u32[]{:S(2)}, u32[]{:S(2)}) collective-permute-start(bf16[2,128,128]{2,1,0:T(8,128)(2,1)S(1)} %slice_select_fusion.2), channel_id=1, source_target_pairs={{1,2},{2,1},{5,6},{6,5},{9,10},{10,9},{13,14},{14,13},{17,18},{18,... | collective-permute-start | bytes 196616 | tf_op jit(solution)/shard_map/ppermute | solution.py:20
  33.3 6.5 %collective-permute-start.9 = (bf16[2,128,128]{2,1,0:T(8,128)(2,1)S(1)}, bf16[2,128,128]{2,1,0:T(8,128)(2,1)S(1)}, u32[]{:S(2)}, u32[]{:S(2)}) collective-permute-start(bf16[2,128,128]{2,1,0:T(8,128)(2,1)S(1)} %slice_select_fusion.3), channel_id=1, source_target_pairs={{1,26},{2,25},{5,14},{6,13},{9,2},{10,1},{13,22},{14,21},{17,10},{... | collective-permute-start | bytes 196616 | tf_op jit(solution)/shard_map/ppermute | solution.py:313
  37.3 5.7 %collective-permute-start.12 = (bf16[4,128,128]{2,1,0:T(8,128)(2,1)S(1)}, bf16[4,128,128]{2,1,0:T(8,128)(2,1)S(1)}, u32[]{:S(2)}, u32[]{:S(2)}) collective-permute-start(bf16[4,128,128]{2,1,0:T(8,128)(2,1)S(1)} %fusion.2), channel_id=1, source_target_pairs={{0,8},{4,28},{8,16},{12,4},{16,24},{20,12},{24,0},{28,20},{1,9},{5... | collective-permute-start | bytes 393224 | tf_op jit(solution)/shard_map/ppermute | solution.py:284
  39.9 5.0 %collective-permute-start.11 = (bf16[4,128,128]{2,1,0:T(8,128)(2,1)S(1)}, bf16[4,128,128]{2,1,0:T(8,128)(2,1)S(1)}, u32[]{:S(2)}, u32[]{:S(2)}) collective-permute-start(bf16[4,128,128]{2,1,0:T(8,128)(2,1)S(1)} %add_convert_fusion.1), channel_id=1, source_target_pairs={{0,4},{4,0},{8,12},{12,8},{16,20},{20,16},{24,28},{28,24},{1,5},{5... | collective-permute-start | bytes 393224 | tf_op jit(solution)/shard_map/ppermute | solution.py:284
